TPU v7x, 32 devices: a whole 2x2x4 slice. The times are simulated.
32 devices in a mesh: row: 16 (over z, y, core), col: 2 (over x).
Axes of the slice: x: 2, y: 2, z: 4, core: 2. Of those that a mesh axis runs over, the one named last changes fastest.
Arguments:
- tokens: bfloat16 [2048, 2048], P('row'), may hold values from -6 to 6
- w_query: bfloat16 [2048, 1280], P('row', 'col'), may hold values from -0.125 to 0.125
- key_value_weight: bfloat16 [2048, 640], P('row'), may hold values from -0.125 to 0.125
- w_out: bfloat16 [1280, 2048], P('col', 'row'), may hold values from -1.25 to 1.25
- w_gate: bfloat16 [2048, 5120], P('row', 'col'), may hold values from -0.125 to 0.125
- w_up: bfloat16 [2048, 5120], P('row', 'col'), may hold values from -0.125 to 0.125
- w_down: bfloat16 [5120, 2048], P('col', 'row'), may hold values from -0.078125 to 0.078125
- attn_gain: float32 [2048], replicated, may hold values from 0.5 to 1.5
- ffn_gain: float32 [2048], replicated, may hold values from 0.5 to 1.5
- query_gain: float32 [64], replicated, may hold values from 0.25 to 1.75
- key_gain: float32 [64], replicated, may hold values from 0.25 to 1.75
- segments: int32 [2048], replicated, may hold values from -1 to 2047, as said below
- positions: int32 [2048], P('row'), may hold values from 0 to 2047, as said below
- out_grad: bfloat16 [2048, 2048], P('row'), may hold values from -6 to 6
Outputs:
- output: bfloat16 [2048, 2048], P('row')
- input_grad: float32 [2048, 2048], P('row')
- grad_query: float32 [2048, 1280], P('row', 'col')
- grad_keyval: float32 [2048, 640], P('row')
- grad_out: float32 [1280, 2048], P('col', 'row')
- grad_gate: float32 [2048, 5120], P('row', 'col')
- grad_up: float32 [2048, 5120], P('row', 'col')
- grad_down: float32 [5120, 2048], P('col', 'row')
- grad_attn_gain: float32 [2048], P('row')
- grad_ffn_gain: float32 [2048], P('row')
- grad_query_gain: float32 [64], P('row')
- grad_key_gain: float32 [64], P('row')
Inputs may be any that keep to these rules, and one draw needn't show every extreme that they name: `segments`: the tokens form 2048 // 2048 sequences of 2048 tokens in order, and documents never cross them. Among live tokens the numbers never fall and rise by at most one from token to token; the last document is numbered 2048 - 1. Each sequence ends in padding (-1) of at least one token and fewer than 32, and holds one document of 1152 to 1536 tokens. Within a document positions rise by one from token to token; padding has position 0.
All inputs are finite; a program needn't handle non-finite values.
Results may differ from a plain program's by a relative error of at most 0.017.
Values may be sent and summed in bfloat16 or wider, within the bound.
No kernel may reach another device: no remote copies, remote signals or barrier semaphores. Data moves between devices by JAX's collectives and lax.ppermute only.
A program may use at most 192 MiB of HBM per device.

v0:
```python
import math

import jax
import jax.numpy as jnp
from jax import lax
from jax.sharding import PartitionSpec as P

SEQ_MAX = 4096


EPSILON = 1e-06
SCALE = 0.125
NEGATIVE = -1e30


def from_behind(block, axis, distance):
    devices = range(lax.axis_size(axis))
    route = [(i - distance, i) for i in devices if i - distance in devices]
    return lax.ppermute(block, axis, route)


def tables(positions, head_dim):
    halves = head_dim // 2
    inverse = jnp.exp(jnp.arange(halves, dtype=jnp.float32) * (-2.0 * math.log(10000.0) / head_dim))
    angles = positions.astype(jnp.float32)[:, None] * inverse[None, :]
    return (jnp.cos(angles)[:, None, :], jnp.sin(angles)[:, None, :])


def apply_rotation(vectors, cosine_table, sine_table):
    halves = vectors.shape[-1] // 2
    first_half = vectors[..., :halves]
    second_half = vectors[..., halves:]
    return jnp.concatenate(
        [
            first_half * cosine_table - second_half * sine_table,
            second_half * cosine_table + first_half * sine_table,
        ],
        axis=-1,
    )


def rotate_back(grads_in, cosine_table, sine_table):
    halves = grads_in.shape[-1] // 2
    first_half = grads_in[..., :halves]
    second_half = grads_in[..., halves:]
    return jnp.concatenate(
        [
            first_half * cosine_table + second_half * sine_table,
            second_half * cosine_table - first_half * sine_table,
        ],
        axis=-1,
    )


def norm_forward(vectors, gains):
    scaler = lax.rsqrt(jnp.mean(vectors * vectors, axis=-1, keepdims=True) + EPSILON)
    return (vectors * scaler * gains, scaler)


def norm_backward(vectors, scaler, gains, grads_in):
    scaled = grads_in * gains
    inner_mean = jnp.mean(scaled * vectors, axis=-1, keepdims=True)
    grad_vec = scaler * scaled - vectors * (scaler * scaler * scaler) * inner_mean
    return (grad_vec, grads_in * (vectors * scaler))


def allowed(seg_query, idx_query, seg_key, idx_key):
    same_doc = (
        (seg_query[:, None] == seg_key[None, :])
        & (idx_key[None, :] <= idx_query[:, None])
        & (seg_key[None, :] >= 0)
    )
    return same_doc | (idx_key[None, :] == idx_query[:, None])


def body(
    tokens,
    w_query,
    key_value_weight,
    w_out,
    w_gate,
    w_up,
    w_down,
    attn_gain,
    ffn_gain,
    query_gain,
    key_gain,
    segments,
    positions,
    out_grad,
):
    tok_rows = tokens.shape[0]
    row_count = lax.axis_size("row")
    row_index = lax.axis_index("row")
    col_index = lax.axis_index("col")
    all_rows = tok_rows * row_count
    seq_len = min(SEQ_MAX, all_rows)
    span = seq_len // tok_rows
    buf_rows = span * tok_rows
    head_dim = query_gain.shape[0]
    q_heads = w_query.shape[1] // head_dim
    kv_width = key_value_weight.shape[1] // 2
    kv_heads = kv_width // head_dim
    query_group_size = q_heads * lax.axis_size("col") // kv_heads
    key_block = 512
    kv_index = (col_index * q_heads + jnp.arange(q_heads, dtype=jnp.int32)) // query_group_size
    kv_pick = (kv_index[:, None] == jnp.arange(kv_heads, dtype=jnp.int32)[None, :]).astype(
        jnp.float32
    )
    w_q_all, w_kv_all, w_o_all, w_g_all, w_u_all, w_d_all = (
        lax.all_gather(w_query, "row", axis=0, tiled=True),
        lax.all_gather(key_value_weight, "row", axis=0, tiled=True),
        lax.all_gather(w_out, "row", axis=1, tiled=True),
        lax.all_gather(w_gate, "row", axis=0, tiled=True),
        lax.all_gather(w_up, "row", axis=0, tiled=True),
        lax.all_gather(w_down, "row", axis=1, tiled=True),
    )
    input_f = tokens.astype(jnp.float32)
    act_norm, act_scale = norm_forward(input_f, attn_gain)
    act_low = act_norm.astype(jnp.bfloat16)
    q_raw = jnp.dot(act_low, w_q_all, preferred_element_type=jnp.float32)
    key_value_projected = jnp.dot(act_low, w_kv_all, preferred_element_type=jnp.float32)
    cosine_table, sine_table = tables(positions, head_dim)
    q_heads_raw = q_raw.reshape(tok_rows, q_heads, head_dim)
    q_normed, q_scale = norm_forward(q_heads_raw, query_gain)
    query = apply_rotation(q_normed, cosine_table, sine_table).astype(jnp.bfloat16)
    k_heads_raw = key_value_projected[:, :kv_width].reshape(tok_rows, kv_heads, head_dim)
    k_normed, k_scale = norm_forward(k_heads_raw, key_gain)
    key_low = apply_rotation(k_normed, cosine_table, sine_table).astype(jnp.bfloat16)
    value_low = key_value_projected[:, kv_width:].astype(jnp.bfloat16)
    local_kv = jnp.concatenate([key_low.reshape(tok_rows, kv_width), value_low], axis=1)

    def pass_step(current, unused):
        arrived = from_behind(current, "row", 1)
        return (arrived, arrived)

    last_piece, earlier = lax.scan(pass_step, local_kv, None, length=span - 1)
    all_kv = jnp.concatenate(
        [jnp.flip(earlier, 0).reshape((span - 1) * tok_rows, 2 * kv_width), local_kv], axis=0
    )
    buf_start = (row_index - (span - 1)) * tok_rows
    first_query = row_index * tok_rows
    seg_query = lax.dynamic_slice_in_dim(segments, first_query, tok_rows, 0)
    idx_query = first_query + jnp.arange(tok_rows, dtype=jnp.int32)
    token_index = jnp.arange(all_rows, dtype=jnp.int32)
    low_index = jnp.min(jnp.where(segments == seg_query[0], token_index, all_rows))
    block_low = jnp.maximum(low_index - buf_start, 0) // key_block
    block_high = buf_rows // key_block

    def scores(first_key, key_count):
        block_kv = lax.dynamic_slice_in_dim(all_kv, first_key, key_count, 0)
        key_rows = jnp.take(
            block_kv[:, :kv_width].reshape(key_count, kv_heads, head_dim), kv_index, axis=1
        )
        val_rows = jnp.take(
            block_kv[:, kv_width:].reshape(key_count, kv_heads, head_dim), kv_index, axis=1
        )
        logits = (
            jnp.einsum("qhd,khd->hqk", query, key_rows, preferred_element_type=jnp.float32) * SCALE
        )
        idx_key = buf_start + first_key + jnp.arange(key_count, dtype=jnp.int32)
        seg_key = jnp.where(idx_key >= 0, jnp.take(segments, jnp.maximum(idx_key, 0)), -2)
        mask_ok = allowed(seg_query, idx_query, seg_key, idx_key)
        return (jnp.where(mask_ok[None], logits, NEGATIVE), mask_ok, key_rows, val_rows)

    def stat_step(block_no, state_pair):
        run_max, run_sum = state_pair
        logits, mask_ok, key_rows, val_rows = scores(block_no * key_block, key_block)
        new_max = jnp.maximum(run_max, jnp.max(logits, axis=2))
        expo = jnp.where(mask_ok[None], jnp.exp(logits - new_max[..., None]), 0.0)
        return (new_max, run_sum * jnp.exp(run_max - new_max) + jnp.sum(expo, axis=2))

    start_max = jnp.full((q_heads, tok_rows), NEGATIVE, jnp.float32)
    run_max, run_sum = lax.fori_loop(
        block_low, block_high, stat_step, (start_max, jnp.zeros((q_heads, tok_rows), jnp.float32))
    )
    log_norm = run_max + jnp.log(run_sum)

    def out_step(block_no, acc_out):
        logits, mask_ok, key_rows, val_rows = scores(block_no * key_block, key_block)
        prob_low = jnp.where(mask_ok[None], jnp.exp(logits - log_norm[..., None]), 0.0).astype(
            jnp.bfloat16
        )
        return acc_out + jnp.einsum(
            "hqk,khd->qhd", prob_low, val_rows, preferred_element_type=jnp.float32
        )

    attn_f = lax.fori_loop(
        block_low, block_high, out_step, jnp.zeros((tok_rows, q_heads, head_dim), jnp.float32)
    )
    attn_low = attn_f.astype(jnp.bfloat16).reshape(tok_rows, q_heads * head_dim)
    attn_part = jnp.dot(attn_low, w_o_all, preferred_element_type=jnp.float32)
    hidden_res = input_f + lax.psum(attn_part.astype(jnp.bfloat16), "col").astype(jnp.float32)
    ffn_norm, ffn_scale = norm_forward(hidden_res, ffn_gain)
    ffn_low = ffn_norm.astype(jnp.bfloat16)
    gate_pre = jnp.dot(ffn_low, w_g_all, preferred_element_type=jnp.float32)
    up_pre = jnp.dot(ffn_low, w_u_all, preferred_element_type=jnp.float32)
    sigma = jax.nn.sigmoid(gate_pre)
    silu_gate = gate_pre * sigma
    inner_low = (silu_gate * up_pre).astype(jnp.bfloat16)
    ffn_part = jnp.dot(inner_low, w_d_all, preferred_element_type=jnp.float32)
    output = (
        hidden_res + lax.psum(ffn_part.astype(jnp.bfloat16), "col").astype(jnp.float32)
    ).astype(jnp.bfloat16)
    grad_inner = jnp.einsum("td,fd->tf", out_grad, w_d_all, preferred_element_type=jnp.float32)
    grad_gate_low = (grad_inner * up_pre * (sigma * (1.0 + gate_pre * (1.0 - sigma)))).astype(
        jnp.bfloat16
    )
    grad_up_low = (grad_inner * silu_gate).astype(jnp.bfloat16)
    grad_down = jnp.einsum("tf,td->fd", inner_low, out_grad, preferred_element_type=jnp.float32)
    grad_gate = jnp.einsum("td,tf->df", ffn_low, grad_gate_low, preferred_element_type=jnp.float32)
    grad_up = jnp.einsum("td,tf->df", ffn_low, grad_up_low, preferred_element_type=jnp.float32)
    ffn_back = jnp.einsum(
        "tf,df->td", grad_gate_low, w_g_all, preferred_element_type=jnp.float32
    ) + jnp.einsum("tf,df->td", grad_up_low, w_u_all, preferred_element_type=jnp.float32)
    ffn_back = lax.psum(ffn_back.astype(jnp.bfloat16), "col").astype(jnp.float32)
    res_grad, ffn_gain_term = norm_backward(hidden_res, ffn_scale, ffn_gain, ffn_back)
    grad_ffn_gain = jnp.sum(ffn_gain_term, axis=0)
    d_hidden = out_grad.astype(jnp.float32) + res_grad
    d_hidden_low = d_hidden.astype(jnp.bfloat16)
    grad_out = jnp.einsum("ta,td->ad", attn_low, d_hidden_low, preferred_element_type=jnp.float32)
    d_attn = (
        jnp.einsum("td,ad->ta", d_hidden_low, w_o_all, preferred_element_type=jnp.float32)
        .astype(jnp.bfloat16)
        .reshape(tok_rows, q_heads, head_dim)
    )
    row_delta = jnp.einsum("qhd,qhd->hq", d_attn.astype(jnp.float32), attn_f)

    def block_terms(first_key, key_count):
        logits, mask_ok, key_rows, val_rows = scores(first_key, key_count)
        prob_full = jnp.where(mask_ok[None], jnp.exp(logits - log_norm[..., None]), 0.0)
        grad_prob = jnp.einsum("qhd,khd->hqk", d_attn, val_rows, preferred_element_type=jnp.float32)
        grad_logit = (prob_full * (grad_prob - row_delta[..., None])).astype(jnp.bfloat16)
        return (prob_full.astype(jnp.bfloat16), grad_logit, key_rows)

    def kv_piece(prob_low, grad_logit, key_count):
        grad_key = (
            jnp.einsum("hqk,qhd->khd", grad_logit, query, preferred_element_type=jnp.float32)
            * SCALE
        )
        grad_val = jnp.einsum("hqk,qhd->khd", prob_low, d_attn, preferred_element_type=jnp.float32)
        grad_key = jnp.einsum("khd,hg->kgd", grad_key, kv_pick).reshape(key_count, kv_width)
        grad_val = jnp.einsum("khd,hg->kgd", grad_val, kv_pick).reshape(key_count, kv_width)
        return jnp.concatenate([grad_key, grad_val], axis=1)

    def back_step(block_no, state_pair):
        grad_query_acc, grad_kv_buf = state_pair
        first_key = block_no * key_block
        prob_low, grad_logit, key_rows = block_terms(first_key, key_block)
        grad_query_acc = (
            grad_query_acc
            + jnp.einsum("hqk,khd->qhd", grad_logit, key_rows, preferred_element_type=jnp.float32)
            * SCALE
        )
        old_rows = lax.dynamic_slice_in_dim(grad_kv_buf, first_key, key_block, 0)
        grad_kv_buf = lax.dynamic_update_slice_in_dim(
            grad_kv_buf, old_rows + kv_piece(prob_low, grad_logit, key_block), first_key, 0
        )
        return (grad_query_acc, grad_kv_buf)

    empty_query = jnp.zeros((tok_rows, q_heads, head_dim), jnp.float32)
    grad_query_acc, grad_kv_buf = lax.fori_loop(
        block_low,
        block_high,
        back_step,
        (empty_query, jnp.zeros((buf_rows, 2 * kv_width), jnp.float32)),
    )
    grad_pieces = grad_kv_buf.reshape(span, tok_rows, 2 * kv_width)

    def return_step(carried, piece):
        moved = from_behind(carried.astype(jnp.bfloat16), "row", -1).astype(carried.dtype)
        return (moved + piece, None)

    kv_local_grad, unused = lax.scan(return_step, grad_pieces[0], grad_pieces[1:])
    q_rot_back = rotate_back(grad_query_acc, cosine_table, sine_table)
    q_grad_raw, q_gain_term = norm_backward(q_heads_raw, q_scale, query_gain, q_rot_back)
    q_gain_part = jnp.sum(q_gain_term, axis=(0, 1))
    q_grad_low = q_grad_raw.reshape(tok_rows, q_heads * head_dim).astype(jnp.bfloat16)
    grad_query = jnp.einsum("td,ta->da", act_low, q_grad_low, preferred_element_type=jnp.float32)
    query_back = jnp.einsum("ta,da->td", q_grad_low, w_q_all, preferred_element_type=jnp.float32)
    query_back, kv_summed, q_gain_sum = (
        lax.psum(query_back.astype(jnp.bfloat16), "col").astype(jnp.float32),
        lax.psum(kv_local_grad.astype(jnp.bfloat16), "col").astype(jnp.float32),
        lax.psum(q_gain_part.astype(jnp.bfloat16), "col").astype(jnp.float32),
    )
    k_rot_back = rotate_back(
        kv_summed[:, :kv_width].reshape(tok_rows, kv_heads, head_dim), cosine_table, sine_table
    )
    k_grad_raw, k_gain_term = norm_backward(k_heads_raw, k_scale, key_gain, k_rot_back)
    k_gain_part = jnp.sum(k_gain_term, axis=(0, 1))
    kv_grad_low = jnp.concatenate(
        [k_grad_raw.reshape(tok_rows, kv_width), kv_summed[:, kv_width:]], axis=1
    ).astype(jnp.bfloat16)
    grad_keyval = jnp.einsum("td,ta->da", act_low, kv_grad_low, preferred_element_type=jnp.float32)
    act_back = query_back + jnp.einsum(
        "ta,da->td", kv_grad_low, w_kv_all, preferred_element_type=jnp.float32
    )
    input_back, attn_gain_term = norm_backward(input_f, act_scale, attn_gain, act_back)
    grad_attn_gain = jnp.sum(attn_gain_term, axis=0)
    input_grad = d_hidden + input_back
    shards = (
        lax.psum_scatter(grad_query, "row", scatter_dimension=0, tiled=True),
        lax.psum_scatter(grad_keyval, "row", scatter_dimension=0, tiled=True),
        lax.psum_scatter(grad_out, "row", scatter_dimension=1, tiled=True),
        lax.psum_scatter(grad_gate, "row", scatter_dimension=0, tiled=True),
        lax.psum_scatter(grad_up, "row", scatter_dimension=0, tiled=True),
        lax.psum_scatter(grad_down, "row", scatter_dimension=1, tiled=True),
        lax.psum_scatter(grad_attn_gain, "row", scatter_dimension=0, tiled=True),
        lax.psum_scatter(grad_ffn_gain, "row", scatter_dimension=0, tiled=True),
        lax.psum_scatter(q_gain_sum, "row", scatter_dimension=0, tiled=True),
        lax.psum_scatter(k_gain_part, "row", scatter_dimension=0, tiled=True),
    )
    return (
        output,
        input_grad,
        shards[0],
        shards[1],
        shards[2],
        shards[3],
        shards[4],
        shards[5],
        shards[6],
        shards[7],
        shards[8],
        shards[9],
    )


def solution(mesh):
    placed = (
        P("row", None),
        P("row", "col"),
        P("row", None),
        P("col", "row"),
        P("row", "col"),
        P("row", "col"),
        P("col", "row"),
        P(),
        P(),
        P(),
        P(),
        P(),
        P("row"),
        P("row", None),
    )
    return jax.shard_map(
        body,
        mesh=mesh,
        in_specs=placed,
        out_specs=(
            P("row", None),
            P("row", None),
            P("row", "col"),
            P("row", None),
            P("col", "row"),
            P("row", "col"),
            P("row", "col"),
            P("col", "row"),
            P("row"),
            P("row"),
            P("row"),
            P("row"),
        ),
        check_vma=False,
    )
```

profile of v0, /device:TPU:0, one launch (start us, length us, event | category | flops | bytes accessed | tf_op | source)
XLA Modules:
  0.0 1734.4 jit_solution(15368597002683394542)
XLA Ops:
  14.9 41.3 %all-gather.7.cloned.1.call-done = bf16[2048,640]{1,0:T(8,128)(2,1)} async-done(((bf16[128,640]{1,0:T(8,128)(2,1)}), bf16[2048,640]{1,0:T(8,128)(2,1)}) %all-gather.7.cloned.1.call-update) | async-done | bytes 2621456 | tf_op jit(solution)/shard_map/all_gather | solution.py:112
  60.6 111.5 %while.59 = (s32[]{:T(128)}, bf16[128,640]{1,0:T(8,128)(2,1)S(1)}, bf16[15,128,640]{2,1,0:T(8,128)(2,1)S(1)}, s32[]{:T(128)}) while((s32[]{:T(128)}, bf16[128,640]{1,0:T(8,128)(2,1)S(1)}, bf16[15,128,640]{2,1,0:T(8,128)(2,1)S(1)}, s32[]{:T(128)}) %tuple.152), condition=%wide.region_4.5_spmd, body=%wide.region_3.4_spmd.sunk | while | flops 2 | bytes 1310825 | solution.py:137
  63.8 3.6 collective-permute-start
  68.5 5.6 collective-permute-start
  75.2 5.6 collective-permute-start
  81.9 8.9 collective-permute-start
  91.8 5.6 collective-permute-start
  98.6 5.6 collective-permute-start
  105.3 5.6 collective-permute-start
  112.0 5.6 collective-permute-start
  118.7 7.3 collective-permute-start
  127.1 10.7 collective-permute-start
  138.9 6.4 collective-permute-start
  146.3 9.5 collective-permute-start
  156.8 6.5 collective-permute-start
  164.5 6.5 collective-permute-start
  181.7 6.5 while.61
  188.3 7.1 while.62
  188.4 3.1 gather_fusion.2
  195.6 3.2 convolution_convert_fusion.1
  204.1 64.2 %all-reduce.10.cloned.1.call-done = bf16[128,2048]{1,0:T(8,128)(2,1)} async-done(((bf16[128,2048]{1,0:T(8,128)(2,1)}), bf16[128,2048]{1,0:T(8,128)(2,1)}) %all-reduce.10.cloned.1.call-update) | async-done | bytes 524304 | tf_op jit(solution)/shard_map/psum | solution.py:193
  270.9 87.7 %all-gather.13.cloned.1.call-done = bf16[2048,2560]{1,0:T(8,128)(2,1)} async-done(((bf16[128,2560]{1,0:T(8,128)(2,1)}), bf16[2048,2560]{1,0:T(8,128)(2,1)}) %all-gather.13.cloned.1.call-update) | async-done | bytes 10485776 | tf_op jit(solution)/shard_map/all_gather | solution.py:114
  358.6 6.6 fusion.128
  365.2 81.9 %all-gather.15.cloned.1.call-done = bf16[2048,2560]{1,0:T(8,128)(2,1)} async-done(((bf16[128,2560]{1,0:T(8,128)(2,1)}), bf16[2048,2560]{1,0:T(8,128)(2,1)}) %all-gather.15.cloned.1.call-update) | async-done | bytes 10485776 | tf_op jit(solution)/shard_map/all_gather | solution.py:115
  447.1 6.6 fusion.129
  453.7 84.8 %all-gather.17.cloned.1.call-done = bf16[2560,2048]{1,0:T(8,128)(2,1)} async-done(((bf16[2560,128]{1,0:T(8,128)(2,1)}), bf16[2560,2048]{1,0:T(8,128)(2,1)}) %all-gather.17.cloned.1.call-update) | async-done | bytes 10485776 | tf_op jit(solution)/shard_map/all_gather | solution.py:116
  538.5 8.6 multiply_convert_fusion
  547.1 8.2 fusion.130
  555.3 4.3 fusion.90
  559.9 6.5 convolution_convert_fusion.2
  566.4 20.1 %all-reduce.12.cloned.1.call-done = bf16[128,2048]{1,0:T(8,128)(2,1)} async-done(((bf16[128,2048]{1,0:T(8,128)(2,1)}), bf16[128,2048]{1,0:T(8,128)(2,1)}) %all-reduce.12.cloned.1.call-update) | async-done | bytes 524304 | tf_op jit(solution)/shard_map/psum | solution.py:216
  595.0 17.7 %while.63 = (s32[]{:T(128)}, f32[128,10,64]{0,2,1:T(8,128)S(1)}, f32[2048,640]{0,1:T(8,128)}, bf16[2048,640]{0,1:T(8,128)(2,1)}, s32[128]{0:T(128)S(1)}, /*index...) while((s32[]{:T(128)}, f32[128,10,64]{0,2,1:T(8,128)S(1)}, ...), condition=%wide.region_18.21_spmd.clone, body=%wide.region_17.20_spmd.clone.sunk | while | flops 436706528 | bytes 40220740 | solution.py:262
  612.7 5.9 copy.171
  619.6 5.0 slice.111
  624.7 134.9 %while.60 = (s32[]{:T(128)}, bf16[128,640]{1,0:T(8,128)(2,1)S(1)}, f32[15,128,640]{2,1,0:T(8,128)}, s32[]{:T(128)}) while((s32[]{:T(128)}, bf16[128,640]{1,0:T(8,128)(2,1)S(1)}, f32[15,128,640]{2,1,0:T(8,128)}, s32[]{:T(128)}) %tuple.203), condition=%wide.region_22.25_spmd, body=%wide.region_21.24_spmd.sunk | while | flops 245762 | bytes 1310825 | solution.py:274
  630.4 4.7 collective-permute-done.1
  637.4 5.3 collective-permute-done.1
  645.0 5.3 collective-permute-done.1
  652.7 5.3 collective-permute-done.1
  660.3 15.1 collective-permute-done.1
  677.8 6.2 collective-permute-done.1
  686.4 6.2 collective-permute-done.1
  694.9 6.2 collective-permute-done.1
  703.5 12.4 collective-permute-done.1
  718.2 6.2 collective-permute-done.1
  726.8 6.2 collective-permute-done.1
  735.3 6.2 collective-permute-done.1
  743.9 6.2 collective-permute-done.1
  752.4 6.2 collective-permute-done.1
  761.9 3.6 convolution_convert_fusion
  765.9 3.3 fusion.108
  769.9 3.2 fusion.117
  773.9 63.3 %all-reduce.14.cloned.1.call-done = (bf16[128,2048]{1,0:T(8,128)(2,1)}, bf16[128,2048]{1,0:T(8,128)(2,1)}, bf16[128,640]{0,1:T(8,128)(2,1)}) async-done(((bf16[128,2048]{1,0:T(8,128)(2,1)}, bf16[128,2048]{1,0:T(8,128)(2,1)}, bf16[128,640]{0,1:T(8,128)(2,1)}), (bf16[128,2048]{1,0:T(8,128)(2,1)}, bf16[128,2048]{1,0:T(8,128)(2,1)}, bf16[128,640]{0,1:T(8,128)(2,1)})) %all-reduce.14.cloned.1.call-update) | async-done | bytes 1212432 | tf_op jit(solution)/shard_map/psum | solution.py:203
  839.6 3.2 fusion.113
  844.0 9.5 fusion.131
  854.6 9.2 fusion.132
  864.8 8.9 fusion.133
  876.4 4.9 psum.47
  884.7 61.1 %all-reduce.4 = (f32[2048]{0:T(1024)S(1)}, f32[2048]{0:T(1024)S(1)}, f32[64]{0:T(128)S(1)}, f32[64]{0:T(128)S(1)}) all-reduce(f32[2048]{0:T(1024)S(1)} %get-tuple-element.505, f32[2048]{0:T(1024)S(1)} %copy-done.42, bf16[64]{0:T(256)(128)(2,1)S(1)} %psum.47, f32[64]{0:T(128)S(1)} %reduce_sum.146), channel_id=8, replica_groups=mesh['row'=16,'col'=2] {'row'}, use_global_device_ids=true, to_apply=%region_33.36.clone | all-reduce | flops 4224 | bytes 33664
  951.1 51.0 %reduce-scatter.7.cloned.1.call-done = f32[128,640]{1,0:T(8,128)} async-done(((f32[2048,640]{1,0:T(8,128)}), f32[128,640]{1,0:T(8,128)}) %reduce-scatter.7.cloned.1.call-update) | async-done | bytes 327696 | tf_op jit(solution)/shard_map/reduce_scatter | solution.py:302
  1002.1 81.8 %reduce-scatter.9.cloned.1.call-done = f32[128,640]{1,0:T(8,128)} async-done(((f32[2048,640]{1,0:T(8,128)}), f32[128,640]{1,0:T(8,128)}) %reduce-scatter.9.cloned.1.call-update) | async-done | bytes 327696 | tf_op jit(solution)/shard_map/reduce_scatter | solution.py:303
  1083.9 214.4 %reduce-scatter.13.cloned.1.call-done = f32[128,2560]{1,0:T(8,128)} async-done(((f32[2048,2560]{1,0:T(8,128)}), f32[128,2560]{1,0:T(8,128)}) %reduce-scatter.13.cloned.1.call-update) | async-done | bytes 1310736 | tf_op jit(solution)/shard_map/reduce_scatter | solution.py:305
  1298.3 214.6 %reduce-scatter.15.cloned.1.call-done = f32[128,2560]{1,0:T(8,128)} async-done(((f32[2048,2560]{1,0:T(8,128)}), f32[128,2560]{1,0:T(8,128)}) %reduce-scatter.15.cloned.1.call-update) | async-done | bytes 1310736 | tf_op jit(solution)/shard_map/reduce_scatter | solution.py:306
  1512.9 214.6 %reduce-scatter.17.cloned.1.call-done = f32[2560,128]{1,0:T(8,128)} async-done(((f32[2560,2048]{1,0:T(8,128)}), f32[2560,128]{1,0:T(8,128)}) %reduce-scatter.17.cloned.1.call-update) | async-done | bytes 1310736 | tf_op jit(solution)/shard_map/reduce_scatter | solution.py:307
  (379 shorter events, 139.9 us)
Async XLA Ops:
  7.2 49.1 %all-gather.7.cloned.1.call-start = ((), (), s32[]{:S(2)}) async-start(), calls=%async_computation.6 | async-start | bytes 2785280 | tf_op jit(solution)/shard_map/all_gather | solution.py:112
  7.9 170.5 %all-gather.9.cloned.1.call-start = ((), (), s32[]{:S(2)}) async-start(), calls=%async_computation.7 | async-start | bytes 2785280 | tf_op jit(solution)/shard_map/all_gather | solution.py:111
  8.7 186.9 %all-gather.11.cloned.1.call-start = ((), (), s32[]{:S(2)}) async-start(), calls=%async_computation.8 | async-start | bytes 2785280 | tf_op jit(solution)/shard_map/all_gather | solution.py:113
  9.4 258.9 %all-reduce.10.cloned.1.call-start = ((), (), s32[]{:S(2)}) async-start(), calls=%async_computation.9 | async-start | bytes 1048576 | tf_op jit(solution)/shard_map/psum | solution.py:193
  9.5 50.2 %copy-start.56 = (f32[64]{0:T(128)S(1)}, f32[64]{0:T(128)}, u32[]{:S(2)}) copy-start(f32[64]{0:T(128)} %param.38) | copy-start | bytes 772
  14.1 164.3 %copy-start.43 = (f32[128]{0:T(128)}, f32[128]{0:T(128)S(1)}, u32[]{:S(2)}) copy-start(f32[128]{0:T(128)S(1)} %get-tuple-element.642) | copy-start | bytes 1540
  60.6 3.2 collective-permute-start
  63.8 4.6 collective-permute-start
  68.5 6.6 collective-permute-start
  75.2 6.6 collective-permute-start
  81.9 9.9 collective-permute-start
  91.8 6.6 collective-permute-start
  98.6 6.6 collective-permute-start
  105.3 6.6 collective-permute-start
  112.0 6.6 collective-permute-start
  118.7 8.4 collective-permute-start
  127.1 11.7 collective-permute-start
  138.9 7.4 collective-permute-start
  146.3 10.5 collective-permute-start
  156.8 7.5 collective-permute-start
  164.5 7.5 collective-permute-start
  198.8 70.8 %copy-start.35 = (f32[2048]{0:T(1024)S(1)}, f32[2048]{0:T(1024)}, u32[]{:S(2)}) copy-start(f32[2048]{0:T(1024)} %param.36) | copy-start | bytes 24580
  198.9 159.8 %all-gather.13.cloned.1.call-start = ((), (), s32[]{:S(2)}) async-start(), calls=%async_computation.10 | async-start | bytes 11141120 | tf_op jit(solution)/shard_map/all_gather | solution.py:114
  199.4 247.7 %all-gather.15.cloned.1.call-start = ((), (), s32[]{:S(2)}) async-start(), calls=%async_computation.11 | async-start | bytes 11141120 | tf_op jit(solution)/shard_map/all_gather | solution.py:115
  200.1 338.4 %all-gather.17.cloned.1.call-start = ((), (), s32[]{:S(2)}) async-start(), calls=%async_computation.12 | async-start | bytes 11141120 | tf_op jit(solution)/shard_map/all_gather | solution.py:116
  200.8 385.7 %all-reduce.12.cloned.1.call-start = ((), (), s32[]{:S(2)}) async-start(), calls=%async_computation.13 | async-start | bytes 1048576 | tf_op jit(solution)/shard_map/psum | solution.py:216
  269.6 319.0 %copy-start.51 = (f32[128]{0:T(128)}, f32[128]{0:T(128)S(1)}, u32[]{:S(2)}) copy-start(f32[128]{0:T(128)S(1)} %get-tuple-element.644) | copy-start | bytes 1540
  269.6 319.0 %copy-start.58 = (f32[128]{0:T(128)}, f32[128]{0:T(128)S(1)}, u32[]{:S(2)}) copy-start(f32[128]{0:T(128)S(1)} %get-tuple-element.643) | copy-start | bytes 1540
  365.2 173.3 %copy-start.7 = (bf16[128,2048]{1,0:T(8,128)(2,1)S(1)}, bf16[128,2048]{1,0:T(8,128)(2,1)}, u32[]{:S(2)}) copy-start(bf16[128,2048]{1,0:T(8,128)(2,1)} %param.41) | copy-start | bytes 1572868
  538.5 16.8 slice-start.1
  559.6 277.5 %all-reduce.14.cloned.1.call-start = ((), (), s32[]{:S(2)}) async-start(), calls=%async_computation.20 | async-start | bytes 2424832 | tf_op jit(solution)/shard_map/psum | solution.py:203
  559.9 26.7 %copy-start.3 = (bf16[128,2048]{1,0:T(8,128)(2,1)S(1)}, bf16[128,2048]{1,0:T(8,128)(2,1)}, u32[]{:S(2)}) copy-start(bf16[128,2048]{1,0:T(8,128)(2,1)} %all-reduce.10.cloned.1.call-done) | copy-start | bytes 1572868
  588.6 177.2 %copy-start.61 = (f32[128]{0:T(128)}, f32[128]{0:T(128)S(1)}, u32[]{:S(2)}) copy-start(f32[128]{0:T(128)S(1)} %broadcast_multiply_fusion.3) | copy-start | bytes 1540
  624.6 136.0 %copy-start.6 = (f32[128,640]{0,1:T(8,128)S(1)}, f32[128,640]{0,1:T(8,128)}, u32[]{:S(2)}) copy-start(f32[128,640]{0,1:T(8,128)} %copy-done.5) | copy-start | bytes 983044
  624.6 136.0 %copy-start.55 = (f32[64]{0:T(128)S(1)}, f32[64]{0:T(128)}, u32[]{:S(2)}) copy-start(f32[64]{0:T(128)} %param.37) | copy-start | bytes 772
  624.7 3.3 collective-permute-start.1
  629.1 6.0 collective-permute-start.1
  636.1 6.6 collective-permute-start.1
  643.7 6.6 collective-permute-start.1
  651.4 6.6 collective-permute-start.1
  659.0 16.4 collective-permute-start.1
  676.5 7.5 collective-permute-start.1
  685.1 7.5 collective-permute-start.1
  693.6 7.5 collective-permute-start.1
  702.2 13.7 collective-permute-start.1
  716.9 7.5 collective-permute-start.1
  725.5 7.5 collective-permute-start.1
  734.0 7.5 collective-permute-start.1
  742.6 7.5 collective-permute-start.1
  751.1 7.5 collective-permute-start.1
  765.5 185.6 %reduce-scatter.11.cloned.1.call-start = ((), (), s32[]{:S(2)}) async-start(), calls=%async_computation.16 | async-start | bytes 5570560 | tf_op jit(solution)/shard_map/reduce_scatter | solution.py:304
  769.2 232.9 %reduce-scatter.7.cloned.1.call-start = ((), (), s32[]{:S(2)}) async-start(), calls=%async_computation.14 | async-start | bytes 5570560 | tf_op jit(solution)/shard_map/reduce_scatter | solution.py:302
  773.1 65.0 %copy-start.13 = (f32[128,320]{0,1:T(8,128)S(1)}, f32[128,320]{0,1:T(8,128)}, u32[]{:S(2)}) copy-start(f32[128,320]{0,1:T(8,128)} %copy-done.12) | copy-start | bytes 491524
  773.2 65.1 %copy-start.41 = (f32[128,5]{0,1:T(8,128)S(1)}, f32[128,5]{0,1:T(8,128)}, u32[]{:S(2)}) copy-start(f32[128,5]{0,1:T(8,128)} %copy-done.40) | copy-start | bytes 7684
  773.2 65.1 %copy-start.46 = (f32[128,5]{0,1:T(8,128)S(1)}, f32[128,5]{0,1:T(8,128)}, u32[]{:S(2)}) copy-start(f32[128,5]{0,1:T(8,128)} %get-tuple-element.637) | copy-start | bytes 7684
  773.2 310.7 %reduce-scatter.9.cloned.1.call-start = ((), (), s32[]{:S(2)}) async-start(), calls=%async_computation.15 | async-start | bytes 5570560 | tf_op jit(solution)/shard_map/reduce_scatter | solution.py:303
  842.9 455.4 %reduce-scatter.13.cloned.1.call-start = ((), (), s32[]{:S(2)}) async-start(), calls=%async_computation.17 | async-start | bytes 22282240 | tf_op jit(solution)/shard_map/reduce_scatter | solution.py:305
  853.4 659.5 %reduce-scatter.15.cloned.1.call-start = ((), (), s32[]{:S(2)}) async-start(), calls=%async_computation.18 | async-start | bytes 22282240 | tf_op jit(solution)/shard_map/reduce_scatter | solution.py:306
  863.8 863.7 %reduce-scatter.17.cloned.1.call-start = ((), (), s32[]{:S(2)}) async-start(), calls=%async_computation.19 | async-start | bytes 22282240 | tf_op jit(solution)/shard_map/reduce_scatter | solution.py:307
  881.3 66.8 %copy-start.36 = (f32[2048]{0:T(1024)S(1)}, f32[2048]{0:T(1024)}, u32[]{:S(2)}) copy-start(f32[2048]{0:T(1024)} %param.36) | copy-start | bytes 24580
  881.3 66.7 %copy-start.53 = (f32[128]{0:T(128)S(1)}, f32[128]{0:T(128)}, u32[]{:S(2)}) copy-start(f32[128]{0:T(128)} %copy-done.51) | copy-start | bytes 1540
  881.3 66.7 %copy-start.60 = (f32[128]{0:T(128)S(1)}, f32[128]{0:T(128)}, u32[]{:S(2)}) copy-start(f32[128]{0:T(128)} %copy-done.58) | copy-start | bytes 1540
  881.3 66.7 %copy-start.62 = (f32[128]{0:T(128)S(1)}, f32[128]{0:T(128)}, u32[]{:S(2)}) copy-start(f32[128]{0:T(128)} %copy-done.61) | copy-start | bytes 1540
  881.4 66.7 %copy-start.63 = (f32[128]{0:T(128)S(1)}, f32[128]{0:T(128)}, u32[]{:S(2)}) copy-start(f32[128]{0:T(128)} %get-tuple-element.641) | copy-start | bytes 1540
  (49 other events, 184.6 us)
Sparse Core Ops, SparseCore 0:
  10.3 45.8 all-gather.6
  58.5 43.0 all-gather.8
  103.8 45.5 all-gather.10
  199.0 69.2 all-reduce.9
  270.7 87.8 all-gather.12
  361.0 86.0 all-gather.14
  449.5 88.9 all-gather.16
  559.7 26.7 all-reduce.11
  765.6 71.4 all-reduce.13
  841.4 78.7 reduce-scatter.10
  924.7 77.3 reduce-scatter.6
  1006.4 77.4 reduce-scatter.8
  1088.6 209.7 reduce-scatter.12
  1302.9 209.9 reduce-scatter.14
  1517.4 209.9 reduce-scatter.16
where the time goes:
time: 1740 us; the launch traced here: 1730 us
  waiting for transfers between devices  1340 us (77%)
  starting transfers between devices  116 us (7%)
  matrix products  106 us (6%)
  blocking collectives  66 us (4%)
  local copies, waits for them, and re-layouts  52.7 us (3%)
  other arithmetic  36.6 us (2%)
    reduce_scatter x1, waiting for transfers between devices, body(): lax.psum_scatter(grad_up, 'row', scatter_dimension=0, tiled=True)  215 us
    reduce_scatter x1, waiting for transfers between devices, body(): lax.psum_scatter(grad_down, 'row', scatter_dimension=1, tiled=True)  215 us
    reduce_scatter x1, waiting for transfers between devices, body(): lax.psum_scatter(grad_gate, 'row', scatter_dimension=0, tiled=True)  214 us
    ppermute x30, waiting for transfers between devices, from_behind(): return lax.ppermute(block, axis, route)  115 us
    ppermute x30, starting transfers between devices, from_behind(): return lax.ppermute(block, axis, route)  115 us
    all_gather x1, waiting for transfers between devices, body(): lax.all_gather(w_gate, 'row', axis=0, tiled=True)  87.7 us
    all_gather x1, waiting for transfers between devices, body(): lax.all_gather(w_down, 'row', axis=1, tiled=True)  84.8 us
    all_gather x1, waiting for transfers between devices, body(): lax.all_gather(w_up, 'row', axis=0, tiled=True)  81.9 us
  transfers between devices with their start and end apart: 45, of which 42 were waited for; matrix products, arithmetic and copies ran while one was open for 6% of the time, Pallas kernels for 0%

commit v1 on v0

v1 whole, which is shorter than its diff:
```python
import math

import jax
import jax.numpy as jnp
from jax import lax
from jax.experimental import pallas as pl
from jax.experimental.pallas import tpu as pltpu
from jax.sharding import PartitionSpec as P

EPSILON = 1e-06
SCALE = 0.125
SEQ_MAX = 4096
MEMBERS = 8
LANES = 128
HALF = 64
F32 = jnp.float32
BF16 = jnp.bfloat16
VMEM_LIMIT = 56 * 1024 * 1024


def dot(a, b, dims=((1,), (0,))):
    return lax.dot_general(a, b, (dims, ((), ())), preferred_element_type=F32)


def swap_core(block):
    rows = lax.axis_size("row")
    return lax.ppermute(block, "row", [(i, i ^ 1) for i in range(rows)])


def swap_col(block):
    return lax.ppermute(block, "col", [(0, 1), (1, 0)])


def plane_groups(span):
    rows = lax.axis_size("row")
    return [
        [first + 2 * j + core for j in range(span // 2)]
        for first in range(0, rows, span)
        for core in range(2)
    ]


def cube_groups():
    rows, cols = lax.axis_size("row"), lax.axis_size("col")
    return [
        [(first + 2 * j + core) * cols + c for j in range(MEMBERS // 2) for c in range(cols)]
        for first in range(0, rows, MEMBERS)
        for core in range(2)
    ]


def exchange_plane(blocks, span):
    return lax.all_to_all(
        blocks, "row", split_axis=0, concat_axis=0, tiled=True, axis_index_groups=plane_groups(span)
    )


def exchange_cube(blocks):
    return lax.all_to_all(
        blocks, ("row", "col"), split_axis=0, concat_axis=0, tiled=True, axis_index_groups=cube_groups()
    )


def gather_plane(block, span):
    copies = jnp.broadcast_to(block[None], (span // 2,) + block.shape)
    same = exchange_plane(copies, span)
    return same, swap_core(same)


def gather_cube(block):
    count = MEMBERS // 2 * lax.axis_size("col")
    copies = jnp.broadcast_to(block[None], (count,) + block.shape)
    same = exchange_cube(copies)
    return same, swap_core(same)


def halves(own, other, col):
    low = jnp.where(col == 0, own, other)
    high = jnp.where(col == 0, other, own)
    return jnp.concatenate([low, high], axis=0)


def partner(v):
    lane = lax.broadcasted_iota(jnp.int32, v.shape, 1)
    ahead = pltpu.roll(v, LANES - HALF // 2, 1)
    behind = pltpu.roll(v, HALF // 2, 1)
    return jnp.where(lane % HALF < HALF // 2, ahead, behind)


def head_mean(v):
    lane = lax.broadcasted_iota(jnp.int32, v.shape, 1)
    first = jnp.sum(jnp.where(lane < HALF, v, 0.0), axis=1, keepdims=True)
    second = jnp.sum(jnp.where(lane < HALF, 0.0, v), axis=1, keepdims=True)
    return jnp.where(lane < HALF, first, second) * (1.0 / HALF)


def head_forward(raw, gain, flag, cosine, sine):
    scaler = jnp.where(flag > 0, lax.rsqrt(head_mean(raw * raw) + EPSILON), 1.0)
    normed = raw * scaler * gain
    cosine = jnp.where(flag > 0, cosine, 1.0)
    sine = jnp.where(flag > 0, sine, 0.0)
    return normed * cosine + partner(normed) * sine


def head_backward(grad, raw, gain, flag, cosine, sine):
    on = flag > 0
    scaler = lax.rsqrt(head_mean(raw * raw) + EPSILON)
    back = grad * cosine - partner(grad) * sine
    scaled = back * gain
    inner = head_mean(scaled * raw)
    grad_raw = scaler * scaled - raw * (scaler * scaler * scaler) * inner
    gain_term = jnp.sum(jnp.where(on, back * raw * scaler, 0.0), axis=0, keepdims=True)
    return jnp.where(on, grad_raw, grad), gain_term


def qkv_kernel(act_ref, w_ref, gain_ref, flag_ref, cos_ref, sin_ref, raw_ref, out_ref):
    raw = dot(act_ref[...], w_ref[...])
    raw_ref[...] = raw
    for part in range(raw.shape[1] // LANES):
        at = slice(part * LANES, (part + 1) * LANES)
        done = head_forward(raw[:, at], gain_ref[:, at], flag_ref[:, at], cos_ref[...], sin_ref[...])
        out_ref[:, at] = done.astype(BF16)


def qkv_call(act, w_all, gain, flag, cosine, sine):
    tok, width = act.shape
    cols = w_all.shape[1]
    block = 256
    whole = lambda shape: pl.BlockSpec(shape, lambda i: (0, 0))
    chunk = lambda rows: pl.BlockSpec((rows, block), lambda i: (0, i))
    return pl.pallas_call(
        qkv_kernel,
        grid=(cols // block,),
        in_specs=[whole((tok, width)), chunk(width), chunk(1), chunk(1), whole((tok, LANES)), whole((tok, LANES))],
        out_specs=[chunk(tok), chunk(tok)],
        out_shape=[jax.ShapeDtypeStruct((tok, cols), F32), jax.ShapeDtypeStruct((tok, cols), BF16)],
        compiler_params=pltpu.CompilerParams(vmem_limit_bytes=VMEM_LIMIT),
        cost_estimate=pl.CostEstimate(flops=2 * tok * width * cols, bytes_accessed=2 * width * cols, transcendentals=0),
        name="qkv_heads",
    )(act, w_all, gain, flag, cosine, sine)


GROUPS = ((0, 4), (4, 4), (8, 2))
K_AT = (0, 64, 128)
V_AT = (256, 320, 192)


def stack_heads(wide, tok):
    turned, tall = [], []
    for pair in range(wide.shape[1] // LANES):
        chunk = wide[:, pair * LANES : (pair + 1) * LANES]
        flat = chunk.astype(F32).T.astype(BF16)
        turned += [flat[:HALF], flat[HALF:]]
        tall += [chunk[:, :HALF], chunk[:, HALF:]]
    return jnp.concatenate(turned, axis=1), jnp.concatenate(tall, axis=0)


def key_mask(base_same, base_other, limits_ref, tok):
    key = lax.broadcasted_iota(jnp.int32, (2 * tok, tok), 0)
    key = key + jnp.where(key < tok, base_same, base_other - tok)
    return (key >= limits_ref[0:1, :]) & (key <= limits_ref[1:2, :])


def forward_kernel(bounds_ref, limits_ref, q_ref, same_ref, other_ref, att_ref, turned_ref, inv_ref, q_turned):
    tok = q_ref.shape[0]
    turned, tall = stack_heads(q_ref[...], tok)
    q_turned[...] = turned
    turned_ref[...] = jnp.zeros_like(turned_ref)
    inv_ref[...] = jnp.zeros_like(inv_ref)
    core = bounds_ref[2]

    @pl.loop(bounds_ref[0], bounds_ref[1])
    def step(j):
        kv = jnp.concatenate([same_ref[j], other_ref[j]], axis=0)
        ok = key_mask((2 * j + core) * tok, (2 * j + 1 - core) * tok, limits_ref, tok)
        for g, (first, count) in enumerate(GROUPS):
            at = slice(first * tok, (first + count) * tok)
            keys = kv[:, K_AT[g] : K_AT[g] + HALF]
            vals = kv[:, V_AT[g] : V_AT[g] + HALF]
            logit = dot(keys, q_turned[:, at])
            allowed = jnp.concatenate([ok] * count, axis=1)
            expo = jnp.where(allowed, jnp.exp(logit), 0.0)
            inv_ref[:, at] += jnp.sum(expo, axis=0, keepdims=True)
            turned_ref[:, at] += dot(vals, expo.astype(BF16), ((0,), (0,)))

    inverse = 1.0 / inv_ref[...]
    inv_ref[...] = inverse
    turned_ref[...] = turned_ref[...] * inverse
    for pair in range(att_ref.shape[1] // LANES):
        at = 2 * pair * tok
        both = jnp.concatenate([turned_ref[:, at : at + tok], turned_ref[:, at + tok : at + 2 * tok]], axis=0)
        att_ref[:, pair * LANES : (pair + 1) * LANES] = both.T.astype(BF16)


def vmem(n):
    return [pl.BlockSpec(memory_space=pltpu.VMEM)] * n


SMEM = pl.BlockSpec(memory_space=pltpu.SMEM)


def forward_call(bounds, limits, q, same, other):
    tok, width = q.shape
    wide = width // HALF * tok
    work = same.shape[0] * 2 * tok * wide
    return pl.pallas_call(
        forward_kernel,
        in_specs=[SMEM] + vmem(4),
        out_specs=vmem(3),
        out_shape=[
            jax.ShapeDtypeStruct((tok, width), BF16),
            jax.ShapeDtypeStruct((HALF, wide), F32),
            jax.ShapeDtypeStruct((1, wide), F32),
        ],
        scratch_shapes=[pltpu.VMEM((HALF, wide), BF16)],
        compiler_params=pltpu.CompilerParams(vmem_limit_bytes=VMEM_LIMIT),
        cost_estimate=pl.CostEstimate(flops=4 * HALF * work, bytes_accessed=4 * same.size, transcendentals=work),
        name="attention_forward",
    )(bounds, limits, q, same, other)


def backward_kernel(
    bounds_ref,
    limits_ref,
    q_ref,
    grad_ref,
    turned_ref,
    inv_ref,
    same_ref,
    other_ref,
    raw_ref,
    gain_ref,
    cos_ref,
    sin_ref,
    dq_ref,
    gain_grad_ref,
    same_out,
    other_out,
    q_turned,
    q_tall,
    g_turned,
    g_tall,
    dq_acc,
):
    tok = q_ref.shape[0]
    q_turned[...], q_tall[...] = stack_heads(q_ref[...], tok)
    g_turned[...], g_tall[...] = stack_heads(grad_ref[...], tok)
    dq_acc[...] = jnp.zeros_like(dq_acc)
    same_out[...] = jnp.zeros_like(same_out)
    other_out[...] = jnp.zeros_like(other_out)
    core = bounds_ref[2]
    delta = jnp.sum(g_turned[...].astype(F32) * turned_ref[...], axis=0, keepdims=True)

    @pl.loop(bounds_ref[0], bounds_ref[1])
    def step(j):
        kv = jnp.concatenate([same_ref[j], other_ref[j]], axis=0)
        ok = key_mask((2 * j + core) * tok, (2 * j + 1 - core) * tok, limits_ref, tok)
        for g, (first, count) in enumerate(GROUPS):
            at = slice(first * tok, (first + count) * tok)
            keys = kv[:, K_AT[g] : K_AT[g] + HALF]
            vals = kv[:, V_AT[g] : V_AT[g] + HALF]
            allowed = jnp.concatenate([ok] * count, axis=1)
            prob = jnp.where(allowed, jnp.exp(dot(keys, q_turned[:, at])) * inv_ref[:, at], 0.0)
            d_score = (prob * (dot(vals, g_turned[:, at]) - delta[:, at])).astype(BF16)
            d_keys = dot(d_score, q_tall[at, :]).astype(BF16)
            d_vals = dot(prob.astype(BF16), g_tall[at, :]).astype(BF16)
            dq_acc[:, at] += dot(keys, d_score, ((0,), (0,)))
            same_out[j, :, K_AT[g] : K_AT[g] + HALF] = d_keys[:tok]
            other_out[j, :, K_AT[g] : K_AT[g] + HALF] = d_keys[tok:]
            same_out[j, :, V_AT[g] : V_AT[g] + HALF] = d_vals[:tok]
            other_out[j, :, V_AT[g] : V_AT[g] + HALF] = d_vals[tok:]

    total = jnp.zeros((1, LANES), F32)
    for pair in range(dq_ref.shape[1] // LANES):
        at = 2 * pair * tok
        both = jnp.concatenate([dq_acc[:, at : at + tok], dq_acc[:, at + tok : at + 2 * tok]], axis=0)
        cols = slice(pair * LANES, (pair + 1) * LANES)
        d_raw, term = head_backward(
            both.T * SCALE, raw_ref[:, cols], gain_ref[...], jnp.ones((1, LANES), F32), cos_ref[...], sin_ref[...]
        )
        dq_ref[:, cols] = d_raw.astype(BF16)
        total += term
    gain_grad_ref[...] = total


def backward_call(bounds, limits, q, grad, turned, inv, same, other, raw, gain, cosine, sine):
    tok, width = q.shape
    wide = width // HALF * tok
    work = same.shape[0] * 2 * tok * wide
    return pl.pallas_call(
        backward_kernel,
        in_specs=[SMEM] + vmem(11),
        out_specs=vmem(4),
        out_shape=[
            jax.ShapeDtypeStruct((tok, width), BF16),
            jax.ShapeDtypeStruct((1, LANES), F32),
            jax.ShapeDtypeStruct(same.shape, BF16),
            jax.ShapeDtypeStruct(other.shape, BF16),
        ],
        scratch_shapes=[
            pltpu.VMEM((HALF, wide), BF16),
            pltpu.VMEM((wide, HALF), BF16),
            pltpu.VMEM((HALF, wide), BF16),
            pltpu.VMEM((wide, HALF), BF16),
            pltpu.VMEM((HALF, wide), F32),
        ],
        compiler_params=pltpu.CompilerParams(vmem_limit_bytes=VMEM_LIMIT),
        cost_estimate=pl.CostEstimate(flops=10 * HALF * work, bytes_accessed=8 * same.size, transcendentals=work),
        name="attention_backward",
    )(bounds, limits, q, grad, turned, inv, same, other, raw, gain, cosine, sine)


def kv_back_kernel(parts_ref, raw_ref, gain_ref, flag_ref, cos_ref, sin_ref, out_ref, gain_grad_ref):
    total = jnp.zeros((1, LANES), F32)
    for part in range(out_ref.shape[1] // LANES):
        at = slice(part * LANES, (part + 1) * LANES)
        grad = jnp.sum(parts_ref[:, :, at].astype(F32), axis=0)
        done, term = head_backward(
            grad, raw_ref[:, at], gain_ref[:, at], flag_ref[:, at], cos_ref[...], sin_ref[...]
        )
        out_ref[:, at] = done.astype(BF16)
        total += term
    gain_grad_ref[...] = total


def kv_back_call(parts, raw, gain, flag, cosine, sine):
    tok, width = raw.shape
    return pl.pallas_call(
        kv_back_kernel,
        in_specs=vmem(6),
        out_specs=vmem(2),
        out_shape=[jax.ShapeDtypeStruct((tok, width), BF16), jax.ShapeDtypeStruct((1, LANES), F32)],
        compiler_params=pltpu.CompilerParams(vmem_limit_bytes=VMEM_LIMIT),
        cost_estimate=pl.CostEstimate(flops=30 * tok * width, bytes_accessed=2 * parts.size, transcendentals=0),
        name="key_value_heads_back",
    )(parts, raw, gain, flag, cosine, sine)


def rope_tables(positions, head_dim):
    half = head_dim // 2
    inverse = jnp.exp(jnp.arange(half, dtype=F32) * (-2.0 * math.log(10000.0) / head_dim))
    angles = positions.astype(F32)[:, None] * inverse[None, :]
    cosine, sine = jnp.cos(angles), jnp.sin(angles)
    return jnp.concatenate([cosine] * 4, axis=1), jnp.concatenate([-sine, sine, -sine, sine], axis=1)


def norm_scale(vectors):
    return lax.rsqrt(jnp.mean(vectors * vectors, axis=-1, keepdims=True) + EPSILON)


def norm_back(vectors, scaler, gains, grads_in):
    scaled = grads_in * gains
    inner_mean = jnp.mean(scaled * vectors, axis=-1, keepdims=True)
    return scaler * scaled - vectors * (scaler * scaler * scaler) * inner_mean


def backwards(array, axis, width):
    count = array.shape[axis] // width
    pieces = [lax.slice_in_dim(array, i * width, (i + 1) * width, axis=axis) for i in range(count)]
    return jnp.concatenate(pieces[::-1], axis=axis)


def body(
    tokens,
    w_query,
    key_value_weight,
    w_out,
    w_gate,
    w_up,
    w_down,
    attn_gain,
    ffn_gain,
    query_gain,
    key_gain,
    segments,
    positions,
    out_grad,
):
    tok, width = tokens.shape
    rows = lax.axis_size("row")
    row = lax.axis_index("row")
    col = lax.axis_index("col")
    core = row % 2
    w_rows = w_query.shape[0]
    q_width = w_query.shape[1]
    kv_half = key_value_weight.shape[1] // 2
    ff_cols = w_gate.shape[1]
    ff = ff_cols // MEMBERS
    seq_len = min(SEQ_MAX, tok * rows)
    span = seq_len // tok
    half = tok // 2

    def kv_pick(order):
        k = [key_value_weight[:, h * HALF : (h + 1) * HALF] for h in order]
        v = [key_value_weight[:, kv_half + h * HALF : kv_half + (h + 1) * HALF] for h in order]
        return jnp.concatenate([k[0], k[1], k[2], v[2], v[0], v[1]], axis=1)

    w_one = jnp.where(
        col == 0,
        jnp.concatenate([w_query, kv_pick((0, 1, 2))], axis=1),
        jnp.concatenate([backwards(w_query, 1, LANES), kv_pick((4, 3, 2))], axis=1),
    )
    w_one_all = lax.all_gather(w_one, "row", axis=0, tiled=True)
    w_o = jnp.where(col == 0, w_out, backwards(w_out, 0, LANES))
    w_o_all = lax.all_gather(w_o, "row", axis=1, tiled=True)

    w_ff = jnp.concatenate(
        [
            w_gate.reshape(w_rows, MEMBERS, ff),
            w_up.reshape(w_rows, MEMBERS, ff),
            w_down.T.reshape(w_rows, MEMBERS, ff),
        ],
        axis=2,
    ).transpose(1, 0, 2)
    w_ff_all = lax.all_to_all(
        jnp.concatenate([w_ff] * (rows // MEMBERS), axis=0), "row", split_axis=0, concat_axis=0, tiled=True
    ).reshape(width, 3 * ff)

    input_f = tokens.astype(F32)
    act_scale = norm_scale(input_f)
    act_low = (input_f * act_scale * attn_gain).astype(BF16)
    cosine, sine = rope_tables(positions, HALF)
    q_lanes = jnp.tile(query_gain, 2)[None, :]
    k_lanes = jnp.tile(key_gain, 2)[None, :]
    kv_flag = jnp.concatenate([jnp.ones((1, 3 * HALF), F32), jnp.zeros((1, 3 * HALF), F32)], axis=1)
    kv_gain = jnp.where(kv_flag > 0, jnp.tile(k_lanes, (1, 3)), 1.0)
    flag = jnp.concatenate([jnp.ones((1, q_width), F32), kv_flag], axis=1)
    gain = jnp.concatenate([jnp.tile(q_lanes * SCALE, (1, q_width // LANES)), kv_gain], axis=1)
    raw, heads = qkv_call(act_low, w_one_all, gain, flag, cosine, sine)
    query, kv_low = heads[:, :q_width], heads[:, q_width:]
    same_kv, other_kv = gather_plane(kv_low, span)

    in_span = row % span
    seq_segments = lax.dynamic_slice_in_dim(segments, (row - in_span) * tok, seq_len, 0)
    own_segments = lax.dynamic_slice_in_dim(segments, row * tok, tok, 0)
    own_index = in_span * tok + jnp.arange(tok, dtype=jnp.int32)
    index = jnp.arange(seq_len, dtype=jnp.int32)
    start = jnp.min(jnp.where(seq_segments[None, :] == own_segments[:, None], index[None, :], seq_len), axis=1)
    start = jnp.where(own_segments < 0, own_index, start)
    limits = jnp.stack([start, own_index])
    bounds = jnp.stack([jnp.min(start) // (2 * tok), in_span // 2 + 1, core])
    attn_low, turned, inv = forward_call(bounds, limits, query, same_kv, other_kv)
    same_att, other_att = gather_plane(attn_low, rows)
    attn_part = dot(attn_low, w_o_all).astype(BF16)

    def mine(array, which):
        return lax.dynamic_slice_in_dim(array, which * half, half, 0)

    arrived = swap_col(mine(attn_part, 1 - col))
    hidden = mine(input_f, col) + (mine(attn_part, col).astype(F32) + arrived.astype(F32))

    ffn_scale = norm_scale(hidden)
    ffn_low = (hidden * ffn_scale * ffn_gain).astype(BF16)
    og_low = mine(out_grad, col)
    og_all = jnp.concatenate([a.reshape(-1, width) for a in gather_cube(og_low)], axis=0)
    ffn_all = jnp.concatenate([a.reshape(-1, width) for a in gather_cube(ffn_low)], axis=0)
    group = ffn_all.shape[0]
    gate_up = dot(ffn_all, w_ff_all[:, : 2 * ff])
    gate_pre, up_pre = gate_up[:, :ff], gate_up[:, ff:]
    d_inner = dot(og_all, w_ff_all[:, 2 * ff :])
    sigma = jax.nn.sigmoid(gate_pre)
    silu_gate = gate_pre * sigma
    inner_low = (silu_gate * up_pre).astype(BF16)
    d_gate = d_inner * up_pre * (sigma * (1.0 + gate_pre * (1.0 - sigma)))
    d_up = d_inner * silu_gate
    d_gate_up = jnp.concatenate([d_gate, d_up], axis=1).astype(BF16)

    def reduce_cube(left, right):
        count = group // 2 // half
        away = dot(left[group // 2 :], right, ((1,), (1,))).astype(BF16)
        here = dot(left[: group // 2], right, ((1,), (1,)))
        total = (here + swap_core(away).astype(F32)).astype(BF16)
        parts = exchange_cube(total.reshape(count, half, width))
        return jnp.sum(parts.astype(F32), axis=0)

    ffn_back = reduce_cube(d_gate_up, w_ff_all[:, : 2 * ff])
    grads_ff = jnp.concatenate(
        [dot(ffn_all, d_gate_up, ((0,), (0,))), dot(og_all, inner_low, ((0,), (0,)))], axis=1
    ).astype(BF16)
    grads_ff = lax.all_to_all(
        grads_ff.reshape(rows, w_rows, 3 * ff), "row", split_axis=0, concat_axis=0, tiled=True
    )
    ffn_out = reduce_cube(inner_low, w_ff_all[:, 2 * ff :])
    out_half = (hidden + ffn_out).astype(BF16)
    output = halves(out_half, swap_col(out_half), col)

    d_hidden = og_low.astype(F32) + norm_back(hidden, ffn_scale, ffn_gain, ffn_back)
    d_hidden_half = d_hidden.astype(BF16)
    d_hidden_low = halves(d_hidden_half, swap_col(d_hidden_half), col)

    d_attn = dot(d_hidden_low, w_o_all, ((1,), (1,))).astype(BF16)
    d_q, q_gain_part, same_d, other_d = backward_call(
        bounds, limits, query, d_attn, turned, inv, same_kv, other_kv, raw[:, :q_width], q_lanes, cosine, sine
    )
    same_dq, other_dq = gather_plane(d_q, rows)
    kv_parts = exchange_plane((same_d.astype(F32) + swap_core(other_d).astype(F32)).astype(BF16), span)
    d_kv, k_gain_part = kv_back_call(kv_parts, raw[:, q_width:], kv_gain, kv_flag, cosine, sine)
    same_dkv, other_dkv = gather_plane(d_kv, rows)

    d_one = jnp.concatenate([d_q, d_kv], axis=1)
    act_back = dot(d_one, w_one_all, ((1,), (1,))).astype(BF16)
    act_back = act_back.astype(F32) + swap_col(act_back).astype(F32)
    input_grad = d_hidden_low.astype(F32) + norm_back(input_f, act_scale, attn_gain, act_back)

    columns = jnp.concatenate([act_low.reshape(tok, rows, w_rows), d_hidden_low.reshape(tok, rows, w_rows)], axis=2)
    columns = lax.all_to_all(columns.transpose(1, 0, 2), "row", split_axis=0, concat_axis=0, tiled=True)
    columns = columns.reshape(rows // 2, 2, tok, 2 * w_rows)
    same_cols = lax.dynamic_index_in_dim(columns, core, 1, keepdims=False).reshape(-1, 2 * w_rows)
    other_cols = lax.dynamic_index_in_dim(columns, 1 - core, 1, keepdims=False).reshape(-1, 2 * w_rows)

    def over_tokens(left, right):
        return dot(left[0], right[0].reshape(left[0].shape[0], -1), ((0,), (0,))) + dot(
            left[1], right[1].reshape(left[1].shape[0], -1), ((0,), (0,))
        )

    act_cols = (same_cols[:, :w_rows], other_cols[:, :w_rows])
    hid_cols = (same_cols[:, w_rows:], other_cols[:, w_rows:])
    grad_q = over_tokens(act_cols, (same_dq, other_dq))
    grad_kv = over_tokens(act_cols, (same_dkv, other_dkv))
    grad_o = over_tokens(
        (same_att.reshape(-1, q_width), other_att.reshape(-1, q_width)), hid_cols
    )
    grad_query = jnp.where(col == 0, grad_q, backwards(grad_q, 1, LANES))
    grad_out = jnp.where(col == 0, grad_o, backwards(grad_o, 0, LANES))

    kv_own = grad_kv.astype(BF16)
    kv_away = swap_col(kv_own)
    kv_first = jnp.where(col == 0, kv_own, kv_away).astype(F32)
    kv_last = jnp.where(col == 0, kv_away, kv_own).astype(F32)

    def head_cols(array, at):
        return array[:, at : at + HALF]

    pieces = []
    for at in (K_AT, V_AT):
        pieces += [head_cols(kv_first, at[0]), head_cols(kv_first, at[1])]
        pieces += [head_cols(kv_first, at[2]) + head_cols(kv_last, at[2])]
        pieces += [head_cols(kv_last, at[1]), head_cols(kv_last, at[0])]
    grad_keyval = jnp.concatenate(pieces, axis=1)

    grads_ff = jnp.sum(grads_ff.reshape(rows // MEMBERS, MEMBERS, w_rows, 3 * ff).astype(F32), axis=0)
    grads_ff = grads_ff.transpose(1, 0, 2)
    grad_gate = grads_ff[:, :, :ff].reshape(w_rows, ff_cols)
    grad_up = grads_ff[:, :, ff : 2 * ff].reshape(w_rows, ff_cols)
    grad_down = grads_ff[:, :, 2 * ff :].reshape(w_rows, ff_cols).T

    attn_part_gain = jnp.sum(jnp.concatenate([grad_q, grad_kv], axis=1) * w_one.astype(F32), axis=1)
    ffn_part_gain = jnp.sum(grad_gate * w_gate.astype(F32) + grad_up * w_up.astype(F32), axis=1)
    per_row = HALF // rows
    small = jnp.concatenate(
        [
            (q_gain_part[0, :HALF] + q_gain_part[0, HALF:]).reshape(rows, per_row),
            (k_gain_part[0, :HALF] + k_gain_part[0, HALF:]).reshape(rows, per_row),
        ],
        axis=1,
    )
    small = jnp.sum(lax.all_to_all(small, "row", split_axis=0, concat_axis=0, tiled=True), axis=0)
    gains = jnp.concatenate([attn_part_gain, ffn_part_gain, small])
    gains = gains + swap_col(gains)
    own_gains = lambda whole: lax.dynamic_slice_in_dim(whole, row * w_rows, w_rows, 0)
    grad_attn_gain = gains[:w_rows] / own_gains(attn_gain)
    grad_ffn_gain = gains[w_rows : 2 * w_rows] / own_gains(ffn_gain)
    grad_query_gain = gains[2 * w_rows : 2 * w_rows + per_row]
    grad_key_gain = gains[2 * w_rows + per_row :]
    return (
        output,
        input_grad,
        grad_query,
        grad_keyval,
        grad_out,
        grad_gate,
        grad_up,
        grad_down,
        grad_attn_gain,
        grad_ffn_gain,
        grad_query_gain,
        grad_key_gain,
    )


def solution(mesh):
    placed = (
        P("row", None),
        P("row", "col"),
        P("row", None),
        P("col", "row"),
        P("row", "col"),
        P("row", "col"),
        P("col", "row"),
        P(),
        P(),
        P(),
        P(),
        P(),
        P("row"),
        P("row", None),
    )
    return jax.shard_map(
        body,
        mesh=mesh,
        in_specs=placed,
        out_specs=(
            P("row", None),
            P("row", None),
            P("row", "col"),
            P("row", None),
            P("col", "row"),
            P("row", "col"),
            P("row", "col"),
            P("col", "row"),
            P("row"),
            P("row"),
            P("row"),
            P("row"),
        ),
        check_vma=False,
    )
```

time: 1740 us -> 646 us (0.37)
  waiting for transfers between devices: 1340 us -> 348 us
  blocking collectives: 66 us -> 0 us
  matrix products: 106 us -> 50.8 us
    reduce_scatter x6 -> x0, waiting for transfers between devices: 776 us -> none  [the longest x1 215 us: body(): lax.psum_scatter(grad_up, 'row', scatter_dimension=0, tiled=True)]
    all_to_all x0 -> x13, waiting for transfers between devices: none -> 265 us  [the longest x5 101 us: exchange_plane(): lax.all_to_all(blocks, 'row', split_axis=0, concat_axis=0, tiled=True, ax...]
    all_gather x6 -> x2, waiting for transfers between devices: 296 us -> 57.2 us  [the longest x1 49.3 us: body(): w_one_all = lax.all_gather(w_one, 'row', axis=0, tiled=True)]
    psum x3 -> x0, waiting for transfers between devices: 148 us -> none  [the longest x1 64.2 us: body(): lax.psum(attn_part.astype(jnp.bfloat16), 'col').astype(jnp.float32)]
    all_to_all x0 -> x13, starting transfers between devices: none -> 90 us  [the longest x5 49.6 us: exchange_plane(): lax.all_to_all(blocks, 'row', split_axis=0, concat_axis=0, tiled=True, ax...]
    ppermute x30 -> x15, waiting for transfers between devices: 115 us -> 26.2 us  [the longest x6 19.5 us: swap_col(): return lax.ppermute(block, 'col', [(0, 1), (1, 0)])]
    ppermute x30 -> x15, starting transfers between devices: 115 us -> 29.1 us  [the longest x6 27.3 us: swap_col(): return lax.ppermute(block, 'col', [(0, 1), (1, 0)])]
    unnamed x1 -> x0, blocking collectives: 61.1 us -> none
  transfers between devices with their start and end apart: 45 -> 30, of which waited for: 42 -> 19; matrix products, arithmetic and copies ran while one was open for 6% -> 18% of each run, Pallas kernels for 0% -> 3%
where the time goes in v1:
time: 646 us; the launch traced here: 639 us
  waiting for transfers between devices  348 us (54%)
  starting transfers between devices  119 us (18%)
  matrix products  50.8 us (8%)
  local copies, waits for them, and re-layouts  49.7 us (8%)
  other arithmetic  36.6 us (6%)
  between operations  18.2 us (3%)
  Pallas kernels  16.1 us (2%)
    all_to_all x5, waiting for transfers between devices, exchange_plane(): lax.all_to_all(blocks, 'row', split_axis=0, concat_axis=0, tiled=True, ax...  101 us
    all_to_all x1, waiting for transfers between devices, body(): lax.all_to_all(jnp.concatenate([w_ff] * (rows // MEMBERS), axis=0), 'row'...  72.4 us
    dot_general x17, matrix products, dot(): return lax.dot_general(a, b, (dims, ((), ())), preferred_element_type=F32)  50.8 us
    all_to_all x5, starting transfers between devices, exchange_plane(): lax.all_to_all(blocks, 'row', split_axis=0, concat_axis=0, tiled=True, ax...  49.6 us
    all_gather x1, waiting for transfers between devices, body(): w_one_all = lax.all_gather(w_one, 'row', axis=0, tiled=True)  49.3 us
    all_to_all x1, waiting for transfers between devices, body(): lax.all_to_all(grads_ff.reshape(rows, w_rows, 3 * ff), 'row', split_axis=...  46.6 us
    all_to_all x4, waiting for transfers between devices, exchange_cube(): lax.all_to_all(blocks, ('row', 'col'), split_axis=0, concat_axis=0, tiled...  44.5 us
    ppermute x6, starting transfers between devices, swap_col(): return lax.ppermute(block, 'col', [(0, 1), (1, 0)])  27.3 us
  transfers between devices with their start and end apart: 30, of which 19 were waited for; matrix products, arithmetic and copies ran while one was open for 18% of the time, Pallas kernels for 3%

profile of v1, /device:TPU:0, one launch (start us, length us, event | category | flops | bytes accessed | tf_op | source)
XLA Modules:
  0.0 639.0 jit_solution(3983903330535936321)
XLA Ops:
  16.9 49.3 %all-gather.3.cloned.1.call-done.w_ref = bf16[2048,1024]{1,0:T(8,128)(2,1)} async-done(((bf16[128,1024]{1,0:T(8,128)(2,1)}), bf16[2048,1024]{1,0:T(8,128)(2,1)}) %all-gather.3.cloned.1.call-update) | async-done | bytes 4194320 | tf_op jit(solution)/shard_map/all_gather | solution.py:403
  66.2 5.0 qkv_heads.1
  73.2 3.5 all-to-all-start
  76.8 24.6 %all-to-all-done.same_ref = bf16[8,128,384]{2,1,0:T(8,128)(2,1)S(1)} async-done(((bf16[8,128,384]{2,1,0:T(8,128)(2,1)}), bf16[8,128,384]{2,1,0:T(8,128)(2,1)S(1)}, u32[]{:S(2)}, u32[]{:S(2)}) %all-to-all-start) | async-done | bytes 786464 | tf_op jit(solution)/shard_map/all_to_all | solution.py:53
  103.0 3.7 all-to-all-start.4
  113.4 3.2 attention_forward.1
  116.6 7.8 %all-gather.5.cloned.1.call-done = bf16[640,2048]{1,0:T(8,128)(2,1)} async-done(((bf16[640,128]{1,0:T(8,128)(2,1)}), bf16[640,2048]{1,0:T(8,128)(2,1)}) %all-gather.5.cloned.1.call-update) | async-done | bytes 2621456 | tf_op jit(solution)/shard_map/all_gather | solution.py:405
  124.4 2.4 convolution_convert_fusion.4
  126.9 18.1 %collective-permute-start.1 = (bf16[64,2048]{1,0:T(8,128)(2,1)S(1)}, bf16[64,2048]{1,0:T(8,128)(2,1)S(1)}, u32[]{:S(2)}, u32[]{:S(2)}) collective-permute-start(bf16[64,2048]{1,0:T(8,128)(2,1)S(1)} %constant_dynamic-slice_fusion.3), channel_id=1, source_target_pairs={{0,1},{1,0},{2,3},{3,2},{4,5},{5,4},{6,7},{7,6},{8,9},{9,8},{10,11... | collective-permute-start | bytes 786440 | tf_op jit(solution)/shard_map/ppermute | solution.py:31
  145.1 6.6 %collective-permute-done.1 = bf16[64,2048]{1,0:T(8,128)(2,1)S(1)} collective-permute-done((bf16[64,2048]{1,0:T(8,128)(2,1)S(1)}, bf16[64,2048]{1,0:T(8,128)(2,1)S(1)}, u32[]{:S(2)}, u32[]{:S(2)}) %collective-permute-start.1) | collective-permute-done | bytes 262176 | tf_op jit(solution)/shard_map/ppermute | solution.py:31
  152.9 1.9 broadcast_in_dim.32
  155.0 4.8 all-to-all-start.1
  162.0 2.2 pad_maximum_fusion.2
  164.2 21.5 %all-to-all-done.1 = bf16[8,64,2048]{2,1,0:T(8,128)(2,1)} async-done(((bf16[8,64,2048]{2,1,0:T(8,128)(2,1)}), bf16[8,64,2048]{2,1,0:T(8,128)(2,1)}, u32[]{:S(2)}, u32[]{:S(2)}) %all-to-all-start.1) | async-done | bytes 2097184 | tf_op jit(solution)/shard_map/all_to_all | solution.py:59
  185.7 6.9 %all-to-all-start.2 = ((bf16[16,128,960]{1,2,0:T(8,128)(2,1)}), bf16[16,128,960]{1,2,0:T(8,128)(2,1)}, u32[]{:S(2)}, u32[]{:S(2)}) async-start(bf16[16,128,960]{1,2,0:T(8,128)(2,1)} %pad_maximum_fusion.2), calls=%async_computation.2 | async-start | bytes 7864320 | tf_op jit(solution)/shard_map/all_to_all | solution.py:415
  193.3 72.4 %all-to-all-done.2 = bf16[16,128,960]{1,2,0:T(8,128)(2,1)} async-done(((bf16[16,128,960]{1,2,0:T(8,128)(2,1)}), bf16[16,128,960]{1,2,0:T(8,128)(2,1)}, u32[]{:S(2)}, u32[]{:S(2)}) %all-to-all-start.2) | async-done | bytes 3932192 | tf_op jit(solution)/shard_map/all_to_all | solution.py:415
  265.7 2.7 copy_bitcast_fusion
  268.4 6.5 %fusion.2 = f32[1024,640]{0,1:T(8,128)S(1)} fusion(bf16[512,2048]{1,0:T(8,128)(2,1)} %bitcast.5, bf16[512,2048]{1,0:T(8,128)(2,1)} %bitcast.4, bf16[2048,960]{0,1:T(8,128)(2,1)S(1)} %copy_bitcast_fusion), kind=kOutput, calls=%fused_computation.15 | convolution fusion | flops 2692743168 | bytes 9437184 | tf_op jit(solution)/shard_map/dot_general | solution.py:22
  275.0 4.7 multiply_convert_fusion
  279.7 2.7 convolution_convert_fusion.1
  284.3 18.0 %all-to-all-start.10 = ((bf16[8,128,640]{2,1,0:T(8,128)(2,1)}), bf16[8,128,640]{2,1,0:T(8,128)(2,1)}, u32[]{:S(2)}, u32[]{:S(2)}) async-start(bf16[8,128,640]{2,1,0:T(8,128)(2,1)} %broadcast_in_dim.36), calls=%async_computation.10 | async-start | bytes 2621440 | tf_op jit(solution)/shard_map/all_to_all | solution.py:53
  302.3 4.0 add_convert_fusion.1
  306.3 27.9 %all-to-all-done.10 = bf16[8,128,640]{2,1,0:T(8,128)(2,1)} async-done(((bf16[8,128,640]{2,1,0:T(8,128)(2,1)}), bf16[8,128,640]{2,1,0:T(8,128)(2,1)}, u32[]{:S(2)}, u32[]{:S(2)}) %all-to-all-start.10) | async-done | bytes 1310752 | tf_op jit(solution)/shard_map/all_to_all | solution.py:53
  334.2 5.6 all-to-all-start.3
  339.8 3.8 convolution_convert_fusion.2
  343.7 4.1 collective-permute-done.6
  347.9 3.3 add_convert_fusion
  351.1 14.2 %all-to-all-done.3 = bf16[8,64,2048]{2,1,0:T(8,128)(2,1)S(1)} async-done(((bf16[8,64,2048]{2,1,0:T(8,128)(2,1)}), bf16[8,64,2048]{2,1,0:T(8,128)(2,1)S(1)}, u32[]{:S(2)}, u32[]{:S(2)}) %all-to-all-start.3) | async-done | bytes 2097184 | tf_op jit(solution)/shard_map/all_to_all | solution.py:59
  366.7 4.6 all-to-all-start.5
  371.3 7.5 %convolution_convert_fusion = bf16[2048,640]{1,0:T(8,128)(2,1)} fusion(bf16[512,2048]{1,0:T(8,128)(2,1)} %bitcast.5, bf16[512,2048]{1,0:T(8,128)(2,1)} %bitcast.4, bf16[1024,320]{0,1:T(8,128)(2,1)S(1)} %copy-done.44, bf16[1024,320]{0,1:T(8,128)(2,1)} %get-tuple-element.114), kind=kOutput, calls=%fused_computation.10 | convolution fusion | flops 2696675328 | bytes 8126464 | tf_op jit(solution)/shard_map/dot_general | solution.py:22
  378.8 3.2 copy.108
  382.0 4.0 fusion.10
  386.3 2.2 pad_maximum_fusion.3
  388.5 8.8 %all-to-all-done.5 = bf16[8,64,2048]{2,1,0:T(8,128)(2,1)} async-done(((bf16[8,64,2048]{2,1,0:T(8,128)(2,1)}), bf16[8,64,2048]{2,1,0:T(8,128)(2,1)}, u32[]{:S(2)}, u32[]{:S(2)}) %all-to-all-start.5) | async-done | bytes 2097184 | tf_op jit(solution)/shard_map/all_to_all | solution.py:59
  397.3 5.1 all-to-all-start.11
  402.4 2.2 convert_reduce_fusion.1
  406.6 2.6 collective-permute-start.7
  411.5 4.5 collective-permute-done.7
  418.7 5.3 attention_backward.1
  424.1 2.5 collective-permute-done.8
  426.5 2.2 add_convert_fusion.2
  428.8 46.6 %all-to-all-done.11 = bf16[16,128,960]{1,2,0:T(8,128)(2,1)} async-done(((bf16[16,128,960]{1,2,0:T(8,128)(2,1)}), bf16[16,128,960]{1,2,0:T(8,128)(2,1)}, u32[]{:S(2)}, u32[]{:S(2)}) %all-to-all-start.11) | async-done | bytes 3932192 | tf_op jit(solution)/shard_map/all_to_all | solution.py:480
  475.4 18.5 %all-to-all-start.6 = ((bf16[8,128,384]{2,1,0:T(8,128)(2,1)}), bf16[8,128,384]{2,1,0:T(8,128)(2,1)S(1)}, u32[]{:S(2)}, u32[]{:S(2)}) async-start(bf16[8,128,384]{2,1,0:T(8,128)(2,1)} %add_convert_fusion.2), calls=%async_computation.6 | async-start | bytes 1572864 | tf_op jit(solution)/shard_map/all_to_all | solution.py:53
  495.5 19.1 %all-to-all-done.6.parts_ref = bf16[8,128,384]{2,1,0:T(8,128)(2,1)S(1)} async-done(((bf16[8,128,384]{2,1,0:T(8,128)(2,1)}), bf16[8,128,384]{2,1,0:T(8,128)(2,1)S(1)}, u32[]{:S(2)}, u32[]{:S(2)}) %all-to-all-start.6) | async-done | bytes 786464 | tf_op jit(solution)/shard_map/all_to_all | solution.py:53
  514.5 4.0 all-to-all-start.7
  518.6 2.6 collective-permute-start.4
  523.2 5.0 collective-permute-done.4
  529.0 5.2 convert_reduce_fusion
  534.3 5.2 copy.122
  539.5 2.5 key_value_heads_back.1
  543.6 5.8 all-to-all-start.12
  549.4 4.8 fusion.49
  554.6 1.9 copy.112
  557.8 5.9 all-to-all-start.8
  568.2 3.0 copy.113
  571.4 2.0 fusion.26
  573.4 1.9 convolution_add_fusion
  578.7 16.8 %all-to-all-done.8 = bf16[8,128,640]{2,1,0:T(8,128)(2,1)} async-done(((bf16[8,128,640]{2,1,0:T(8,128)(2,1)}), bf16[8,128,640]{2,1,0:T(8,128)(2,1)}, u32[]{:S(2)}, u32[]{:S(2)}) %all-to-all-start.8) | async-done | bytes 1310752 | tf_op jit(solution)/shard_map/all_to_all | solution.py:53
  596.4 3.6 all-to-all-start.9
  600.9 2.5 fusion.35
  604.8 2.5 subtract_add_fusion
  607.3 13.1 %all-to-all-done.9 = bf16[8,128,384]{2,1,0:T(8,128)(2,1)S(1)} async-done(((bf16[8,128,384]{2,1,0:T(8,128)(2,1)}), bf16[8,128,384]{2,1,0:T(8,128)(2,1)S(1)}, u32[]{:S(2)}, u32[]{:S(2)}) %all-to-all-start.9) | async-done | bytes 786464 | tf_op jit(solution)/shard_map/all_to_all | solution.py:53
  620.8 1.8 convolution_add_fusion.1
  628.1 2.6 collective-permute-done.12
  (224 shorter events, 57.6 us)
Async XLA Ops:
  7.2 6.6 %copy-start.38 = (pred[3,128]{1,0:T(4,128)(4,1)S(1)}, pred[3,128]{1,0:T(4,128)(4,1)}, u32[]{:S(2)}) copy-start(pred[3,128]{1,0:T(4,128)(4,1)} %constant.100.clone.1) | copy-start | bytes 1156
  7.2 5.7 copy-start.27
  7.2 6.5 %copy-start.39 = (s32[128]{0:T(128)S(1)}, s32[128]{0:T(128)}, u32[]{:S(2)}) copy-start(s32[128]{0:T(128)} %param.26) | copy-start | bytes 1540
  7.2 6.5 %copy-start.40 = (f32[64]{0:T(128)S(1)}, f32[64]{0:T(128)}, u32[]{:S(2)}) copy-start(f32[64]{0:T(128)} %param.24) | copy-start | bytes 772
  7.2 6.6 %copy-start.41 = (f32[64]{0:T(128)S(1)}, f32[64]{0:T(128)}, u32[]{:S(2)}) copy-start(f32[64]{0:T(128)} %param.23) | copy-start | bytes 772
  7.2 59.0 %all-gather.3.cloned.1.call-start = ((), (), s32[]{:S(2)}) async-start(), calls=%async_computation.13 | async-start | bytes 4456448 | tf_op jit(solution)/shard_map/all_gather | solution.py:403
  7.3 8.4 %copy-start = (bf16[128,2048]{1,0:T(8,128)(2,1)S(1)}, bf16[128,2048]{1,0:T(8,128)(2,1)}, u32[]{:S(2)}) copy-start(bf16[128,2048]{1,0:T(8,128)(2,1)} %param.14) | copy-start | bytes 1572868
  9.1 6.7 %copy-start.34 = (f32[2048]{0:T(1024)S(1)}, f32[2048]{0:T(1024)}, u32[]{:S(2)}) copy-start(f32[2048]{0:T(1024)} %param.21) | copy-start | bytes 24580
  12.8 111.6 %all-gather.5.cloned.1.call-start = ((), (), s32[]{:S(2)}) async-start(), calls=%async_computation.14 | async-start | bytes 2785280 | tf_op jit(solution)/shard_map/all_gather | solution.py:405
  13.8 57.5 %copy-start.36 = (f32[1,1,3,128]{3,1,2,0:T(1,128)}, f32[1,1,3,128]{3,1,2,0:T(1,128)S(1)}, u32[]{:S(2)}) copy-start(f32[1,1,3,128]{3,1,2,0:T(1,128)S(1)} %copy.137) | copy-start | bytes 4612
  71.3 5.5 copy-start.30
  73.2 28.2 %all-to-all-start = ((bf16[8,128,384]{2,1,0:T(8,128)(2,1)}), bf16[8,128,384]{2,1,0:T(8,128)(2,1)S(1)}, u32[]{:S(2)}, u32[]{:S(2)}) async-start(bf16[8,128,384]{2,1,0:T(8,128)(2,1)} %broadcast_in_dim.31), calls=%async_computation | async-start | bytes 1572864 | tf_op jit(solution)/shard_map/all_to_all | solution.py:53
  101.4 5.4 copy-start.24
  103.0 3.9 copy-start.37
  103.0 49.9 %all-to-all-start.4 = ((bf16[8,64,2048]{2,1,0:T(8,128)(2,1)}), bf16[8,64,2048]{2,1,0:T(8,128)(2,1)S(1)}, u32[]{:S(2)}, u32[]{:S(2)}) async-start(bf16[8,64,2048]{2,1,0:T(8,128)(2,1)} %broadcast_in_dim.33), calls=%async_computation.4 | async-start | bytes 4194304 | tf_op jit(solution)/shard_map/all_to_all | solution.py:59
  106.8 6.6 %collective-permute-start = (bf16[8,128,384]{2,1,0:T(8,128)(2,1)S(1)}, bf16[8,128,384]{2,1,0:T(8,128)(2,1)}, u32[]{:S(2)}, u32[]{:S(2)}) collective-permute-start(bf16[8,128,384]{2,1,0:T(8,128)(2,1)S(1)} %all-to-all-done.same_ref), channel_id=1, source_target_pairs={{0,2},{2,0},{4,6},{6,4},{8,10},{10,8},{12,14},{14,12},{16,18},{18,... | collective-permute-start | bytes 2359304 | tf_op jit(solution)/shard_map/ppermute | solution.py:27
  126.9 25.9 %copy-start.35 = (f32[2048]{0:T(1024)S(1)}, f32[2048]{0:T(1024)}, u32[]{:S(2)}) copy-start(f32[2048]{0:T(1024)} %param.22) | copy-start | bytes 24580
  126.9 24.9 %collective-permute-start.1 = (bf16[64,2048]{1,0:T(8,128)(2,1)S(1)}, bf16[64,2048]{1,0:T(8,128)(2,1)S(1)}, u32[]{:S(2)}, u32[]{:S(2)}) collective-permute-start(bf16[64,2048]{1,0:T(8,128)(2,1)S(1)} %constant_dynamic-slice_fusion.3), channel_id=1, source_target_pairs={{0,1},{1,0},{2,3},{3,2},{4,5},{5,4},{6,7},{7,6},{8,9},{9,8},{10,11... | collective-permute-start | bytes 786440 | tf_op jit(solution)/shard_map/ppermute | solution.py:31
  154.8 5.0 copy-start.28
  155.0 30.7 %all-to-all-start.1 = ((bf16[8,64,2048]{2,1,0:T(8,128)(2,1)}), bf16[8,64,2048]{2,1,0:T(8,128)(2,1)}, u32[]{:S(2)}, u32[]{:S(2)}) async-start(bf16[8,64,2048]{2,1,0:T(8,128)(2,1)} %broadcast_in_dim.32), calls=%async_computation.1 | async-start | bytes 4194304 | tf_op jit(solution)/shard_map/all_to_all | solution.py:59
  185.7 7.5 %copy-start.21 = (bf16[8,64,2048]{2,1,0:T(8,128)(2,1)S(1)}, bf16[8,64,2048]{2,1,0:T(8,128)(2,1)}, u32[]{:S(2)}) copy-start(bf16[8,64,2048]{2,1,0:T(8,128)(2,1)} %copy-done.20) | copy-start | bytes 6291460
  185.7 80.1 %all-to-all-start.2 = ((bf16[16,128,960]{1,2,0:T(8,128)(2,1)}), bf16[16,128,960]{1,2,0:T(8,128)(2,1)}, u32[]{:S(2)}, u32[]{:S(2)}) async-start(bf16[16,128,960]{1,2,0:T(8,128)(2,1)} %pad_maximum_fusion.2), calls=%async_computation.2 | async-start | bytes 7864320 | tf_op jit(solution)/shard_map/all_to_all | solution.py:415
  192.6 75.8 %collective-permute-start.2 = (bf16[8,64,2048]{2,1,0:T(8,128)(2,1)}, bf16[8,64,2048]{2,1,0:T(8,128)(2,1)}, u32[]{:S(2)}, u32[]{:S(2)}) collective-permute-start(bf16[8,64,2048]{2,1,0:T(8,128)(2,1)} %all-to-all-done.1), channel_id=1, source_target_pairs={{0,2},{2,0},{4,6},{6,4},{8,10},{10,8},{12,14},{14,12},{16,18},{18,... | collective-permute-start | bytes 6291464 | tf_op jit(solution)/shard_map/ppermute | solution.py:27
  193.2 81.8 %collective-permute-start.5 = (bf16[8,64,2048]{2,1,0:T(8,128)(2,1)S(1)}, bf16[8,64,2048]{2,1,0:T(8,128)(2,1)}, u32[]{:S(2)}, u32[]{:S(2)}) collective-permute-start(bf16[8,64,2048]{2,1,0:T(8,128)(2,1)S(1)} %copy-done.21), channel_id=1, source_target_pairs={{0,2},{2,0},{4,6},{6,4},{8,10},{10,8},{12,14},{14,12},{16,18},{18,... | collective-permute-start | bytes 6291464 | tf_op jit(solution)/shard_map/ppermute | solution.py:27
  268.4 11.3 %copy-start.10 = (bf16[2048,960]{0,1:T(8,128)(2,1)}, bf16[2048,960]{0,1:T(8,128)(2,1)S(1)}, u32[]{:S(2)}) copy-start(bf16[2048,960]{0,1:T(8,128)(2,1)S(1)} %copy_bitcast_fusion) | copy-start | bytes 11796484
  279.7 22.6 %copy-start.43 = (bf16[1024,320]{0,1:T(8,128)(2,1)}, bf16[1024,320]{0,1:T(8,128)(2,1)S(1)}, u32[]{:S(2)}) copy-start(bf16[1024,320]{0,1:T(8,128)(2,1)S(1)} %get-tuple-element.115) | copy-start | bytes 1966084
  279.7 3.4 copy-start.26
  282.3 19.9 %collective-permute-start.3 = (bf16[512,2048]{1,0:T(8,128)(2,1)}, bf16[512,2048]{1,0:T(8,128)(2,1)S(1)}, u32[]{:S(2)}, u32[]{:S(2)}) collective-permute-start(bf16[512,2048]{1,0:T(8,128)(2,1)} %convolution_convert_fusion.1), channel_id=1, source_target_pairs={{0,2},{2,0},{4,6},{6,4},{8,10},{10,8},{12,14},{14,12},{16,18},{18,... | collective-permute-start | bytes 6291464 | tf_op jit(solution)/shard_map/ppermute | solution.py:27
  284.3 49.9 %all-to-all-start.10 = ((bf16[8,128,640]{2,1,0:T(8,128)(2,1)}), bf16[8,128,640]{2,1,0:T(8,128)(2,1)}, u32[]{:S(2)}, u32[]{:S(2)}) async-start(bf16[8,128,640]{2,1,0:T(8,128)(2,1)} %broadcast_in_dim.36), calls=%async_computation.10 | async-start | bytes 2621440 | tf_op jit(solution)/shard_map/all_to_all | solution.py:53
  334.2 5.6 copy-start.44
  334.2 31.1 %all-to-all-start.3 = ((bf16[8,64,2048]{2,1,0:T(8,128)(2,1)}), bf16[8,64,2048]{2,1,0:T(8,128)(2,1)S(1)}, u32[]{:S(2)}, u32[]{:S(2)}) async-start(bf16[8,64,2048]{2,1,0:T(8,128)(2,1)} %bitcast.103), calls=%async_computation.3 | async-start | bytes 4194304 | tf_op jit(solution)/shard_map/all_to_all | solution.py:59
  339.8 8.1 %copy-start.11 = (bf16[2048,960]{0,1:T(8,128)(2,1)S(1)}, bf16[2048,960]{0,1:T(8,128)(2,1)}, u32[]{:S(2)}) copy-start(bf16[2048,960]{0,1:T(8,128)(2,1)} %copy-done.10) | copy-start | bytes 11796484
  339.8 8.1 %copy-start.45 = (bf16[1024,320]{0,1:T(8,128)(2,1)S(1)}, bf16[1024,320]{0,1:T(8,128)(2,1)}, u32[]{:S(2)}) copy-start(bf16[1024,320]{0,1:T(8,128)(2,1)} %get-tuple-element.114) | copy-start | bytes 1966084
  343.6 4.2 collective-permute-start.6
  366.7 30.6 %all-to-all-start.5 = ((bf16[8,64,2048]{2,1,0:T(8,128)(2,1)}), bf16[8,64,2048]{2,1,0:T(8,128)(2,1)}, u32[]{:S(2)}, u32[]{:S(2)}) async-start(bf16[8,64,2048]{2,1,0:T(8,128)(2,1)} %bitcast.102), calls=%async_computation.5 | async-start | bytes 4194304 | tf_op jit(solution)/shard_map/all_to_all | solution.py:59
  397.3 78.2 %all-to-all-start.11 = ((bf16[16,128,960]{1,2,0:T(8,128)(2,1)}), bf16[16,128,960]{1,2,0:T(8,128)(2,1)}, u32[]{:S(2)}, u32[]{:S(2)}) async-start(bf16[16,128,960]{1,2,0:T(8,128)(2,1)} %pad_maximum_fusion.3), calls=%async_computation.11 | async-start | bytes 7864320 | tf_op jit(solution)/shard_map/all_to_all | solution.py:480
  405.1 12.0 %copy-start.13 = (bf16[640,2048]{1,0:T(8,128)(2,1)S(1)}, bf16[640,2048]{1,0:T(8,128)(2,1)}, u32[]{:S(2)}) copy-start(bf16[640,2048]{1,0:T(8,128)(2,1)} %all-gather.5.cloned.1.call-done) | copy-start | bytes 7864324
  406.6 5.0 copy-start.23
  406.6 9.4 %collective-permute-start.7 = (bf16[64,2048]{1,0:T(8,128)(2,1)S(1)}, bf16[64,2048]{1,0:T(8,128)(2,1)}, u32[]{:S(2)}, u32[]{:S(2)}) collective-permute-start(bf16[64,2048]{1,0:T(8,128)(2,1)S(1)} %get-tuple-element.120), channel_id=1, source_target_pairs={{0,1},{1,0},{2,3},{3,2},{4,5},{5,4},{6,7},{7,6},{8,9},{9,8},{10,11... | collective-permute-start | bytes 786440 | tf_op jit(solution)/shard_map/ppermute | solution.py:31
  417.1 77.1 %copy-start.14 = (bf16[64,2048]{1,0:T(8,128)(2,1)}, bf16[64,2048]{1,0:T(8,128)(2,1)S(1)}, u32[]{:S(2)}) copy-start(bf16[64,2048]{1,0:T(8,128)(2,1)S(1)} %get-tuple-element.118) | copy-start | bytes 786436
  424.1 2.5 collective-permute-start.8
  426.5 67.6 %copy-start.17 = (bf16[64,2048]{1,0:T(8,128)(2,1)S(1)}, bf16[64,2048]{1,0:T(8,128)(2,1)}, u32[]{:S(2)}) copy-start(bf16[64,2048]{1,0:T(8,128)(2,1)} %copy-done.16) | copy-start | bytes 786436
  475.4 39.1 %all-to-all-start.6 = ((bf16[8,128,384]{2,1,0:T(8,128)(2,1)}), bf16[8,128,384]{2,1,0:T(8,128)(2,1)S(1)}, u32[]{:S(2)}, u32[]{:S(2)}) async-start(bf16[8,128,384]{2,1,0:T(8,128)(2,1)} %add_convert_fusion.2), calls=%async_computation.6 | async-start | bytes 1572864 | tf_op jit(solution)/shard_map/all_to_all | solution.py:53
  494.3 24.2 %copy-start.22 = (bf16[64,2048]{1,0:T(8,128)(2,1)S(1)}, bf16[64,2048]{1,0:T(8,128)(2,1)}, u32[]{:S(2)}) copy-start(bf16[64,2048]{1,0:T(8,128)(2,1)} %get-tuple-element.121) | copy-start | bytes 786436
  494.3 28.7 %copy-start.42 = (f32[1,128]{1,0:T(1,128)S(1)}, f32[1,128]{1,0:T(1,128)}, u32[]{:S(2)}) copy-start(f32[1,128]{1,0:T(1,128)} %get-tuple-element.32) | copy-start | bytes 1540
  514.5 14.5 %copy-start.12 = (bf16[8,128,384]{2,1,0:T(8,128)(2,1)}, bf16[8,128,384]{2,1,0:T(8,128)(2,1)S(1)}, u32[]{:S(2)}) copy-start(bf16[8,128,384]{2,1,0:T(8,128)(2,1)S(1)} %all-to-all-done.6.parts_ref) | copy-start | bytes 2359300
  514.5 29.0 %all-to-all-start.7 = ((bf16[16,128,256]{2,1,0:T(8,128)(2,1)}), bf16[16,128,256]{2,1,0:T(8,128)(2,1)S(1)}, u32[]{:S(2)}, u32[]{:S(2)}) async-start(bf16[16,128,256]{2,1,0:T(8,128)(2,1)} %maximum_bitcast_fusion.1), calls=%async_computation.7 | async-start | bytes 2097152 | tf_op jit(solution)/shard_map/all_to_all | solution.py:506
  518.6 9.6 %collective-permute-start.4 = (bf16[64,2048]{1,0:T(8,128)(2,1)S(1)}, bf16[64,2048]{1,0:T(8,128)(2,1)S(1)}, u32[]{:S(2)}, u32[]{:S(2)}) collective-permute-start(bf16[64,2048]{1,0:T(8,128)(2,1)S(1)} %copy-done.22), channel_id=1, source_target_pairs={{0,1},{1,0},{2,3},{3,2},{4,5},{5,4},{6,7},{7,6},{8,9},{9,8},{10,11... | collective-permute-start | bytes 786440 | tf_op jit(solution)/shard_map/ppermute | solution.py:31
  522.8 50.6 %collective-permute-start.13 = (bf16[8,128,640]{2,1,0:T(8,128)(2,1)}, bf16[8,128,640]{2,1,0:T(8,128)(2,1)}, u32[]{:S(2)}, u32[]{:S(2)}) collective-permute-start(bf16[8,128,640]{2,1,0:T(8,128)(2,1)} %all-to-all-done.10), channel_id=1, source_target_pairs={{0,2},{2,0},{4,6},{6,4},{8,10},{10,8},{12,14},{14,12},{16,18},{18,... | collective-permute-start | bytes 3932168 | tf_op jit(solution)/shard_map/ppermute | solution.py:27
  543.6 10.5 %copy-start.8 = (bf16[16,128,256]{2,1,0:T(8,128)(2,1)}, bf16[16,128,256]{2,1,0:T(8,128)(2,1)S(1)}, u32[]{:S(2)}) copy-start(bf16[16,128,256]{2,1,0:T(8,128)(2,1)S(1)} %all-to-all-done.7) | copy-start | bytes 3145732
  543.6 12.9 %all-to-all-start.12 = ((f32[16,1,8]{2,1,0:T(1,128)}), f32[16,1,8]{2,1,0:T(1,128)S(1)}, u32[]{:S(2)}, u32[]{:S(2)}) async-start(f32[16,1,8]{2,1,0:T(1,128)} %bitcast.36), calls=%async_computation.12 | async-start | bytes 16384 | tf_op jit(solution)/shard_map/all_to_all | solution.py:557
  557.8 37.7 %all-to-all-start.8 = ((bf16[8,128,640]{2,1,0:T(8,128)(2,1)}), bf16[8,128,640]{2,1,0:T(8,128)(2,1)}, u32[]{:S(2)}, u32[]{:S(2)}) async-start(bf16[8,128,640]{2,1,0:T(8,128)(2,1)} %broadcast_in_dim.34), calls=%async_computation.8 | async-start | bytes 2621440 | tf_op jit(solution)/shard_map/all_to_all | solution.py:53
  568.2 3.0 copy-start.9
  571.3 4.0 copy-start.1
  571.3 4.0 copy-start.33
  576.9 26.5 %collective-permute-start.9 = (bf16[128,2048]{1,0:T(8,128)(2,1)S(1)}, bf16[128,2048]{1,0:T(8,128)(2,1)}, u32[]{:S(2)}, u32[]{:S(2)}) collective-permute-start(bf16[128,2048]{1,0:T(8,128)(2,1)S(1)} %convolution_convert_fusion.3), channel_id=1, source_target_pairs={{0,1},{1,0},{2,3},{3,2},{4,5},{5,4},{6,7},{7,6},{8,9},{9,8},{10,11... | collective-permute-start | bytes 1572872 | tf_op jit(solution)/shard_map/ppermute | solution.py:31
  578.7 17.7 %copy-start.32 = (f32[640,128]{1,0:T(8,128)}, f32[640,128]{1,0:T(8,128)S(1)}, u32[]{:S(2)}) copy-start(f32[640,128]{1,0:T(8,128)S(1)} %slice_dynamic-update-slice_fusion) | copy-start | bytes 983044
  596.4 24.0 %all-to-all-start.9 = ((bf16[8,128,384]{2,1,0:T(8,128)(2,1)}), bf16[8,128,384]{2,1,0:T(8,128)(2,1)S(1)}, u32[]{:S(2)}, u32[]{:S(2)}) async-start(bf16[8,128,384]{2,1,0:T(8,128)(2,1)} %broadcast_in_dim.35), calls=%async_computation.9 | async-start | bytes 1572864 | tf_op jit(solution)/shard_map/all_to_all | solution.py:53
  600.8 4.0 copy-start.15
  600.8 4.0 copy-start.18
  600.8 19.9 %collective-permute-start.10 = (bf16[8,128,640]{2,1,0:T(8,128)(2,1)}, bf16[8,128,640]{2,1,0:T(8,128)(2,1)}, u32[]{:S(2)}, u32[]{:S(2)}) collective-permute-start(bf16[8,128,640]{2,1,0:T(8,128)(2,1)} %all-to-all-done.8), channel_id=1, source_target_pairs={{0,2},{2,0},{4,6},{6,4},{8,10},{10,8},{12,14},{14,12},{16,18},{18,... | collective-permute-start | bytes 3932168 | tf_op jit(solution)/shard_map/ppermute | solution.py:27
  620.4 2.3 collective-permute-start.11
  623.2 3.6 collective-permute-start.14
  625.8 4.9 collective-permute-start.12
  (12 other events, 22.0 us)
Sparse Core Ops, SparseCore 0:
  12.9 53.2 all-gather.2
  68.9 55.4 all-gather.4

commit v2 on v1

--- a/solution.py
+++ b/solution.py
@@ -31,47 +31,139 @@
     return lax.ppermute(block, "col", [(0, 1), (1, 0)])
 
 
-def plane_groups(span):
+def shift_far(block, steps, span, wrap):
     rows = lax.axis_size("row")
-    return [
-        [first + 2 * j + core for j in range(span // 2)]
-        for first in range(0, rows, span)
-        for core in range(2)
-    ]
-
-
-def cube_groups():
+    route = []
+    for i in range(rows):
+        first, at = i // span * span, i % span + 4 * steps
+        if wrap or 0 <= at < span:
+            route.append((i, first + at % span))
+    return lax.ppermute(block, "row", route)
+
+
+def swap_near(block):
+    rows = lax.axis_size("row")
+    return lax.ppermute(block, "row", [(i, i ^ 2) for i in range(rows)])
+
+
+def swap_cube(block, number):
     rows, cols = lax.axis_size("row"), lax.axis_size("col")
-    return [
-        [(first + 2 * j + core) * cols + c for j in range(MEMBERS // 2) for c in range(cols)]
-        for first in range(0, rows, MEMBERS)
-        for core in range(2)
-    ]
-
-
-def exchange_plane(blocks, span):
+    route = []
+    for i in range(rows):
+        first, chip, core = i // MEMBERS * MEMBERS, i % MEMBERS // 2, i % 2
+        there = first + 2 * (chip ^ (number // cols)) + core
+        route += [(i * cols + c, there * cols + (c ^ (number % cols))) for c in range(cols)]
+    return lax.ppermute(block, ("row", "col"), route)
+
+
+def gather_earlier(block, span):
+    far = jnp.stack([block] + [shift_far(block, k, span, False) for k in range(1, span // 4)])
+    same = jnp.stack([far, swap_near(far)])
+    return same, swap_core(same)
+
+
+def over_core(same, other):
+    return (same.astype(F32) + swap_core(other.astype(BF16)).astype(F32)).astype(BF16)
+
+
+def over_near(total):
+    count = total.shape[0] // 2
+    return (total[:count].astype(F32) + swap_near(total[count:]).astype(F32)).astype(BF16)
+
+
+def over_far(total, span, wrap, forward):
+    sign = 1 if forward else -1
+    return [total[0]] + [shift_far(total[k], sign * k, span, wrap) for k in range(1, span // 4)]
+
+
+def add_up(parts):
+    return sum(p.astype(F32) for p in parts)
+
+
+def gather_rows(block):
+    rows = lax.axis_size("row")
+    far = jnp.concatenate([block] + [shift_far(block, -k, rows, True) for k in range(1, rows // 4)], axis=0)
+    same = jnp.concatenate([far, swap_near(far)], axis=0)
+    return jnp.concatenate([same, swap_core(same)], axis=0)
+
+
+def distances():
+    rows, row = lax.axis_size("row"), lax.axis_index("row")
+    order = [((row ^ near) + 4 * k) % rows for near in (0, 2, 1, 3) for k in range(rows // 4)]
+    inverse = []
+    for r in range(rows):
+        step = r ^ row
+        place = (step & 1) * 2 + (step >> 1 & 1)
+        inverse.append(place * (rows // 4) + (r // 4 - row // 4) % (rows // 4))
+    return jnp.stack(order), jnp.stack(inverse)
+
+
+def reorder_kernel(order_ref, in_ref, out_ref):
+    for at in range(in_ref.shape[1] // LANES):
+        there = pl.multiple_of(order_ref[at] * LANES, LANES)
+        out_ref[:, at * LANES : (at + 1) * LANES] = in_ref[:, pl.ds(there, LANES)]
+
+
+def reorder_columns(array, order):
+    tok, width = array.shape
+    if width // order.shape[0] != LANES:
+        blocks = array.reshape(tok, order.shape[0], -1)
+        return jnp.take(blocks, order, axis=1).reshape(tok, width)
+    return pl.pallas_call(
+        reorder_kernel,
+        in_specs=[pl.BlockSpec(memory_space=pltpu.SMEM), pl.BlockSpec(memory_space=pltpu.VMEM)],
+        out_specs=pl.BlockSpec(memory_space=pltpu.VMEM),
+        out_shape=jax.ShapeDtypeStruct(array.shape, array.dtype),
+        cost_estimate=pl.CostEstimate(flops=0, bytes_accessed=4 * array.size, transcendentals=0),
+        name="reorder_columns",
+    )(order, array)
+
+
+def after_all(arrays, *others):
+    return lax.optimization_barrier(tuple(arrays) + others)[: len(arrays)]
+
+
+def after(array, *others):
+    return after_all((array,), *others)[0]
+
+
+def cube_numbers():
+    cols = lax.axis_size("col")
+    return [(2 * pair + near) * cols + c for c in range(cols) for near in range(2) for pair in range(2)]
+
+
+def gather_cube(block):
+    same = jnp.concatenate([block] + [swap_cube(block, e) for e in cube_numbers()[1:]], axis=0)
+    return same, swap_core(same)
+
+
+def gather_cube_slowly(block):
+    cols = lax.axis_size("col")
+    block = jnp.concatenate([block, swap_cube(block, 2 * cols)], axis=0)
+    block = jnp.concatenate([block, swap_cube(block, cols)], axis=0)
+    block = jnp.concatenate([block, swap_cube(block, 1)], axis=0)
+    return jnp.concatenate([block, swap_core(block)], axis=0)
+
+
+def halve_cube(total, number):
+    count = total.shape[0] // 2
+    return total[:count].astype(F32) + swap_cube(total[count:].astype(BF16), number).astype(F32)
+
+
+def group_rows():
+    rows = lax.axis_size("row")
+    return [list(range(first, first + MEMBERS)) for first in range(0, rows, MEMBERS)]
+
+
+def across_groups():
+    rows = lax.axis_size("row")
+    return [list(range(member, rows, MEMBERS)) for member in range(MEMBERS)]
+
+
+def exchange_group(blocks):
     return lax.all_to_all(
-        blocks, "row", split_axis=0, concat_axis=0, tiled=True, axis_index_groups=plane_groups(span)
+        blocks, "row", split_axis=0, concat_axis=0, tiled=True, axis_index_groups=group_rows()
     )
-
-
-def exchange_cube(blocks):
-    return lax.all_to_all(
-        blocks, ("row", "col"), split_axis=0, concat_axis=0, tiled=True, axis_index_groups=cube_groups()
-    )
-
-
-def gather_plane(block, span):
-    copies = jnp.broadcast_to(block[None], (span // 2,) + block.shape)
-    same = exchange_plane(copies, span)
-    return same, swap_core(same)
-
-
-def gather_cube(block):
-    count = MEMBERS // 2 * lax.axis_size("col")
-    copies = jnp.broadcast_to(block[None], (count,) + block.shape)
-    same = exchange_cube(copies)
-    return same, swap_core(same)
 
 
 def halves(own, other, col):
@@ -113,7 +205,7 @@
     return jnp.where(on, grad_raw, grad), gain_term
 
 
-def qkv_kernel(act_ref, w_ref, gain_ref, flag_ref, cos_ref, sin_ref, raw_ref, out_ref):
+def heads_kernel(act_ref, w_ref, gain_ref, flag_ref, cos_ref, sin_ref, raw_ref, out_ref):
     raw = dot(act_ref[...], w_ref[...])
     raw_ref[...] = raw
     for part in range(raw.shape[1] // LANES):
@@ -122,21 +214,21 @@
         out_ref[:, at] = done.astype(BF16)
 
 
-def qkv_call(act, w_all, gain, flag, cosine, sine):
+def heads_call(act, w_all, gain, flag, cosine, sine):
     tok, width = act.shape
-    cols = w_all.shape[1]
+    cols = gain.shape[1]
     block = 256
     whole = lambda shape: pl.BlockSpec(shape, lambda i: (0, 0))
     chunk = lambda rows: pl.BlockSpec((rows, block), lambda i: (0, i))
     return pl.pallas_call(
-        qkv_kernel,
+        heads_kernel,
         grid=(cols // block,),
         in_specs=[whole((tok, width)), chunk(width), chunk(1), chunk(1), whole((tok, LANES)), whole((tok, LANES))],
         out_specs=[chunk(tok), chunk(tok)],
         out_shape=[jax.ShapeDtypeStruct((tok, cols), F32), jax.ShapeDtypeStruct((tok, cols), BF16)],
         compiler_params=pltpu.CompilerParams(vmem_limit_bytes=VMEM_LIMIT),
         cost_estimate=pl.CostEstimate(flops=2 * tok * width * cols, bytes_accessed=2 * width * cols, transcendentals=0),
-        name="qkv_heads",
+        name="project_heads",
     )(act, w_all, gain, flag, cosine, sine)
 
 
@@ -155,10 +247,14 @@
     return jnp.concatenate(turned, axis=1), jnp.concatenate(tall, axis=0)
 
 
-def key_mask(base_same, base_other, limits_ref, tok):
+def key_block(i, bounds_ref, limits_ref, same_ref, other_ref):
+    tok = same_ref.shape[2]
+    pair, near = i // 2, i % 2
+    row = (bounds_ref[1] ^ (2 * near)) - 4 * pair
+    kv = jnp.concatenate([same_ref[near, pair], other_ref[near, pair]], axis=0)
     key = lax.broadcasted_iota(jnp.int32, (2 * tok, tok), 0)
-    key = key + jnp.where(key < tok, base_same, base_other - tok)
-    return (key >= limits_ref[0:1, :]) & (key <= limits_ref[1:2, :])
+    key = key + jnp.where(key < tok, row * tok, (row ^ 1) * tok - tok)
+    return near, pair, kv, (key >= limits_ref[0:1, :]) & (key <= limits_ref[1:2, :])
 
 
 def forward_kernel(bounds_ref, limits_ref, q_ref, same_ref, other_ref, att_ref, turned_ref, inv_ref, q_turned):
@@ -167,12 +263,10 @@
     q_turned[...] = turned
     turned_ref[...] = jnp.zeros_like(turned_ref)
     inv_ref[...] = jnp.zeros_like(inv_ref)
-    core = bounds_ref[2]
-
-    @pl.loop(bounds_ref[0], bounds_ref[1])
-    def step(j):
-        kv = jnp.concatenate([same_ref[j], other_ref[j]], axis=0)
-        ok = key_mask((2 * j + core) * tok, (2 * j + 1 - core) * tok, limits_ref, tok)
+
+    @pl.loop(0, bounds_ref[0])
+    def step(i):
+        near, pair, kv, ok = key_block(i, bounds_ref, limits_ref, same_ref, other_ref)
         for g, (first, count) in enumerate(GROUPS):
             at = slice(first * tok, (first + count) * tok)
             keys = kv[:, K_AT[g] : K_AT[g] + HALF]
@@ -202,7 +296,7 @@
 def forward_call(bounds, limits, q, same, other):
     tok, width = q.shape
     wide = width // HALF * tok
-    work = same.shape[0] * 2 * tok * wide
+    work = same.size // same.shape[3] * 2 * wide
     return pl.pallas_call(
         forward_kernel,
         in_specs=[SMEM] + vmem(4),
@@ -248,13 +342,11 @@
     dq_acc[...] = jnp.zeros_like(dq_acc)
     same_out[...] = jnp.zeros_like(same_out)
     other_out[...] = jnp.zeros_like(other_out)
-    core = bounds_ref[2]
     delta = jnp.sum(g_turned[...].astype(F32) * turned_ref[...], axis=0, keepdims=True)
 
-    @pl.loop(bounds_ref[0], bounds_ref[1])
-    def step(j):
-        kv = jnp.concatenate([same_ref[j], other_ref[j]], axis=0)
-        ok = key_mask((2 * j + core) * tok, (2 * j + 1 - core) * tok, limits_ref, tok)
+    @pl.loop(0, bounds_ref[0])
+    def step(i):
+        near, pair, kv, ok = key_block(i, bounds_ref, limits_ref, same_ref, other_ref)
         for g, (first, count) in enumerate(GROUPS):
             at = slice(first * tok, (first + count) * tok)
             keys = kv[:, K_AT[g] : K_AT[g] + HALF]
@@ -265,10 +357,10 @@
             d_keys = dot(d_score, q_tall[at, :]).astype(BF16)
             d_vals = dot(prob.astype(BF16), g_tall[at, :]).astype(BF16)
             dq_acc[:, at] += dot(keys, d_score, ((0,), (0,)))
-            same_out[j, :, K_AT[g] : K_AT[g] + HALF] = d_keys[:tok]
-            other_out[j, :, K_AT[g] : K_AT[g] + HALF] = d_keys[tok:]
-            same_out[j, :, V_AT[g] : V_AT[g] + HALF] = d_vals[:tok]
-            other_out[j, :, V_AT[g] : V_AT[g] + HALF] = d_vals[tok:]
+            same_out[near, pair, :, K_AT[g] : K_AT[g] + HALF] = d_keys[:tok]
+            other_out[near, pair, :, K_AT[g] : K_AT[g] + HALF] = d_keys[tok:]
+            same_out[near, pair, :, V_AT[g] : V_AT[g] + HALF] = d_vals[:tok]
+            other_out[near, pair, :, V_AT[g] : V_AT[g] + HALF] = d_vals[tok:]
 
     total = jnp.zeros((1, LANES), F32)
     for pair in range(dq_ref.shape[1] // LANES):
@@ -286,7 +378,7 @@
 def backward_call(bounds, limits, q, grad, turned, inv, same, other, raw, gain, cosine, sine):
     tok, width = q.shape
     wide = width // HALF * tok
-    work = same.shape[0] * 2 * tok * wide
+    work = same.size // same.shape[3] * 2 * wide
     return pl.pallas_call(
         backward_kernel,
         in_specs=[SMEM] + vmem(11),
@@ -310,11 +402,12 @@
     )(bounds, limits, q, grad, turned, inv, same, other, raw, gain, cosine, sine)
 
 
-def kv_back_kernel(parts_ref, raw_ref, gain_ref, flag_ref, cos_ref, sin_ref, out_ref, gain_grad_ref):
+def kv_back_kernel(raw_ref, gain_ref, flag_ref, cos_ref, sin_ref, *refs):
+    *part_refs, out_ref, gain_grad_ref = refs
     total = jnp.zeros((1, LANES), F32)
     for part in range(out_ref.shape[1] // LANES):
         at = slice(part * LANES, (part + 1) * LANES)
-        grad = jnp.sum(parts_ref[:, :, at].astype(F32), axis=0)
+        grad = sum(ref[:, at].astype(F32) for ref in part_refs)
         done, term = head_backward(
             grad, raw_ref[:, at], gain_ref[:, at], flag_ref[:, at], cos_ref[...], sin_ref[...]
         )
@@ -327,13 +420,13 @@
     tok, width = raw.shape
     return pl.pallas_call(
         kv_back_kernel,
-        in_specs=vmem(6),
+        in_specs=vmem(5 + len(parts)),
         out_specs=vmem(2),
         out_shape=[jax.ShapeDtypeStruct((tok, width), BF16), jax.ShapeDtypeStruct((1, LANES), F32)],
         compiler_params=pltpu.CompilerParams(vmem_limit_bytes=VMEM_LIMIT),
-        cost_estimate=pl.CostEstimate(flops=30 * tok * width, bytes_accessed=2 * parts.size, transcendentals=0),
+        cost_estimate=pl.CostEstimate(flops=30 * tok * width, bytes_accessed=2 * tok * width * len(parts), transcendentals=0),
         name="key_value_heads_back",
-    )(parts, raw, gain, flag, cosine, sine)
+    )(raw, gain, flag, cosine, sine, *parts)
 
 
 def rope_tables(positions, head_dim):
@@ -380,7 +473,7 @@
     rows = lax.axis_size("row")
     row = lax.axis_index("row")
     col = lax.axis_index("col")
-    core = row % 2
+    cols = lax.axis_size("col")
     w_rows = w_query.shape[0]
     q_width = w_query.shape[1]
     kv_half = key_value_weight.shape[1] // 2
@@ -395,14 +488,17 @@
         v = [key_value_weight[:, kv_half + h * HALF : kv_half + (h + 1) * HALF] for h in order]
         return jnp.concatenate([k[0], k[1], k[2], v[2], v[0], v[1]], axis=1)
 
-    w_one = jnp.where(
-        col == 0,
-        jnp.concatenate([w_query, kv_pick((0, 1, 2))], axis=1),
-        jnp.concatenate([backwards(w_query, 1, LANES), kv_pick((4, 3, 2))], axis=1),
-    )
-    w_one_all = lax.all_gather(w_one, "row", axis=0, tiled=True)
+    w_kv = jnp.where(col == 0, kv_pick((0, 1, 2)), kv_pick((4, 3, 2)))
+    w_q = jnp.where(col == 0, w_query, backwards(w_query, 1, LANES))
     w_o = jnp.where(col == 0, w_out, backwards(w_out, 0, LANES))
-    w_o_all = lax.all_gather(w_o, "row", axis=1, tiled=True)
+    w_all = lax.all_gather(jnp.concatenate([w_q, w_kv, w_o.T], axis=1), "row", axis=0, tiled=True)
+    kv_width = w_kv.shape[1]
+    head_cols = q_width + kv_width
+    w_o_all = w_all[:, head_cols:]
+    og_low = lax.dynamic_slice_in_dim(out_grad, col * half, half, 0)
+    og_all = gather_cube_slowly(og_low)
+    order, inverse_order = distances()
+    group = og_all.shape[0]
 
     w_ff = jnp.concatenate(
         [
@@ -412,9 +508,8 @@
         ],
         axis=2,
     ).transpose(1, 0, 2)
-    w_ff_all = lax.all_to_all(
-        jnp.concatenate([w_ff] * (rows // MEMBERS), axis=0), "row", split_axis=0, concat_axis=0, tiled=True
-    ).reshape(width, 3 * ff)
+    w_ff = jnp.concatenate([after(w_ff, w_all)] * (rows // MEMBERS), axis=0)
+    w_ff_all = lax.all_to_all(w_ff, "row", split_axis=0, concat_axis=0, tiled=True).reshape(width, 3 * ff)
 
     input_f = tokens.astype(F32)
     act_scale = norm_scale(input_f)
@@ -424,11 +519,16 @@
     k_lanes = jnp.tile(key_gain, 2)[None, :]
     kv_flag = jnp.concatenate([jnp.ones((1, 3 * HALF), F32), jnp.zeros((1, 3 * HALF), F32)], axis=1)
     kv_gain = jnp.where(kv_flag > 0, jnp.tile(k_lanes, (1, 3)), 1.0)
-    flag = jnp.concatenate([jnp.ones((1, q_width), F32), kv_flag], axis=1)
-    gain = jnp.concatenate([jnp.tile(q_lanes * SCALE, (1, q_width // LANES)), kv_gain], axis=1)
-    raw, heads = qkv_call(act_low, w_one_all, gain, flag, cosine, sine)
+    q_flag = jnp.ones((1, q_width), F32)
+    q_gain = jnp.tile(q_lanes * SCALE, (1, q_width // LANES))
+    act_blocks = reorder_columns(act_low, order)
+    gain = jnp.concatenate([q_gain, kv_gain], axis=1)
+    flag = jnp.concatenate([q_flag, kv_flag], axis=1)
+    act_low, og_all = lax.optimization_barrier((act_low, og_all))
+    raw, heads = heads_call(act_low, w_all, gain, flag, cosine, sine)
     query, kv_low = heads[:, :q_width], heads[:, q_width:]
-    same_kv, other_kv = gather_plane(kv_low, span)
+    q_raw, kv_raw = raw[:, :q_width], raw[:, q_width:]
+    same_kv, other_kv = gather_earlier(kv_low, span)
 
     in_span = row % span
     seq_segments = lax.dynamic_slice_in_dim(segments, (row - in_span) * tok, seq_len, 0)
@@ -438,10 +538,9 @@
     start = jnp.min(jnp.where(seq_segments[None, :] == own_segments[:, None], index[None, :], seq_len), axis=1)
     start = jnp.where(own_segments < 0, own_index, start)
     limits = jnp.stack([start, own_index])
-    bounds = jnp.stack([jnp.min(start) // (2 * tok), in_span // 2 + 1, core])
+    bounds = jnp.stack([2 * (in_span // 4 + 1 - jnp.min(start) // (4 * tok)), in_span])
     attn_low, turned, inv = forward_call(bounds, limits, query, same_kv, other_kv)
-    same_att, other_att = gather_plane(attn_low, rows)
-    attn_part = dot(attn_low, w_o_all).astype(BF16)
+    attn_part = dot(attn_low, w_o_all, ((1,), (1,))).astype(BF16)
 
     def mine(array, which):
         return lax.dynamic_slice_in_dim(array, which * half, half, 0)
@@ -451,10 +550,7 @@
 
     ffn_scale = norm_scale(hidden)
     ffn_low = (hidden * ffn_scale * ffn_gain).astype(BF16)
-    og_low = mine(out_grad, col)
-    og_all = jnp.concatenate([a.reshape(-1, width) for a in gather_cube(og_low)], axis=0)
-    ffn_all = jnp.concatenate([a.reshape(-1, width) for a in gather_cube(ffn_low)], axis=0)
-    group = ffn_all.shape[0]
+    ffn_all = jnp.concatenate(gather_cube(ffn_low), axis=0)
     gate_up = dot(ffn_all, w_ff_all[:, : 2 * ff])
     gate_pre, up_pre = gate_up[:, :ff], gate_up[:, ff:]
     d_inner = dot(og_all, w_ff_all[:, 2 * ff :])
@@ -465,61 +561,69 @@
     d_up = d_inner * silu_gate
     d_gate_up = jnp.concatenate([d_gate, d_up], axis=1).astype(BF16)
 
-    def reduce_cube(left, right):
-        count = group // 2 // half
-        away = dot(left[group // 2 :], right, ((1,), (1,))).astype(BF16)
-        here = dot(left[: group // 2], right, ((1,), (1,)))
-        total = (here + swap_core(away).astype(F32)).astype(BF16)
-        parts = exchange_cube(total.reshape(count, half, width))
-        return jnp.sum(parts.astype(F32), axis=0)
-
-    ffn_back = reduce_cube(d_gate_up, w_ff_all[:, : 2 * ff])
+    w_gate_up = w_ff_all[:, : 2 * ff]
+    away = dot(d_gate_up[group // 2 :], w_gate_up, ((1,), (1,))).astype(BF16)
+    here = dot(d_gate_up[: group // 2], w_gate_up, ((1,), (1,)))
     grads_ff = jnp.concatenate(
         [dot(ffn_all, d_gate_up, ((0,), (0,))), dot(og_all, inner_low, ((0,), (0,)))], axis=1
     ).astype(BF16)
-    grads_ff = lax.all_to_all(
-        grads_ff.reshape(rows, w_rows, 3 * ff), "row", split_axis=0, concat_axis=0, tiled=True
+    total = (here + swap_core(away).astype(F32)).astype(BF16).reshape(-1, half, width)
+    total, grads_ff = lax.optimization_barrier((total, grads_ff))
+    grads_ff = lax.psum_scatter(
+        grads_ff, "row", scatter_dimension=0, tiled=True, axis_index_groups=across_groups()
     )
-    ffn_out = reduce_cube(inner_low, w_ff_all[:, 2 * ff :])
-    out_half = (hidden + ffn_out).astype(BF16)
-    output = halves(out_half, swap_col(out_half), col)
-
+    for number in (1, cols, 2 * cols):
+        total = halve_cube(total, number)
+    ffn_back = total[0]
     d_hidden = og_low.astype(F32) + norm_back(hidden, ffn_scale, ffn_gain, ffn_back)
     d_hidden_half = d_hidden.astype(BF16)
     d_hidden_low = halves(d_hidden_half, swap_col(d_hidden_half), col)
 
-    d_attn = dot(d_hidden_low, w_o_all, ((1,), (1,))).astype(BF16)
+    d_attn = dot(d_hidden_low, w_o_all).astype(BF16)
     d_q, q_gain_part, same_d, other_d = backward_call(
-        bounds, limits, query, d_attn, turned, inv, same_kv, other_kv, raw[:, :q_width], q_lanes, cosine, sine
+        bounds, limits, query, d_attn, turned, inv, same_kv, other_kv, q_raw, q_lanes, cosine, sine
     )
-    same_dq, other_dq = gather_plane(d_q, rows)
-    kv_parts = exchange_plane((same_d.astype(F32) + swap_core(other_d).astype(F32)).astype(BF16), span)
-    d_kv, k_gain_part = kv_back_call(kv_parts, raw[:, q_width:], kv_gain, kv_flag, cosine, sine)
-    same_dkv, other_dkv = gather_plane(d_kv, rows)
+    d_kv_total = over_core(same_d, other_d).reshape(-1, tok, same_d.shape[3])
+
+    inner_low = after(inner_low, d_hidden_low)
+    w_down_all = w_ff_all[:, 2 * ff :]
+    away = dot(inner_low[group // 2 :], w_down_all, ((1,), (1,))).astype(BF16)
+    here = dot(inner_low[: group // 2], w_down_all, ((1,), (1,)))
+    ffn_out = over_core(here, away).reshape(-1, half, width)
+    ffn_out = halve_cube(ffn_out, 1)
+
+    grad_oq = jnp.concatenate(
+        [dot(d_hidden_low, attn_low, ((0,), (0,))), dot(act_low, d_q, ((0,), (0,)))], axis=1
+    ).astype(BF16)
+    grad_oq = lax.psum_scatter(grad_oq, "row", scatter_dimension=0, tiled=True).astype(F32)
+
+    def partial_grad(left, right):
+        return dot(left, right, ((0,), (0,))).reshape(rows, w_rows, -1)
+
+    d_kv_total = over_near(d_kv_total)
+    kv_parts = over_far(d_kv_total, span, False, False)
+    d_kv, k_gain_part = kv_back_call(kv_parts, kv_raw, kv_gain, kv_flag, cosine, sine)
+    ffn_out = after(ffn_out, d_kv)
+    for number in (cols, 2 * cols):
+        ffn_out = halve_cube(ffn_out, number)
+    out_half = (hidden + ffn_out[0]).astype(BF16)
+    output = halves(out_half, swap_col(out_half), col)
 
     d_one = jnp.concatenate([d_q, d_kv], axis=1)
-    act_back = dot(d_one, w_one_all, ((1,), (1,))).astype(BF16)
+    act_back = dot(d_one, w_all[:, :head_cols], ((1,), (1,))).astype(BF16)
     act_back = act_back.astype(F32) + swap_col(act_back).astype(F32)
     input_grad = d_hidden_low.astype(F32) + norm_back(input_f, act_scale, attn_gain, act_back)
 
-    columns = jnp.concatenate([act_low.reshape(tok, rows, w_rows), d_hidden_low.reshape(tok, rows, w_rows)], axis=2)
-    columns = lax.all_to_all(columns.transpose(1, 0, 2), "row", split_axis=0, concat_axis=0, tiled=True)
-    columns = columns.reshape(rows // 2, 2, tok, 2 * w_rows)
-    same_cols = lax.dynamic_index_in_dim(columns, core, 1, keepdims=False).reshape(-1, 2 * w_rows)
-    other_cols = lax.dynamic_index_in_dim(columns, 1 - core, 1, keepdims=False).reshape(-1, 2 * w_rows)
-
-    def over_tokens(left, right):
-        return dot(left[0], right[0].reshape(left[0].shape[0], -1), ((0,), (0,))) + dot(
-            left[1], right[1].reshape(left[1].shape[0], -1), ((0,), (0,))
-        )
-
-    act_cols = (same_cols[:, :w_rows], other_cols[:, :w_rows])
-    hid_cols = (same_cols[:, w_rows:], other_cols[:, w_rows:])
-    grad_q = over_tokens(act_cols, (same_dq, other_dq))
-    grad_kv = over_tokens(act_cols, (same_dkv, other_dkv))
-    grad_o = over_tokens(
-        (same_att.reshape(-1, q_width), other_att.reshape(-1, q_width)), hid_cols
-    )
+    grad_o, grad_q = grad_oq[:, :q_width].T, grad_oq[:, q_width:]
+    per_row = HALF // rows
+    fold = lambda part: (part[0, :HALF] + part[0, HALF:]).reshape(rows, 1, per_row)
+    small = jnp.concatenate([fold(q_gain_part), fold(k_gain_part)], axis=2)
+    small = jnp.take(small, order, axis=0)
+    small = jnp.pad(small, ((0, 0), (0, 15), (0, d_kv.shape[1] - 2 * per_row)))
+    kv_partial = jnp.concatenate([partial_grad(act_blocks, d_kv), small], axis=1)
+    kv_partial = over_near(over_core(kv_partial[: rows // 2], kv_partial[rows // 2 :]))
+    grad_kv = add_up(over_far(kv_partial, rows, True, True))
+    grad_kv, small = grad_kv[:w_rows], grad_kv[w_rows, : 2 * per_row]
     grad_query = jnp.where(col == 0, grad_q, backwards(grad_q, 1, LANES))
     grad_out = jnp.where(col == 0, grad_o, backwards(grad_o, 0, LANES))
 
@@ -528,33 +632,24 @@
     kv_first = jnp.where(col == 0, kv_own, kv_away).astype(F32)
     kv_last = jnp.where(col == 0, kv_away, kv_own).astype(F32)
 
-    def head_cols(array, at):
+    def one_head(array, at):
         return array[:, at : at + HALF]
 
     pieces = []
     for at in (K_AT, V_AT):
-        pieces += [head_cols(kv_first, at[0]), head_cols(kv_first, at[1])]
-        pieces += [head_cols(kv_first, at[2]) + head_cols(kv_last, at[2])]
-        pieces += [head_cols(kv_last, at[1]), head_cols(kv_last, at[0])]
+        pieces += [one_head(kv_first, at[0]), one_head(kv_first, at[1])]
+        pieces += [one_head(kv_first, at[2]) + one_head(kv_last, at[2])]
+        pieces += [one_head(kv_last, at[1]), one_head(kv_last, at[0])]
     grad_keyval = jnp.concatenate(pieces, axis=1)
 
-    grads_ff = jnp.sum(grads_ff.reshape(rows // MEMBERS, MEMBERS, w_rows, 3 * ff).astype(F32), axis=0)
-    grads_ff = grads_ff.transpose(1, 0, 2)
+    grads_ff = exchange_group(grads_ff.reshape(MEMBERS, w_rows, 3 * ff))
+    grads_ff = grads_ff.astype(F32).transpose(1, 0, 2)
     grad_gate = grads_ff[:, :, :ff].reshape(w_rows, ff_cols)
     grad_up = grads_ff[:, :, ff : 2 * ff].reshape(w_rows, ff_cols)
     grad_down = grads_ff[:, :, 2 * ff :].reshape(w_rows, ff_cols).T
 
-    attn_part_gain = jnp.sum(jnp.concatenate([grad_q, grad_kv], axis=1) * w_one.astype(F32), axis=1)
+    attn_part_gain = jnp.sum(jnp.concatenate([grad_q * w_q.astype(F32), grad_kv * w_kv.astype(F32)], axis=1), axis=1)
     ffn_part_gain = jnp.sum(grad_gate * w_gate.astype(F32) + grad_up * w_up.astype(F32), axis=1)
-    per_row = HALF // rows
-    small = jnp.concatenate(
-        [
-            (q_gain_part[0, :HALF] + q_gain_part[0, HALF:]).reshape(rows, per_row),
-            (k_gain_part[0, :HALF] + k_gain_part[0, HALF:]).reshape(rows, per_row),
-        ],
-        axis=1,
-    )
-    small = jnp.sum(lax.all_to_all(small, "row", split_axis=0, concat_axis=0, tiled=True), axis=0)
     gains = jnp.concatenate([attn_part_gain, ffn_part_gain, small])
     gains = gains + swap_col(gains)
     own_gains = lambda whole: lax.dynamic_slice_in_dim(whole, row * w_rows, w_rows, 0)

time: 646 us -> 490 us (0.76)
  waiting for transfers between devices: 348 us -> 233 us
  starting transfers between devices: 119 us -> 78.2 us
    all_to_all x13 -> x2, waiting for transfers between devices: 265 us -> 15.9 us  [the longest x1 15.9 us: exchange_group(): lax.all_to_all(blocks, 'row', split_axis=0, concat_axis=0, tiled=True, ax...]
    ppermute x0 -> x28, waiting for transfers between devices: none -> 190 us  [the longest x16 152 us: swap_cube(): return lax.ppermute(block, ('row', 'col'), route)]
    all_to_all x13 -> x2, starting transfers between devices: 90 us -> 14.2 us  [the longest x1 7.76 us: body(): lax.all_to_all(w_ff, 'row', split_axis=0, concat_axis=0, tiled=True)]
    ppermute x0 -> x28, starting transfers between devices: none -> 55.2 us  [the longest x16 32.2 us: swap_cube(): return lax.ppermute(block, ('row', 'col'), route)]
    all_gather x2 -> x1, waiting for transfers between devices: 57.2 us -> 5.68 us  [body(): lax.all_gather(jnp.concatenate([w_q, w_kv, w_o.T], axis=1), 'row', axis=0...]
    ppermute x6, starting transfers between devices: 27.3 us -> 7.42 us  [swap_col(): return lax.ppermute(block, 'col', [(0, 1), (1, 0)])]
    unnamed x112 -> x110, local copies, waits for them, and re-layouts: 13.3 us -> 22.3 us
    broadcast_in_dim x6 -> x0, local copies, waits for them, and re-layouts: 7.79 us -> none  [the longest x4 4.27 us: gather_plane(): copies = jnp.broadcast_to(block[None], (span // 2,) + block.shape)]
  transfers between devices with their start and end apart: 30 -> 46, of which waited for: 19 -> 28; matrix products, arithmetic and copies ran while one was open for 18% -> 20% of each run, Pallas kernels for 3% -> 3%
where the time goes in v2:
time: 490 us; the launch traced here: 482 us
  waiting for transfers between devices  233 us (48%)
  starting transfers between devices  78.2 us (16%)
  matrix products  48.6 us (10%)
  local copies, waits for them, and re-layouts  47 us (10%)
  other arithmetic  36.7 us (7%)
  Pallas kernels  20.2 us (4%)
  between operations  17.9 us (4%)
    ppermute x16, waiting for transfers between devices, swap_cube(): return lax.ppermute(block, ('row', 'col'), route)  152 us
    dot_general x14, matrix products, dot(): return lax.dot_general(a, b, (dims, ((), ())), preferred_element_type=F32)  48.6 us
    ppermute x16, starting transfers between devices, swap_cube(): return lax.ppermute(block, ('row', 'col'), route)  32.2 us
    ppermute x9, waiting for transfers between devices, shift_far(): return lax.ppermute(block, 'row', route)  25.5 us
    unnamed x110, local copies, waits for them, and re-layouts  22.3 us
    ppermute x6, waiting for transfers between devices, swap_col(): return lax.ppermute(block, 'col', [(0, 1), (1, 0)])  17.8 us
    all_to_all x1, waiting for transfers between devices, exchange_group(): lax.all_to_all(blocks, 'row', split_axis=0, concat_axis=0, tiled=True, ax...  15.9 us
    ppermute x9, starting transfers between devices, shift_far(): return lax.ppermute(block, 'row', route)  15.5 us
  transfers between devices with their start and end apart: 46, of which 28 were waited for; matrix products, arithmetic and copies ran while one was open for 20% of the time, Pallas kernels for 3%

profile of v2, /device:TPU:0, one launch (start us, length us, event | category | flops | bytes accessed | tf_op | source)
XLA Modules:
  0.0 482.1 jit_solution(14246268943701010258)
XLA Ops:
  17.1 3.0 collective-permute-start
  20.1 6.3 %collective-permute-done = bf16[64,2048]{1,0:T(8,128)(2,1)S(1)} collective-permute-done((bf16[64,2048]{1,0:T(8,128)(2,1)S(1)}, bf16[64,2048]{1,0:T(8,128)(2,1)S(1)}, u32[]{:S(2)}, u32[]{:S(2)}) %collective-permute-start) | collective-permute-done | bytes 262176 | tf_op jit(solution)/shard_map/ppermute | solution.py:56
  26.5 1.8 collective-permute-start.1
  28.2 16.0 %collective-permute-done.1 = bf16[128,2048]{1,0:T(8,128)(2,1)S(1)} collective-permute-done((bf16[128,2048]{1,0:T(8,128)(2,1)S(1)}, bf16[128,2048]{1,0:T(8,128)(2,1)S(1)}, u32[]{:S(2)}, u32[]{:S(2)}) %collective-permute-start.1) | collective-permute-done | bytes 524320 | tf_op jit(solution)/shard_map/ppermute | solution.py:56
  48.0 22.1 %collective-permute-done.2 = bf16[256,2048]{1,0:T(8,128)(2,1)} collective-permute-done((bf16[256,2048]{1,0:T(8,128)(2,1)}, bf16[256,2048]{1,0:T(8,128)(2,1)}, u32[]{:S(2)}, u32[]{:S(2)}) %collective-permute-start.2) | collective-permute-done | bytes 1048608 | tf_op jit(solution)/shard_map/ppermute | solution.py:56
  76.7 2.3 constant_dynamic-update-slice_fusion.1
  80.4 5.7 %all-gather.2.cloned.1.call-done.w_ref = bf16[2048,1664]{1,0:T(8,128)(2,1)} async-done(((bf16[128,1664]{1,0:T(8,128)(2,1)}), bf16[2048,1664]{1,0:T(8,128)(2,1)}) %all-gather.2.cloned.1.call-update) | async-done | bytes 6815760 | tf_op jit(solution)/shard_map/all_gather | solution.py:494
  86.1 5.1 %project_heads.1 = (f32[128,1024]{1,0:T(8,128)}, bf16[128,1024]{1,0:T(8,128)(2,1)}) custom-call(bf16[128,2048]{1,0:T(8,128)(2,1)} %multiply_convert_fusion.3.act_ref.in_ref, bf16[2048,1664]{1,0:T(8,128)(2,1)} %all-gather.2.cloned.1.call-done.w_ref, f32[1,1024]{1,0:T(1,128)} %pad_maximum_fusion.15.gain_ref, f32[1,1024]{1,0:T(1,128)} %constant.168.clone.1.flag_ref, ...), custom_call_target="tpu_custom_call" | custom-call | flops 536870912 | bytes 4194304 | tf_op jit(solution)/shard_map/project_heads/pallas_call | solution.py:223
  92.1 3.3 collective-permute-start.4
  95.4 2.9 collective-permute-start.5
  103.4 2.2 pad_maximum_fusion.1
  105.7 7.8 %all-to-all-start = ((bf16[16,128,960]{1,2,0:T(8,128)(2,1)}), bf16[16,128,960]{1,2,0:T(8,128)(2,1)}, u32[]{:S(2)}, u32[]{:S(2)}) async-start(bf16[16,128,960]{1,2,0:T(8,128)(2,1)} %pad_maximum_fusion.1), calls=%async_computation | async-start | bytes 7864320 | tf_op jit(solution)/shard_map/all_to_all | solution.py:512
  119.6 4.2 attention_forward.1
  123.8 2.8 convolution_convert_fusion.6
  128.3 6.8 %collective-permute-done.9 = bf16[64,2048]{1,0:T(8,128)(2,1)S(1)} collective-permute-done((bf16[64,2048]{1,0:T(8,128)(2,1)S(1)}, bf16[64,2048]{1,0:T(8,128)(2,1)S(1)}, u32[]{:S(2)}, u32[]{:S(2)}) %collective-permute-start.9) | collective-permute-done | bytes 262176 | tf_op jit(solution)/shard_map/ppermute | solution.py:31
  135.4 2.2 collective-permute-start.10
  141.4 1.9 collective-permute-start.14
  143.3 40.3 %collective-permute-done.10 = bf16[64,2048]{1,0:T(8,128)(2,1)S(1)} collective-permute-done((bf16[64,2048]{1,0:T(8,128)(2,1)S(1)}, bf16[64,2048]{1,0:T(8,128)(2,1)S(1)}, u32[]{:S(2)}, u32[]{:S(2)}) %collective-permute-start.10) | collective-permute-done | bytes 262176 | tf_op jit(solution)/shard_map/ppermute | solution.py:56
  183.7 3.9 collective-permute-start.15
  188.3 1.9 collective-permute-start.16
  193.8 4.1 collective-permute-done.14
  198.7 4.9 %collective-permute-done.15 = bf16[64,2048]{1,0:T(8,128)(2,1)S(1)} collective-permute-done((bf16[64,2048]{1,0:T(8,128)(2,1)S(1)}, bf16[64,2048]{1,0:T(8,128)(2,1)S(1)}, u32[]{:S(2)}, u32[]{:S(2)}) %collective-permute-start.15) | collective-permute-done | bytes 262176 | tf_op jit(solution)/shard_map/ppermute | solution.py:56
  205.1 4.2 collective-permute-done.17
  210.7 2.7 copy_bitcast_fusion
  213.4 6.2 %fusion.11 = f32[1024,640]{0,1:T(8,128)S(1)} fusion(bf16[1024,2048]{1,0:T(8,128)(2,1)} %constant_dynamic-update-slice_fusion.23, bf16[2048,960]{0,1:T(8,128)(2,1)S(1)} %copy_bitcast_fusion), kind=kOutput, calls=%fused_computation.29 | convolution fusion | flops 2684354560 | bytes 9437184 | tf_op jit(solution)/shard_map/dot_general | solution.py:22
  219.5 4.2 multiply_convert_fusion
  223.8 1.9 convolution_convert_fusion.4
  225.9 3.7 convolution_convert_fusion.5
  229.6 5.8 %convolution_convert_fusion = bf16[2048,640]{0,1:T(8,128)(2,1)S(1)} fusion(bf16[1024,2048]{1,0:T(8,128)(2,1)} %constant_dynamic-update-slice_fusion.23, bf16[1024,320]{0,1:T(8,128)(2,1)S(1)} %get-tuple-element.107, bf16[1024,320]{0,1:T(8,128)(2,1)S(1)} %get-tuple-element.108), kind=kOutput, calls=%fused_computation.12 | convolution fusion | flops 2688286720 | bytes 8126464 | tf_op jit(solution)/shard_map/dot_general | solution.py:22
  235.5 2.4 pad_maximum_fusion.2
  237.9 4.4 add_convert_fusion.1
  245.2 4.0 convolution_convert_fusion.3
  250.5 2.0 reorder_columns.1
  252.7 16.7 %collective-permute-done.19 = bf16[4,64,2048]{2,1,0:T(8,128)(2,1)} collective-permute-done((bf16[4,64,2048]{2,1,0:T(8,128)(2,1)}, bf16[4,64,2048]{2,1,0:T(8,128)(2,1)}, u32[]{:S(2)}, u32[]{:S(2)}) %collective-permute-start.19) | collective-permute-done | bytes 1048608 | tf_op jit(solution)/shard_map/ppermute | solution.py:56
  271.0 3.1 collective-permute-start.20
  276.2 9.6 %collective-permute-done.20 = bf16[2,64,2048]{2,1,0:T(8,128)(2,1)S(1)} collective-permute-done((bf16[2,64,2048]{2,1,0:T(8,128)(2,1)S(1)}, bf16[2,64,2048]{2,1,0:T(8,128)(2,1)S(1)}, u32[]{:S(2)}, u32[]{:S(2)}) %collective-permute-start.20) | collective-permute-done | bytes 524320 | tf_op jit(solution)/shard_map/ppermute | solution.py:56
  285.9 7.6 %collective-permute-start.21 = (bf16[1,64,2048]{2,1,0:T(8,128)(2,1)S(1)}, bf16[1,64,2048]{2,1,0:T(8,128)(2,1)S(1)}, u32[]{:S(2)}, u32[]{:S(2)}) collective-permute-start(bf16[1,64,2048]{2,1,0:T(8,128)(2,1)S(1)} %slice.610), channel_id=1, source_target_pairs={{0,8},{1,9},{2,10},{3,11},{4,12},{5,13},{6,14},{7,15},{8,0},{9,1},... | collective-permute-start | bytes 786440 | tf_op jit(solution)/shard_map/ppermute | solution.py:56
  293.5 3.3 add_convert_fusion
  296.8 6.3 %collective-permute-done.21 = bf16[1,64,2048]{2,1,0:T(8,128)(2,1)S(1)} collective-permute-done((bf16[1,64,2048]{2,1,0:T(8,128)(2,1)S(1)}, bf16[1,64,2048]{2,1,0:T(8,128)(2,1)S(1)}, u32[]{:S(2)}, u32[]{:S(2)}) %collective-permute-start.21) | collective-permute-done | bytes 262176 | tf_op jit(solution)/shard_map/ppermute | solution.py:56
  303.5 1.8 collective-permute-start.22
  306.7 6.1 %collective-permute-done.22 = bf16[64,2048]{1,0:T(8,128)(2,1)S(1)} collective-permute-done((bf16[64,2048]{1,0:T(8,128)(2,1)S(1)}, bf16[64,2048]{1,0:T(8,128)(2,1)S(1)}, u32[]{:S(2)}, u32[]{:S(2)}) %collective-permute-start.22) | collective-permute-done | bytes 262176 | tf_op jit(solution)/shard_map/ppermute | solution.py:31
  312.9 3.1 fusion.17.grad_ref
  316.0 6.5 %attention_backward.1 = (bf16[128,640]{1,0:T(8,128)(2,1)}, f32[1,128]{1,0:T(1,128)}, bf16[2,4,128,384]{3,2,1,0:T(8,128)(2,1)}, bf16[2,4,128,384]{3,2,1,0:T(8,128)(2,1)}) custom-call(s32[2]{0:T(128)} %pad_add_fusion.1.bounds_ref, s32[2,128]{1,0:T(2,128)} %pad_add_fusion.limits_ref, bf16[128,640]{1,0:T(8,128)(2,1)} %slice.327.q_ref, ...), custom_call_target="tpu_custom_call" | custom-call | flops 1677721600 | bytes 3145728 | tf_op jit(solution)/shard_map/attention_backward/pallas_call | solution.py:382
  322.6 1.8 convolution_convert_fusion.1
  325.3 2.8 pad_maximum_fusion
  330.6 1.8 collective-permute-start.26
  335.5 6.6 %collective-permute-done.26 = bf16[4,128,384]{2,1,0:T(8,128)(2,1)S(1)} collective-permute-done((bf16[4,128,384]{2,1,0:T(8,128)(2,1)S(1)}, bf16[4,128,384]{2,1,0:T(8,128)(2,1)S(1)}, u32[]{:S(2)}, u32[]{:S(2)}) %collective-permute-start.26) | collective-permute-done | bytes 393248 | tf_op jit(solution)/shard_map/ppermute | solution.py:46
  347.3 5.3 %collective-permute-done.27.refs_1_ = bf16[128,384]{1,0:T(8,128)(2,1)} collective-permute-done((bf16[128,384]{1,0:T(8,128)(2,1)}, bf16[128,384]{1,0:T(8,128)(2,1)}, u32[]{:S(2)}, u32[]{:S(2)}) %collective-permute-start.27) | collective-permute-done | bytes 98336 | tf_op jit(solution)/shard_map/ppermute | solution.py:41
  352.6 8.4 %collective-permute-done.28.refs_2_ = bf16[128,384]{1,0:T(8,128)(2,1)} collective-permute-done((bf16[128,384]{1,0:T(8,128)(2,1)}, bf16[128,384]{1,0:T(8,128)(2,1)}, u32[]{:S(2)}, u32[]{:S(2)}) %collective-permute-start.28) | collective-permute-done | bytes 98336 | tf_op jit(solution)/shard_map/ppermute | solution.py:41
  361.0 2.5 key_value_heads_back.1
  364.4 4.9 %fusion.2 = bf16[128,2048]{1,0:T(8,128)(2,1)} fusion(bf16[2048,1664]{1,0:T(8,128)(2,1)} %all-gather.2.cloned.1.call-done.w_ref, bf16[128,384]{1,0:T(8,128)(2,1)} %get-tuple-element.42, bf16[128,640]{1,0:T(8,128)(2,1)} %get-tuple-element.44), kind=kOutput, calls=%fused_computation.18 | convolution fusion | flops 537657344 | bytes 4980736 | tf_op jit(solution)/shard_map/dot_general | solution.py:22
  376.7 14.6 %collective-permute-done.30 = bf16[2,64,2048]{2,1,0:T(8,128)(2,1)} collective-permute-done((bf16[2,64,2048]{2,1,0:T(8,128)(2,1)}, bf16[2,64,2048]{2,1,0:T(8,128)(2,1)}, u32[]{:S(2)}, u32[]{:S(2)}) %collective-permute-start.30) | collective-permute-done | bytes 524320 | tf_op jit(solution)/shard_map/ppermute | solution.py:56
  394.1 2.7 subtract_add_fusion
  396.8 7.9 %collective-permute-done.31 = bf16[1,64,2048]{2,1,0:T(8,128)(2,1)S(1)} collective-permute-done((bf16[1,64,2048]{2,1,0:T(8,128)(2,1)S(1)}, bf16[1,64,2048]{2,1,0:T(8,128)(2,1)S(1)}, u32[]{:S(2)}, u32[]{:S(2)}) %collective-permute-start.31) | collective-permute-done | bytes 262176 | tf_op jit(solution)/shard_map/ppermute | solution.py:56
  405.3 5.0 %collective-permute-start.35 = (bf16[4,144,384]{2,1,0:T(8,128)(2,1)S(1)}, bf16[4,144,384]{2,1,0:T(8,128)(2,1)S(1)}, u32[]{:S(2)}, u32[]{:S(2)}) collective-permute-start(bf16[4,144,384]{2,1,0:T(8,128)(2,1)S(1)} %slice.445), channel_id=1, source_target_pairs={{0,4},{2,6},{4,0},{6,2},{8,12},{10,14},{12,8},{14,10},{16,20},{18,... | collective-permute-start | bytes 1327112 | tf_op jit(solution)/shard_map/ppermute | solution.py:46
  411.3 5.9 %collective-permute-done.35 = bf16[4,144,384]{2,1,0:T(8,128)(2,1)S(1)} collective-permute-done((bf16[4,144,384]{2,1,0:T(8,128)(2,1)S(1)}, bf16[4,144,384]{2,1,0:T(8,128)(2,1)S(1)}, u32[]{:S(2)}, u32[]{:S(2)}) %collective-permute-start.35) | collective-permute-done | bytes 442400 | tf_op jit(solution)/shard_map/ppermute | solution.py:46
  417.7 3.5 collective-permute-start.38
  422.1 3.1 collective-permute-done.36
  425.2 5.8 %collective-permute-done.37 = bf16[144,384]{1,0:T(8,128)(2,1)S(1)} collective-permute-done((bf16[144,384]{1,0:T(8,128)(2,1)S(1)}, bf16[144,384]{1,0:T(8,128)(2,1)S(1)}, u32[]{:S(2)}, u32[]{:S(2)}) %collective-permute-start.37) | collective-permute-done | bytes 110624 | tf_op jit(solution)/shard_map/ppermute | solution.py:41
  431.1 3.2 copy_bitcast_fusion.1
  434.3 6.5 %all-to-all-start.1 = ((bf16[8,128,960]{1,2,0:T(8,128)(2,1)}), bf16[8,128,960]{1,2,0:T(8,128)(2,1)S(1)}, u32[]{:S(2)}, u32[]{:S(2)}) async-start(bf16[8,128,960]{1,2,0:T(8,128)(2,1)} %copy_bitcast_fusion.1), calls=%async_computation.3 | async-start | bytes 3932160 | tf_op jit(solution)/shard_map/all_to_all | solution.py:164
  442.1 3.9 collective-permute-done.39
  449.1 15.9 %all-to-all-done.1 = bf16[8,128,960]{1,2,0:T(8,128)(2,1)S(1)} async-done(((bf16[8,128,960]{1,2,0:T(8,128)(2,1)}), bf16[8,128,960]{1,2,0:T(8,128)(2,1)S(1)}, u32[]{:S(2)}, u32[]{:S(2)}) %all-to-all-start.1) | async-done | bytes 1966112 | tf_op jit(solution)/shard_map/all_to_all | solution.py:164
  469.1 1.9 copy.105
  (279 shorter events, 93.1 us)
Async XLA Ops:
  7.2 78.9 %all-gather.2.cloned.1.call-start = ((), (), s32[]{:S(2)}) async-start(), calls=%async_computation.4 | async-start | bytes 7241728 | tf_op jit(solution)/shard_map/all_gather | solution.py:494
  15.2 30.1 %copy-start.10 = (bf16[128,640]{1,0:T(8,128)(2,1)}, bf16[128,640]{1,0:T(8,128)(2,1)S(1)}, u32[]{:S(2)}) copy-start(bf16[128,640]{1,0:T(8,128)(2,1)S(1)} %broadcast_select_fusion.5) | copy-start | bytes 491524
  15.4 30.3 %copy-start.29 = (s32[128]{0:T(128)S(1)}, s32[128]{0:T(128)}, u32[]{:S(2)}) copy-start(s32[128]{0:T(128)} %param.26) | copy-start | bytes 1540
  15.4 30.3 %copy-start.30 = (f32[64]{0:T(128)S(1)}, f32[64]{0:T(128)}, u32[]{:S(2)}) copy-start(f32[64]{0:T(128)} %param.24) | copy-start | bytes 772
  15.4 30.4 %copy-start.28 = (pred[3,128]{1,0:T(4,128)(4,1)S(1)}, pred[3,128]{1,0:T(4,128)(4,1)}, u32[]{:S(2)}) copy-start(pred[3,128]{1,0:T(4,128)(4,1)} %constant.166.clone.1) | copy-start | bytes 1156
  15.4 30.4 %copy-start.31 = (f32[64]{0:T(128)S(1)}, f32[64]{0:T(128)}, u32[]{:S(2)}) copy-start(f32[64]{0:T(128)} %param.23) | copy-start | bytes 772
  15.5 30.5 %copy-start.14 = (bf16[128,2560]{1,0:T(8,128)(2,1)S(1)}, bf16[128,2560]{1,0:T(8,128)(2,1)}, u32[]{:S(2)}) copy-start(bf16[128,2560]{1,0:T(8,128)(2,1)} %param.18) | copy-start | bytes 1966084
  17.1 9.3 %collective-permute-start = (bf16[64,2048]{1,0:T(8,128)(2,1)S(1)}, bf16[64,2048]{1,0:T(8,128)(2,1)S(1)}, u32[]{:S(2)}, u32[]{:S(2)}) collective-permute-start(bf16[64,2048]{1,0:T(8,128)(2,1)S(1)} %get-tuple-element.101), channel_id=1, source_target_pairs={{0,8},{1,9},{2,10},{3,11},{4,12},{5,13},{6,14},{7,15},{8,0},{9,1},... | collective-permute-start | bytes 786440 | tf_op jit(solution)/shard_map/ppermute | solution.py:56
  26.5 17.7 %collective-permute-start.1 = (bf16[128,2048]{1,0:T(8,128)(2,1)S(1)}, bf16[128,2048]{1,0:T(8,128)(2,1)S(1)}, u32[]{:S(2)}, u32[]{:S(2)}) collective-permute-start(bf16[128,2048]{1,0:T(8,128)(2,1)S(1)} %pad_maximum_fusion.8), channel_id=1, source_target_pairs={{0,4},{1,5},{2,6},{3,7},{4,0},{5,1},{6,2},{7,3},{8,12},{9,13},{10,... | collective-permute-start | bytes 1572872 | tf_op jit(solution)/shard_map/ppermute | solution.py:56
  45.3 24.8 %collective-permute-start.2 = (bf16[256,2048]{1,0:T(8,128)(2,1)}, bf16[256,2048]{1,0:T(8,128)(2,1)}, u32[]{:S(2)}, u32[]{:S(2)}) collective-permute-start(bf16[256,2048]{1,0:T(8,128)(2,1)} %pad_maximum_fusion.6), channel_id=1, source_target_pairs={{0,1},{1,0},{2,3},{3,2},{4,5},{5,4},{6,7},{7,6},{8,9},{9,8},{10,11... | collective-permute-start | bytes 3145736 | tf_op jit(solution)/shard_map/ppermute | solution.py:56
  45.8 25.8 %copy-start.24 = (f32[1,1,3,128]{3,1,2,0:T(1,128)}, f32[1,1,3,128]{3,1,2,0:T(1,128)S(1)}, u32[]{:S(2)}) copy-start(f32[1,1,3,128]{3,1,2,0:T(1,128)S(1)} %copy.122) | copy-start | bytes 4612
  46.3 53.4 %copy-start.2 = (bf16[128,2560]{0,1:T(8,128)(2,1)}, bf16[128,2560]{0,1:T(8,128)(2,1)S(1)}, u32[]{:S(2)}) copy-start(bf16[128,2560]{0,1:T(8,128)(2,1)S(1)} %copy.93) | copy-start | bytes 1966084
  47.9 51.7 %copy-start.4 = (bf16[128,2560]{0,1:T(8,128)(2,1)}, bf16[128,2560]{0,1:T(8,128)(2,1)S(1)}, u32[]{:S(2)}) copy-start(bf16[128,2560]{0,1:T(8,128)(2,1)S(1)} %copy.94) | copy-start | bytes 1966084
  47.9 25.4 %copy-start = (bf16[128,2048]{1,0:T(8,128)(2,1)S(1)}, bf16[128,2048]{1,0:T(8,128)(2,1)}, u32[]{:S(2)}) copy-start(bf16[128,2048]{1,0:T(8,128)(2,1)} %param.14) | copy-start | bytes 1572868
  47.9 26.1 %copy-start.22 = (f32[2048]{0:T(1024)S(1)}, f32[2048]{0:T(1024)}, u32[]{:S(2)}) copy-start(f32[2048]{0:T(1024)} %param.21) | copy-start | bytes 24580
  71.5 7.5 %collective-permute-start.3 = (bf16[512,2048]{1,0:T(8,128)(2,1)S(1)}, bf16[512,2048]{1,0:T(8,128)(2,1)S(1)}, u32[]{:S(2)}, u32[]{:S(2)}) collective-permute-start(bf16[512,2048]{1,0:T(8,128)(2,1)S(1)} %pad_maximum_fusion.3), channel_id=1, source_target_pairs={{0,2},{2,0},{4,6},{6,4},{8,10},{10,8},{12,14},{14,12},{16,18},{18,... | collective-permute-start | bytes 6291464 | tf_op jit(solution)/shard_map/ppermute | solution.py:27
  86.1 13.5 %copy-start.15 = (bf16[2560,128]{1,0:T(8,128)(2,1)S(1)}, bf16[2560,128]{1,0:T(8,128)(2,1)}, u32[]{:S(2)}) copy-start(bf16[2560,128]{1,0:T(8,128)(2,1)} %param.20) | copy-start | bytes 1966084
  92.1 7.7 %collective-permute-start.4 = (bf16[128,384]{1,0:T(8,128)(2,1)S(1)}, bf16[128,384]{1,0:T(8,128)(2,1)S(1)}, u32[]{:S(2)}, u32[]{:S(2)}) collective-permute-start(bf16[128,384]{1,0:T(8,128)(2,1)S(1)} %get-tuple-element.145), channel_id=1, source_target_pairs={{0,8},{2,10},{4,12},{6,14},{8,16},{10,18},{12,20},{14,22},{16,24},... | collective-permute-start | bytes 294920 | tf_op jit(solution)/shard_map/ppermute | solution.py:41
  95.4 6.0 %collective-permute-start.5 = (bf16[128,384]{1,0:T(8,128)(2,1)S(1)}, bf16[128,384]{1,0:T(8,128)(2,1)S(1)}, u32[]{:S(2)}, u32[]{:S(2)}) collective-permute-start(bf16[128,384]{1,0:T(8,128)(2,1)S(1)} %get-tuple-element.145), channel_id=1, source_target_pairs={{0,16},{2,18},{4,20},{6,22},{8,24},{10,26},{12,28},{14,30},{1,17},... | collective-permute-start | bytes 294920 | tf_op jit(solution)/shard_map/ppermute | solution.py:41
  98.3 4.3 collective-permute-start.6
  102.7 10.8 %collective-permute-start.7 = (bf16[4,128,384]{2,1,0:T(8,128)(2,1)S(1)}, bf16[4,128,384]{2,1,0:T(8,128)(2,1)S(1)}, u32[]{:S(2)}, u32[]{:S(2)}) collective-permute-start(bf16[4,128,384]{2,1,0:T(8,128)(2,1)S(1)} %get-tuple-element.129), channel_id=1, source_target_pairs={{0,4},{2,6},{4,0},{6,2},{8,12},{10,14},{12,8},{14,10},{16,20},{18,... | collective-permute-start | bytes 1179656 | tf_op jit(solution)/shard_map/ppermute | solution.py:46
  105.7 105.0 %all-to-all-start = ((bf16[16,128,960]{1,2,0:T(8,128)(2,1)}), bf16[16,128,960]{1,2,0:T(8,128)(2,1)}, u32[]{:S(2)}, u32[]{:S(2)}) async-start(bf16[16,128,960]{1,2,0:T(8,128)(2,1)} %pad_maximum_fusion.1), calls=%async_computation | async-start | bytes 7864320 | tf_op jit(solution)/shard_map/all_to_all | solution.py:512
  113.4 317.6 %reduce-scatter.5.cloned.1.call-start = ((), (), s32[]{:S(2)}) async-start(), calls=%async_computation.6 | async-start | bytes 5898240 | tf_op jit(solution)/shard_map/reduce_scatter | solution.py:572
  113.6 6.0 %collective-permute-start.8 = (bf16[2,4,128,384]{3,2,1,0:T(8,128)(2,1)S(1)}, bf16[2,4,128,384]{3,2,1,0:T(8,128)(2,1)}, u32[]{:S(2)}, u32[]{:S(2)}) collective-permute-start(bf16[2,4,128,384]{3,2,1,0:T(8,128)(2,1)S(1)} %pad_maximum_fusion.7.same_ref), channel_id=1, source_target_pairs={{0,2},{2,0},{4,6},{6,4},{8,10},{10,8},{12,14},{14,12},{16,18},{18,... | collective-permute-start | bytes 2359304 | tf_op jit(solution)/shard_map/ppermute | solution.py:27
  126.7 8.4 %collective-permute-start.9 = (bf16[64,2048]{1,0:T(8,128)(2,1)S(1)}, bf16[64,2048]{1,0:T(8,128)(2,1)S(1)}, u32[]{:S(2)}, u32[]{:S(2)}) collective-permute-start(bf16[64,2048]{1,0:T(8,128)(2,1)S(1)} %constant_dynamic-slice_fusion), channel_id=1, source_target_pairs={{0,1},{1,0},{2,3},{3,2},{4,5},{5,4},{6,7},{7,6},{8,9},{9,8},{10,11... | collective-permute-start | bytes 786440 | tf_op jit(solution)/shard_map/ppermute | solution.py:31
  135.4 48.2 %collective-permute-start.10 = (bf16[64,2048]{1,0:T(8,128)(2,1)S(1)}, bf16[64,2048]{1,0:T(8,128)(2,1)S(1)}, u32[]{:S(2)}, u32[]{:S(2)}) collective-permute-start(bf16[64,2048]{1,0:T(8,128)(2,1)S(1)} %get-tuple-element.97), channel_id=1, source_target_pairs={{0,8},{1,9},{2,10},{3,11},{4,12},{5,13},{6,14},{7,15},{8,0},{9,1},... | collective-permute-start | bytes 786440 | tf_op jit(solution)/shard_map/ppermute | solution.py:56
  137.7 50.6 %collective-permute-start.11 = (bf16[64,2048]{1,0:T(8,128)(2,1)S(1)}, bf16[64,2048]{1,0:T(8,128)(2,1)S(1)}, u32[]{:S(2)}, u32[]{:S(2)}) collective-permute-start(bf16[64,2048]{1,0:T(8,128)(2,1)S(1)} %get-tuple-element.97), channel_id=1, source_target_pairs={{0,4},{1,5},{2,6},{3,7},{4,0},{5,1},{6,2},{7,3},{8,12},{9,13},{10,... | collective-permute-start | bytes 786440 | tf_op jit(solution)/shard_map/ppermute | solution.py:56
  139.6 52.7 %collective-permute-start.12 = (bf16[64,2048]{1,0:T(8,128)(2,1)S(1)}, bf16[64,2048]{1,0:T(8,128)(2,1)S(1)}, u32[]{:S(2)}, u32[]{:S(2)}) collective-permute-start(bf16[64,2048]{1,0:T(8,128)(2,1)S(1)} %get-tuple-element.97), channel_id=1, source_target_pairs={{0,12},{1,13},{2,14},{3,15},{4,8},{5,9},{6,10},{7,11},{8,4},{9,5},... | collective-permute-start | bytes 786440 | tf_op jit(solution)/shard_map/ppermute | solution.py:56
  139.9 53.1 %collective-permute-start.13 = (bf16[64,2048]{1,0:T(8,128)(2,1)S(1)}, bf16[64,2048]{1,0:T(8,128)(2,1)S(1)}, u32[]{:S(2)}, u32[]{:S(2)}) collective-permute-start(bf16[64,2048]{1,0:T(8,128)(2,1)S(1)} %get-tuple-element.97), channel_id=1, source_target_pairs={{0,1},{1,0},{2,3},{3,2},{4,5},{5,4},{6,7},{7,6},{8,9},{9,8},{10,11... | collective-permute-start | bytes 786440 | tf_op jit(solution)/shard_map/ppermute | solution.py:56
  141.4 56.5 %collective-permute-start.14 = (bf16[64,2048]{1,0:T(8,128)(2,1)S(1)}, bf16[64,2048]{1,0:T(8,128)(2,1)S(1)}, u32[]{:S(2)}, u32[]{:S(2)}) collective-permute-start(bf16[64,2048]{1,0:T(8,128)(2,1)S(1)} %get-tuple-element.97), channel_id=1, source_target_pairs={{0,9},{1,8},{2,11},{3,10},{4,13},{5,12},{6,15},{7,14},{8,1},{9,0},... | collective-permute-start | bytes 786440 | tf_op jit(solution)/shard_map/ppermute | solution.py:56
  183.7 19.9 %collective-permute-start.15 = (bf16[64,2048]{1,0:T(8,128)(2,1)S(1)}, bf16[64,2048]{1,0:T(8,128)(2,1)S(1)}, u32[]{:S(2)}, u32[]{:S(2)}) collective-permute-start(bf16[64,2048]{1,0:T(8,128)(2,1)S(1)} %get-tuple-element.97), channel_id=1, source_target_pairs={{0,5},{1,4},{2,7},{3,6},{4,1},{5,0},{6,3},{7,2},{8,13},{9,12},{10,... | collective-permute-start | bytes 786440 | tf_op jit(solution)/shard_map/ppermute | solution.py:56
  188.3 16.0 %collective-permute-start.16 = (bf16[64,2048]{1,0:T(8,128)(2,1)S(1)}, bf16[64,2048]{1,0:T(8,128)(2,1)S(1)}, u32[]{:S(2)}, u32[]{:S(2)}) collective-permute-start(bf16[64,2048]{1,0:T(8,128)(2,1)S(1)} %get-tuple-element.97), channel_id=1, source_target_pairs={{0,13},{1,12},{2,15},{3,14},{4,9},{5,8},{6,11},{7,10},{8,5},{9,4},... | collective-permute-start | bytes 786440 | tf_op jit(solution)/shard_map/ppermute | solution.py:56
  205.1 4.2 collective-permute-start.17
  225.7 12.2 %collective-permute-start.18 = (bf16[512,2048]{1,0:T(8,128)(2,1)S(1)}, bf16[512,2048]{1,0:T(8,128)(2,1)}, u32[]{:S(2)}, u32[]{:S(2)}) collective-permute-start(bf16[512,2048]{1,0:T(8,128)(2,1)S(1)} %convolution_convert_fusion.4), channel_id=1, source_target_pairs={{0,2},{2,0},{4,6},{6,4},{8,10},{10,8},{12,14},{14,12},{16,18},{18,... | collective-permute-start | bytes 6291464 | tf_op jit(solution)/shard_map/ppermute | solution.py:27
  242.3 204.8 %reduce-scatter.3.cloned.1.call-start = ((), (), s32[]{:S(2)}) async-start(), calls=%async_computation.5 | async-start | bytes 5570560 | tf_op jit(solution)/shard_map/reduce_scatter | solution.py:598
  243.6 25.7 %collective-permute-start.19 = (bf16[4,64,2048]{2,1,0:T(8,128)(2,1)}, bf16[4,64,2048]{2,1,0:T(8,128)(2,1)}, u32[]{:S(2)}, u32[]{:S(2)}) collective-permute-start(bf16[4,64,2048]{2,1,0:T(8,128)(2,1)} %slice.337), channel_id=1, source_target_pairs={{0,1},{1,0},{2,3},{3,2},{4,5},{5,4},{6,7},{7,6},{8,9},{9,8},{10,11... | collective-permute-start | bytes 3145736 | tf_op jit(solution)/shard_map/ppermute | solution.py:56
  249.2 44.4 %collective-permute-start.23 = (bf16[512,2048]{1,0:T(8,128)(2,1)}, bf16[512,2048]{1,0:T(8,128)(2,1)}, u32[]{:S(2)}, u32[]{:S(2)}) collective-permute-start(bf16[512,2048]{1,0:T(8,128)(2,1)} %convolution_convert_fusion.3), channel_id=1, source_target_pairs={{0,2},{2,0},{4,6},{6,4},{8,10},{10,8},{12,14},{14,12},{16,18},{18,... | collective-permute-start | bytes 6291464 | tf_op jit(solution)/shard_map/ppermute | solution.py:27
  252.6 21.5 %copy-start.26 = (s32[16]{0:T(128)S(1)}, s32[16]{0:T(128)}, u32[]{:S(2)}) copy-start(s32[16]{0:T(128)} %stack.151.order_ref) | copy-start | bytes 196
  252.7 22.1 %copy-start.16 = (f32[128,1024]{1,0:T(8,128)S(1)}, f32[128,1024]{1,0:T(8,128)}, u32[]{:S(2)}) copy-start(f32[128,1024]{1,0:T(8,128)} %get-tuple-element.37) | copy-start | bytes 1572868
  271.0 22.6 %copy-start.34 = (bf16[1024,320]{0,1:T(8,128)(2,1)S(1)}, bf16[1024,320]{0,1:T(8,128)(2,1)}, u32[]{:S(2)}) copy-start(bf16[1024,320]{0,1:T(8,128)(2,1)} %copy-done.33) | copy-start | bytes 1966084
  271.0 14.7 %collective-permute-start.20 = (bf16[2,64,2048]{2,1,0:T(8,128)(2,1)S(1)}, bf16[2,64,2048]{2,1,0:T(8,128)(2,1)S(1)}, u32[]{:S(2)}, u32[]{:S(2)}) collective-permute-start(bf16[2,64,2048]{2,1,0:T(8,128)(2,1)S(1)} %slice.608), channel_id=1, source_target_pairs={{0,4},{1,5},{2,6},{3,7},{4,0},{5,1},{6,2},{7,3},{8,12},{9,13},{10,... | collective-permute-start | bytes 1572872 | tf_op jit(solution)/shard_map/ppermute | solution.py:56
  285.9 17.2 %collective-permute-start.21 = (bf16[1,64,2048]{2,1,0:T(8,128)(2,1)S(1)}, bf16[1,64,2048]{2,1,0:T(8,128)(2,1)S(1)}, u32[]{:S(2)}, u32[]{:S(2)}) collective-permute-start(bf16[1,64,2048]{2,1,0:T(8,128)(2,1)S(1)} %slice.610), channel_id=1, source_target_pairs={{0,8},{1,9},{2,10},{3,11},{4,12},{5,13},{6,14},{7,15},{8,0},{9,1},... | collective-permute-start | bytes 786440 | tf_op jit(solution)/shard_map/ppermute | solution.py:56
  303.5 9.3 %collective-permute-start.22 = (bf16[64,2048]{1,0:T(8,128)(2,1)S(1)}, bf16[64,2048]{1,0:T(8,128)(2,1)S(1)}, u32[]{:S(2)}, u32[]{:S(2)}) collective-permute-start(bf16[64,2048]{1,0:T(8,128)(2,1)S(1)} %add_convert_fusion.4), channel_id=1, source_target_pairs={{0,1},{1,0},{2,3},{3,2},{4,5},{5,4},{6,7},{7,6},{8,9},{9,8},{10,11... | collective-permute-start | bytes 786440 | tf_op jit(solution)/shard_map/ppermute | solution.py:31
  306.4 27.5 %collective-permute-start.24 = (bf16[4,64,2048]{2,1,0:T(8,128)(2,1)S(1)}, bf16[4,64,2048]{2,1,0:T(8,128)(2,1)}, u32[]{:S(2)}, u32[]{:S(2)}) collective-permute-start(bf16[4,64,2048]{2,1,0:T(8,128)(2,1)S(1)} %bitcast.160), channel_id=1, source_target_pairs={{0,1},{1,0},{2,3},{3,2},{4,5},{5,4},{6,7},{7,6},{8,9},{9,8},{10,11... | collective-permute-start | bytes 3145736 | tf_op jit(solution)/shard_map/ppermute | solution.py:56
  322.5 5.6 %collective-permute-start.25 = (bf16[2,4,128,384]{3,2,1,0:T(8,128)(2,1)}, bf16[2,4,128,384]{3,2,1,0:T(8,128)(2,1)}, u32[]{:S(2)}, u32[]{:S(2)}) collective-permute-start(bf16[2,4,128,384]{3,2,1,0:T(8,128)(2,1)} %get-tuple-element.41), channel_id=1, source_target_pairs={{0,2},{2,0},{4,6},{6,4},{8,10},{10,8},{12,14},{14,12},{16,18},{18,... | collective-permute-start | bytes 2359304 | tf_op jit(solution)/shard_map/ppermute | solution.py:27
  330.6 11.6 %collective-permute-start.26 = (bf16[4,128,384]{2,1,0:T(8,128)(2,1)S(1)}, bf16[4,128,384]{2,1,0:T(8,128)(2,1)S(1)}, u32[]{:S(2)}, u32[]{:S(2)}) collective-permute-start(bf16[4,128,384]{2,1,0:T(8,128)(2,1)S(1)} %slice_bitcast_fusion), channel_id=1, source_target_pairs={{0,4},{2,6},{4,0},{6,2},{8,12},{10,14},{12,8},{14,10},{16,20},{18,... | collective-permute-start | bytes 1179656 | tf_op jit(solution)/shard_map/ppermute | solution.py:46
  343.0 9.6 %collective-permute-start.27 = (bf16[128,384]{1,0:T(8,128)(2,1)}, bf16[128,384]{1,0:T(8,128)(2,1)}, u32[]{:S(2)}, u32[]{:S(2)}) collective-permute-start(bf16[128,384]{1,0:T(8,128)(2,1)} %get-tuple-element.126), channel_id=1, source_target_pairs={{8,0},{10,2},{12,4},{14,6},{16,8},{18,10},{20,12},{22,14},{24,16},... | collective-permute-start | bytes 294920 | tf_op jit(solution)/shard_map/ppermute | solution.py:41
  344.3 16.8 %collective-permute-start.28 = (bf16[128,384]{1,0:T(8,128)(2,1)}, bf16[128,384]{1,0:T(8,128)(2,1)}, u32[]{:S(2)}, u32[]{:S(2)}) collective-permute-start(bf16[128,384]{1,0:T(8,128)(2,1)} %get-tuple-element.125), channel_id=1, source_target_pairs={{16,0},{18,2},{20,4},{22,6},{24,8},{26,10},{28,12},{30,14},{17,1},... | collective-permute-start | bytes 294920 | tf_op jit(solution)/shard_map/ppermute | solution.py:41
  345.6 15.5 %collective-permute-start.29 = (bf16[128,384]{1,0:T(8,128)(2,1)}, bf16[128,384]{1,0:T(8,128)(2,1)}, u32[]{:S(2)}, u32[]{:S(2)}) collective-permute-start(bf16[128,384]{1,0:T(8,128)(2,1)} %get-tuple-element.124), channel_id=1, source_target_pairs={{24,0},{26,2},{28,4},{30,6},{25,1},{27,3},{29,5},{31,7}} | collective-permute-start | bytes 294920 | tf_op jit(solution)/shard_map/ppermute | solution.py:41
  369.4 23.2 %collective-permute-start.33 = (bf16[128,2048]{1,0:T(8,128)(2,1)}, bf16[128,2048]{1,0:T(8,128)(2,1)}, u32[]{:S(2)}, u32[]{:S(2)}) collective-permute-start(bf16[128,2048]{1,0:T(8,128)(2,1)} %fusion.2), channel_id=1, source_target_pairs={{0,1},{1,0},{2,3},{3,2},{4,5},{5,4},{6,7},{7,6},{8,9},{9,8},{10,11... | collective-permute-start | bytes 1572872 | tf_op jit(solution)/shard_map/ppermute | solution.py:31
  371.7 19.6 %collective-permute-start.30 = (bf16[2,64,2048]{2,1,0:T(8,128)(2,1)}, bf16[2,64,2048]{2,1,0:T(8,128)(2,1)}, u32[]{:S(2)}, u32[]{:S(2)}) collective-permute-start(bf16[2,64,2048]{2,1,0:T(8,128)(2,1)} %slice.607), channel_id=1, source_target_pairs={{0,4},{1,5},{2,6},{3,7},{4,0},{5,1},{6,2},{7,3},{8,12},{9,13},{10,... | collective-permute-start | bytes 1572872 | tf_op jit(solution)/shard_map/ppermute | solution.py:56
  376.6 17.5 %copy-start.9 = (bf16[64,2048]{1,0:T(8,128)(2,1)S(1)}, bf16[64,2048]{1,0:T(8,128)(2,1)}, u32[]{:S(2)}) copy-start(bf16[64,2048]{1,0:T(8,128)(2,1)} %copy-done.8) | copy-start | bytes 786436
  376.6 17.5 %copy-start.27 = (f32[128]{0:T(128)S(1)}, f32[128]{0:T(128)}, u32[]{:S(2)}) copy-start(f32[128]{0:T(128)} %get-tuple-element.169) | copy-start | bytes 1540
  376.6 28.3 %collective-permute-start.34 = (bf16[8,144,384]{2,1,0:T(8,128)(2,1)S(1)}, bf16[8,144,384]{2,1,0:T(8,128)(2,1)S(1)}, u32[]{:S(2)}, u32[]{:S(2)}) collective-permute-start(bf16[8,144,384]{2,1,0:T(8,128)(2,1)S(1)} %slice.606), channel_id=1, source_target_pairs={{0,2},{2,0},{4,6},{6,4},{8,10},{10,8},{12,14},{14,12},{16,18},{18,... | collective-permute-start | bytes 2654216 | tf_op jit(solution)/shard_map/ppermute | solution.py:27
  392.5 12.3 %collective-permute-start.31 = (bf16[1,64,2048]{2,1,0:T(8,128)(2,1)S(1)}, bf16[1,64,2048]{2,1,0:T(8,128)(2,1)S(1)}, u32[]{:S(2)}, u32[]{:S(2)}) collective-permute-start(bf16[1,64,2048]{2,1,0:T(8,128)(2,1)S(1)} %slice.609), channel_id=1, source_target_pairs={{0,8},{1,9},{2,10},{3,11},{4,12},{5,13},{6,14},{7,15},{8,0},{9,1},... | collective-permute-start | bytes 786440 | tf_op jit(solution)/shard_map/ppermute | solution.py:56
  404.9 6.4 %collective-permute-start.32 = (bf16[64,2048]{1,0:T(8,128)(2,1)S(1)}, bf16[64,2048]{1,0:T(8,128)(2,1)S(1)}, u32[]{:S(2)}, u32[]{:S(2)}) collective-permute-start(bf16[64,2048]{1,0:T(8,128)(2,1)S(1)} %fusion.34), channel_id=1, source_target_pairs={{0,1},{1,0},{2,3},{3,2},{4,5},{5,4},{6,7},{7,6},{8,9},{9,8},{10,11... | collective-permute-start | bytes 786440 | tf_op jit(solution)/shard_map/ppermute | solution.py:31
  405.3 11.9 %collective-permute-start.35 = (bf16[4,144,384]{2,1,0:T(8,128)(2,1)S(1)}, bf16[4,144,384]{2,1,0:T(8,128)(2,1)S(1)}, u32[]{:S(2)}, u32[]{:S(2)}) collective-permute-start(bf16[4,144,384]{2,1,0:T(8,128)(2,1)S(1)} %slice.445), channel_id=1, source_target_pairs={{0,4},{2,6},{4,0},{6,2},{8,12},{10,14},{12,8},{14,10},{16,20},{18,... | collective-permute-start | bytes 1327112 | tf_op jit(solution)/shard_map/ppermute | solution.py:46
  417.4 7.8 %collective-permute-start.36 = (bf16[144,384]{1,0:T(8,128)(2,1)S(1)}, bf16[144,384]{1,0:T(8,128)(2,1)S(1)}, u32[]{:S(2)}, u32[]{:S(2)}) collective-permute-start(bf16[144,384]{1,0:T(8,128)(2,1)S(1)} %get-tuple-element.119), channel_id=1, source_target_pairs={{0,8},{2,10},{4,12},{6,14},{8,16},{10,18},{12,20},{14,22},{16,24},... | collective-permute-start | bytes 331784 | tf_op jit(solution)/shard_map/ppermute | solution.py:41
  417.4 13.6 %collective-permute-start.37 = (bf16[144,384]{1,0:T(8,128)(2,1)S(1)}, bf16[144,384]{1,0:T(8,128)(2,1)S(1)}, u32[]{:S(2)}, u32[]{:S(2)}) collective-permute-start(bf16[144,384]{1,0:T(8,128)(2,1)S(1)} %get-tuple-element.121), channel_id=1, source_target_pairs={{0,16},{2,18},{4,20},{6,22},{8,24},{10,26},{12,28},{14,30},{16,0},... | collective-permute-start | bytes 331784 | tf_op jit(solution)/shard_map/ppermute | solution.py:41
  417.7 13.3 %collective-permute-start.38 = (bf16[144,384]{1,0:T(8,128)(2,1)S(1)}, bf16[144,384]{1,0:T(8,128)(2,1)S(1)}, u32[]{:S(2)}, u32[]{:S(2)}) collective-permute-start(bf16[144,384]{1,0:T(8,128)(2,1)S(1)} %get-tuple-element.120), channel_id=1, source_target_pairs={{0,24},{2,26},{4,28},{6,30},{8,0},{10,2},{12,4},{14,6},{16,8},{18,... | collective-permute-start | bytes 331784 | tf_op jit(solution)/shard_map/ppermute | solution.py:41
  434.3 30.8 %all-to-all-start.1 = ((bf16[8,128,960]{1,2,0:T(8,128)(2,1)}), bf16[8,128,960]{1,2,0:T(8,128)(2,1)S(1)}, u32[]{:S(2)}, u32[]{:S(2)}) async-start(bf16[8,128,960]{1,2,0:T(8,128)(2,1)} %copy_bitcast_fusion.1), calls=%async_computation.3 | async-start | bytes 3932160 | tf_op jit(solution)/shard_map/all_to_all | solution.py:164
  440.8 5.3 %collective-permute-start.39 = (bf16[128,384]{1,0:T(8,128)(2,1)S(1)}, bf16[128,384]{1,0:T(8,128)(2,1)S(1)}, u32[]{:S(2)}, u32[]{:S(2)}) collective-permute-start(bf16[128,384]{1,0:T(8,128)(2,1)S(1)} %slice.611), channel_id=1, source_target_pairs={{0,1},{1,0},{2,3},{3,2},{4,5},{5,4},{6,7},{7,6},{8,9},{9,8},{10,11... | collective-permute-start | bytes 294920 | tf_op jit(solution)/shard_map/ppermute | solution.py:31
  449.1 16.0 %copy-start.17 = (f32[640,128]{0,1:T(8,128)}, f32[640,128]{0,1:T(8,128)S(1)}, u32[]{:S(2)}) copy-start(f32[640,128]{0,1:T(8,128)S(1)} %constant_dynamic-update-slice_fusion.37) | copy-start | bytes 983044
  467.1 6.8 %collective-permute-start.40 = (f32[264]{0:T(512)S(1)}, f32[264]{0:T(512)S(1)}, u32[]{:S(2)}, u32[]{:S(2)}) collective-permute-start(f32[264]{0:T(512)S(1)} %pad_maximum_fusion.16), channel_id=1, source_target_pairs={{0,1},{1,0},{2,3},{3,2},{4,5},{5,4},{6,7},{7,6},{8,9},{9,8},{10,11... | collective-permute-start | bytes 3176 | tf_op jit(solution)/shard_map/ppermute | solution.py:31
  (20 other events, 129.9 us)
Sparse Core Ops, SparseCore 0:
  16.4 69.6 all-gather.1
  242.5 102.0 reduce-scatter.4
  348.9 86.1 reduce-scatter.2

commit v3 on v2

--- a/solution.py
+++ b/solution.py
@@ -87,15 +87,12 @@
     return jnp.concatenate([same, swap_core(same)], axis=0)
 
 
-def distances():
+def distances(far):
     rows, row = lax.axis_size("row"), lax.axis_index("row")
-    order = [((row ^ near) + 4 * k) % rows for near in (0, 2, 1, 3) for k in range(rows // 4)]
-    inverse = []
-    for r in range(rows):
-        step = r ^ row
-        place = (step & 1) * 2 + (step >> 1 & 1)
-        inverse.append(place * (rows // 4) + (r // 4 - row // 4) % (rows // 4))
-    return jnp.stack(order), jnp.stack(inverse)
+    order = [
+        ((row ^ near) + 4 * k) % rows if far else (row ^ near) % 4 + 4 * k for near in (0, 2, 1, 3) for k in range(rows // 4)
+    ]
+    return jnp.stack(order)
 
 
 def reorder_kernel(order_ref, in_ref, out_ref):
@@ -145,9 +142,20 @@
     return jnp.concatenate([block, swap_core(block)], axis=0)
 
 
-def halve_cube(total, number):
-    count = total.shape[0] // 2
-    return total[:count].astype(F32) + swap_cube(total[count:].astype(BF16), number).astype(F32)
+def halve(total, axis, number):
+    here, away = (lax.index_in_dim(total, i, axis, keepdims=False) for i in range(2))
+    return here.astype(F32) + swap_cube(away.astype(BF16), number).astype(F32)
+
+
+def far_groups():
+    rows = lax.axis_size("row")
+    return [list(range(near, rows, 4)) for near in range(4)]
+
+
+def pick(array, place, axis):
+    first = lax.index_in_dim(array, 0, axis, keepdims=False)
+    second = lax.index_in_dim(array, 1, axis, keepdims=False)
+    return jnp.where(place == 0, first, second), jnp.where(place == 0, second, first)
 
 
 def group_rows():
@@ -230,6 +238,42 @@
         cost_estimate=pl.CostEstimate(flops=2 * tok * width * cols, bytes_accessed=2 * width * cols, transcendentals=0),
         name="project_heads",
     )(act, w_all, gain, flag, cosine, sine)
+
+
+def pack_kernel(col_ref, q_ref, kv_ref, o_ref, out_ref):
+    first = col_ref[0] == 0
+    pairs = q_ref.shape[1] // LANES
+    half = kv_ref.shape[1] // 2
+    heads = half // HALF
+
+    def head(number, offset):
+        one = kv_ref[:, offset + number * HALF : offset + (number + 1) * HALF]
+        two = kv_ref[:, offset + (heads - 1 - number) * HALF : offset + (heads - number) * HALF]
+        return jnp.where(first, one, two)
+
+    for pair in range(pairs):
+        here = slice(pair * LANES, (pair + 1) * LANES)
+        there = slice((pairs - 1 - pair) * LANES, (pairs - pair) * LANES)
+        out_ref[:, here] = jnp.where(first, q_ref[:, here], q_ref[:, there])
+        turned = jnp.where(first, o_ref[here, :].astype(F32), o_ref[there, :].astype(F32)).T
+        at = q_ref.shape[1] + 6 * HALF + pair * LANES
+        out_ref[:, at : at + LANES] = turned.astype(BF16)
+    at = q_ref.shape[1]
+    for one, two in ((head(0, 0), head(1, 0)), (head(2, 0), head(2, half)), (head(0, half), head(1, half))):
+        out_ref[:, at : at + LANES] = jnp.concatenate([one, two], axis=1)
+        at += LANES
+
+
+def pack_call(col, w_query, w_kv, w_out):
+    lines, width = w_query.shape
+    return pl.pallas_call(
+        pack_kernel,
+        in_specs=[pl.BlockSpec(memory_space=pltpu.SMEM)] + [pl.BlockSpec(memory_space=pltpu.VMEM)] * 3,
+        out_specs=pl.BlockSpec(memory_space=pltpu.VMEM),
+        out_shape=jax.ShapeDtypeStruct((lines, 2 * width + 6 * HALF), BF16),
+        cost_estimate=pl.CostEstimate(flops=0, bytes_accessed=10 * w_query.size, transcendentals=0),
+        name="pack_weights",
+    )(col.reshape(1), w_query, w_kv, w_out)
 
 
 GROUPS = ((0, 4), (4, 4), (8, 2))
@@ -483,21 +527,13 @@
     span = seq_len // tok
     half = tok // 2
 
-    def kv_pick(order):
-        k = [key_value_weight[:, h * HALF : (h + 1) * HALF] for h in order]
-        v = [key_value_weight[:, kv_half + h * HALF : kv_half + (h + 1) * HALF] for h in order]
-        return jnp.concatenate([k[0], k[1], k[2], v[2], v[0], v[1]], axis=1)
-
-    w_kv = jnp.where(col == 0, kv_pick((0, 1, 2)), kv_pick((4, 3, 2)))
-    w_q = jnp.where(col == 0, w_query, backwards(w_query, 1, LANES))
-    w_o = jnp.where(col == 0, w_out, backwards(w_out, 0, LANES))
-    w_all = lax.all_gather(jnp.concatenate([w_q, w_kv, w_o.T], axis=1), "row", axis=0, tiled=True)
-    kv_width = w_kv.shape[1]
-    head_cols = q_width + kv_width
+    w_packed = pack_call(col, w_query, key_value_weight, w_out)
+    head_cols = w_packed.shape[1] - q_width
+    w_all = lax.all_gather(w_packed, "row", axis=0, tiled=True)
     w_o_all = w_all[:, head_cols:]
     og_low = lax.dynamic_slice_in_dim(out_grad, col * half, half, 0)
     og_all = gather_cube_slowly(og_low)
-    order, inverse_order = distances()
+    order, near_order = distances(True), distances(False)
     group = og_all.shape[0]
 
     w_ff = jnp.concatenate(
@@ -564,17 +600,28 @@
     w_gate_up = w_ff_all[:, : 2 * ff]
     away = dot(d_gate_up[group // 2 :], w_gate_up, ((1,), (1,))).astype(BF16)
     here = dot(d_gate_up[: group // 2], w_gate_up, ((1,), (1,)))
+    total = (here + swap_core(away).astype(F32)).astype(BF16).reshape(2, 2, 2, half, width)
+
+    left, right = total[..., : width // 2], total[..., width // 2 :]
+    left = halve(left, 0, 1)
+    right = halve(right, 1, cols)
     grads_ff = jnp.concatenate(
         [dot(ffn_all, d_gate_up, ((0,), (0,))), dot(og_all, inner_low, ((0,), (0,)))], axis=1
     ).astype(BF16)
-    total = (here + swap_core(away).astype(F32)).astype(BF16).reshape(-1, half, width)
-    total, grads_ff = lax.optimization_barrier((total, grads_ff))
+    left, right, grads_low = lax.optimization_barrier((left, right, grads_ff))
     grads_ff = lax.psum_scatter(
-        grads_ff, "row", scatter_dimension=0, tiled=True, axis_index_groups=across_groups()
+        grads_low, "row", scatter_dimension=0, tiled=True, axis_index_groups=across_groups()
     )
-    for number in (1, cols, 2 * cols):
-        total = halve_cube(total, number)
-    ffn_back = total[0]
+    left = halve(left, 0, cols)
+    right = halve(right, 1, 2 * cols)
+    w_down_all = w_ff_all[:, 2 * ff :]
+    inner_low = after(inner_low, grads_low)
+    away = dot(inner_low[group // 2 :], w_down_all, ((1,), (1,))).astype(BF16)
+    here = dot(inner_low[: group // 2], w_down_all, ((1,), (1,)))
+    ffn_out = over_core(here, away).reshape(2, 2, 2, half, width)
+    left = halve(left, 0, 2 * cols)
+    right = halve(right, 0, 1)
+    ffn_back = jnp.concatenate([left, right], axis=1)
     d_hidden = og_low.astype(F32) + norm_back(hidden, ffn_scale, ffn_gain, ffn_back)
     d_hidden_half = d_hidden.astype(BF16)
     d_hidden_low = halves(d_hidden_half, swap_col(d_hidden_half), col)
@@ -585,44 +632,49 @@
     )
     d_kv_total = over_core(same_d, other_d).reshape(-1, tok, same_d.shape[3])
 
-    inner_low = after(inner_low, d_hidden_low)
-    w_down_all = w_ff_all[:, 2 * ff :]
-    away = dot(inner_low[group // 2 :], w_down_all, ((1,), (1,))).astype(BF16)
-    here = dot(inner_low[: group // 2], w_down_all, ((1,), (1,)))
-    ffn_out = over_core(here, away).reshape(-1, half, width)
-    ffn_out = halve_cube(ffn_out, 1)
-
-    grad_oq = jnp.concatenate(
-        [dot(d_hidden_low, attn_low, ((0,), (0,))), dot(act_low, d_q, ((0,), (0,)))], axis=1
-    ).astype(BF16)
-    grad_oq = lax.psum_scatter(grad_oq, "row", scatter_dimension=0, tiled=True).astype(F32)
+    ffn_out = halve(after(ffn_out, d_hidden_low), 0, 1)
 
     def partial_grad(left, right):
         return dot(left, right, ((0,), (0,))).reshape(rows, w_rows, -1)
 
+    def over_core_only(left, right):
+        partial = partial_grad(left, right)
+        return over_core(partial[: rows // 2], partial[rows // 2 :])
+
+    grad_o = over_near(over_core_only(reorder_columns(d_hidden_low, near_order), attn_low))
+    act_near, d_q_late = after_all((reorder_columns(act_low, near_order), d_q), d_kv_total)
+    grad_q = over_core_only(act_near, d_q_late)
     d_kv_total = over_near(d_kv_total)
+    grad_q = over_near(after(grad_q, d_kv_total))
     kv_parts = over_far(d_kv_total, span, False, False)
+    *kv_parts, ffn_out = lax.optimization_barrier((*kv_parts, ffn_out))
+    grad_oq = jnp.concatenate([grad_o, grad_q], axis=2)
+    grad_oq = lax.psum_scatter(
+        grad_oq, "row", scatter_dimension=0, tiled=True, axis_index_groups=far_groups()
+    )[0].astype(F32)
+    grad_o, grad_q = grad_oq[:, :q_width].T, grad_oq[:, q_width:]
     d_kv, k_gain_part = kv_back_call(kv_parts, kv_raw, kv_gain, kv_flag, cosine, sine)
-    ffn_out = after(ffn_out, d_kv)
-    for number in (cols, 2 * cols):
-        ffn_out = halve_cube(ffn_out, number)
-    out_half = (hidden + ffn_out[0]).astype(BF16)
-    output = halves(out_half, swap_col(out_half), col)
-
     d_one = jnp.concatenate([d_q, d_kv], axis=1)
-    act_back = dot(d_one, w_all[:, :head_cols], ((1,), (1,))).astype(BF16)
-    act_back = act_back.astype(F32) + swap_col(act_back).astype(F32)
-    input_grad = d_hidden_low.astype(F32) + norm_back(input_f, act_scale, attn_gain, act_back)
-
-    grad_o, grad_q = grad_oq[:, :q_width].T, grad_oq[:, q_width:]
+
     per_row = HALF // rows
     fold = lambda part: (part[0, :HALF] + part[0, HALF:]).reshape(rows, 1, per_row)
     small = jnp.concatenate([fold(q_gain_part), fold(k_gain_part)], axis=2)
     small = jnp.take(small, order, axis=0)
     small = jnp.pad(small, ((0, 0), (0, 15), (0, d_kv.shape[1] - 2 * per_row)))
     kv_partial = jnp.concatenate([partial_grad(act_blocks, d_kv), small], axis=1)
-    kv_partial = over_near(over_core(kv_partial[: rows // 2], kv_partial[rows // 2 :]))
+    kv_partial = over_core(kv_partial[: rows // 2], kv_partial[rows // 2 :])
+    d_one = after(d_one, kv_partial)
+    kv_partial = over_near(kv_partial)
+    grads_ff = exchange_group(after(grads_ff, kv_partial).reshape(MEMBERS, w_rows, 3 * ff))
+    for number in (cols, 2 * cols):
+        ffn_out = halve(ffn_out, 0, number)
+    out_half = (hidden + ffn_out).astype(BF16)
+    output = halves(out_half, swap_col(out_half), col)
     grad_kv = add_up(over_far(kv_partial, rows, True, True))
+    grad_kv, grads_ff = lax.optimization_barrier((grad_kv, grads_ff))
+    act_back = dot(d_one, w_all[:, :head_cols], ((1,), (1,))).astype(BF16)
+    act_back = act_back.astype(F32) + swap_col(act_back).astype(F32)
+    input_grad = d_hidden_low.astype(F32) + norm_back(input_f, act_scale, attn_gain, act_back)
     grad_kv, small = grad_kv[:w_rows], grad_kv[w_rows, : 2 * per_row]
     grad_query = jnp.where(col == 0, grad_q, backwards(grad_q, 1, LANES))
     grad_out = jnp.where(col == 0, grad_o, backwards(grad_o, 0, LANES))
@@ -642,13 +694,14 @@
         pieces += [one_head(kv_last, at[1]), one_head(kv_last, at[0])]
     grad_keyval = jnp.concatenate(pieces, axis=1)
 
-    grads_ff = exchange_group(grads_ff.reshape(MEMBERS, w_rows, 3 * ff))
     grads_ff = grads_ff.astype(F32).transpose(1, 0, 2)
     grad_gate = grads_ff[:, :, :ff].reshape(w_rows, ff_cols)
     grad_up = grads_ff[:, :, ff : 2 * ff].reshape(w_rows, ff_cols)
     grad_down = grads_ff[:, :, 2 * ff :].reshape(w_rows, ff_cols).T
 
-    attn_part_gain = jnp.sum(jnp.concatenate([grad_q * w_q.astype(F32), grad_kv * w_kv.astype(F32)], axis=1), axis=1)
+    attn_part_gain = jnp.sum(
+        jnp.concatenate([grad_q, grad_kv], axis=1) * w_packed[:, :head_cols].astype(F32), axis=1
+    )
     ffn_part_gain = jnp.sum(grad_gate * w_gate.astype(F32) + grad_up * w_up.astype(F32), axis=1)
     gains = jnp.concatenate([attn_part_gain, ffn_part_gain, small])
     gains = gains + swap_col(gains)

time: 490 us -> 469 us (0.957)
  waiting for transfers between devices: 233 us -> 185 us
  local copies, waits for them, and re-layouts: 47 us -> 57.8 us
  starting transfers between devices: 78.2 us -> 85.8 us
  other arithmetic: 36.7 us -> 42.9 us
  Pallas kernels: 20.2 us -> 26.3 us
    ppermute x16 -> x19, waiting for transfers between devices: 152 us -> 121 us  [swap_cube(): return lax.ppermute(block, ('row', 'col'), route)]
    ppermute x9, waiting for transfers between devices: 25.5 us -> 6.71 us  [shift_far(): return lax.ppermute(block, 'row', route)]
    ppermute x16 -> x19, starting transfers between devices: 32.2 us -> 43.8 us  [swap_cube(): return lax.ppermute(block, ('row', 'col'), route)]
    unnamed x110 -> x132, local copies, waits for them, and re-layouts: 22.3 us -> 28.8 us
    ppermute x3 -> x5, waiting for transfers between devices: 12.5 us -> 17.7 us  [swap_near(): return lax.ppermute(block, 'row', [(i, i ^ 2) for i in range(rows)])]
  transfers between devices with their start and end apart: 46 -> 53, of which waited for: 28 -> 28; matrix products, arithmetic and copies ran while one was open for 20% -> 25% of each run, Pallas kernels for 3% -> 4%
where the time goes in v3:
time: 469 us; the launch traced here: 461 us
  waiting for transfers between devices  185 us (39%)
  starting transfers between devices  85.8 us (18%)
  local copies, waits for them, and re-layouts  57.8 us (12%)
  matrix products  45.1 us (10%)
  other arithmetic  42.9 us (9%)
  Pallas kernels  26.3 us (6%)
  between operations  18 us (4%)
    ppermute x19, waiting for transfers between devices, swap_cube(): return lax.ppermute(block, ('row', 'col'), route)  121 us
    dot_general x14, matrix products, dot(): return lax.dot_general(a, b, (dims, ((), ())), preferred_element_type=F32)  45.1 us
    ppermute x19, starting transfers between devices, swap_cube(): return lax.ppermute(block, ('row', 'col'), route)  43.8 us
    unnamed x132, local copies, waits for them, and re-layouts  28.8 us
    ppermute x5, waiting for transfers between devices, swap_near(): return lax.ppermute(block, 'row', [(i, i ^ 2) for i in range(rows)])  17.7 us
    ppermute x9, starting transfers between devices, shift_far(): return lax.ppermute(block, 'row', route)  15.6 us
    all_to_all x1, waiting for transfers between devices, exchange_group(): lax.all_to_all(blocks, 'row', split_axis=0, concat_axis=0, tiled=True, ax...  14.4 us
    ppermute x6, waiting for transfers between devices, swap_col(): return lax.ppermute(block, 'col', [(0, 1), (1, 0)])  13.6 us
  transfers between devices with their start and end apart: 53, of which 28 were waited for; matrix products, arithmetic and copies ran while one was open for 25% of the time, Pallas kernels for 4%

profile of v3, /device:TPU:0, one launch (start us, length us, event | category | flops | bytes accessed | tf_op | source)
XLA Modules:
  0.0 460.8 jit_solution(16892284676604109291)
XLA Ops:
  7.3 2.1 pack_weights.1
  11.2 3.0 collective-permute-start
  14.2 6.3 %collective-permute-done = bf16[64,2048]{1,0:T(8,128)(2,1)S(1)} collective-permute-done((bf16[64,2048]{1,0:T(8,128)(2,1)S(1)}, bf16[64,2048]{1,0:T(8,128)(2,1)S(1)}, u32[]{:S(2)}, u32[]{:S(2)}) %collective-permute-start) | collective-permute-done | bytes 262176 | tf_op jit(solution)/shard_map/ppermute | solution.py:56
  22.3 16.0 %collective-permute-done.1 = bf16[128,2048]{1,0:T(8,128)(2,1)S(1)} collective-permute-done((bf16[128,2048]{1,0:T(8,128)(2,1)S(1)}, bf16[128,2048]{1,0:T(8,128)(2,1)S(1)}, u32[]{:S(2)}, u32[]{:S(2)}) %collective-permute-start.1) | collective-permute-done | bytes 524320 | tf_op jit(solution)/shard_map/ppermute | solution.py:56
  41.6 22.0 %collective-permute-done.2 = bf16[256,2048]{1,0:T(8,128)(2,1)} collective-permute-done((bf16[256,2048]{1,0:T(8,128)(2,1)}, bf16[256,2048]{1,0:T(8,128)(2,1)}, u32[]{:S(2)}, u32[]{:S(2)}) %collective-permute-start.2) | collective-permute-done | bytes 1048608 | tf_op jit(solution)/shard_map/ppermute | solution.py:56
  69.7 2.3 constant_dynamic-update-slice_fusion.1
  73.5 7.3 %all-gather.2.cloned.1.call-done.w_ref = bf16[2048,1664]{1,0:T(8,128)(2,1)} async-done(((bf16[128,1664]{1,0:T(8,128)(2,1)}), bf16[2048,1664]{1,0:T(8,128)(2,1)}) %all-gather.2.cloned.1.call-update) | async-done | bytes 6815760 | tf_op jit(solution)/shard_map/all_gather | solution.py:532
  80.8 5.1 %project_heads.1 = (f32[128,1024]{1,0:T(8,128)}, bf16[128,1024]{1,0:T(8,128)(2,1)}) custom-call(bf16[128,2048]{1,0:T(8,128)(2,1)} %multiply_convert_fusion.3.act_ref.in_ref, bf16[2048,1664]{1,0:T(8,128)(2,1)} %all-gather.2.cloned.1.call-done.w_ref, f32[1,1024]{1,0:T(1,128)} %pad_maximum_fusion.15.gain_ref, f32[1,1024]{1,0:T(1,128)} %constant.211.clone.1.flag_ref, ...), custom_call_target="tpu_custom_call" | custom-call | flops 536870912 | bytes 4194304 | tf_op jit(solution)/shard_map/project_heads/pallas_call | solution.py:231
  86.8 3.3 collective-permute-start.4
  90.1 2.9 collective-permute-start.5
  98.1 2.2 pad_maximum_fusion
  100.3 7.8 %all-to-all-start = ((bf16[16,128,960]{1,2,0:T(8,128)(2,1)}), bf16[16,128,960]{1,2,0:T(8,128)(2,1)}, u32[]{:S(2)}, u32[]{:S(2)}) async-start(bf16[16,128,960]{1,2,0:T(8,128)(2,1)} %pad_maximum_fusion), calls=%async_computation | async-start | bytes 7864320 | tf_op jit(solution)/shard_map/all_to_all | solution.py:548
  114.3 4.0 attention_forward.1
  118.3 2.8 convolution_convert_fusion.4
  122.8 6.8 %collective-permute-done.9 = bf16[64,2048]{1,0:T(8,128)(2,1)S(1)} collective-permute-done((bf16[64,2048]{1,0:T(8,128)(2,1)S(1)}, bf16[64,2048]{1,0:T(8,128)(2,1)S(1)}, u32[]{:S(2)}, u32[]{:S(2)}) %collective-permute-start.9) | collective-permute-done | bytes 262176 | tf_op jit(solution)/shard_map/ppermute | solution.py:31
  129.9 3.9 collective-permute-start.10
  137.6 1.9 collective-permute-start.14
  139.5 38.9 %collective-permute-done.10 = bf16[64,2048]{1,0:T(8,128)(2,1)S(1)} collective-permute-done((bf16[64,2048]{1,0:T(8,128)(2,1)S(1)}, bf16[64,2048]{1,0:T(8,128)(2,1)S(1)}, u32[]{:S(2)}, u32[]{:S(2)}) %collective-permute-start.10) | collective-permute-done | bytes 262176 | tf_op jit(solution)/shard_map/ppermute | solution.py:56
  178.3 3.9 collective-permute-start.15
  183.0 1.9 collective-permute-start.16
  188.5 4.2 collective-permute-done.14
  193.4 4.9 %collective-permute-done.15 = bf16[64,2048]{1,0:T(8,128)(2,1)S(1)} collective-permute-done((bf16[64,2048]{1,0:T(8,128)(2,1)S(1)}, bf16[64,2048]{1,0:T(8,128)(2,1)S(1)}, u32[]{:S(2)}, u32[]{:S(2)}) %collective-permute-start.15) | collective-permute-done | bytes 262176 | tf_op jit(solution)/shard_map/ppermute | solution.py:56
  199.8 4.2 collective-permute-done.17
  205.4 2.7 copy_bitcast_fusion
  208.0 6.1 %fusion.11 = f32[1024,640]{0,1:T(8,128)S(1)} fusion(bf16[1024,2048]{1,0:T(8,128)(2,1)} %constant_dynamic-update-slice_fusion.13, bf16[2048,960]{0,1:T(8,128)(2,1)S(1)} %copy_bitcast_fusion), kind=kOutput, calls=%fused_computation.29 | convolution fusion | flops 2684354560 | bytes 9437184 | tf_op jit(solution)/shard_map/dot_general | solution.py:22
  214.2 4.2 multiply_convert_fusion.1
  220.5 3.7 convolution_convert_fusion.3
  224.2 5.8 %convolution_convert_fusion = bf16[2048,640]{0,1:T(8,128)(2,1)S(1)} fusion(bf16[1024,2048]{1,0:T(8,128)(2,1)} %constant_dynamic-update-slice_fusion.13, bf16[1024,320]{0,1:T(8,128)(2,1)S(1)} %get-tuple-element.133, bf16[1024,320]{0,1:T(8,128)(2,1)S(1)} %get-tuple-element.134), kind=kOutput, calls=%fused_computation.11 | convolution fusion | flops 2688286720 | bytes 8126464 | tf_op jit(solution)/shard_map/dot_general | solution.py:22
  230.1 1.9 add_convert_fusion.1
  236.0 2.9 collective-permute-start.20
  238.9 2.5 pad_maximum_fusion.1
  241.4 5.9 %collective-permute-done.19 = bf16[2,2,64,1024]{3,2,1,0:T(8,128)(2,1)} collective-permute-done((bf16[2,2,64,1024]{3,2,1,0:T(8,128)(2,1)}, bf16[2,2,64,1024]{3,2,1,0:T(8,128)(2,1)}, u32[]{:S(2)}, u32[]{:S(2)}) %collective-permute-start.19) | collective-permute-done | bytes 524320 | tf_op jit(solution)/shard_map/ppermute | solution.py:56
  248.5 2.9 collective-permute-done.20
  254.7 7.6 %collective-permute-start.23 = (bf16[2,64,1024]{2,1,0:T(8,128)(2,1)S(1)}, bf16[2,64,1024]{2,1,0:T(8,128)(2,1)S(1)}, u32[]{:S(2)}, u32[]{:S(2)}) collective-permute-start(bf16[2,64,1024]{2,1,0:T(8,128)(2,1)S(1)} %fusion.40), channel_id=1, source_target_pairs={{0,8},{1,9},{2,10},{3,11},{4,12},{5,13},{6,14},{7,15},{8,0},{9,1},... | collective-permute-start | bytes 786440 | tf_op jit(solution)/shard_map/ppermute | solution.py:56
  262.3 6.0 %collective-permute-start.22 = (bf16[64,1024]{1,0:T(8,128)(2,1)S(1)}, bf16[64,1024]{1,0:T(8,128)(2,1)S(1)}, u32[]{:S(2)}, u32[]{:S(2)}) collective-permute-start(bf16[64,1024]{1,0:T(8,128)(2,1)S(1)} %fusion.46), channel_id=1, source_target_pairs={{0,8},{1,9},{2,10},{3,11},{4,12},{5,13},{6,14},{7,15},{8,0},{9,1},... | collective-permute-start | bytes 393224 | tf_op jit(solution)/shard_map/ppermute | solution.py:56
  269.2 2.1 collective-permute-done.22
  271.3 2.2 collective-permute-done.24
  277.1 3.2 collective-permute-done.25
  280.3 3.1 fusion.17.grad_ref
  283.5 6.7 %attention_backward.1 = (bf16[128,640]{1,0:T(8,128)(2,1)}, f32[1,128]{1,0:T(1,128)}, bf16[2,4,128,384]{3,2,1,0:T(8,128)(2,1)}, bf16[2,4,128,384]{3,2,1,0:T(8,128)(2,1)}) custom-call(s32[2]{0:T(128)} %pad_add_fusion.1.bounds_ref, s32[2,128]{1,0:T(2,128)} %pad_add_fusion.limits_ref, bf16[128,640]{1,0:T(8,128)(2,1)} %slice.308.q_ref, ...), custom_call_target="tpu_custom_call" | custom-call | flops 1677721600 | bytes 3145728 | tf_op jit(solution)/shard_map/attention_backward/pallas_call | solution.py:426
  290.2 4.0 convolution_convert_fusion.1
  295.5 2.0 reorder_columns.4
  297.5 1.9 fusion.63
  301.1 1.9 add_convert_fusion.4
  304.7 2.0 reorder_columns.5
  308.8 2.4 copy-done.1
  311.3 3.0 collective-permute-done.27
  318.6 3.5 add_convert_fusion
  327.0 2.0 reorder_columns.3
  336.6 2.1 add_convert_fusion.6
  338.6 8.7 %collective-permute-done.41 = bf16[4,128,640]{2,1,0:T(8,128)(2,1)} collective-permute-done((bf16[4,128,640]{2,1,0:T(8,128)(2,1)}, bf16[4,128,640]{2,1,0:T(8,128)(2,1)}, u32[]{:S(2)}, u32[]{:S(2)}) %collective-permute-start.41) | collective-permute-done | bytes 655392 | tf_op jit(solution)/shard_map/ppermute | solution.py:46
  347.4 2.1 add_convert_fusion.5
  351.0 2.7 collective-permute-done.29.refs_2_
  354.5 2.4 key_value_heads_back.1
  364.5 6.4 %collective-permute-done.33 = bf16[2,64,2048]{2,1,0:T(8,128)(2,1)} collective-permute-done((bf16[2,64,2048]{2,1,0:T(8,128)(2,1)}, bf16[2,64,2048]{2,1,0:T(8,128)(2,1)}, u32[]{:S(2)}, u32[]{:S(2)}) %collective-permute-start.33) | collective-permute-done | bytes 524320 | tf_op jit(solution)/shard_map/ppermute | solution.py:56
  375.6 8.1 %collective-permute-done.34 = bf16[64,2048]{1,0:T(8,128)(2,1)} collective-permute-done((bf16[64,2048]{1,0:T(8,128)(2,1)S(1)}, bf16[64,2048]{1,0:T(8,128)(2,1)}, u32[]{:S(2)}, u32[]{:S(2)}) %collective-permute-start.34) | collective-permute-done | bytes 262176 | tf_op jit(solution)/shard_map/ppermute | solution.py:56
  386.2 2.1 fusion.15
  389.9 3.7 fusion.2
  395.0 5.3 %collective-permute-done.42 = bf16[4,144,384]{2,1,0:T(8,128)(2,1)S(1)} collective-permute-done((bf16[4,144,384]{2,1,0:T(8,128)(2,1)S(1)}, bf16[4,144,384]{2,1,0:T(8,128)(2,1)S(1)}, u32[]{:S(2)}, u32[]{:S(2)}) %collective-permute-start.42) | collective-permute-done | bytes 442400 | tf_op jit(solution)/shard_map/ppermute | solution.py:46
  401.1 3.8 collective-permute-start.45
  407.2 3.2 copy_bitcast_fusion.1
  410.4 3.7 all-to-all-start.1
  414.2 2.7 subtract_add_fusion
  424.2 14.4 %all-to-all-done.1 = bf16[8,128,960]{1,2,0:T(8,128)(2,1)S(1)} async-done(((bf16[8,128,960]{1,2,0:T(8,128)(2,1)}), bf16[8,128,960]{1,2,0:T(8,128)(2,1)S(1)}, u32[]{:S(2)}, u32[]{:S(2)}) %all-to-all-start.1) | async-done | bytes 1966112 | tf_op jit(solution)/shard_map/all_to_all | solution.py:172
  (329 shorter events, 122.0 us)
Async XLA Ops:
  7.2 73.6 %all-gather.2.cloned.1.call-start = ((), (), s32[]{:S(2)}) async-start(), calls=%async_computation.4 | async-start | bytes 7241728 | tf_op jit(solution)/shard_map/all_gather | solution.py:532
  7.2 33.5 %copy-start.45 = (s32[128]{0:T(128)S(1)}, s32[128]{0:T(128)}, u32[]{:S(2)}) copy-start(s32[128]{0:T(128)} %param.26) | copy-start | bytes 1540
  7.2 33.5 %copy-start.46 = (f32[64]{0:T(128)S(1)}, f32[64]{0:T(128)}, u32[]{:S(2)}) copy-start(f32[64]{0:T(128)} %param.24) | copy-start | bytes 772
  7.3 33.5 %copy-start.44 = (pred[3,128]{1,0:T(4,128)(4,1)S(1)}, pred[3,128]{1,0:T(4,128)(4,1)}, u32[]{:S(2)}) copy-start(pred[3,128]{1,0:T(4,128)(4,1)} %constant.209.clone.1) | copy-start | bytes 1156
  7.3 33.5 %copy-start.47 = (f32[64]{0:T(128)S(1)}, f32[64]{0:T(128)}, u32[]{:S(2)}) copy-start(f32[64]{0:T(128)} %param.23) | copy-start | bytes 772
  7.3 33.7 %copy-start.27 = (bf16[128,2560]{1,0:T(8,128)(2,1)S(1)}, bf16[128,2560]{1,0:T(8,128)(2,1)}, u32[]{:S(2)}) copy-start(bf16[128,2560]{1,0:T(8,128)(2,1)} %param.18) | copy-start | bytes 1966084
  9.4 31.9 %copy-start.28 = (bf16[128,2560]{1,0:T(8,128)(2,1)S(1)}, bf16[128,2560]{1,0:T(8,128)(2,1)}, u32[]{:S(2)}) copy-start(bf16[128,2560]{1,0:T(8,128)(2,1)} %param.19) | copy-start | bytes 1966084
  11.2 9.3 %collective-permute-start = (bf16[64,2048]{1,0:T(8,128)(2,1)S(1)}, bf16[64,2048]{1,0:T(8,128)(2,1)S(1)}, u32[]{:S(2)}, u32[]{:S(2)}) collective-permute-start(bf16[64,2048]{1,0:T(8,128)(2,1)S(1)} %get-tuple-element.127), channel_id=1, source_target_pairs={{0,8},{1,9},{2,10},{3,11},{4,12},{5,13},{6,14},{7,15},{8,0},{9,1},... | collective-permute-start | bytes 786440 | tf_op jit(solution)/shard_map/ppermute | solution.py:56
  20.6 17.7 %collective-permute-start.1 = (bf16[128,2048]{1,0:T(8,128)(2,1)S(1)}, bf16[128,2048]{1,0:T(8,128)(2,1)S(1)}, u32[]{:S(2)}, u32[]{:S(2)}) collective-permute-start(bf16[128,2048]{1,0:T(8,128)(2,1)S(1)} %pad_maximum_fusion.8), channel_id=1, source_target_pairs={{0,4},{1,5},{2,6},{3,7},{4,0},{5,1},{6,2},{7,3},{8,12},{9,13},{10,... | collective-permute-start | bytes 1572872 | tf_op jit(solution)/shard_map/ppermute | solution.py:56
  39.4 24.3 %collective-permute-start.2 = (bf16[256,2048]{1,0:T(8,128)(2,1)}, bf16[256,2048]{1,0:T(8,128)(2,1)}, u32[]{:S(2)}, u32[]{:S(2)}) collective-permute-start(bf16[256,2048]{1,0:T(8,128)(2,1)} %pad_maximum_fusion.6), channel_id=1, source_target_pairs={{0,1},{1,0},{2,3},{3,2},{4,5},{5,4},{6,7},{7,6},{8,9},{9,8},{10,11... | collective-permute-start | bytes 3145736 | tf_op jit(solution)/shard_map/ppermute | solution.py:56
  41.3 53.1 %copy-start.4 = (bf16[128,2560]{0,1:T(8,128)(2,1)}, bf16[128,2560]{0,1:T(8,128)(2,1)S(1)}, u32[]{:S(2)}) copy-start(bf16[128,2560]{0,1:T(8,128)(2,1)S(1)} %copy.68) | copy-start | bytes 1966084
  41.6 52.7 %copy-start.6 = (bf16[128,2560]{0,1:T(8,128)(2,1)}, bf16[128,2560]{0,1:T(8,128)(2,1)S(1)}, u32[]{:S(2)}) copy-start(bf16[128,2560]{0,1:T(8,128)(2,1)S(1)} %copy.69) | copy-start | bytes 1966084
  41.6 25.3 %copy-start.2 = (bf16[128,2048]{1,0:T(8,128)(2,1)S(1)}, bf16[128,2048]{1,0:T(8,128)(2,1)}, u32[]{:S(2)}) copy-start(bf16[128,2048]{1,0:T(8,128)(2,1)} %param.14) | copy-start | bytes 1572868
  41.6 25.5 %copy-start.39 = (f32[2048]{0:T(1024)S(1)}, f32[2048]{0:T(1024)}, u32[]{:S(2)}) copy-start(f32[2048]{0:T(1024)} %param.21) | copy-start | bytes 24580
  65.1 6.9 %collective-permute-start.3 = (bf16[512,2048]{1,0:T(8,128)(2,1)S(1)}, bf16[512,2048]{1,0:T(8,128)(2,1)S(1)}, u32[]{:S(2)}, u32[]{:S(2)}) collective-permute-start(bf16[512,2048]{1,0:T(8,128)(2,1)S(1)} %pad_maximum_fusion.2), channel_id=1, source_target_pairs={{0,2},{2,0},{4,6},{6,4},{8,10},{10,8},{12,14},{14,12},{16,18},{18,... | collective-permute-start | bytes 6291464 | tf_op jit(solution)/shard_map/ppermute | solution.py:27
  86.8 7.7 %collective-permute-start.4 = (bf16[128,384]{1,0:T(8,128)(2,1)S(1)}, bf16[128,384]{1,0:T(8,128)(2,1)S(1)}, u32[]{:S(2)}, u32[]{:S(2)}) collective-permute-start(bf16[128,384]{1,0:T(8,128)(2,1)S(1)} %get-tuple-element.171), channel_id=1, source_target_pairs={{0,8},{2,10},{4,12},{6,14},{8,16},{10,18},{12,20},{14,22},{16,24},... | collective-permute-start | bytes 294920 | tf_op jit(solution)/shard_map/ppermute | solution.py:41
  90.1 6.0 %collective-permute-start.5 = (bf16[128,384]{1,0:T(8,128)(2,1)S(1)}, bf16[128,384]{1,0:T(8,128)(2,1)S(1)}, u32[]{:S(2)}, u32[]{:S(2)}) collective-permute-start(bf16[128,384]{1,0:T(8,128)(2,1)S(1)} %get-tuple-element.171), channel_id=1, source_target_pairs={{0,16},{2,18},{4,20},{6,22},{8,24},{10,26},{12,28},{14,30},{1,17},... | collective-permute-start | bytes 294920 | tf_op jit(solution)/shard_map/ppermute | solution.py:41
  93.0 4.3 collective-permute-start.6
  97.4 10.7 %collective-permute-start.7 = (bf16[4,128,384]{2,1,0:T(8,128)(2,1)S(1)}, bf16[4,128,384]{2,1,0:T(8,128)(2,1)S(1)}, u32[]{:S(2)}, u32[]{:S(2)}) collective-permute-start(bf16[4,128,384]{2,1,0:T(8,128)(2,1)S(1)} %get-tuple-element.155), channel_id=1, source_target_pairs={{0,4},{2,6},{4,0},{6,2},{8,12},{10,14},{12,8},{14,10},{16,20},{18,... | collective-permute-start | bytes 1179656 | tf_op jit(solution)/shard_map/ppermute | solution.py:46
  100.3 105.0 %all-to-all-start = ((bf16[16,128,960]{1,2,0:T(8,128)(2,1)}), bf16[16,128,960]{1,2,0:T(8,128)(2,1)}, u32[]{:S(2)}, u32[]{:S(2)}) async-start(bf16[16,128,960]{1,2,0:T(8,128)(2,1)} %pad_maximum_fusion), calls=%async_computation | async-start | bytes 7864320 | tf_op jit(solution)/shard_map/all_to_all | solution.py:548
  108.1 299.1 %reduce-scatter.5.cloned.1.call-start = ((), (), s32[]{:S(2)}) async-start(), calls=%async_computation.6 | async-start | bytes 5898240 | tf_op jit(solution)/shard_map/reduce_scatter | solution.py:612
  108.3 6.0 %collective-permute-start.8 = (bf16[2,4,128,384]{3,2,1,0:T(8,128)(2,1)S(1)}, bf16[2,4,128,384]{3,2,1,0:T(8,128)(2,1)}, u32[]{:S(2)}, u32[]{:S(2)}) collective-permute-start(bf16[2,4,128,384]{3,2,1,0:T(8,128)(2,1)S(1)} %pad_maximum_fusion.7.same_ref), channel_id=1, source_target_pairs={{0,2},{2,0},{4,6},{6,4},{8,10},{10,8},{12,14},{14,12},{16,18},{18,... | collective-permute-start | bytes 2359304 | tf_op jit(solution)/shard_map/ppermute | solution.py:27
  121.2 8.4 %collective-permute-start.9 = (bf16[64,2048]{1,0:T(8,128)(2,1)S(1)}, bf16[64,2048]{1,0:T(8,128)(2,1)S(1)}, u32[]{:S(2)}, u32[]{:S(2)}) collective-permute-start(bf16[64,2048]{1,0:T(8,128)(2,1)S(1)} %constant_dynamic-slice_fusion), channel_id=1, source_target_pairs={{0,1},{1,0},{2,3},{3,2},{4,5},{5,4},{6,7},{7,6},{8,9},{9,8},{10,11... | collective-permute-start | bytes 786440 | tf_op jit(solution)/shard_map/ppermute | solution.py:31
  129.9 48.4 %collective-permute-start.10 = (bf16[64,2048]{1,0:T(8,128)(2,1)S(1)}, bf16[64,2048]{1,0:T(8,128)(2,1)S(1)}, u32[]{:S(2)}, u32[]{:S(2)}) collective-permute-start(bf16[64,2048]{1,0:T(8,128)(2,1)S(1)} %get-tuple-element.123), channel_id=1, source_target_pairs={{0,8},{1,9},{2,10},{3,11},{4,12},{5,13},{6,14},{7,15},{8,0},{9,1},... | collective-permute-start | bytes 786440 | tf_op jit(solution)/shard_map/ppermute | solution.py:56
  133.8 49.2 %collective-permute-start.11 = (bf16[64,2048]{1,0:T(8,128)(2,1)S(1)}, bf16[64,2048]{1,0:T(8,128)(2,1)S(1)}, u32[]{:S(2)}, u32[]{:S(2)}) collective-permute-start(bf16[64,2048]{1,0:T(8,128)(2,1)S(1)} %get-tuple-element.123), channel_id=1, source_target_pairs={{0,4},{1,5},{2,6},{3,7},{4,0},{5,1},{6,2},{7,3},{8,12},{9,13},{10,... | collective-permute-start | bytes 786440 | tf_op jit(solution)/shard_map/ppermute | solution.py:56
  135.7 51.3 %collective-permute-start.12 = (bf16[64,2048]{1,0:T(8,128)(2,1)S(1)}, bf16[64,2048]{1,0:T(8,128)(2,1)S(1)}, u32[]{:S(2)}, u32[]{:S(2)}) collective-permute-start(bf16[64,2048]{1,0:T(8,128)(2,1)S(1)} %get-tuple-element.123), channel_id=1, source_target_pairs={{0,12},{1,13},{2,14},{3,15},{4,8},{5,9},{6,10},{7,11},{8,4},{9,5},... | collective-permute-start | bytes 786440 | tf_op jit(solution)/shard_map/ppermute | solution.py:56
  136.1 51.6 %collective-permute-start.13 = (bf16[64,2048]{1,0:T(8,128)(2,1)S(1)}, bf16[64,2048]{1,0:T(8,128)(2,1)S(1)}, u32[]{:S(2)}, u32[]{:S(2)}) collective-permute-start(bf16[64,2048]{1,0:T(8,128)(2,1)S(1)} %get-tuple-element.123), channel_id=1, source_target_pairs={{0,1},{1,0},{2,3},{3,2},{4,5},{5,4},{6,7},{7,6},{8,9},{9,8},{10,11... | collective-permute-start | bytes 786440 | tf_op jit(solution)/shard_map/ppermute | solution.py:56
  137.6 55.1 %collective-permute-start.14 = (bf16[64,2048]{1,0:T(8,128)(2,1)S(1)}, bf16[64,2048]{1,0:T(8,128)(2,1)S(1)}, u32[]{:S(2)}, u32[]{:S(2)}) collective-permute-start(bf16[64,2048]{1,0:T(8,128)(2,1)S(1)} %get-tuple-element.123), channel_id=1, source_target_pairs={{0,9},{1,8},{2,11},{3,10},{4,13},{5,12},{6,15},{7,14},{8,1},{9,0},... | collective-permute-start | bytes 786440 | tf_op jit(solution)/shard_map/ppermute | solution.py:56
  178.3 19.9 %collective-permute-start.15 = (bf16[64,2048]{1,0:T(8,128)(2,1)S(1)}, bf16[64,2048]{1,0:T(8,128)(2,1)S(1)}, u32[]{:S(2)}, u32[]{:S(2)}) collective-permute-start(bf16[64,2048]{1,0:T(8,128)(2,1)S(1)} %get-tuple-element.123), channel_id=1, source_target_pairs={{0,5},{1,4},{2,7},{3,6},{4,1},{5,0},{6,3},{7,2},{8,13},{9,12},{10,... | collective-permute-start | bytes 786440 | tf_op jit(solution)/shard_map/ppermute | solution.py:56
  183.0 16.0 %collective-permute-start.16 = (bf16[64,2048]{1,0:T(8,128)(2,1)S(1)}, bf16[64,2048]{1,0:T(8,128)(2,1)S(1)}, u32[]{:S(2)}, u32[]{:S(2)}) collective-permute-start(bf16[64,2048]{1,0:T(8,128)(2,1)S(1)} %get-tuple-element.123), channel_id=1, source_target_pairs={{0,13},{1,12},{2,15},{3,14},{4,9},{5,8},{6,11},{7,10},{8,5},{9,4},... | collective-permute-start | bytes 786440 | tf_op jit(solution)/shard_map/ppermute | solution.py:56
  199.8 4.2 collective-permute-start.17
  220.3 9.7 %collective-permute-start.18 = (bf16[512,2048]{1,0:T(8,128)(2,1)S(1)}, bf16[512,2048]{1,0:T(8,128)(2,1)S(1)}, u32[]{:S(2)}, u32[]{:S(2)}) collective-permute-start(bf16[512,2048]{1,0:T(8,128)(2,1)S(1)} %convolution_convert_fusion.2), channel_id=1, source_target_pairs={{0,2},{2,0},{4,6},{6,4},{8,10},{10,8},{12,14},{14,12},{16,18},{18,... | collective-permute-start | bytes 6291464 | tf_op jit(solution)/shard_map/ppermute | solution.py:27
  232.8 14.5 %collective-permute-start.19 = (bf16[2,2,64,1024]{3,2,1,0:T(8,128)(2,1)}, bf16[2,2,64,1024]{3,2,1,0:T(8,128)(2,1)}, u32[]{:S(2)}, u32[]{:S(2)}) collective-permute-start(bf16[2,2,64,1024]{3,2,1,0:T(8,128)(2,1)} %slice_bitcast_fusion.2), channel_id=1, source_target_pairs={{0,1},{1,0},{2,3},{3,2},{4,5},{5,4},{6,7},{7,6},{8,9},{9,8},{10,11... | collective-permute-start | bytes 1572872 | tf_op jit(solution)/shard_map/ppermute | solution.py:56
  236.0 15.3 %collective-permute-start.20 = (bf16[2,2,64,1024]{3,2,0,1:T(8,128)(2,1)}, bf16[2,2,64,1024]{3,2,0,1:T(8,128)(2,1)}, u32[]{:S(2)}, u32[]{:S(2)}) collective-permute-start(bf16[2,2,64,1024]{3,2,0,1:T(8,128)(2,1)} %bitcast.210), channel_id=1, source_target_pairs={{0,4},{1,5},{2,6},{3,7},{4,0},{5,1},{6,2},{7,3},{8,12},{9,13},{10,... | collective-permute-start | bytes 1572872 | tf_op jit(solution)/shard_map/ppermute | solution.py:56
  252.8 9.4 %collective-permute-start.21 = (bf16[2,64,1024]{2,1,0:T(8,128)(2,1)S(1)}, bf16[2,64,1024]{2,1,0:T(8,128)(2,1)S(1)}, u32[]{:S(2)}, u32[]{:S(2)}) collective-permute-start(bf16[2,64,1024]{2,1,0:T(8,128)(2,1)S(1)} %fusion.39), channel_id=1, source_target_pairs={{0,4},{1,5},{2,6},{3,7},{4,0},{5,1},{6,2},{7,3},{8,12},{9,13},{10,... | collective-permute-start | bytes 786440 | tf_op jit(solution)/shard_map/ppermute | solution.py:56
  254.7 13.6 %collective-permute-start.23 = (bf16[2,64,1024]{2,1,0:T(8,128)(2,1)S(1)}, bf16[2,64,1024]{2,1,0:T(8,128)(2,1)S(1)}, u32[]{:S(2)}, u32[]{:S(2)}) collective-permute-start(bf16[2,64,1024]{2,1,0:T(8,128)(2,1)S(1)} %fusion.40), channel_id=1, source_target_pairs={{0,8},{1,9},{2,10},{3,11},{4,12},{5,13},{6,14},{7,15},{8,0},{9,1},... | collective-permute-start | bytes 786440 | tf_op jit(solution)/shard_map/ppermute | solution.py:56
  262.3 8.9 %collective-permute-start.22 = (bf16[64,1024]{1,0:T(8,128)(2,1)S(1)}, bf16[64,1024]{1,0:T(8,128)(2,1)S(1)}, u32[]{:S(2)}, u32[]{:S(2)}) collective-permute-start(bf16[64,1024]{1,0:T(8,128)(2,1)S(1)} %fusion.46), channel_id=1, source_target_pairs={{0,8},{1,9},{2,10},{3,11},{4,12},{5,13},{6,14},{7,15},{8,0},{9,1},... | collective-permute-start | bytes 393224 | tf_op jit(solution)/shard_map/ppermute | solution.py:56
  268.4 5.0 %collective-permute-start.24 = (bf16[64,1024]{1,0:T(8,128)(2,1)S(1)}, bf16[64,1024]{1,0:T(8,128)(2,1)S(1)}, u32[]{:S(2)}, u32[]{:S(2)}) collective-permute-start(bf16[64,1024]{1,0:T(8,128)(2,1)S(1)} %fusion.47), channel_id=1, source_target_pairs={{0,1},{1,0},{2,3},{3,2},{4,5},{5,4},{6,7},{7,6},{8,9},{9,8},{10,11... | collective-permute-start | bytes 393224 | tf_op jit(solution)/shard_map/ppermute | solution.py:56
  273.8 6.4 %collective-permute-start.25 = (bf16[64,2048]{1,0:T(8,128)(2,1)S(1)}, bf16[64,2048]{1,0:T(8,128)(2,1)S(1)}, u32[]{:S(2)}, u32[]{:S(2)}) collective-permute-start(bf16[64,2048]{1,0:T(8,128)(2,1)S(1)} %add_convert_fusion.8), channel_id=1, source_target_pairs={{0,1},{1,0},{2,3},{3,2},{4,5},{5,4},{6,7},{7,6},{8,9},{9,8},{10,11... | collective-permute-start | bytes 786440 | tf_op jit(solution)/shard_map/ppermute | solution.py:31
  275.3 29.4 %copy-start.43 = (s32[16]{0:T(128)}, s32[16]{0:T(128)S(1)}, u32[]{:S(2)}) copy-start(s32[16]{0:T(128)S(1)} %stack.202.order_ref) | copy-start | bytes 196
  276.9 142.2 %reduce-scatter.3.cloned.1.call-start = ((), (), s32[]{:S(2)}) async-start(), calls=%async_computation.5 | async-start | bytes 1638400 | tf_op jit(solution)/shard_map/reduce_scatter | solution.py:652
  290.1 10.5 %collective-permute-start.26 = (bf16[2,4,128,384]{3,2,1,0:T(8,128)(2,1)}, bf16[2,4,128,384]{3,2,1,0:T(8,128)(2,1)}, u32[]{:S(2)}, u32[]{:S(2)}) collective-permute-start(bf16[2,4,128,384]{3,2,1,0:T(8,128)(2,1)} %get-tuple-element.54), channel_id=1, source_target_pairs={{0,2},{2,0},{4,6},{6,4},{8,10},{10,8},{12,14},{14,12},{16,18},{18,... | collective-permute-start | bytes 2359304 | tf_op jit(solution)/shard_map/ppermute | solution.py:27
  294.2 24.4 %collective-permute-start.31 = (bf16[512,2048]{1,0:T(8,128)(2,1)}, bf16[512,2048]{1,0:T(8,128)(2,1)}, u32[]{:S(2)}, u32[]{:S(2)}) collective-permute-start(bf16[512,2048]{1,0:T(8,128)(2,1)} %convolution_convert_fusion.1), channel_id=1, source_target_pairs={{0,2},{2,0},{4,6},{6,4},{8,10},{10,8},{12,14},{14,12},{16,18},{18,... | collective-permute-start | bytes 6291464 | tf_op jit(solution)/shard_map/ppermute | solution.py:27
  300.7 13.7 %collective-permute-start.38 = (bf16[8,128,640]{2,1,0:T(8,128)(2,1)}, bf16[8,128,640]{2,1,0:T(8,128)(2,1)}, u32[]{:S(2)}, u32[]{:S(2)}) collective-permute-start(bf16[8,128,640]{2,1,0:T(8,128)(2,1)} %bitcast.93), channel_id=1, source_target_pairs={{0,2},{2,0},{4,6},{6,4},{8,10},{10,8},{12,14},{14,12},{16,18},{18,... | collective-permute-start | bytes 3932168 | tf_op jit(solution)/shard_map/ppermute | solution.py:27
  303.1 11.1 %collective-permute-start.27 = (bf16[4,128,384]{2,1,0:T(8,128)(2,1)S(1)}, bf16[4,128,384]{2,1,0:T(8,128)(2,1)S(1)}, u32[]{:S(2)}, u32[]{:S(2)}) collective-permute-start(bf16[4,128,384]{2,1,0:T(8,128)(2,1)S(1)} %slice_bitcast_fusion.4), channel_id=1, source_target_pairs={{0,4},{2,6},{4,0},{6,2},{8,12},{10,14},{12,8},{14,10},{16,20},{18,... | collective-permute-start | bytes 1179656 | tf_op jit(solution)/shard_map/ppermute | solution.py:46
  311.3 12.9 %collective-permute-start.40 = (bf16[8,128,640]{2,1,0:T(8,128)(2,1)S(1)}, bf16[8,128,640]{2,1,0:T(8,128)(2,1)S(1)}, u32[]{:S(2)}, u32[]{:S(2)}) collective-permute-start(bf16[8,128,640]{2,1,0:T(8,128)(2,1)S(1)} %bitcast.225), channel_id=1, source_target_pairs={{0,2},{2,0},{4,6},{6,4},{8,10},{10,8},{12,14},{14,12},{16,18},{18,... | collective-permute-start | bytes 3932168 | tf_op jit(solution)/shard_map/ppermute | solution.py:27
  317.0 18.0 %collective-permute-start.39 = (bf16[4,128,640]{2,1,0:T(8,128)(2,1)}, bf16[4,128,640]{2,1,0:T(8,128)(2,1)}, u32[]{:S(2)}, u32[]{:S(2)}) collective-permute-start(bf16[4,128,640]{2,1,0:T(8,128)(2,1)} %slice.437), channel_id=1, source_target_pairs={{0,4},{2,6},{4,0},{6,2},{8,12},{10,14},{12,8},{14,10},{16,20},{18,... | collective-permute-start | bytes 1966088 | tf_op jit(solution)/shard_map/ppermute | solution.py:46
  323.2 26.3 %collective-permute-start.32 = (bf16[2,2,64,2048]{3,2,1,0:T(8,128)(2,1)}, bf16[2,2,64,2048]{3,2,1,0:T(8,128)(2,1)}, u32[]{:S(2)}, u32[]{:S(2)}) collective-permute-start(bf16[2,2,64,2048]{3,2,1,0:T(8,128)(2,1)} %slice_bitcast_fusion), channel_id=1, source_target_pairs={{0,1},{1,0},{2,3},{3,2},{4,5},{5,4},{6,7},{7,6},{8,9},{9,8},{10,11... | collective-permute-start | bytes 3145736 | tf_op jit(solution)/shard_map/ppermute | solution.py:56
  326.4 21.0 %collective-permute-start.41 = (bf16[4,128,640]{2,1,0:T(8,128)(2,1)}, bf16[4,128,640]{2,1,0:T(8,128)(2,1)}, u32[]{:S(2)}, u32[]{:S(2)}) collective-permute-start(bf16[4,128,640]{2,1,0:T(8,128)(2,1)} %slice.362), channel_id=1, source_target_pairs={{0,4},{2,6},{4,0},{6,2},{8,12},{10,14},{12,8},{14,10},{16,20},{18,... | collective-permute-start | bytes 1966088 | tf_op jit(solution)/shard_map/ppermute | solution.py:46
  331.5 19.5 %collective-permute-start.28 = (bf16[128,384]{1,0:T(8,128)(2,1)S(1)}, bf16[128,384]{1,0:T(8,128)(2,1)S(1)}, u32[]{:S(2)}, u32[]{:S(2)}) collective-permute-start(bf16[128,384]{1,0:T(8,128)(2,1)S(1)} %get-tuple-element.152), channel_id=1, source_target_pairs={{8,0},{10,2},{12,4},{14,6},{16,8},{18,10},{20,12},{22,14},{24,16},... | collective-permute-start | bytes 294920 | tf_op jit(solution)/shard_map/ppermute | solution.py:41
  332.9 20.9 %collective-permute-start.29 = (bf16[128,384]{1,0:T(8,128)(2,1)S(1)}, bf16[128,384]{1,0:T(8,128)(2,1)S(1)}, u32[]{:S(2)}, u32[]{:S(2)}) collective-permute-start(bf16[128,384]{1,0:T(8,128)(2,1)S(1)} %get-tuple-element.151), channel_id=1, source_target_pairs={{16,0},{18,2},{20,4},{22,6},{24,8},{26,10},{28,12},{30,14},{17,1},... | collective-permute-start | bytes 294920 | tf_op jit(solution)/shard_map/ppermute | solution.py:41
  335.0 18.8 %collective-permute-start.30 = (bf16[128,384]{1,0:T(8,128)(2,1)S(1)}, bf16[128,384]{1,0:T(8,128)(2,1)S(1)}, u32[]{:S(2)}, u32[]{:S(2)}) collective-permute-start(bf16[128,384]{1,0:T(8,128)(2,1)S(1)} %get-tuple-element.150), channel_id=1, source_target_pairs={{24,0},{26,2},{28,4},{30,6},{25,1},{27,3},{29,5},{31,7}} | collective-permute-start | bytes 294920 | tf_op jit(solution)/shard_map/ppermute | solution.py:41
  358.7 12.2 %collective-permute-start.33 = (bf16[2,64,2048]{2,1,0:T(8,128)(2,1)}, bf16[2,64,2048]{2,1,0:T(8,128)(2,1)}, u32[]{:S(2)}, u32[]{:S(2)}) collective-permute-start(bf16[2,64,2048]{2,1,0:T(8,128)(2,1)} %fusion.32), channel_id=1, source_target_pairs={{0,4},{1,5},{2,6},{3,7},{4,0},{5,1},{6,2},{7,3},{8,12},{9,13},{10,... | collective-permute-start | bytes 1572872 | tf_op jit(solution)/shard_map/ppermute | solution.py:56
  364.5 21.7 %collective-permute-start.36 = (bf16[8,144,384]{2,1,0:T(8,128)(2,1)}, bf16[8,144,384]{2,1,0:T(8,128)(2,1)}, u32[]{:S(2)}, u32[]{:S(2)}) collective-permute-start(bf16[8,144,384]{2,1,0:T(8,128)(2,1)} %slice.619), channel_id=1, source_target_pairs={{0,2},{2,0},{4,6},{6,4},{8,10},{10,8},{12,14},{14,12},{16,18},{18,... | collective-permute-start | bytes 2654216 | tf_op jit(solution)/shard_map/ppermute | solution.py:27
  373.1 10.6 %collective-permute-start.34 = (bf16[64,2048]{1,0:T(8,128)(2,1)S(1)}, bf16[64,2048]{1,0:T(8,128)(2,1)}, u32[]{:S(2)}, u32[]{:S(2)}) collective-permute-start(bf16[64,2048]{1,0:T(8,128)(2,1)S(1)} %fusion.41), channel_id=1, source_target_pairs={{0,8},{1,9},{2,10},{3,11},{4,12},{5,13},{6,14},{7,15},{8,0},{9,1},... | collective-permute-start | bytes 786440 | tf_op jit(solution)/shard_map/ppermute | solution.py:56
  384.7 9.4 %collective-permute-start.35 = (bf16[64,2048]{1,0:T(8,128)(2,1)S(1)}, bf16[64,2048]{1,0:T(8,128)(2,1)S(1)}, u32[]{:S(2)}, u32[]{:S(2)}) collective-permute-start(bf16[64,2048]{1,0:T(8,128)(2,1)S(1)} %fusion.35), channel_id=1, source_target_pairs={{0,1},{1,0},{2,3},{3,2},{4,5},{5,4},{6,7},{7,6},{8,9},{9,8},{10,11... | collective-permute-start | bytes 786440 | tf_op jit(solution)/shard_map/ppermute | solution.py:31
  388.4 11.8 %collective-permute-start.42 = (bf16[4,144,384]{2,1,0:T(8,128)(2,1)S(1)}, bf16[4,144,384]{2,1,0:T(8,128)(2,1)S(1)}, u32[]{:S(2)}, u32[]{:S(2)}) collective-permute-start(bf16[4,144,384]{2,1,0:T(8,128)(2,1)S(1)} %slice.447), channel_id=1, source_target_pairs={{0,4},{2,6},{4,0},{6,2},{8,12},{10,14},{12,8},{14,10},{16,20},{18,... | collective-permute-start | bytes 1327112 | tf_op jit(solution)/shard_map/ppermute | solution.py:46
  393.7 13.2 %collective-permute-start.37 = (bf16[128,2048]{1,0:T(8,128)(2,1)S(1)}, bf16[128,2048]{1,0:T(8,128)(2,1)S(1)}, u32[]{:S(2)}, u32[]{:S(2)}) collective-permute-start(bf16[128,2048]{1,0:T(8,128)(2,1)S(1)} %fusion.2), channel_id=1, source_target_pairs={{0,1},{1,0},{2,3},{3,2},{4,5},{5,4},{6,7},{7,6},{8,9},{9,8},{10,11... | collective-permute-start | bytes 1572872 | tf_op jit(solution)/shard_map/ppermute | solution.py:31
  401.1 15.8 %collective-permute-start.43 = (bf16[144,384]{1,0:T(8,128)(2,1)}, bf16[144,384]{1,0:T(8,128)(2,1)S(1)}, u32[]{:S(2)}, u32[]{:S(2)}) collective-permute-start(bf16[144,384]{1,0:T(8,128)(2,1)} %get-tuple-element.145), channel_id=1, source_target_pairs={{0,8},{2,10},{4,12},{6,14},{8,16},{10,18},{12,20},{14,22},{16,24},... | collective-permute-start | bytes 331784 | tf_op jit(solution)/shard_map/ppermute | solution.py:41
  401.1 16.9 %collective-permute-start.44 = (bf16[144,384]{1,0:T(8,128)(2,1)S(1)}, bf16[144,384]{1,0:T(8,128)(2,1)S(1)}, u32[]{:S(2)}, u32[]{:S(2)}) collective-permute-start(bf16[144,384]{1,0:T(8,128)(2,1)S(1)} %get-tuple-element.147), channel_id=1, source_target_pairs={{0,16},{2,18},{4,20},{6,22},{8,24},{10,26},{12,28},{14,30},{16,0},... | collective-permute-start | bytes 331784 | tf_op jit(solution)/shard_map/ppermute | solution.py:41
  401.1 16.9 %collective-permute-start.45 = (bf16[144,384]{1,0:T(8,128)(2,1)S(1)}, bf16[144,384]{1,0:T(8,128)(2,1)}, u32[]{:S(2)}, u32[]{:S(2)}) collective-permute-start(bf16[144,384]{1,0:T(8,128)(2,1)S(1)} %get-tuple-element.146), channel_id=1, source_target_pairs={{0,24},{2,26},{4,28},{6,30},{8,0},{10,2},{12,4},{14,6},{16,8},{18,... | collective-permute-start | bytes 331784 | tf_op jit(solution)/shard_map/ppermute | solution.py:41
  410.4 28.1 %all-to-all-start.1 = ((bf16[8,128,960]{1,2,0:T(8,128)(2,1)}), bf16[8,128,960]{1,2,0:T(8,128)(2,1)S(1)}, u32[]{:S(2)}, u32[]{:S(2)}) async-start(bf16[8,128,960]{1,2,0:T(8,128)(2,1)} %copy_bitcast_fusion.1), calls=%async_computation.3 | async-start | bytes 3932160 | tf_op jit(solution)/shard_map/all_to_all | solution.py:172
  441.2 8.6 %collective-permute-start.47 = (f32[264]{0:T(512)S(1)}, f32[264]{0:T(512)S(1)}, u32[]{:S(2)}, u32[]{:S(2)}) collective-permute-start(f32[264]{0:T(512)S(1)} %pad_maximum_fusion.16), channel_id=1, source_target_pairs={{0,1},{1,0},{2,3},{3,2},{4,5},{5,4},{6,7},{7,6},{8,9},{9,8},{10,11... | collective-permute-start | bytes 3176 | tf_op jit(solution)/shard_map/ppermute | solution.py:31
  448.2 4.6 %collective-permute-start.46 = (bf16[128,384]{1,0:T(8,128)(2,1)S(1)}, bf16[128,384]{1,0:T(8,128)(2,1)S(1)}, u32[]{:S(2)}, u32[]{:S(2)}) collective-permute-start(bf16[128,384]{1,0:T(8,128)(2,1)S(1)} %slice.620), channel_id=1, source_target_pairs={{0,1},{1,0},{2,3},{3,2},{4,5},{5,4},{6,7},{7,6},{8,9},{9,8},{10,11... | collective-permute-start | bytes 294920 | tf_op jit(solution)/shard_map/ppermute | solution.py:31
  (43 other events, 284.7 us)
Sparse Core Ops, SparseCore 0:
  10.3 70.4 all-gather.1
  277.0 102.9 reduce-scatter.4
  383.0 35.3 reduce-scatter.2

commit v4 on v3

--- a/solution.py
+++ b/solution.py
@@ -62,6 +62,10 @@
     return same, swap_core(same)
 
 
+def add_low(one, two):
+    return (one.astype(F32) + two.astype(F32)).astype(BF16)
+
+
 def over_core(same, other):
     return (same.astype(F32) + swap_core(other.astype(BF16)).astype(F32)).astype(BF16)
 
@@ -95,29 +99,13 @@
     return jnp.stack(order)
 
 
-def reorder_kernel(order_ref, in_ref, out_ref):
-    for at in range(in_ref.shape[1] // LANES):
-        there = pl.multiple_of(order_ref[at] * LANES, LANES)
-        out_ref[:, at * LANES : (at + 1) * LANES] = in_ref[:, pl.ds(there, LANES)]
-
-
-def reorder_columns(array, order):
-    tok, width = array.shape
-    if width // order.shape[0] != LANES:
-        blocks = array.reshape(tok, order.shape[0], -1)
-        return jnp.take(blocks, order, axis=1).reshape(tok, width)
-    return pl.pallas_call(
-        reorder_kernel,
-        in_specs=[pl.BlockSpec(memory_space=pltpu.SMEM), pl.BlockSpec(memory_space=pltpu.VMEM)],
-        out_specs=pl.BlockSpec(memory_space=pltpu.VMEM),
-        out_shape=jax.ShapeDtypeStruct(array.shape, array.dtype),
-        cost_estimate=pl.CostEstimate(flops=0, bytes_accessed=4 * array.size, transcendentals=0),
-        name="reorder_columns",
-    )(order, array)
-
-
 def after_all(arrays, *others):
     return lax.optimization_barrier(tuple(arrays) + others)[: len(arrays)]
+
+
+def beside(operands, send, inputs, work):
+    operands, inputs = lax.optimization_barrier((operands, inputs))
+    return lax.optimization_barrier((send(*operands), work(*inputs)))
 
 
 def after(array, *others):
@@ -213,16 +201,23 @@
     return jnp.where(on, grad_raw, grad), gain_term
 
 
-def heads_kernel(act_ref, w_ref, gain_ref, flag_ref, cos_ref, sin_ref, raw_ref, out_ref):
+def heads_kernel(act_ref, w_ref, gain_ref, flag_ref, cos_ref, sin_ref, raw_ref, out_ref, kv_ref):
     raw = dot(act_ref[...], w_ref[...])
     raw_ref[...] = raw
-    for part in range(raw.shape[1] // LANES):
+    parts = raw.shape[1] // LANES
+    query_parts = pl.num_programs(0) * parts - kv_ref.shape[1] // LANES
+    for part in range(parts):
         at = slice(part * LANES, (part + 1) * LANES)
-        done = head_forward(raw[:, at], gain_ref[:, at], flag_ref[:, at], cos_ref[...], sin_ref[...])
-        out_ref[:, at] = done.astype(BF16)
-
-
-def heads_call(act, w_all, gain, flag, cosine, sine):
+        done = head_forward(raw[:, at], gain_ref[:, at], flag_ref[:, at], cos_ref[...], sin_ref[...]).astype(BF16)
+        out_ref[:, at] = done
+        place = pl.program_id(0) * parts + part - query_parts
+
+        @pl.when(place >= 0)
+        def keep():
+            kv_ref[:, pl.ds(pl.multiple_of(jnp.maximum(place, 0) * LANES, LANES), LANES)] = done
+
+
+def heads_call(act, w_all, gain, flag, cosine, sine, kv_width):
     tok, width = act.shape
     cols = gain.shape[1]
     block = 256
@@ -232,8 +227,12 @@
         heads_kernel,
         grid=(cols // block,),
         in_specs=[whole((tok, width)), chunk(width), chunk(1), chunk(1), whole((tok, LANES)), whole((tok, LANES))],
-        out_specs=[chunk(tok), chunk(tok)],
-        out_shape=[jax.ShapeDtypeStruct((tok, cols), F32), jax.ShapeDtypeStruct((tok, cols), BF16)],
+        out_specs=[chunk(tok), chunk(tok), whole((tok, kv_width))],
+        out_shape=[
+            jax.ShapeDtypeStruct((tok, cols), F32),
+            jax.ShapeDtypeStruct((tok, cols), BF16),
+            jax.ShapeDtypeStruct((tok, kv_width), BF16),
+        ],
         compiler_params=pltpu.CompilerParams(vmem_limit_bytes=VMEM_LIMIT),
         cost_estimate=pl.CostEstimate(flops=2 * tok * width * cols, bytes_accessed=2 * width * cols, transcendentals=0),
         name="project_heads",
@@ -276,6 +275,107 @@
     )(col.reshape(1), w_query, w_kv, w_out)
 
 
+BESIDE = pl.CostEstimate(flops=0, bytes_accessed=0, transcendentals=0)
+
+
+def turn(block):
+    return block.astype(F32).T.astype(BF16)
+
+
+def rows_kernel(order_ref, left_ref, right_ref, *refs):
+    *more, own_ref, away_ref = refs
+    count = own_ref.shape[0]
+    for at in range(2 * count):
+        to, place = (own_ref, at) if at < count else (away_ref, at - count)
+        row = order_ref[at]
+        block = turn(left_ref[:, pl.ds(pl.multiple_of(row * LANES, LANES), LANES)])
+        to[place, :LANES] = dot(block, right_ref[...]).astype(BF16)
+        if more:
+            to[place, LANES:] = more[0][row]
+
+
+def rows_call(order, left, right, *more):
+    count = order.shape[0] // 2
+    lines = left.shape[1] // (2 * count)
+    if lines != LANES:
+        blocks = jnp.take(left.reshape(left.shape[0], 2 * count, lines), order, axis=1)
+        product = jnp.einsum("trl,tn->rln", blocks, right, preferred_element_type=F32).astype(BF16)
+        if more:
+            product = jnp.concatenate([product, jnp.take(more[0], order, axis=0)], axis=1)
+        return product[:count], product[count:]
+    shape = (count, lines + (more[0].shape[1] if more else 0), right.shape[1])
+    return pl.pallas_call(
+        rows_kernel,
+        in_specs=[pl.BlockSpec(memory_space=pltpu.SMEM)] + [pl.BlockSpec(memory_space=pltpu.VMEM)] * (2 + len(more)),
+        out_specs=[pl.BlockSpec(memory_space=pltpu.VMEM)] * 2,
+        out_shape=[jax.ShapeDtypeStruct(shape, BF16)] * 2,
+        compiler_params=pltpu.CompilerParams(vmem_limit_bytes=VMEM_LIMIT),
+        cost_estimate=BESIDE,
+        name="weight_rows",
+    )(order, left, right, *more)
+
+
+def ff_grads_kernel(ffn_ref, og_ref, d_ref, inner_ref, out_ref, d_turned, inner_turned):
+    @pl.when(pl.program_id(0) == 0)
+    def prepare():
+        d_turned[...] = turn(d_ref[...])
+        inner_turned[...] = turn(inner_ref[...])
+
+    both = d_turned.shape[0]
+    gate_up = dot(d_turned[...], ffn_ref[...]).astype(BF16)
+    down = dot(inner_turned[...], og_ref[...]).astype(BF16)
+    for part in range(out_ref.shape[0]):
+        at = slice(part * LANES, (part + 1) * LANES)
+        out_ref[part, :both] = gate_up[:, at]
+        out_ref[part, both:] = down[:, at]
+
+
+def ff_grads_call(ffn, og, d_gate_up, inner, rows):
+    tokens, width = ffn.shape
+    both, ff = d_gate_up.shape[1], inner.shape[1]
+    lines = width // rows
+    if lines != LANES:
+        products = jnp.concatenate([dot(d_gate_up, ffn, ((0,), (0,))), dot(inner, og, ((0,), (0,)))], axis=0)
+        return products.astype(BF16).reshape(both + ff, rows, lines).transpose(1, 0, 2)
+    parts = 2
+    whole = lambda array: pl.BlockSpec(array.shape, lambda i: (0, 0))
+    column = pl.BlockSpec((tokens, parts * LANES), lambda i: (0, i))
+    return pl.pallas_call(
+        ff_grads_kernel,
+        grid=(rows // parts,),
+        in_specs=[column, column, whole(d_gate_up), whole(inner)],
+        out_specs=pl.BlockSpec((parts, both + ff, LANES), lambda i: (i, 0, 0)),
+        out_shape=jax.ShapeDtypeStruct((rows, both + ff, LANES), BF16),
+        scratch_shapes=[pltpu.VMEM((both, tokens), BF16), pltpu.VMEM((ff, tokens), BF16)],
+        compiler_params=pltpu.CompilerParams(vmem_limit_bytes=VMEM_LIMIT),
+        cost_estimate=BESIDE,
+        name="feed_forward_weight_grads",
+    )(ffn, og, d_gate_up, inner)
+
+
+def ff_format_kernel(in_ref, gate_ref, up_ref, down_ref):
+    members, units, lines = in_ref.shape
+    ff = units // 3
+    for member in range(members):
+        at = slice(member * ff, (member + 1) * ff)
+        gate_ref[:, at] = in_ref[member, :ff].astype(F32).T
+        up_ref[:, at] = in_ref[member, ff : 2 * ff].astype(F32).T
+        down_ref[at] = in_ref[member, 2 * ff :].astype(F32)
+
+
+def ff_format_call(blocks):
+    members, units, lines = blocks.shape
+    cols = members * units // 3
+    return pl.pallas_call(
+        ff_format_kernel,
+        in_specs=[pl.BlockSpec(memory_space=pltpu.VMEM)],
+        out_specs=[pl.BlockSpec(memory_space=pltpu.VMEM)] * 3,
+        out_shape=[jax.ShapeDtypeStruct(shape, F32) for shape in ((lines, cols), (lines, cols), (cols, lines))],
+        compiler_params=pltpu.CompilerParams(vmem_limit_bytes=VMEM_LIMIT),
+        name="feed_forward_grads",
+    )(blocks)
+
+
 GROUPS = ((0, 4), (4, 4), (8, 2))
 K_AT = (0, 64, 128)
 V_AT = (256, 320, 192)
@@ -303,7 +403,7 @@
 
 def forward_kernel(bounds_ref, limits_ref, q_ref, same_ref, other_ref, att_ref, turned_ref, inv_ref, q_turned):
     tok = q_ref.shape[0]
-    turned, tall = stack_heads(q_ref[...], tok)
+    turned, tall = stack_heads(q_ref[:, : att_ref.shape[1]], tok)
     q_turned[...] = turned
     turned_ref[...] = jnp.zeros_like(turned_ref)
     inv_ref[...] = jnp.zeros_like(inv_ref)
@@ -337,8 +437,8 @@
 SMEM = pl.BlockSpec(memory_space=pltpu.SMEM)
 
 
-def forward_call(bounds, limits, q, same, other):
-    tok, width = q.shape
+def forward_call(bounds, limits, q, same, other, width):
+    tok = q.shape[0]
     wide = width // HALF * tok
     work = same.size // same.shape[3] * 2 * wide
     return pl.pallas_call(
@@ -381,7 +481,7 @@
     dq_acc,
 ):
     tok = q_ref.shape[0]
-    q_turned[...], q_tall[...] = stack_heads(q_ref[...], tok)
+    q_turned[...], q_tall[...] = stack_heads(q_ref[:, : dq_ref.shape[1]], tok)
     g_turned[...], g_tall[...] = stack_heads(grad_ref[...], tok)
     dq_acc[...] = jnp.zeros_like(dq_acc)
     same_out[...] = jnp.zeros_like(same_out)
@@ -420,7 +520,7 @@
 
 
 def backward_call(bounds, limits, q, grad, turned, inv, same, other, raw, gain, cosine, sine):
-    tok, width = q.shape
+    tok, width = grad.shape
     wide = width // HALF * tok
     work = same.size // same.shape[3] * 2 * wide
     return pl.pallas_call(
@@ -448,12 +548,13 @@
 
 def kv_back_kernel(raw_ref, gain_ref, flag_ref, cos_ref, sin_ref, *refs):
     *part_refs, out_ref, gain_grad_ref = refs
+    skip = raw_ref.shape[1] - out_ref.shape[1]
     total = jnp.zeros((1, LANES), F32)
     for part in range(out_ref.shape[1] // LANES):
         at = slice(part * LANES, (part + 1) * LANES)
         grad = sum(ref[:, at].astype(F32) for ref in part_refs)
         done, term = head_backward(
-            grad, raw_ref[:, at], gain_ref[:, at], flag_ref[:, at], cos_ref[...], sin_ref[...]
+            grad, raw_ref[:, skip + at.start : skip + at.stop], gain_ref[:, at], flag_ref[:, at], cos_ref[...], sin_ref[...]
         )
         out_ref[:, at] = done.astype(BF16)
         total += term
@@ -461,7 +562,7 @@
 
 
 def kv_back_call(parts, raw, gain, flag, cosine, sine):
-    tok, width = raw.shape
+    tok, width = parts[0].shape
     return pl.pallas_call(
         kv_back_kernel,
         in_specs=vmem(5 + len(parts)),
@@ -557,13 +658,10 @@
     kv_gain = jnp.where(kv_flag > 0, jnp.tile(k_lanes, (1, 3)), 1.0)
     q_flag = jnp.ones((1, q_width), F32)
     q_gain = jnp.tile(q_lanes * SCALE, (1, q_width // LANES))
-    act_blocks = reorder_columns(act_low, order)
     gain = jnp.concatenate([q_gain, kv_gain], axis=1)
     flag = jnp.concatenate([q_flag, kv_flag], axis=1)
     act_low, og_all = lax.optimization_barrier((act_low, og_all))
-    raw, heads = heads_call(act_low, w_all, gain, flag, cosine, sine)
-    query, kv_low = heads[:, :q_width], heads[:, q_width:]
-    q_raw, kv_raw = raw[:, :q_width], raw[:, q_width:]
+    raw, heads, kv_low = heads_call(act_low, w_all, gain, flag, cosine, sine, head_cols - q_width)
     same_kv, other_kv = gather_earlier(kv_low, span)
 
     in_span = row % span
@@ -575,7 +673,7 @@
     start = jnp.where(own_segments < 0, own_index, start)
     limits = jnp.stack([start, own_index])
     bounds = jnp.stack([2 * (in_span // 4 + 1 - jnp.min(start) // (4 * tok)), in_span])
-    attn_low, turned, inv = forward_call(bounds, limits, query, same_kv, other_kv)
+    attn_low, turned, inv = forward_call(bounds, limits, heads, same_kv, other_kv, q_width)
     attn_part = dot(attn_low, w_o_all, ((1,), (1,))).astype(BF16)
 
     def mine(array, which):
@@ -603,48 +701,58 @@
     total = (here + swap_core(away).astype(F32)).astype(BF16).reshape(2, 2, 2, half, width)
 
     left, right = total[..., : width // 2], total[..., width // 2 :]
-    left = halve(left, 0, 1)
-    right = halve(right, 1, cols)
-    grads_ff = jnp.concatenate(
-        [dot(ffn_all, d_gate_up, ((0,), (0,))), dot(og_all, inner_low, ((0,), (0,)))], axis=1
-    ).astype(BF16)
-    left, right, grads_low = lax.optimization_barrier((left, right, grads_ff))
+    (left_away, right_away), grads_ff = beside(
+        (left[1], right[:, 1]),
+        lambda one, two: (swap_cube(one, 1), swap_cube(two, cols)),
+        (ffn_all, og_all, d_gate_up, inner_low),
+        lambda *arrays: ff_grads_call(*arrays, rows),
+    )
+    left, right = add_low(left[0], left_away), add_low(right[:, 0], right_away)
     grads_ff = lax.psum_scatter(
-        grads_low, "row", scatter_dimension=0, tiled=True, axis_index_groups=across_groups()
-    )
-    left = halve(left, 0, cols)
-    right = halve(right, 1, 2 * cols)
-    w_down_all = w_ff_all[:, 2 * ff :]
-    inner_low = after(inner_low, grads_low)
-    away = dot(inner_low[group // 2 :], w_down_all, ((1,), (1,))).astype(BF16)
-    here = dot(inner_low[: group // 2], w_down_all, ((1,), (1,)))
-    ffn_out = over_core(here, away).reshape(2, 2, 2, half, width)
+        grads_ff, "row", scatter_dimension=0, tiled=True, axis_index_groups=across_groups()
+    )
+
+    def down(inner_low):
+        w_down_all = w_ff_all[:, 2 * ff :]
+        away = dot(inner_low[group // 2 :], w_down_all, ((1,), (1,))).astype(BF16)
+        return away, dot(inner_low[: group // 2], w_down_all, ((1,), (1,))).astype(BF16)
+
+    (left_away, right_away), (out_away, out_here) = beside(
+        (left[1], right[:, 1]),
+        lambda one, two: (swap_cube(one, cols), swap_cube(two, 2 * cols)),
+        (inner_low,),
+        down,
+    )
+    left, right = add_low(left[0], left_away), add_low(right[:, 0], right_away)
+    ffn_out = over_core(out_here, out_away).reshape(2, 2, 2, half, width)
     left = halve(left, 0, 2 * cols)
     right = halve(right, 0, 1)
     ffn_back = jnp.concatenate([left, right], axis=1)
+    ffn_gain_part = jnp.sum(ffn_back * hidden * ffn_scale, axis=0)
     d_hidden = og_low.astype(F32) + norm_back(hidden, ffn_scale, ffn_gain, ffn_back)
     d_hidden_half = d_hidden.astype(BF16)
     d_hidden_low = halves(d_hidden_half, swap_col(d_hidden_half), col)
 
     d_attn = dot(d_hidden_low, w_o_all).astype(BF16)
     d_q, q_gain_part, same_d, other_d = backward_call(
-        bounds, limits, query, d_attn, turned, inv, same_kv, other_kv, q_raw, q_lanes, cosine, sine
+        bounds, limits, heads, d_attn, turned, inv, same_kv, other_kv, raw, q_lanes, cosine, sine
     )
     d_kv_total = over_core(same_d, other_d).reshape(-1, tok, same_d.shape[3])
 
     ffn_out = halve(after(ffn_out, d_hidden_low), 0, 1)
 
-    def partial_grad(left, right):
-        return dot(left, right, ((0,), (0,))).reshape(rows, w_rows, -1)
-
-    def over_core_only(left, right):
-        partial = partial_grad(left, right)
-        return over_core(partial[: rows // 2], partial[rows // 2 :])
-
-    grad_o = over_near(over_core_only(reorder_columns(d_hidden_low, near_order), attn_low))
-    act_near, d_q_late = after_all((reorder_columns(act_low, near_order), d_q), d_kv_total)
-    grad_q = over_core_only(act_near, d_q_late)
-    d_kv_total = over_near(d_kv_total)
+    count = d_kv_total.shape[0] // 2
+    (kv_away,), (grad_o, grad_q) = beside(
+        (d_kv_total[count:],),
+        lambda block: (swap_near(block),),
+        (d_hidden_low, act_low, d_q),
+        lambda hid, act, grad: (
+            over_core(*rows_call(near_order, hid, attn_low)),
+            over_core(*rows_call(near_order, act, grad)),
+        ),
+    )
+    d_kv_total = add_low(d_kv_total[:count], kv_away)
+    grad_o = over_near(grad_o)
     grad_q = over_near(after(grad_q, d_kv_total))
     kv_parts = over_far(d_kv_total, span, False, False)
     *kv_parts, ffn_out = lax.optimization_barrier((*kv_parts, ffn_out))
@@ -653,19 +761,22 @@
         grad_oq, "row", scatter_dimension=0, tiled=True, axis_index_groups=far_groups()
     )[0].astype(F32)
     grad_o, grad_q = grad_oq[:, :q_width].T, grad_oq[:, q_width:]
-    d_kv, k_gain_part = kv_back_call(kv_parts, kv_raw, kv_gain, kv_flag, cosine, sine)
+    d_kv, k_gain_part = kv_back_call(kv_parts, raw, kv_gain, kv_flag, cosine, sine)
     d_one = jnp.concatenate([d_q, d_kv], axis=1)
 
     per_row = HALF // rows
     fold = lambda part: (part[0, :HALF] + part[0, HALF:]).reshape(rows, 1, per_row)
-    small = jnp.concatenate([fold(q_gain_part), fold(k_gain_part)], axis=2)
-    small = jnp.take(small, order, axis=0)
-    small = jnp.pad(small, ((0, 0), (0, 15), (0, d_kv.shape[1] - 2 * per_row)))
-    kv_partial = jnp.concatenate([partial_grad(act_blocks, d_kv), small], axis=1)
-    kv_partial = over_core(kv_partial[: rows // 2], kv_partial[rows // 2 :])
+    line = lambda values: jnp.pad(values, ((0, 0), (0, 0), (0, d_kv.shape[1] - values.shape[2])))
+    small = [
+        line(jnp.concatenate([fold(q_gain_part), fold(k_gain_part)], axis=2)),
+        line(ffn_gain_part.reshape(rows, 1, w_rows)),
+        jnp.zeros((rows, 14, d_kv.shape[1]), F32),
+    ]
+    small = jnp.concatenate(small, axis=1).astype(BF16)
+    kv_partial = over_core(*rows_call(order, act_low, d_kv, small))
     d_one = after(d_one, kv_partial)
     kv_partial = over_near(kv_partial)
-    grads_ff = exchange_group(after(grads_ff, kv_partial).reshape(MEMBERS, w_rows, 3 * ff))
+    grads_ff = exchange_group(after(grads_ff, kv_partial))
     for number in (cols, 2 * cols):
         ffn_out = halve(ffn_out, 0, number)
     out_half = (hidden + ffn_out).astype(BF16)
@@ -675,7 +786,7 @@
     act_back = dot(d_one, w_all[:, :head_cols], ((1,), (1,))).astype(BF16)
     act_back = act_back.astype(F32) + swap_col(act_back).astype(F32)
     input_grad = d_hidden_low.astype(F32) + norm_back(input_f, act_scale, attn_gain, act_back)
-    grad_kv, small = grad_kv[:w_rows], grad_kv[w_rows, : 2 * per_row]
+    grad_kv, small = grad_kv[:w_rows], grad_kv[w_rows : w_rows + 2]
     grad_query = jnp.where(col == 0, grad_q, backwards(grad_q, 1, LANES))
     grad_out = jnp.where(col == 0, grad_o, backwards(grad_o, 0, LANES))
 
@@ -694,20 +805,16 @@
         pieces += [one_head(kv_last, at[1]), one_head(kv_last, at[0])]
     grad_keyval = jnp.concatenate(pieces, axis=1)
 
-    grads_ff = grads_ff.astype(F32).transpose(1, 0, 2)
-    grad_gate = grads_ff[:, :, :ff].reshape(w_rows, ff_cols)
-    grad_up = grads_ff[:, :, ff : 2 * ff].reshape(w_rows, ff_cols)
-    grad_down = grads_ff[:, :, 2 * ff :].reshape(w_rows, ff_cols).T
+    grad_gate, grad_up, grad_down = ff_format_call(grads_ff)
 
     attn_part_gain = jnp.sum(
         jnp.concatenate([grad_q, grad_kv], axis=1) * w_packed[:, :head_cols].astype(F32), axis=1
     )
-    ffn_part_gain = jnp.sum(grad_gate * w_gate.astype(F32) + grad_up * w_up.astype(F32), axis=1)
-    gains = jnp.concatenate([attn_part_gain, ffn_part_gain, small])
+    gains = jnp.concatenate([attn_part_gain, small[1, :w_rows], small[0, : 2 * per_row]])
     gains = gains + swap_col(gains)
     own_gains = lambda whole: lax.dynamic_slice_in_dim(whole, row * w_rows, w_rows, 0)
     grad_attn_gain = gains[:w_rows] / own_gains(attn_gain)
-    grad_ffn_gain = gains[w_rows : 2 * w_rows] / own_gains(ffn_gain)
+    grad_ffn_gain = gains[w_rows : 2 * w_rows]
     grad_query_gain = gains[2 * w_rows : 2 * w_rows + per_row]
     grad_key_gain = gains[2 * w_rows + per_row :]
     return (

time: 469 us -> 457 us (0.974); the launches traced: 461 us -> 456 us
  local copies, waits for them, and re-layouts: 57.8 us -> 38.4 us
  Pallas kernels: 26.3 us -> 45.4 us
  waiting for transfers between devices: 185 us -> 200 us
  matrix products: 45.1 us -> 32.4 us
    pallas_call x3 -> x5, Pallas kernels: 5.99 us -> 24.5 us  [the longest x1 11.2 us: ff_grads_call(): pl.pallas_call(ff_grads_kernel, grid=(rows // parts,), in_specs=[column,...]
    dot_general x14 -> x9, matrix products: 45.1 us -> 32.4 us  [dot(): return lax.dot_general(a, b, (dims, ((), ())), preferred_element_type=F32)]
    ppermute x19, waiting for transfers between devices: 121 us -> 130 us  [swap_cube(): return lax.ppermute(block, ('row', 'col'), route)]
    ppermute x9, waiting for transfers between devices: 6.71 us -> 15.7 us  [shift_far(): return lax.ppermute(block, 'row', route)]
    unnamed x132 -> x104, local copies, waits for them, and re-layouts: 28.8 us -> 19.9 us
    slice x14 -> x4, local copies, waits for them, and re-layouts: 7.7 us -> 1.75 us  [the longest x1 0.93 us: body(): right[:, 0]]
    ppermute x5, waiting for transfers between devices: 17.7 us -> 11.9 us  [swap_near(): return lax.ppermute(block, 'row', [(i, i ^ 2) for i in range(rows)])]
  transfers between devices with their start and end apart: 53 -> 53, of which waited for: 28 -> 26; matrix products, arithmetic and copies ran while one was open for 25% -> 18% of each run, Pallas kernels for 4% -> 8%
where the time goes in v4:
time: 457 us; the launch traced here: 456 us
  waiting for transfers between devices  200 us (44%)
  starting transfers between devices  83.4 us (18%)
  Pallas kernels  45.4 us (10%)
  other arithmetic  39 us (9%)
  local copies, waits for them, and re-layouts  38.4 us (8%)
  matrix products  32.4 us (7%)
  between operations  17.3 us (4%)
    ppermute x19, waiting for transfers between devices, swap_cube(): return lax.ppermute(block, ('row', 'col'), route)  130 us
    ppermute x19, starting transfers between devices, swap_cube(): return lax.ppermute(block, ('row', 'col'), route)  43.8 us
    dot_general x9, matrix products, dot(): return lax.dot_general(a, b, (dims, ((), ())), preferred_element_type=F32)  32.4 us
    unnamed x104, local copies, waits for them, and re-layouts  19.9 us
    ppermute x9, waiting for transfers between devices, shift_far(): return lax.ppermute(block, 'row', route)  15.7 us
    ppermute x9, starting transfers between devices, shift_far(): return lax.ppermute(block, 'row', route)  13.8 us
    all_to_all x1, waiting for transfers between devices, exchange_group(): lax.all_to_all(blocks, 'row', split_axis=0, concat_axis=0, tiled=True, ax...  13 us
    ppermute x5, waiting for transfers between devices, swap_near(): return lax.ppermute(block, 'row', [(i, i ^ 2) for i in range(rows)])  11.9 us
  transfers between devices with their start and end apart: 53, of which 26 were waited for; matrix products, arithmetic and copies ran while one was open for 18% of the time, Pallas kernels for 8%

profile of v4, /device:TPU:0, one launch (start us, length us, event | category | flops | bytes accessed | tf_op | source)
XLA Modules:
  0.0 455.6 jit_solution(2251431778201724329)
XLA Ops:
  7.2 2.0 pack_weights.1
  9.3 1.8 constant_dynamic-update-slice_fusion.4
  11.0 3.0 collective-permute-start
  14.1 6.3 %collective-permute-done = bf16[64,2048]{1,0:T(8,128)(2,1)S(1)} collective-permute-done((bf16[64,2048]{1,0:T(8,128)(2,1)S(1)}, bf16[64,2048]{1,0:T(8,128)(2,1)S(1)}, u32[]{:S(2)}, u32[]{:S(2)}) %collective-permute-start) | collective-permute-done | bytes 262176 | tf_op jit(solution)/shard_map/ppermute | solution.py:56
  20.4 1.8 collective-permute-start.1
  22.2 16.0 %collective-permute-done.1 = bf16[128,2048]{1,0:T(8,128)(2,1)S(1)} collective-permute-done((bf16[128,2048]{1,0:T(8,128)(2,1)S(1)}, bf16[128,2048]{1,0:T(8,128)(2,1)S(1)}, u32[]{:S(2)}, u32[]{:S(2)}) %collective-permute-start.1) | collective-permute-done | bytes 524320 | tf_op jit(solution)/shard_map/ppermute | solution.py:56
  42.2 2.2 copy.77
  44.4 18.8 %collective-permute-done.2 = bf16[256,2048]{1,0:T(8,128)(2,1)S(1)} collective-permute-done((bf16[256,2048]{1,0:T(8,128)(2,1)}, bf16[256,2048]{1,0:T(8,128)(2,1)S(1)}, u32[]{:S(2)}, u32[]{:S(2)}) %collective-permute-start.2) | collective-permute-done | bytes 1048608 | tf_op jit(solution)/shard_map/ppermute | solution.py:56
  70.5 10.3 %all-gather.2.cloned.1.call-done.w_ref = bf16[2048,1664]{1,0:T(8,128)(2,1)} async-done(((bf16[128,1664]{1,0:T(8,128)(2,1)}), bf16[2048,1664]{1,0:T(8,128)(2,1)}) %all-gather.2.cloned.1.call-update) | async-done | bytes 6815760 | tf_op jit(solution)/shard_map/all_gather | solution.py:633
  80.9 5.8 %project_heads.1 = (f32[128,1024]{1,0:T(8,128)}, bf16[128,1024]{1,0:T(8,128)(2,1)}, bf16[128,384]{1,0:T(8,128)(2,1)}) custom-call(bf16[128,2048]{1,0:T(8,128)(2,1)} %multiply_convert_fusion.3.act_ref.left_ref, bf16[2048,1664]{1,0:T(8,128)(2,1)} %all-gather.2.cloned.1.call-done.w_ref, f32[1,1024]{1,0:T(1,128)} %pad_maximum_fusion.14.gain_ref, ...), custom_call_target="tpu_custom_call" | custom-call | flops 536870912 | bytes 4194304 | tf_op jit(solution)/shard_map/project_heads/pallas_call | solution.py:226
  86.7 3.9 collective-permute-start.6
  91.8 2.5 collective-permute-start.4
  94.5 1.6 collective-permute-done.5
  98.3 2.2 pad_maximum_fusion
  100.6 7.7 %all-to-all-start = ((bf16[16,128,960]{1,2,0:T(8,128)(2,1)}), bf16[16,128,960]{1,2,0:T(8,128)(2,1)}, u32[]{:S(2)}, u32[]{:S(2)}) async-start(bf16[16,128,960]{1,2,0:T(8,128)(2,1)} %pad_maximum_fusion), calls=%async_computation | async-start | bytes 7864320 | tf_op jit(solution)/shard_map/all_to_all | solution.py:649
  114.6 4.0 attention_forward.1
  118.6 2.8 convolution_convert_fusion.3
  121.5 1.5 collective-permute-start.9
  123.1 6.8 %collective-permute-done.9 = bf16[64,2048]{1,0:T(8,128)(2,1)S(1)} collective-permute-done((bf16[64,2048]{1,0:T(8,128)(2,1)S(1)}, bf16[64,2048]{1,0:T(8,128)(2,1)S(1)}, u32[]{:S(2)}, u32[]{:S(2)}) %collective-permute-start.9) | collective-permute-done | bytes 262176 | tf_op jit(solution)/shard_map/ppermute | solution.py:31
  130.2 5.6 %collective-permute-start.10 = (bf16[64,2048]{1,0:T(8,128)(2,1)S(1)}, bf16[64,2048]{1,0:T(8,128)(2,1)S(1)}, u32[]{:S(2)}, u32[]{:S(2)}) collective-permute-start(bf16[64,2048]{1,0:T(8,128)(2,1)S(1)} %get-tuple-element.191), channel_id=1, source_target_pairs={{0,8},{1,9},{2,10},{3,11},{4,12},{5,13},{6,14},{7,15},{8,0},{9,1},... | collective-permute-start | bytes 786440 | tf_op jit(solution)/shard_map/ppermute | solution.py:56
  139.6 1.9 collective-permute-start.14
  141.5 37.0 %collective-permute-done.10 = bf16[64,2048]{1,0:T(8,128)(2,1)S(1)} collective-permute-done((bf16[64,2048]{1,0:T(8,128)(2,1)S(1)}, bf16[64,2048]{1,0:T(8,128)(2,1)S(1)}, u32[]{:S(2)}, u32[]{:S(2)}) %collective-permute-start.10) | collective-permute-done | bytes 262176 | tf_op jit(solution)/shard_map/ppermute | solution.py:56
  178.5 3.9 collective-permute-start.15
  183.2 1.9 collective-permute-start.16
  188.7 4.2 collective-permute-done.14
  193.5 4.9 %collective-permute-done.15 = bf16[64,2048]{1,0:T(8,128)(2,1)S(1)} collective-permute-done((bf16[64,2048]{1,0:T(8,128)(2,1)S(1)}, bf16[64,2048]{1,0:T(8,128)(2,1)S(1)}, u32[]{:S(2)}, u32[]{:S(2)}) %collective-permute-start.15) | collective-permute-done | bytes 262176 | tf_op jit(solution)/shard_map/ppermute | solution.py:56
  199.9 4.2 collective-permute-done.17
  205.5 2.7 copy_bitcast_fusion
  208.2 6.7 %fusion.11 = f32[1024,640]{1,0:T(8,128)S(1)} fusion(bf16[1024,2048]{1,0:T(8,128)(2,1)} %constant_dynamic-update-slice_fusion.13.ffn_ref, bf16[2048,960]{0,1:T(8,128)(2,1)S(1)} %copy_bitcast_fusion), kind=kOutput, calls=%fused_computation.21 | convolution fusion | flops 2684354560 | bytes 9437184 | tf_op jit(solution)/shard_map/dot_general | solution.py:22
  214.9 5.7 %multiply_convert_fusion.1 = (bf16[1024,320]{1,0:T(8,128)(2,1)S(1)}, bf16[1024,320]{1,0:T(8,128)(2,1)S(1)}, bf16[1024,320]{1,0:T(8,128)(2,1)}) fusion(f32[1024,640]{1,0:T(8,128)S(1)} %fusion.11, bf16[1024,2048]{1,0:T(8,128)(2,1)} %constant_dynamic-update-slice_fusion.og_ref, bf16[2048,960]{0,1:T(8,128)(2,1)S(1)} %copy_bitcast_fusion), kind=kOutput, calls=%fused_computation.27 | convolution fusion | flops 1347092480 | bytes 10616832 | tf_op jit(solution)/shard_map/dot_general | solution.py:22
  220.6 1.8 convolution_convert_fusion.2
  224.1 2.5 collective-permute-done.18
  226.6 1.9 add_convert_fusion.1
  232.6 2.9 collective-permute-start.20
  235.5 11.2 %feed_forward_weight_grads.1 = bf16[16,960,128]{2,1,0:T(8,128)(2,1)} custom-call(bf16[1024,2048]{1,0:T(8,128)(2,1)} %constant_dynamic-update-slice_fusion.13.ffn_ref, bf16[1024,2048]{1,0:T(8,128)(2,1)} %constant_dynamic-update-slice_fusion.og_ref, bf16[1024,640]{1,0:T(8,128)(2,1)} %pad_maximum_fusion.2.d_ref, bf16[1024,320]{1,0:T(8,128)(2,1)} %get-tuple-element.86.inner_ref), custom_call_target="tpu_custom_call" | custom-call | tf_op jit(solution)/shard_map/feed_forward_weight_grads/pallas_call | solution.py:343
  250.5 1.7 collective-permute-start.21
  252.3 7.5 %collective-permute-start.22 = (bf16[2,64,1024]{2,1,0:T(8,128)(2,1)S(1)}, bf16[2,64,1024]{2,1,0:T(8,128)(2,1)S(1)}, u32[]{:S(2)}, u32[]{:S(2)}) collective-permute-start(bf16[2,64,1024]{2,1,0:T(8,128)(2,1)S(1)} %slice_bitcast_fusion.8), channel_id=1, source_target_pairs={{0,8},{1,9},{2,10},{3,11},{4,12},{5,13},{6,14},{7,15},{8,0},{9,1},... | collective-permute-start | bytes 786440 | tf_op jit(solution)/shard_map/ppermute | solution.py:56
  259.7 3.6 convolution_convert_fusion.1
  263.3 2.6 convolution_convert_fusion
  267.7 3.4 collective-permute-done.24
  274.7 4.1 collective-permute-done.25
  278.9 3.6 fusion.16.grad_ref
  282.5 6.7 %attention_backward.1 = (bf16[128,640]{1,0:T(8,128)(2,1)}, f32[1,128]{1,0:T(1,128)}, bf16[2,4,128,384]{3,2,1,0:T(8,128)(2,1)}, bf16[2,4,128,384]{3,2,1,0:T(8,128)(2,1)}) custom-call(s32[2]{0:T(128)} %pad_add_fusion.1.bounds_ref, s32[2,128]{1,0:T(2,128)} %pad_add_fusion.limits_ref, bf16[128,1024]{1,0:T(8,128)(2,1)} %get-tuple-element.71.q_ref, ...), custom_call_target="tpu_custom_call" | custom-call | flops 1677721600 | bytes 3145728 | tf_op jit(solution)/shard_map/attention_backward/pallas_call | solution.py:526
  293.8 3.1 weight_rows.3
  298.4 3.1 weight_rows.4
  301.6 3.0 add_convert_fusion
  307.0 2.6 collective-permute-done.27
  313.0 1.6 collective-permute-start.32
  316.7 13.6 %collective-permute-done.34 = bf16[2,2,64,2048]{3,2,1,0:T(8,128)(2,1)S(1)} collective-permute-done((bf16[2,2,64,2048]{3,2,1,0:T(8,128)(2,1)S(1)}, bf16[2,2,64,2048]{3,2,1,0:T(8,128)(2,1)S(1)}, u32[]{:S(2)}, u32[]{:S(2)}) %collective-permute-start.34) | collective-permute-done | bytes 1048608 | tf_op jit(solution)/shard_map/ppermute | solution.py:56
  330.3 1.6 collective-permute-start.40
  332.3 5.2 %collective-permute-done.31.refs_2_ = bf16[128,384]{1,0:T(8,128)(2,1)S(1)} collective-permute-done((bf16[128,384]{1,0:T(8,128)(2,1)S(1)}, bf16[128,384]{1,0:T(8,128)(2,1)S(1)}, u32[]{:S(2)}, u32[]{:S(2)}) %collective-permute-start.31) | collective-permute-done | bytes 98336 | tf_op jit(solution)/shard_map/ppermute | solution.py:41
  339.9 2.5 key_value_heads_back.1
  344.1 2.9 weight_rows.5
  349.8 8.5 %collective-permute-done.35 = bf16[2,64,2048]{2,1,0:T(8,128)(2,1)} collective-permute-done((bf16[2,64,2048]{2,1,0:T(8,128)(2,1)}, bf16[2,64,2048]{2,1,0:T(8,128)(2,1)}, u32[]{:S(2)}, u32[]{:S(2)}) %collective-permute-start.35) | collective-permute-done | bytes 524320 | tf_op jit(solution)/shard_map/ppermute | solution.py:56
  361.1 3.3 collective-permute-start.36
  365.7 14.5 %collective-permute-done.36 = bf16[64,2048]{1,0:T(8,128)(2,1)} collective-permute-done((bf16[64,2048]{1,0:T(8,128)(2,1)}, bf16[64,2048]{1,0:T(8,128)(2,1)}, u32[]{:S(2)}, u32[]{:S(2)}) %collective-permute-start.36) | collective-permute-done | bytes 262176 | tf_op jit(solution)/shard_map/ppermute | solution.py:56
  384.3 3.7 fusion.2
  391.0 9.3 %collective-permute-done.42 = bf16[4,144,384]{2,1,0:T(8,128)(2,1)S(1)} collective-permute-done((bf16[4,144,384]{2,1,0:T(8,128)(2,1)S(1)}, bf16[4,144,384]{2,1,0:T(8,128)(2,1)S(1)}, u32[]{:S(2)}, u32[]{:S(2)}) %collective-permute-start.42) | collective-permute-done | bytes 442400 | tf_op jit(solution)/shard_map/ppermute | solution.py:46
  404.0 3.8 all-to-all-start.1
  407.8 2.7 subtract_add_fusion
  410.5 7.4 %collective-permute-done.44 = bf16[144,384]{1,0:T(8,128)(2,1)} collective-permute-done((bf16[144,384]{1,0:T(8,128)(2,1)}, bf16[144,384]{1,0:T(8,128)(2,1)}, u32[]{:S(2)}, u32[]{:S(2)}) %collective-permute-start.44) | collective-permute-done | bytes 110624 | tf_op jit(solution)/shard_map/ppermute | solution.py:41
  424.2 13.0 %all-to-all-done.1.in_ref = bf16[8,960,128]{2,1,0:T(8,128)(2,1)S(1)} async-done(((bf16[8,960,128]{2,1,0:T(8,128)(2,1)}), bf16[8,960,128]{2,1,0:T(8,128)(2,1)S(1)}, u32[]{:S(2)}, u32[]{:S(2)}) %all-to-all-start.1) | async-done | bytes 1966112 | tf_op jit(solution)/shard_map/all_to_all | solution.py:160
  441.0 1.7 collective-permute-start.46
  442.7 4.2 feed_forward_grads.1
  (282 shorter events, 94.2 us)
Async XLA Ops:
  7.2 73.7 %all-gather.2.cloned.1.call-start = ((), (), s32[]{:S(2)}) async-start(), calls=%async_computation.4 | async-start | bytes 7241728 | tf_op jit(solution)/shard_map/all_gather | solution.py:633
  9.2 31.3 %copy-start.34 = (f32[64]{0:T(128)S(1)}, f32[64]{0:T(128)}, u32[]{:S(2)}) copy-start(f32[64]{0:T(128)} %param.24) | copy-start | bytes 772
  9.2 31.4 %copy-start.32 = (pred[3,128]{1,0:T(4,128)(4,1)S(1)}, pred[3,128]{1,0:T(4,128)(4,1)}, u32[]{:S(2)}) copy-start(pred[3,128]{1,0:T(4,128)(4,1)} %constant.199.clone.1) | copy-start | bytes 1156
  9.2 31.4 %copy-start.36 = (f32[64]{0:T(128)S(1)}, f32[64]{0:T(128)}, u32[]{:S(2)}) copy-start(f32[64]{0:T(128)} %param.23) | copy-start | bytes 772
  9.2 31.5 %copy-start.35 = (s32[128]{0:T(128)S(1)}, s32[128]{0:T(128)}, u32[]{:S(2)}) copy-start(s32[128]{0:T(128)} %param.26) | copy-start | bytes 1540
  11.0 9.3 %collective-permute-start = (bf16[64,2048]{1,0:T(8,128)(2,1)S(1)}, bf16[64,2048]{1,0:T(8,128)(2,1)S(1)}, u32[]{:S(2)}, u32[]{:S(2)}) collective-permute-start(bf16[64,2048]{1,0:T(8,128)(2,1)S(1)} %get-tuple-element.195), channel_id=1, source_target_pairs={{0,8},{1,9},{2,10},{3,11},{4,12},{5,13},{6,14},{7,15},{8,0},{9,1},... | collective-permute-start | bytes 786440 | tf_op jit(solution)/shard_map/ppermute | solution.py:56
  20.4 17.7 %collective-permute-start.1 = (bf16[128,2048]{1,0:T(8,128)(2,1)S(1)}, bf16[128,2048]{1,0:T(8,128)(2,1)S(1)}, u32[]{:S(2)}, u32[]{:S(2)}) collective-permute-start(bf16[128,2048]{1,0:T(8,128)(2,1)S(1)} %pad_maximum_fusion.6), channel_id=1, source_target_pairs={{0,4},{1,5},{2,6},{3,7},{4,0},{5,1},{6,2},{7,3},{8,12},{9,13},{10,... | collective-permute-start | bytes 1572872 | tf_op jit(solution)/shard_map/ppermute | solution.py:56
  39.2 24.0 %collective-permute-start.2 = (bf16[256,2048]{1,0:T(8,128)(2,1)}, bf16[256,2048]{1,0:T(8,128)(2,1)S(1)}, u32[]{:S(2)}, u32[]{:S(2)}) collective-permute-start(bf16[256,2048]{1,0:T(8,128)(2,1)} %pad_maximum_fusion.4), channel_id=1, source_target_pairs={{0,1},{1,0},{2,3},{3,2},{4,5},{5,4},{6,7},{7,6},{8,9},{9,8},{10,11... | collective-permute-start | bytes 3145736 | tf_op jit(solution)/shard_map/ppermute | solution.py:56
  40.6 22.9 %copy-start.30 = (f32[1,1,3,128]{3,1,2,0:T(1,128)}, f32[1,1,3,128]{3,1,2,0:T(1,128)S(1)}, u32[]{:S(2)}) copy-start(f32[1,1,3,128]{3,1,2,0:T(1,128)S(1)} %copy.106) | copy-start | bytes 4612
  44.4 20.9 %copy-start = (bf16[128,2048]{1,0:T(8,128)(2,1)S(1)}, bf16[128,2048]{1,0:T(8,128)(2,1)}, u32[]{:S(2)}) copy-start(bf16[128,2048]{1,0:T(8,128)(2,1)} %param.14) | copy-start | bytes 1572868
  44.4 21.1 %copy-start.28 = (f32[2048]{0:T(1024)S(1)}, f32[2048]{0:T(1024)}, u32[]{:S(2)}) copy-start(f32[2048]{0:T(1024)} %param.21) | copy-start | bytes 24580
  63.4 5.7 %collective-permute-start.3 = (bf16[512,2048]{1,0:T(8,128)(2,1)S(1)}, bf16[512,2048]{1,0:T(8,128)(2,1)S(1)}, u32[]{:S(2)}, u32[]{:S(2)}) collective-permute-start(bf16[512,2048]{1,0:T(8,128)(2,1)S(1)} %pad_maximum_fusion.1), channel_id=1, source_target_pairs={{0,2},{2,0},{4,6},{6,4},{8,10},{10,8},{12,14},{14,12},{16,18},{18,... | collective-permute-start | bytes 6291464 | tf_op jit(solution)/shard_map/ppermute | solution.py:27
  86.7 7.8 %collective-permute-start.6 = (bf16[128,384]{1,0:T(8,128)(2,1)}, bf16[128,384]{1,0:T(8,128)(2,1)S(1)}, u32[]{:S(2)}, u32[]{:S(2)}) collective-permute-start(bf16[128,384]{1,0:T(8,128)(2,1)} %get-tuple-element.72), channel_id=1, source_target_pairs={{0,24},{2,26},{4,28},{6,30},{1,25},{3,27},{5,29},{7,31}} | collective-permute-start | bytes 294920 | tf_op jit(solution)/shard_map/ppermute | solution.py:41
  90.5 5.6 %collective-permute-start.5 = (bf16[128,384]{1,0:T(8,128)(2,1)}, bf16[128,384]{1,0:T(8,128)(2,1)S(1)}, u32[]{:S(2)}, u32[]{:S(2)}) collective-permute-start(bf16[128,384]{1,0:T(8,128)(2,1)} %get-tuple-element.72), channel_id=1, source_target_pairs={{0,16},{2,18},{4,20},{6,22},{8,24},{10,26},{12,28},{14,30},{1,17},... | collective-permute-start | bytes 294920 | tf_op jit(solution)/shard_map/ppermute | solution.py:41
  91.8 5.7 %collective-permute-start.4 = (bf16[128,384]{1,0:T(8,128)(2,1)}, bf16[128,384]{1,0:T(8,128)(2,1)S(1)}, u32[]{:S(2)}, u32[]{:S(2)}) collective-permute-start(bf16[128,384]{1,0:T(8,128)(2,1)} %get-tuple-element.72), channel_id=1, source_target_pairs={{0,8},{2,10},{4,12},{6,14},{8,16},{10,18},{12,20},{14,22},{16,24},... | collective-permute-start | bytes 294920 | tf_op jit(solution)/shard_map/ppermute | solution.py:41
  97.6 10.7 %collective-permute-start.7 = (bf16[4,128,384]{2,1,0:T(8,128)(2,1)S(1)}, bf16[4,128,384]{2,1,0:T(8,128)(2,1)S(1)}, u32[]{:S(2)}, u32[]{:S(2)}) collective-permute-start(bf16[4,128,384]{2,1,0:T(8,128)(2,1)S(1)} %get-tuple-element.220), channel_id=1, source_target_pairs={{0,4},{2,6},{4,0},{6,2},{8,12},{10,14},{12,8},{14,10},{16,20},{18,... | collective-permute-start | bytes 1179656 | tf_op jit(solution)/shard_map/ppermute | solution.py:46
  100.6 105.0 %all-to-all-start = ((bf16[16,128,960]{1,2,0:T(8,128)(2,1)}), bf16[16,128,960]{1,2,0:T(8,128)(2,1)}, u32[]{:S(2)}, u32[]{:S(2)}) async-start(bf16[16,128,960]{1,2,0:T(8,128)(2,1)} %pad_maximum_fusion), calls=%async_computation | async-start | bytes 7864320 | tf_op jit(solution)/shard_map/all_to_all | solution.py:649
  108.3 295.7 %reduce-scatter.5.cloned.1.call-start = ((), (), s32[]{:S(2)}) async-start(), calls=%async_computation.6 | async-start | bytes 5898240 | tf_op jit(solution)/shard_map/reduce_scatter | solution.py:711
  108.5 5.3 %collective-permute-start.8 = (bf16[2,4,128,384]{3,2,1,0:T(8,128)(2,1)S(1)}, bf16[2,4,128,384]{3,2,1,0:T(8,128)(2,1)S(1)}, u32[]{:S(2)}, u32[]{:S(2)}) collective-permute-start(bf16[2,4,128,384]{3,2,1,0:T(8,128)(2,1)S(1)} %pad_maximum_fusion.5.same_ref), channel_id=1, source_target_pairs={{0,2},{2,0},{4,6},{6,4},{8,10},{10,8},{12,14},{14,12},{16,18},{18,... | collective-permute-start | bytes 2359304 | tf_op jit(solution)/shard_map/ppermute | solution.py:27
  121.5 8.4 %collective-permute-start.9 = (bf16[64,2048]{1,0:T(8,128)(2,1)S(1)}, bf16[64,2048]{1,0:T(8,128)(2,1)S(1)}, u32[]{:S(2)}, u32[]{:S(2)}) collective-permute-start(bf16[64,2048]{1,0:T(8,128)(2,1)S(1)} %constant_dynamic-slice_fusion), channel_id=1, source_target_pairs={{0,1},{1,0},{2,3},{3,2},{4,5},{5,4},{6,7},{7,6},{8,9},{9,8},{10,11... | collective-permute-start | bytes 786440 | tf_op jit(solution)/shard_map/ppermute | solution.py:31
  130.2 48.3 %collective-permute-start.10 = (bf16[64,2048]{1,0:T(8,128)(2,1)S(1)}, bf16[64,2048]{1,0:T(8,128)(2,1)S(1)}, u32[]{:S(2)}, u32[]{:S(2)}) collective-permute-start(bf16[64,2048]{1,0:T(8,128)(2,1)S(1)} %get-tuple-element.191), channel_id=1, source_target_pairs={{0,8},{1,9},{2,10},{3,11},{4,12},{5,13},{6,14},{7,15},{8,0},{9,1},... | collective-permute-start | bytes 786440 | tf_op jit(solution)/shard_map/ppermute | solution.py:56
  135.8 47.4 %collective-permute-start.11 = (bf16[64,2048]{1,0:T(8,128)(2,1)S(1)}, bf16[64,2048]{1,0:T(8,128)(2,1)S(1)}, u32[]{:S(2)}, u32[]{:S(2)}) collective-permute-start(bf16[64,2048]{1,0:T(8,128)(2,1)S(1)} %get-tuple-element.191), channel_id=1, source_target_pairs={{0,4},{1,5},{2,6},{3,7},{4,0},{5,1},{6,2},{7,3},{8,12},{9,13},{10,... | collective-permute-start | bytes 786440 | tf_op jit(solution)/shard_map/ppermute | solution.py:56
  137.2 50.0 %collective-permute-start.12 = (bf16[64,2048]{1,0:T(8,128)(2,1)S(1)}, bf16[64,2048]{1,0:T(8,128)(2,1)S(1)}, u32[]{:S(2)}, u32[]{:S(2)}) collective-permute-start(bf16[64,2048]{1,0:T(8,128)(2,1)S(1)} %get-tuple-element.191), channel_id=1, source_target_pairs={{0,12},{1,13},{2,14},{3,15},{4,8},{5,9},{6,10},{7,11},{8,4},{9,5},... | collective-permute-start | bytes 786440 | tf_op jit(solution)/shard_map/ppermute | solution.py:56
  138.1 49.8 %collective-permute-start.13 = (bf16[64,2048]{1,0:T(8,128)(2,1)S(1)}, bf16[64,2048]{1,0:T(8,128)(2,1)S(1)}, u32[]{:S(2)}, u32[]{:S(2)}) collective-permute-start(bf16[64,2048]{1,0:T(8,128)(2,1)S(1)} %get-tuple-element.191), channel_id=1, source_target_pairs={{0,1},{1,0},{2,3},{3,2},{4,5},{5,4},{6,7},{7,6},{8,9},{9,8},{10,11... | collective-permute-start | bytes 786440 | tf_op jit(solution)/shard_map/ppermute | solution.py:56
  139.6 53.3 %collective-permute-start.14 = (bf16[64,2048]{1,0:T(8,128)(2,1)S(1)}, bf16[64,2048]{1,0:T(8,128)(2,1)S(1)}, u32[]{:S(2)}, u32[]{:S(2)}) collective-permute-start(bf16[64,2048]{1,0:T(8,128)(2,1)S(1)} %get-tuple-element.191), channel_id=1, source_target_pairs={{0,9},{1,8},{2,11},{3,10},{4,13},{5,12},{6,15},{7,14},{8,1},{9,0},... | collective-permute-start | bytes 786440 | tf_op jit(solution)/shard_map/ppermute | solution.py:56
  178.5 19.9 %collective-permute-start.15 = (bf16[64,2048]{1,0:T(8,128)(2,1)S(1)}, bf16[64,2048]{1,0:T(8,128)(2,1)S(1)}, u32[]{:S(2)}, u32[]{:S(2)}) collective-permute-start(bf16[64,2048]{1,0:T(8,128)(2,1)S(1)} %get-tuple-element.191), channel_id=1, source_target_pairs={{0,5},{1,4},{2,7},{3,6},{4,1},{5,0},{6,3},{7,2},{8,13},{9,12},{10,... | collective-permute-start | bytes 786440 | tf_op jit(solution)/shard_map/ppermute | solution.py:56
  183.2 16.0 %collective-permute-start.16 = (bf16[64,2048]{1,0:T(8,128)(2,1)S(1)}, bf16[64,2048]{1,0:T(8,128)(2,1)S(1)}, u32[]{:S(2)}, u32[]{:S(2)}) collective-permute-start(bf16[64,2048]{1,0:T(8,128)(2,1)S(1)} %get-tuple-element.191), channel_id=1, source_target_pairs={{0,13},{1,12},{2,15},{3,14},{4,9},{5,8},{6,11},{7,10},{8,5},{9,4},... | collective-permute-start | bytes 786440 | tf_op jit(solution)/shard_map/ppermute | solution.py:56
  199.9 4.2 collective-permute-start.17
  208.2 18.4 %copy-start.5 = (bf16[2048,960]{0,1:T(8,128)(2,1)}, bf16[2048,960]{0,1:T(8,128)(2,1)S(1)}, u32[]{:S(2)}) copy-start(bf16[2048,960]{0,1:T(8,128)(2,1)S(1)} %copy_bitcast_fusion) | copy-start | bytes 11796484
  222.4 4.2 collective-permute-start.18
  231.1 15.6 %collective-permute-start.19 = (bf16[2,2,64,1024]{3,2,1,0:T(8,128)(2,1)}, bf16[2,2,64,1024]{3,2,1,0:T(8,128)(2,1)}, u32[]{:S(2)}, u32[]{:S(2)}) collective-permute-start(bf16[2,2,64,1024]{3,2,1,0:T(8,128)(2,1)} %slice_bitcast_fusion.2), channel_id=1, source_target_pairs={{0,1},{1,0},{2,3},{3,2},{4,5},{5,4},{6,7},{7,6},{8,9},{9,8},{10,11... | collective-permute-start | bytes 1572872 | tf_op jit(solution)/shard_map/ppermute | solution.py:56
  232.6 15.1 %collective-permute-start.20 = (bf16[2,2,64,1024]{3,2,0,1:T(8,128)(2,1)}, bf16[2,2,64,1024]{3,2,0,1:T(8,128)(2,1)}, u32[]{:S(2)}, u32[]{:S(2)}) collective-permute-start(bf16[2,2,64,1024]{3,2,0,1:T(8,128)(2,1)} %bitcast.171), channel_id=1, source_target_pairs={{0,4},{1,5},{2,6},{3,7},{4,0},{5,1},{6,2},{7,3},{8,12},{9,13},{10,... | collective-permute-start | bytes 1572872 | tf_op jit(solution)/shard_map/ppermute | solution.py:56
  250.5 15.4 %collective-permute-start.21 = (bf16[2,64,1024]{2,1,0:T(8,128)(2,1)S(1)}, bf16[2,64,1024]{2,1,0:T(8,128)(2,1)S(1)}, u32[]{:S(2)}, u32[]{:S(2)}) collective-permute-start(bf16[2,64,1024]{2,1,0:T(8,128)(2,1)S(1)} %slice_bitcast_fusion.9), channel_id=1, source_target_pairs={{0,4},{1,5},{2,6},{3,7},{4,0},{5,1},{6,2},{7,3},{8,12},{9,13},{10,... | collective-permute-start | bytes 786440 | tf_op jit(solution)/shard_map/ppermute | solution.py:56
  252.3 13.7 %collective-permute-start.22 = (bf16[2,64,1024]{2,1,0:T(8,128)(2,1)S(1)}, bf16[2,64,1024]{2,1,0:T(8,128)(2,1)S(1)}, u32[]{:S(2)}, u32[]{:S(2)}) collective-permute-start(bf16[2,64,1024]{2,1,0:T(8,128)(2,1)S(1)} %slice_bitcast_fusion.8), channel_id=1, source_target_pairs={{0,8},{1,9},{2,10},{3,11},{4,12},{5,13},{6,14},{7,15},{8,0},{9,1},... | collective-permute-start | bytes 786440 | tf_op jit(solution)/shard_map/ppermute | solution.py:56
  266.0 5.0 %collective-permute-start.24 = (bf16[64,1024]{1,0:T(8,128)(2,1)S(1)}, bf16[64,1024]{1,0:T(8,128)(2,1)S(1)}, u32[]{:S(2)}, u32[]{:S(2)}) collective-permute-start(bf16[64,1024]{1,0:T(8,128)(2,1)S(1)} %slice_bitcast_fusion.11), channel_id=1, source_target_pairs={{0,1},{1,0},{2,3},{3,2},{4,5},{5,4},{6,7},{7,6},{8,9},{9,8},{10,11... | collective-permute-start | bytes 393224 | tf_op jit(solution)/shard_map/ppermute | solution.py:56
  266.9 5.0 %collective-permute-start.23 = (bf16[64,1024]{1,0:T(8,128)(2,1)S(1)}, bf16[64,1024]{1,0:T(8,128)(2,1)S(1)}, u32[]{:S(2)}, u32[]{:S(2)}) collective-permute-start(bf16[64,1024]{1,0:T(8,128)(2,1)S(1)} %slice_bitcast_fusion.13), channel_id=1, source_target_pairs={{0,8},{1,9},{2,10},{3,11},{4,12},{5,13},{6,14},{7,15},{8,0},{9,1},... | collective-permute-start | bytes 393224 | tf_op jit(solution)/shard_map/ppermute | solution.py:56
  272.4 6.4 %collective-permute-start.25 = (bf16[64,2048]{1,0:T(8,128)(2,1)S(1)}, bf16[64,2048]{1,0:T(8,128)(2,1)S(1)}, u32[]{:S(2)}, u32[]{:S(2)}) collective-permute-start(bf16[64,2048]{1,0:T(8,128)(2,1)S(1)} %add_convert_fusion.9), channel_id=1, source_target_pairs={{0,1},{1,0},{2,3},{3,2},{4,5},{5,4},{6,7},{7,6},{8,9},{9,8},{10,11... | collective-permute-start | bytes 786440 | tf_op jit(solution)/shard_map/ppermute | solution.py:31
  274.4 144.7 %reduce-scatter.3.cloned.1.call-start = ((), (), s32[]{:S(2)}) async-start(), calls=%async_computation.5 | async-start | bytes 1638400 | tf_op jit(solution)/shard_map/reduce_scatter | solution.py:760
  274.6 27.0 %collective-permute-start.33 = (bf16[512,2048]{1,0:T(8,128)(2,1)}, bf16[512,2048]{1,0:T(8,128)(2,1)}, u32[]{:S(2)}, u32[]{:S(2)}) collective-permute-start(bf16[512,2048]{1,0:T(8,128)(2,1)} %convolution_convert_fusion.1), channel_id=1, source_target_pairs={{0,2},{2,0},{4,6},{6,4},{8,10},{10,8},{12,14},{14,12},{16,18},{18,... | collective-permute-start | bytes 6291464 | tf_op jit(solution)/shard_map/ppermute | solution.py:27
  289.1 2.5 collective-permute-start.26
  296.9 9.3 %collective-permute-start.28 = (bf16[8,128,640]{2,1,0:T(8,128)(2,1)}, bf16[8,128,640]{2,1,0:T(8,128)(2,1)S(1)}, u32[]{:S(2)}, u32[]{:S(2)}) collective-permute-start(bf16[8,128,640]{2,1,0:T(8,128)(2,1)} %get-tuple-element.98), channel_id=1, source_target_pairs={{0,2},{2,0},{4,6},{6,4},{8,10},{10,8},{12,14},{14,12},{16,18},{18,... | collective-permute-start | bytes 3932168 | tf_op jit(solution)/shard_map/ppermute | solution.py:27
  297.9 11.7 %collective-permute-start.27 = (bf16[4,128,384]{2,1,0:T(8,128)(2,1)}, bf16[4,128,384]{2,1,0:T(8,128)(2,1)S(1)}, u32[]{:S(2)}, u32[]{:S(2)}) collective-permute-start(bf16[4,128,384]{2,1,0:T(8,128)(2,1)} %slice_bitcast_fusion.4), channel_id=1, source_target_pairs={{0,4},{2,6},{4,0},{6,2},{8,12},{10,14},{12,8},{14,10},{16,20},{18,... | collective-permute-start | bytes 1179656 | tf_op jit(solution)/shard_map/ppermute | solution.py:46
  301.5 5.0 %collective-permute-start.29 = (bf16[8,128,640]{2,1,0:T(8,128)(2,1)}, bf16[8,128,640]{2,1,0:T(8,128)(2,1)S(1)}, u32[]{:S(2)}, u32[]{:S(2)}) collective-permute-start(bf16[8,128,640]{2,1,0:T(8,128)(2,1)} %get-tuple-element.102), channel_id=1, source_target_pairs={{0,2},{2,0},{4,6},{6,4},{8,10},{10,8},{12,14},{14,12},{16,18},{18,... | collective-permute-start | bytes 3932168 | tf_op jit(solution)/shard_map/ppermute | solution.py:27
  304.7 25.6 %collective-permute-start.34 = (bf16[2,2,64,2048]{3,2,1,0:T(8,128)(2,1)S(1)}, bf16[2,2,64,2048]{3,2,1,0:T(8,128)(2,1)S(1)}, u32[]{:S(2)}, u32[]{:S(2)}) collective-permute-start(bf16[2,2,64,2048]{3,2,1,0:T(8,128)(2,1)S(1)} %slice_bitcast_fusion), channel_id=1, source_target_pairs={{0,1},{1,0},{2,3},{3,2},{4,5},{5,4},{6,7},{7,6},{8,9},{9,8},{10,11... | collective-permute-start | bytes 3145736 | tf_op jit(solution)/shard_map/ppermute | solution.py:56
  310.4 21.9 %collective-permute-start.30 = (bf16[128,384]{1,0:T(8,128)(2,1)S(1)}, bf16[128,384]{1,0:T(8,128)(2,1)S(1)}, u32[]{:S(2)}, u32[]{:S(2)}) collective-permute-start(bf16[128,384]{1,0:T(8,128)(2,1)S(1)} %get-tuple-element.217), channel_id=1, source_target_pairs={{8,0},{10,2},{12,4},{14,6},{16,8},{18,10},{20,12},{22,14},{24,16},... | collective-permute-start | bytes 294920 | tf_op jit(solution)/shard_map/ppermute | solution.py:41
  311.7 25.8 %collective-permute-start.31 = (bf16[128,384]{1,0:T(8,128)(2,1)S(1)}, bf16[128,384]{1,0:T(8,128)(2,1)S(1)}, u32[]{:S(2)}, u32[]{:S(2)}) collective-permute-start(bf16[128,384]{1,0:T(8,128)(2,1)S(1)} %get-tuple-element.216), channel_id=1, source_target_pairs={{16,0},{18,2},{20,4},{22,6},{24,8},{26,10},{28,12},{30,14},{17,1},... | collective-permute-start | bytes 294920 | tf_op jit(solution)/shard_map/ppermute | solution.py:41
  313.0 24.5 %collective-permute-start.32 = (bf16[128,384]{1,0:T(8,128)(2,1)S(1)}, bf16[128,384]{1,0:T(8,128)(2,1)S(1)}, u32[]{:S(2)}, u32[]{:S(2)}) collective-permute-start(bf16[128,384]{1,0:T(8,128)(2,1)S(1)} %get-tuple-element.215), channel_id=1, source_target_pairs={{24,0},{26,2},{28,4},{30,6},{25,1},{27,3},{29,5},{31,7}} | collective-permute-start | bytes 294920 | tf_op jit(solution)/shard_map/ppermute | solution.py:41
  315.4 31.6 %collective-permute-start.41 = (bf16[4,128,640]{2,1,0:T(8,128)(2,1)}, bf16[4,128,640]{2,1,0:T(8,128)(2,1)}, u32[]{:S(2)}, u32[]{:S(2)}) collective-permute-start(bf16[4,128,640]{2,1,0:T(8,128)(2,1)} %slice.302), channel_id=1, source_target_pairs={{0,4},{2,6},{4,0},{6,2},{8,12},{10,14},{12,8},{14,10},{16,20},{18,... | collective-permute-start | bytes 1966088 | tf_op jit(solution)/shard_map/ppermute | solution.py:46
  330.3 18.2 %collective-permute-start.40 = (bf16[4,128,640]{2,1,0:T(8,128)(2,1)}, bf16[4,128,640]{2,1,0:T(8,128)(2,1)}, u32[]{:S(2)}, u32[]{:S(2)}) collective-permute-start(bf16[4,128,640]{2,1,0:T(8,128)(2,1)} %slice.300), channel_id=1, source_target_pairs={{0,4},{2,6},{4,0},{6,2},{8,12},{10,14},{12,8},{14,10},{16,20},{18,... | collective-permute-start | bytes 1966088 | tf_op jit(solution)/shard_map/ppermute | solution.py:46
  338.4 19.9 %collective-permute-start.35 = (bf16[2,64,2048]{2,1,0:T(8,128)(2,1)}, bf16[2,64,2048]{2,1,0:T(8,128)(2,1)}, u32[]{:S(2)}, u32[]{:S(2)}) collective-permute-start(bf16[2,64,2048]{2,1,0:T(8,128)(2,1)} %fusion.30), channel_id=1, source_target_pairs={{0,4},{1,5},{2,6},{3,7},{4,0},{5,1},{6,2},{7,3},{8,12},{9,13},{10,... | collective-permute-start | bytes 1572872 | tf_op jit(solution)/shard_map/ppermute | solution.py:56
  347.0 35.6 %collective-permute-start.38 = (bf16[8,144,384]{2,1,0:T(8,128)(2,1)}, bf16[8,144,384]{2,1,0:T(8,128)(2,1)}, u32[]{:S(2)}, u32[]{:S(2)}) collective-permute-start(bf16[8,144,384]{2,1,0:T(8,128)(2,1)} %get-tuple-element.116), channel_id=1, source_target_pairs={{0,2},{2,0},{4,6},{6,4},{8,10},{10,8},{12,14},{14,12},{16,18},{18,... | collective-permute-start | bytes 2654216 | tf_op jit(solution)/shard_map/ppermute | solution.py:27
  361.1 19.0 %copy-start.8 = (f32[2,64,2048]{2,1,0:T(8,128)S(1)}, f32[2,64,2048]{2,1,0:T(8,128)}, u32[]{:S(2)}) copy-start(f32[2,64,2048]{2,1,0:T(8,128)} %copy-done.7) | copy-start | bytes 3145732
  361.1 19.0 %collective-permute-start.36 = (bf16[64,2048]{1,0:T(8,128)(2,1)}, bf16[64,2048]{1,0:T(8,128)(2,1)}, u32[]{:S(2)}, u32[]{:S(2)}) collective-permute-start(bf16[64,2048]{1,0:T(8,128)(2,1)} %fusion.41), channel_id=1, source_target_pairs={{0,8},{1,9},{2,10},{3,11},{4,12},{5,13},{6,14},{7,15},{8,0},{9,1},... | collective-permute-start | bytes 786440 | tf_op jit(solution)/shard_map/ppermute | solution.py:56
  365.6 17.1 %copy-start.18 = (bf16[8,144,384]{2,1,0:T(8,128)(2,1)S(1)}, bf16[8,144,384]{2,1,0:T(8,128)(2,1)}, u32[]{:S(2)}) copy-start(bf16[8,144,384]{2,1,0:T(8,128)(2,1)} %get-tuple-element.115) | copy-start | bytes 2654212
  381.2 9.0 %collective-permute-start.37 = (bf16[64,2048]{1,0:T(8,128)(2,1)S(1)}, bf16[64,2048]{1,0:T(8,128)(2,1)S(1)}, u32[]{:S(2)}, u32[]{:S(2)}) collective-permute-start(bf16[64,2048]{1,0:T(8,128)(2,1)S(1)} %fusion.33), channel_id=1, source_target_pairs={{0,1},{1,0},{2,3},{3,2},{4,5},{5,4},{6,7},{7,6},{8,9},{9,8},{10,11... | collective-permute-start | bytes 786440 | tf_op jit(solution)/shard_map/ppermute | solution.py:31
  388.0 15.2 %collective-permute-start.39 = (bf16[128,2048]{1,0:T(8,128)(2,1)S(1)}, bf16[128,2048]{1,0:T(8,128)(2,1)S(1)}, u32[]{:S(2)}, u32[]{:S(2)}) collective-permute-start(bf16[128,2048]{1,0:T(8,128)(2,1)S(1)} %fusion.2), channel_id=1, source_target_pairs={{0,1},{1,0},{2,3},{3,2},{4,5},{5,4},{6,7},{7,6},{8,9},{9,8},{10,11... | collective-permute-start | bytes 1572872 | tf_op jit(solution)/shard_map/ppermute | solution.py:31
  388.7 11.6 %collective-permute-start.42 = (bf16[4,144,384]{2,1,0:T(8,128)(2,1)S(1)}, bf16[4,144,384]{2,1,0:T(8,128)(2,1)S(1)}, u32[]{:S(2)}, u32[]{:S(2)}) collective-permute-start(bf16[4,144,384]{2,1,0:T(8,128)(2,1)S(1)} %slice.377), channel_id=1, source_target_pairs={{0,4},{2,6},{4,0},{6,2},{8,12},{10,14},{12,8},{14,10},{16,20},{18,... | collective-permute-start | bytes 1327112 | tf_op jit(solution)/shard_map/ppermute | solution.py:46
  401.2 9.3 %collective-permute-start.45 = (bf16[144,384]{1,0:T(8,128)(2,1)}, bf16[144,384]{1,0:T(8,128)(2,1)S(1)}, u32[]{:S(2)}, u32[]{:S(2)}) collective-permute-start(bf16[144,384]{1,0:T(8,128)(2,1)} %get-tuple-element.211), channel_id=1, source_target_pairs={{0,24},{2,26},{4,28},{6,30},{8,0},{10,2},{12,4},{14,6},{16,8},{18,... | collective-permute-start | bytes 331784 | tf_op jit(solution)/shard_map/ppermute | solution.py:41
  401.2 16.7 %collective-permute-start.44 = (bf16[144,384]{1,0:T(8,128)(2,1)}, bf16[144,384]{1,0:T(8,128)(2,1)}, u32[]{:S(2)}, u32[]{:S(2)}) collective-permute-start(bf16[144,384]{1,0:T(8,128)(2,1)} %get-tuple-element.212), channel_id=1, source_target_pairs={{0,16},{2,18},{4,20},{6,22},{8,24},{10,26},{12,28},{14,30},{16,0},... | collective-permute-start | bytes 331784 | tf_op jit(solution)/shard_map/ppermute | solution.py:41
  402.0 16.0 %collective-permute-start.43 = (bf16[144,384]{1,0:T(8,128)(2,1)S(1)}, bf16[144,384]{1,0:T(8,128)(2,1)}, u32[]{:S(2)}, u32[]{:S(2)}) collective-permute-start(bf16[144,384]{1,0:T(8,128)(2,1)S(1)} %get-tuple-element.210), channel_id=1, source_target_pairs={{0,8},{2,10},{4,12},{6,14},{8,16},{10,18},{12,20},{14,22},{16,24},... | collective-permute-start | bytes 331784 | tf_op jit(solution)/shard_map/ppermute | solution.py:41
  404.0 33.2 %all-to-all-start.1 = ((bf16[8,960,128]{2,1,0:T(8,128)(2,1)}), bf16[8,960,128]{2,1,0:T(8,128)(2,1)S(1)}, u32[]{:S(2)}, u32[]{:S(2)}) async-start(bf16[8,960,128]{2,1,0:T(8,128)(2,1)} %reduce-scatter.5.cloned.1.call-done), calls=%async_computation.3 | async-start | bytes 3932160 | tf_op jit(solution)/shard_map/all_to_all | solution.py:160
  419.0 18.2 %copy-start.9 = (bf16[128,1664]{1,0:T(8,128)(2,1)S(1)}, bf16[128,1664]{1,0:T(8,128)(2,1)}, u32[]{:S(2)}) copy-start(bf16[128,1664]{1,0:T(8,128)(2,1)} %pack_weights.1) | copy-start | bytes 1277956
  438.6 8.2 %collective-permute-start.47 = (f32[264]{0:T(512)S(1)}, f32[264]{0:T(512)S(1)}, u32[]{:S(2)}, u32[]{:S(2)}) collective-permute-start(f32[264]{0:T(512)S(1)} %pad_maximum_fusion.15), channel_id=1, source_target_pairs={{0,1},{1,0},{2,3},{3,2},{4,5},{5,4},{6,7},{7,6},{8,9},{9,8},{10,11... | collective-permute-start | bytes 3176 | tf_op jit(solution)/shard_map/ppermute | solution.py:31
  441.0 7.1 %collective-permute-start.46 = (bf16[128,384]{1,0:T(8,128)(2,1)S(1)}, bf16[128,384]{1,0:T(8,128)(2,1)S(1)}, u32[]{:S(2)}, u32[]{:S(2)}) collective-permute-start(bf16[128,384]{1,0:T(8,128)(2,1)S(1)} %slice.531), channel_id=1, source_target_pairs={{0,1},{1,0},{2,3},{3,2},{4,5},{5,4},{6,7},{7,6},{8,9},{9,8},{10,11... | collective-permute-start | bytes 294920 | tf_op jit(solution)/shard_map/ppermute | solution.py:31
  (28 other events, 189.6 us)
Sparse Core Ops, SparseCore 0:
  10.3 70.5 all-gather.1
  274.5 101.8 reduce-scatter.4
  379.4 36.0 reduce-scatter.2

commit v5 on v4

--- a/solution.py
+++ b/solution.py
@@ -56,10 +56,10 @@
     return lax.ppermute(block, ("row", "col"), route)
 
 
-def gather_earlier(block, span):
+def gather_earlier(block, span, weights):
     far = jnp.stack([block] + [shift_far(block, k, span, False) for k in range(1, span // 4)])
-    same = jnp.stack([far, swap_near(far)])
-    return same, swap_core(same)
+    same, weights = lax.optimization_barrier((jnp.stack([far, swap_near(far)]), weights))
+    return same, swap_core(same), weights
 
 
 def add_low(one, two):
@@ -112,14 +112,13 @@
     return after_all((array,), *others)[0]
 
 
-def cube_numbers():
+def gather_cube(block, weights):
     cols = lax.axis_size("col")
-    return [(2 * pair + near) * cols + c for c in range(cols) for near in range(2) for pair in range(2)]
-
-
-def gather_cube(block):
-    same = jnp.concatenate([block] + [swap_cube(block, e) for e in cube_numbers()[1:]], axis=0)
-    return same, swap_core(same)
+    both = jnp.stack([block, swap_cube(block, 1)])
+    *pieces, weights = lax.optimization_barrier((*(swap_cube(both, number * cols) for number in (2, 1, 3)), weights))
+    pieces = [both] + pieces
+    same = jnp.concatenate([piece[c] for c in range(2) for piece in pieces], axis=0)
+    return same, swap_core(same), weights
 
 
 def gather_cube_slowly(block):
@@ -541,7 +540,7 @@
             pltpu.VMEM((HALF, wide), F32),
         ],
         compiler_params=pltpu.CompilerParams(vmem_limit_bytes=VMEM_LIMIT),
-        cost_estimate=pl.CostEstimate(flops=10 * HALF * work, bytes_accessed=8 * same.size, transcendentals=work),
+        cost_estimate=BESIDE,
         name="attention_backward",
     )(bounds, limits, q, grad, turned, inv, same, other, raw, gain, cosine, sine)
 
@@ -569,7 +568,7 @@
         out_specs=vmem(2),
         out_shape=[jax.ShapeDtypeStruct((tok, width), BF16), jax.ShapeDtypeStruct((1, LANES), F32)],
         compiler_params=pltpu.CompilerParams(vmem_limit_bytes=VMEM_LIMIT),
-        cost_estimate=pl.CostEstimate(flops=30 * tok * width, bytes_accessed=2 * tok * width * len(parts), transcendentals=0),
+        cost_estimate=BESIDE,
         name="key_value_heads_back",
     )(raw, gain, flag, cosine, sine, *parts)
 
@@ -645,8 +644,7 @@
         ],
         axis=2,
     ).transpose(1, 0, 2)
-    w_ff = jnp.concatenate([after(w_ff, w_all)] * (rows // MEMBERS), axis=0)
-    w_ff_all = lax.all_to_all(w_ff, "row", split_axis=0, concat_axis=0, tiled=True).reshape(width, 3 * ff)
+    w_ff = jnp.concatenate([w_ff] * (rows // MEMBERS), axis=0)
 
     input_f = tokens.astype(F32)
     act_scale = norm_scale(input_f)
@@ -662,7 +660,8 @@
     flag = jnp.concatenate([q_flag, kv_flag], axis=1)
     act_low, og_all = lax.optimization_barrier((act_low, og_all))
     raw, heads, kv_low = heads_call(act_low, w_all, gain, flag, cosine, sine, head_cols - q_width)
-    same_kv, other_kv = gather_earlier(kv_low, span)
+    same_kv, other_kv, w_ff = gather_earlier(kv_low, span, w_ff)
+    w_ff_all = lax.all_to_all(w_ff, "row", split_axis=0, concat_axis=0, tiled=True).reshape(width, 3 * ff)
 
     in_span = row % span
     seq_segments = lax.dynamic_slice_in_dim(segments, (row - in_span) * tok, seq_len, 0)
@@ -684,7 +683,8 @@
 
     ffn_scale = norm_scale(hidden)
     ffn_low = (hidden * ffn_scale * ffn_gain).astype(BF16)
-    ffn_all = jnp.concatenate(gather_cube(ffn_low), axis=0)
+    ffn_same, ffn_other, w_ff_all = gather_cube(ffn_low, w_ff_all)
+    ffn_all = jnp.concatenate([ffn_same, ffn_other], axis=0)
     gate_up = dot(ffn_all, w_ff_all[:, : 2 * ff])
     gate_pre, up_pre = gate_up[:, :ff], gate_up[:, ff:]
     d_inner = dot(og_all, w_ff_all[:, 2 * ff :])
@@ -777,12 +777,13 @@
     d_one = after(d_one, kv_partial)
     kv_partial = over_near(kv_partial)
     grads_ff = exchange_group(after(grads_ff, kv_partial))
-    for number in (cols, 2 * cols):
-        ffn_out = halve(ffn_out, 0, number)
+    ffn_out = halve(after(ffn_out, kv_partial), 0, cols)
+    grad_kv, grads_ff, ffn_out = lax.optimization_barrier(
+        (over_far(kv_partial, rows, True, True), grads_ff, halve(ffn_out, 0, 2 * cols))
+    )
     out_half = (hidden + ffn_out).astype(BF16)
     output = halves(out_half, swap_col(out_half), col)
-    grad_kv = add_up(over_far(kv_partial, rows, True, True))
-    grad_kv, grads_ff = lax.optimization_barrier((grad_kv, grads_ff))
+    grad_kv = add_up(grad_kv)
     act_back = dot(d_one, w_all[:, :head_cols], ((1,), (1,))).astype(BF16)
     act_back = act_back.astype(F32) + swap_col(act_back).astype(F32)
     input_grad = d_hidden_low.astype(F32) + norm_back(input_f, act_scale, attn_gain, act_back)

time: 457 us -> 451 us (0.987); the launches traced: 456 us -> 445 us
  local copies, waits for them, and re-layouts: 38.4 us -> 25.8 us
  other arithmetic: 39 us -> 46.2 us
    all_to_all x1, waiting for transfers between devices: 0.01 us -> 37 us  [body(): lax.all_to_all(w_ff, 'row', split_axis=0, concat_axis=0, tiled=True)]
    ppermute x19 -> x16, waiting for transfers between devices: 130 us -> 97.4 us  [swap_cube(): return lax.ppermute(block, ('row', 'col'), route)]
    ppermute x19 -> x16, starting transfers between devices: 43.8 us -> 29.9 us  [swap_cube(): return lax.ppermute(block, ('row', 'col'), route)]
    ppermute x9, waiting for transfers between devices: 15.7 us -> 3.25 us  [shift_far(): return lax.ppermute(block, 'row', route)]
    ppermute x9, starting transfers between devices: 13.8 us -> 24.3 us  [shift_far(): return lax.ppermute(block, 'row', route)]
    unnamed x104 -> x100, local copies, waits for them, and re-layouts: 19.9 us -> 12 us
    ppermute x5, waiting for transfers between devices: 11.9 us -> 16.9 us  [swap_near(): return lax.ppermute(block, 'row', [(i, i ^ 2) for i in range(rows)])]
  transfers between devices with their start and end apart: 53 -> 50, of which waited for: 26 -> 26; matrix products, arithmetic and copies ran while one was open for 18% -> 17% of each run, Pallas kernels for 8% -> 8%
where the time goes in v5:
time: 451 us; the launch traced here: 445 us
  waiting for transfers between devices  198 us (44%)
  starting transfers between devices  80.5 us (18%)
  other arithmetic  46.2 us (10%)
  Pallas kernels  45.5 us (10%)
  matrix products  30.7 us (7%)
  local copies, waits for them, and re-layouts  25.8 us (6%)
  between operations  18 us (4%)
    ppermute x16, waiting for transfers between devices, swap_cube(): return lax.ppermute(block, ('row', 'col'), route)  97.4 us
    all_to_all x1, waiting for transfers between devices, body(): lax.all_to_all(w_ff, 'row', split_axis=0, concat_axis=0, tiled=True)  37 us
    dot_general x9, matrix products, dot(): return lax.dot_general(a, b, (dims, ((), ())), preferred_element_type=F32)  30.7 us
    ppermute x16, starting transfers between devices, swap_cube(): return lax.ppermute(block, ('row', 'col'), route)  29.9 us
    ppermute x9, starting transfers between devices, shift_far(): return lax.ppermute(block, 'row', route)  24.3 us
    ppermute x5, waiting for transfers between devices, swap_near(): return lax.ppermute(block, 'row', [(i, i ^ 2) for i in range(rows)])  16.9 us
    all_to_all x1, waiting for transfers between devices, exchange_group(): lax.all_to_all(blocks, 'row', split_axis=0, concat_axis=0, tiled=True, ax...  14.2 us
    unnamed x100, local copies, waits for them, and re-layouts  12 us
  transfers between devices with their start and end apart: 50, of which 26 were waited for; matrix products, arithmetic and copies ran while one was open for 17% of the time, Pallas kernels for 8%

profile of v5, /device:TPU:0, one launch (start us, length us, event | category | flops | bytes accessed | tf_op | source)
XLA Modules:
  0.0 445.0 jit_solution(14740714514073620790)
XLA Ops:
  7.2 2.0 pack_weights.1
  9.3 1.7 constant_dynamic-update-slice_fusion.4
  11.0 3.0 collective-permute-start
  14.0 6.3 %collective-permute-done = bf16[64,2048]{1,0:T(8,128)(2,1)S(1)} collective-permute-done((bf16[64,2048]{1,0:T(8,128)(2,1)S(1)}, bf16[64,2048]{1,0:T(8,128)(2,1)S(1)}, u32[]{:S(2)}, u32[]{:S(2)}) %collective-permute-start) | collective-permute-done | bytes 262176 | tf_op jit(solution)/shard_map/ppermute | solution.py:56
  20.4 1.8 collective-permute-start.1
  22.1 16.0 %collective-permute-done.1 = bf16[128,2048]{1,0:T(8,128)(2,1)S(1)} collective-permute-done((bf16[128,2048]{1,0:T(8,128)(2,1)S(1)}, bf16[128,2048]{1,0:T(8,128)(2,1)S(1)}, u32[]{:S(2)}, u32[]{:S(2)}) %collective-permute-start.1) | collective-permute-done | bytes 524320 | tf_op jit(solution)/shard_map/ppermute | solution.py:56
  40.8 22.4 %collective-permute-done.2 = bf16[256,2048]{1,0:T(8,128)(2,1)S(1)} collective-permute-done((bf16[256,2048]{1,0:T(8,128)(2,1)}, bf16[256,2048]{1,0:T(8,128)(2,1)S(1)}, u32[]{:S(2)}, u32[]{:S(2)}) %collective-permute-start.2) | collective-permute-done | bytes 1048608 | tf_op jit(solution)/shard_map/ppermute | solution.py:56
  70.5 10.4 %all-gather.2.cloned.1.call-done.w_ref = bf16[2048,1664]{1,0:T(8,128)(2,1)} async-done(((bf16[128,1664]{1,0:T(8,128)(2,1)}), bf16[2048,1664]{1,0:T(8,128)(2,1)}) %all-gather.2.cloned.1.call-update) | async-done | bytes 6815760 | tf_op jit(solution)/shard_map/all_gather | solution.py:632
  80.9 5.7 %project_heads.1 = (f32[128,1024]{1,0:T(8,128)}, bf16[128,1024]{1,0:T(8,128)(2,1)}, bf16[128,384]{1,0:T(8,128)(2,1)}) custom-call(bf16[128,2048]{1,0:T(8,128)(2,1)} %multiply_convert_fusion.3.act_ref.left_ref, bf16[2048,1664]{1,0:T(8,128)(2,1)} %all-gather.2.cloned.1.call-done.w_ref, f32[1,1024]{1,0:T(1,128)} %pad_maximum_fusion.15.gain_ref, ...), custom_call_target="tpu_custom_call" | custom-call | flops 536870912 | bytes 4194304 | tf_op jit(solution)/shard_map/project_heads/pallas_call | solution.py:225
  86.6 3.9 collective-permute-start.6
  91.8 2.5 collective-permute-start.4
  94.3 1.8 collective-permute-done.5
  97.5 1.7 fusion.44
  101.8 2.2 pad_maximum_fusion
  104.0 6.0 %collective-permute-done.7 = bf16[4,128,384]{2,1,0:T(8,128)(2,1)} collective-permute-done((bf16[4,128,384]{2,1,0:T(8,128)(2,1)}, bf16[4,128,384]{2,1,0:T(8,128)(2,1)}, u32[]{:S(2)}, u32[]{:S(2)}) %collective-permute-start.7) | collective-permute-done | bytes 393248 | tf_op jit(solution)/shard_map/ppermute | solution.py:46
  111.1 7.6 %all-to-all-start = ((bf16[16,128,960]{1,2,0:T(8,128)(2,1)}), bf16[16,128,960]{1,2,0:T(8,128)(2,1)}, u32[]{:S(2)}, u32[]{:S(2)}) async-start(bf16[16,128,960]{1,2,0:T(8,128)(2,1)} %pad_maximum_fusion), calls=%async_computation | async-start | bytes 7864320 | tf_op jit(solution)/shard_map/all_to_all | solution.py:664
  124.9 4.2 attention_forward.1
  129.1 2.8 convolution_convert_fusion.3
  133.5 6.9 %collective-permute-done.9 = bf16[64,2048]{1,0:T(8,128)(2,1)S(1)} collective-permute-done((bf16[64,2048]{1,0:T(8,128)(2,1)S(1)}, bf16[64,2048]{1,0:T(8,128)(2,1)S(1)}, u32[]{:S(2)}, u32[]{:S(2)}) %collective-permute-start.9) | collective-permute-done | bytes 262176 | tf_op jit(solution)/shard_map/ppermute | solution.py:31
  143.6 5.5 %collective-permute-done.10 = bf16[64,2048]{1,0:T(8,128)(2,1)S(1)} collective-permute-done((bf16[64,2048]{1,0:T(8,128)(2,1)S(1)}, bf16[64,2048]{1,0:T(8,128)(2,1)S(1)}, u32[]{:S(2)}, u32[]{:S(2)}) %collective-permute-start.10) | collective-permute-done | bytes 262176 | tf_op jit(solution)/shard_map/ppermute | solution.py:56
  149.9 4.6 %collective-permute-start.13 = (bf16[2,64,2048]{2,1,0:T(8,128)(2,1)}, bf16[2,64,2048]{2,1,0:T(8,128)(2,1)S(1)}, u32[]{:S(2)}, u32[]{:S(2)}) collective-permute-start(bf16[2,64,2048]{2,1,0:T(8,128)(2,1)} %pad_maximum_fusion.7), channel_id=1, source_target_pairs={{0,12},{1,13},{2,14},{3,15},{4,8},{5,9},{6,10},{7,11},{8,4},{9,5},... | collective-permute-start | bytes 1572872 | tf_op jit(solution)/shard_map/ppermute | solution.py:56
  155.1 37.0 %all-to-all-done = bf16[16,128,960]{1,2,0:T(8,128)(2,1)} async-done(((bf16[16,128,960]{1,2,0:T(8,128)(2,1)}), bf16[16,128,960]{1,2,0:T(8,128)(2,1)}, u32[]{:S(2)}, u32[]{:S(2)}) %all-to-all-start) | async-done | bytes 3932192 | tf_op jit(solution)/shard_map/all_to_all | solution.py:664
  192.0 2.8 copy_bitcast_fusion
  194.9 2.6 collective-permute-done.13
  197.5 10.0 %collective-permute-done.11 = bf16[2,64,2048]{2,1,0:T(8,128)(2,1)S(1)} collective-permute-done((bf16[2,64,2048]{2,1,0:T(8,128)(2,1)}, bf16[2,64,2048]{2,1,0:T(8,128)(2,1)S(1)}, u32[]{:S(2)}, u32[]{:S(2)}) %collective-permute-start.11) | collective-permute-done | bytes 524320 | tf_op jit(solution)/shard_map/ppermute | solution.py:56
  208.0 4.0 collective-permute-done.14
  212.2 3.5 fusion.10
  215.7 5.8 %multiply_convert_fusion.1 = (bf16[1024,320]{1,0:T(8,128)(2,1)S(1)}, bf16[1024,320]{1,0:T(8,128)(2,1)S(1)}, bf16[1024,320]{1,0:T(8,128)(2,1)}) fusion(f32[1024,640]{1,0:T(8,128)S(1)} %fusion.10, bf16[1024,2048]{1,0:T(8,128)(2,1)} %constant_dynamic-update-slice_fusion.og_ref, bf16[2048,960]{0,1:T(8,128)(2,1)S(1)} %copy_bitcast_fusion), kind=kOutput, calls=%fused_computation.26 | convolution fusion | flops 1347092480 | bytes 10616832 | tf_op jit(solution)/shard_map/dot_general | solution.py:22
  221.5 1.8 convolution_convert_fusion.2
  225.0 2.5 collective-permute-done.15
  227.5 1.9 add_convert_fusion.1
  232.4 1.6 collective-permute-start.17
  234.0 11.2 %feed_forward_weight_grads.1 = bf16[16,960,128]{2,1,0:T(8,128)(2,1)} custom-call(bf16[1024,2048]{1,0:T(8,128)(2,1)} %copy-done.6, bf16[1024,2048]{1,0:T(8,128)(2,1)} %constant_dynamic-update-slice_fusion.og_ref, bf16[1024,640]{1,0:T(8,128)(2,1)} %pad_maximum_fusion.2.d_ref, bf16[1024,320]{1,0:T(8,128)(2,1)} %get-tuple-element.102.inner_ref), custom_call_target="tpu_custom_call" | custom-call | tf_op jit(solution)/shard_map/feed_forward_weight_grads/pallas_call | solution.py:342
  249.3 1.7 collective-permute-start.18
  250.9 5.1 %collective-permute-start.19 = (bf16[2,64,1024]{2,1,0:T(8,128)(2,1)S(1)}, bf16[2,64,1024]{2,1,0:T(8,128)(2,1)S(1)}, u32[]{:S(2)}, u32[]{:S(2)}) collective-permute-start(bf16[2,64,1024]{2,1,0:T(8,128)(2,1)S(1)} %slice_bitcast_fusion.8), channel_id=1, source_target_pairs={{0,8},{1,9},{2,10},{3,11},{4,12},{5,13},{6,14},{7,15},{8,0},{9,1},... | collective-permute-start | bytes 786440 | tf_op jit(solution)/shard_map/ppermute | solution.py:56
  256.1 4.0 convolution_convert_fusion
  260.0 4.2 convolution_convert_fusion.1
  266.4 3.0 collective-permute-done.21
  269.5 2.4 collective-permute-done.20
  272.3 1.9 collective-permute-start.22
  274.8 3.9 collective-permute-done.22
  278.8 3.1 fusion.13.grad_ref
  281.9 6.7 %attention_backward.1 = (bf16[128,640]{1,0:T(8,128)(2,1)}, f32[1,128]{1,0:T(1,128)}, bf16[2,4,128,384]{3,2,1,0:T(8,128)(2,1)}, bf16[2,4,128,384]{3,2,1,0:T(8,128)(2,1)}) custom-call(s32[2]{0:T(128)} %pad_add_fusion.1.bounds_ref, s32[2,128]{1,0:T(2,128)} %pad_add_fusion.limits_ref, bf16[128,1024]{1,0:T(8,128)(2,1)} %get-tuple-element.81.q_ref, ...), custom_call_target="tpu_custom_call" | custom-call | tf_op jit(solution)/shard_map/attention_backward/pallas_call | solution.py:525
  293.2 3.2 weight_rows.3
  298.6 3.1 weight_rows.4
  301.8 3.0 add_convert_fusion
  304.9 1.8 collective-permute-start.31
  306.8 1.6 add_convert_fusion.3
  317.0 13.6 %collective-permute-done.31 = bf16[2,2,64,2048]{3,2,1,0:T(8,128)(2,1)S(1)} collective-permute-done((bf16[2,2,64,2048]{3,2,1,0:T(8,128)(2,1)S(1)}, bf16[2,2,64,2048]{3,2,1,0:T(8,128)(2,1)S(1)}, u32[]{:S(2)}, u32[]{:S(2)}) %collective-permute-start.31) | collective-permute-done | bytes 1048608 | tf_op jit(solution)/shard_map/ppermute | solution.py:56
  332.6 2.5 key_value_heads_back.1
  336.9 2.8 weight_rows.5
  341.2 6.1 %collective-permute-done.42 = bf16[4,128,640]{2,1,0:T(8,128)(2,1)} collective-permute-done((bf16[4,128,640]{2,1,0:T(8,128)(2,1)}, bf16[4,128,640]{2,1,0:T(8,128)(2,1)}, u32[]{:S(2)}, u32[]{:S(2)}) %collective-permute-start.42) | collective-permute-done | bytes 655392 | tf_op jit(solution)/shard_map/ppermute | solution.py:46
  349.8 1.7 add_convert_fusion.4
  352.7 3.7 fusion.2
  356.5 1.7 collective-permute-start.40
  358.2 4.5 %collective-permute-done.33 = bf16[4,144,384]{2,1,0:T(8,128)(2,1)S(1)} collective-permute-done((bf16[4,144,384]{2,1,0:T(8,128)(2,1)S(1)}, bf16[4,144,384]{2,1,0:T(8,128)(2,1)S(1)}, u32[]{:S(2)}, u32[]{:S(2)}) %collective-permute-start.33) | collective-permute-done | bytes 442400 | tf_op jit(solution)/shard_map/ppermute | solution.py:46
  364.8 11.4 %collective-permute-start.36 = (bf16[144,384]{1,0:T(8,128)(2,1)}, bf16[144,384]{1,0:T(8,128)(2,1)}, u32[]{:S(2)}, u32[]{:S(2)}) collective-permute-start(bf16[144,384]{1,0:T(8,128)(2,1)} %get-tuple-element.236), channel_id=1, source_target_pairs={{0,24},{2,26},{4,28},{6,30},{8,0},{10,2},{12,4},{14,6},{16,8},{18,... | collective-permute-start | bytes 331784 | tf_op jit(solution)/shard_map/ppermute | solution.py:41
  379.6 2.3 collective-permute-start.38
  383.5 3.6 all-to-all-start.1
  387.1 14.5 %collective-permute-done.38 = bf16[64,2048]{1,0:T(8,128)(2,1)} collective-permute-done((bf16[64,2048]{1,0:T(8,128)(2,1)}, bf16[64,2048]{1,0:T(8,128)(2,1)}, u32[]{:S(2)}, u32[]{:S(2)}) %collective-permute-start.38) | collective-permute-done | bytes 262176 | tf_op jit(solution)/shard_map/ppermute | solution.py:56
  405.6 1.9 copy.89
  407.5 14.2 %all-to-all-done.1.in_ref = bf16[8,960,128]{2,1,0:T(8,128)(2,1)S(1)} async-done(((bf16[8,960,128]{2,1,0:T(8,128)(2,1)}), bf16[8,960,128]{2,1,0:T(8,128)(2,1)S(1)}, u32[]{:S(2)}, u32[]{:S(2)}) %all-to-all-start.1) | async-done | bytes 1966112 | tf_op jit(solution)/shard_map/all_to_all | solution.py:159
  421.7 1.6 convert_add_fusion.8
  428.9 4.2 feed_forward_grads.1
  (274 shorter events, 84.6 us)
Async XLA Ops:
  7.2 73.7 %all-gather.2.cloned.1.call-start = ((), (), s32[]{:S(2)}) async-start(), calls=%async_computation.4 | async-start | bytes 7241728 | tf_op jit(solution)/shard_map/all_gather | solution.py:632
  9.2 31.3 %copy-start.31 = (s32[128]{0:T(128)S(1)}, s32[128]{0:T(128)}, u32[]{:S(2)}) copy-start(s32[128]{0:T(128)} %param.26) | copy-start | bytes 1540
  9.2 31.3 %copy-start.33 = (f32[64]{0:T(128)S(1)}, f32[64]{0:T(128)}, u32[]{:S(2)}) copy-start(f32[64]{0:T(128)} %param.23) | copy-start | bytes 772
  9.2 31.4 %copy-start.32 = (f32[64]{0:T(128)S(1)}, f32[64]{0:T(128)}, u32[]{:S(2)}) copy-start(f32[64]{0:T(128)} %param.24) | copy-start | bytes 772
  9.2 31.5 %copy-start.30 = (pred[3,128]{1,0:T(4,128)(4,1)S(1)}, pred[3,128]{1,0:T(4,128)(4,1)}, u32[]{:S(2)}) copy-start(pred[3,128]{1,0:T(4,128)(4,1)} %constant.199.clone.1) | copy-start | bytes 1156
  11.0 9.3 %collective-permute-start = (bf16[64,2048]{1,0:T(8,128)(2,1)S(1)}, bf16[64,2048]{1,0:T(8,128)(2,1)S(1)}, u32[]{:S(2)}, u32[]{:S(2)}) collective-permute-start(bf16[64,2048]{1,0:T(8,128)(2,1)S(1)} %get-tuple-element.215), channel_id=1, source_target_pairs={{0,8},{1,9},{2,10},{3,11},{4,12},{5,13},{6,14},{7,15},{8,0},{9,1},... | collective-permute-start | bytes 786440 | tf_op jit(solution)/shard_map/ppermute | solution.py:56
  20.4 17.7 %collective-permute-start.1 = (bf16[128,2048]{1,0:T(8,128)(2,1)S(1)}, bf16[128,2048]{1,0:T(8,128)(2,1)S(1)}, u32[]{:S(2)}, u32[]{:S(2)}) collective-permute-start(bf16[128,2048]{1,0:T(8,128)(2,1)S(1)} %pad_maximum_fusion.6), channel_id=1, source_target_pairs={{0,4},{1,5},{2,6},{3,7},{4,0},{5,1},{6,2},{7,3},{8,12},{9,13},{10,... | collective-permute-start | bytes 1572872 | tf_op jit(solution)/shard_map/ppermute | solution.py:56
  39.2 24.0 %collective-permute-start.2 = (bf16[256,2048]{1,0:T(8,128)(2,1)}, bf16[256,2048]{1,0:T(8,128)(2,1)S(1)}, u32[]{:S(2)}, u32[]{:S(2)}) collective-permute-start(bf16[256,2048]{1,0:T(8,128)(2,1)} %pad_maximum_fusion.4), channel_id=1, source_target_pairs={{0,1},{1,0},{2,3},{3,2},{4,5},{5,4},{6,7},{7,6},{8,9},{9,8},{10,11... | collective-permute-start | bytes 3145736 | tf_op jit(solution)/shard_map/ppermute | solution.py:56
  40.7 22.7 %copy-start.28 = (f32[1,1,3,128]{3,1,2,0:T(1,128)}, f32[1,1,3,128]{3,1,2,0:T(1,128)S(1)}, u32[]{:S(2)}) copy-start(f32[1,1,3,128]{3,1,2,0:T(1,128)S(1)} %copy.106) | copy-start | bytes 4612
  40.7 24.5 %copy-start = (bf16[128,2048]{1,0:T(8,128)(2,1)S(1)}, bf16[128,2048]{1,0:T(8,128)(2,1)}, u32[]{:S(2)}) copy-start(bf16[128,2048]{1,0:T(8,128)(2,1)} %param.14) | copy-start | bytes 1572868
  40.8 24.6 %copy-start.25 = (f32[2048]{0:T(1024)S(1)}, f32[2048]{0:T(1024)}, u32[]{:S(2)}) copy-start(f32[2048]{0:T(1024)} %param.21) | copy-start | bytes 24580
  63.4 5.7 %collective-permute-start.3 = (bf16[512,2048]{1,0:T(8,128)(2,1)S(1)}, bf16[512,2048]{1,0:T(8,128)(2,1)S(1)}, u32[]{:S(2)}, u32[]{:S(2)}) collective-permute-start(bf16[512,2048]{1,0:T(8,128)(2,1)S(1)} %pad_maximum_fusion.1), channel_id=1, source_target_pairs={{0,2},{2,0},{4,6},{6,4},{8,10},{10,8},{12,14},{14,12},{16,18},{18,... | collective-permute-start | bytes 6291464 | tf_op jit(solution)/shard_map/ppermute | solution.py:27
  80.9 19.0 %copy-start.18 = (bf16[128,2560]{1,0:T(8,128)(2,1)S(1)}, bf16[128,2560]{1,0:T(8,128)(2,1)}, u32[]{:S(2)}) copy-start(bf16[128,2560]{1,0:T(8,128)(2,1)} %param.18) | copy-start | bytes 1966084
  86.6 13.6 %copy-start.19 = (bf16[128,2560]{1,0:T(8,128)(2,1)S(1)}, bf16[128,2560]{1,0:T(8,128)(2,1)}, u32[]{:S(2)}) copy-start(bf16[128,2560]{1,0:T(8,128)(2,1)} %param.19) | copy-start | bytes 1966084
  86.6 7.7 %collective-permute-start.6 = (bf16[128,384]{1,0:T(8,128)(2,1)}, bf16[128,384]{1,0:T(8,128)(2,1)S(1)}, u32[]{:S(2)}, u32[]{:S(2)}) collective-permute-start(bf16[128,384]{1,0:T(8,128)(2,1)} %get-tuple-element.82), channel_id=1, source_target_pairs={{0,24},{2,26},{4,28},{6,30},{1,25},{3,27},{5,29},{7,31}} | collective-permute-start | bytes 294920 | tf_op jit(solution)/shard_map/ppermute | solution.py:41
  90.5 5.6 %collective-permute-start.5 = (bf16[128,384]{1,0:T(8,128)(2,1)}, bf16[128,384]{1,0:T(8,128)(2,1)S(1)}, u32[]{:S(2)}, u32[]{:S(2)}) collective-permute-start(bf16[128,384]{1,0:T(8,128)(2,1)} %get-tuple-element.82), channel_id=1, source_target_pairs={{0,16},{2,18},{4,20},{6,22},{8,24},{10,26},{12,28},{14,30},{1,17},... | collective-permute-start | bytes 294920 | tf_op jit(solution)/shard_map/ppermute | solution.py:41
  91.8 5.7 %collective-permute-start.4 = (bf16[128,384]{1,0:T(8,128)(2,1)}, bf16[128,384]{1,0:T(8,128)(2,1)S(1)}, u32[]{:S(2)}, u32[]{:S(2)}) collective-permute-start(bf16[128,384]{1,0:T(8,128)(2,1)} %get-tuple-element.82), channel_id=1, source_target_pairs={{0,8},{2,10},{4,12},{6,14},{8,16},{10,18},{12,20},{14,22},{16,24},... | collective-permute-start | bytes 294920 | tf_op jit(solution)/shard_map/ppermute | solution.py:41
  99.2 10.8 %collective-permute-start.7 = (bf16[4,128,384]{2,1,0:T(8,128)(2,1)}, bf16[4,128,384]{2,1,0:T(8,128)(2,1)}, u32[]{:S(2)}, u32[]{:S(2)}) collective-permute-start(bf16[4,128,384]{2,1,0:T(8,128)(2,1)} %get-tuple-element.247), channel_id=1, source_target_pairs={{0,4},{2,6},{4,0},{6,2},{8,12},{10,14},{12,8},{14,10},{16,20},{18,... | collective-permute-start | bytes 1179656 | tf_op jit(solution)/shard_map/ppermute | solution.py:46
  111.1 80.9 %all-to-all-start = ((bf16[16,128,960]{1,2,0:T(8,128)(2,1)}), bf16[16,128,960]{1,2,0:T(8,128)(2,1)}, u32[]{:S(2)}, u32[]{:S(2)}) async-start(bf16[16,128,960]{1,2,0:T(8,128)(2,1)} %pad_maximum_fusion), calls=%async_computation | async-start | bytes 7864320 | tf_op jit(solution)/shard_map/all_to_all | solution.py:664
  118.7 264.8 %reduce-scatter.3.cloned.1.call-start = ((), (), s32[]{:S(2)}) async-start(), calls=%async_computation.5 | async-start | bytes 5898240 | tf_op jit(solution)/shard_map/reduce_scatter | solution.py:711
  118.8 5.3 %collective-permute-start.8 = (bf16[2,4,128,384]{3,2,1,0:T(8,128)(2,1)S(1)}, bf16[2,4,128,384]{3,2,1,0:T(8,128)(2,1)S(1)}, u32[]{:S(2)}, u32[]{:S(2)}) collective-permute-start(bf16[2,4,128,384]{3,2,1,0:T(8,128)(2,1)S(1)} %pad_maximum_fusion.5.same_ref), channel_id=1, source_target_pairs={{0,2},{2,0},{4,6},{6,4},{8,10},{10,8},{12,14},{14,12},{16,18},{18,... | collective-permute-start | bytes 2359304 | tf_op jit(solution)/shard_map/ppermute | solution.py:27
  132.0 8.4 %collective-permute-start.9 = (bf16[64,2048]{1,0:T(8,128)(2,1)S(1)}, bf16[64,2048]{1,0:T(8,128)(2,1)S(1)}, u32[]{:S(2)}, u32[]{:S(2)}) collective-permute-start(bf16[64,2048]{1,0:T(8,128)(2,1)S(1)} %constant_dynamic-slice_fusion), channel_id=1, source_target_pairs={{0,1},{1,0},{2,3},{3,2},{4,5},{5,4},{6,7},{7,6},{8,9},{9,8},{10,11... | collective-permute-start | bytes 786440 | tf_op jit(solution)/shard_map/ppermute | solution.py:31
  141.4 7.6 %collective-permute-start.10 = (bf16[64,2048]{1,0:T(8,128)(2,1)S(1)}, bf16[64,2048]{1,0:T(8,128)(2,1)S(1)}, u32[]{:S(2)}, u32[]{:S(2)}) collective-permute-start(bf16[64,2048]{1,0:T(8,128)(2,1)S(1)} %get-tuple-element.211), channel_id=1, source_target_pairs={{0,1},{1,0},{2,3},{3,2},{4,5},{5,4},{6,7},{7,6},{8,9},{9,8},{10,11... | collective-permute-start | bytes 786440 | tf_op jit(solution)/shard_map/ppermute | solution.py:56
  149.9 47.6 %collective-permute-start.13 = (bf16[2,64,2048]{2,1,0:T(8,128)(2,1)}, bf16[2,64,2048]{2,1,0:T(8,128)(2,1)S(1)}, u32[]{:S(2)}, u32[]{:S(2)}) collective-permute-start(bf16[2,64,2048]{2,1,0:T(8,128)(2,1)} %pad_maximum_fusion.7), channel_id=1, source_target_pairs={{0,12},{1,13},{2,14},{3,15},{4,8},{5,9},{6,10},{7,11},{8,4},{9,5},... | collective-permute-start | bytes 1572872 | tf_op jit(solution)/shard_map/ppermute | solution.py:56
  154.5 43.0 %collective-permute-start.12 = (bf16[2,64,2048]{2,1,0:T(8,128)(2,1)}, bf16[2,64,2048]{2,1,0:T(8,128)(2,1)S(1)}, u32[]{:S(2)}, u32[]{:S(2)}) collective-permute-start(bf16[2,64,2048]{2,1,0:T(8,128)(2,1)} %pad_maximum_fusion.7), channel_id=1, source_target_pairs={{0,4},{1,5},{2,6},{3,7},{4,0},{5,1},{6,2},{7,3},{8,12},{9,13},{10,... | collective-permute-start | bytes 1572872 | tf_op jit(solution)/shard_map/ppermute | solution.py:56
  155.0 52.5 %collective-permute-start.11 = (bf16[2,64,2048]{2,1,0:T(8,128)(2,1)}, bf16[2,64,2048]{2,1,0:T(8,128)(2,1)S(1)}, u32[]{:S(2)}, u32[]{:S(2)}) collective-permute-start(bf16[2,64,2048]{2,1,0:T(8,128)(2,1)} %pad_maximum_fusion.7), channel_id=1, source_target_pairs={{0,8},{1,9},{2,10},{3,11},{4,12},{5,13},{6,14},{7,15},{8,0},{9,1},... | collective-permute-start | bytes 1572872 | tf_op jit(solution)/shard_map/ppermute | solution.py:56
  192.0 15.5 %copy-start.27 = (bf16[512,2048]{1,0:T(8,128)(2,1)S(1)}, bf16[512,2048]{1,0:T(8,128)(2,1)}, u32[]{:S(2)}) copy-start(bf16[512,2048]{1,0:T(8,128)(2,1)} %get-tuple-element.210) | copy-start | bytes 6291460
  192.0 15.6 %copy-start.5 = (bf16[1024,2048]{1,0:T(8,128)(2,1)S(1)}, bf16[1024,2048]{1,0:T(8,128)(2,1)}, u32[]{:S(2)}) copy-start(bf16[1024,2048]{1,0:T(8,128)(2,1)} %constant_dynamic-update-slice_fusion.9) | copy-start | bytes 12582916
  194.9 32.7 %copy-start.7 = (bf16[2048,960]{0,1:T(8,128)(2,1)}, bf16[2048,960]{0,1:T(8,128)(2,1)S(1)}, u32[]{:S(2)}) copy-start(bf16[2048,960]{0,1:T(8,128)(2,1)S(1)} %copy_bitcast_fusion) | copy-start | bytes 11796484
  207.8 4.2 collective-permute-start.14
  223.3 4.2 collective-permute-start.15
  231.0 14.2 %collective-permute-start.16 = (bf16[2,2,64,1024]{3,2,1,0:T(8,128)(2,1)S(1)}, bf16[2,2,64,1024]{3,2,1,0:T(8,128)(2,1)S(1)}, u32[]{:S(2)}, u32[]{:S(2)}) collective-permute-start(bf16[2,2,64,1024]{3,2,1,0:T(8,128)(2,1)S(1)} %slice_bitcast_fusion.2), channel_id=1, source_target_pairs={{0,1},{1,0},{2,3},{3,2},{4,5},{5,4},{6,7},{7,6},{8,9},{9,8},{10,11... | collective-permute-start | bytes 1572872 | tf_op jit(solution)/shard_map/ppermute | solution.py:56
  232.4 14.0 %collective-permute-start.17 = (bf16[2,2,64,1024]{3,2,0,1:T(8,128)(2,1)}, bf16[2,2,64,1024]{3,2,0,1:T(8,128)(2,1)}, u32[]{:S(2)}, u32[]{:S(2)}) collective-permute-start(bf16[2,2,64,1024]{3,2,0,1:T(8,128)(2,1)} %bitcast.184), channel_id=1, source_target_pairs={{0,4},{1,5},{2,6},{3,7},{4,0},{5,1},{6,2},{7,3},{8,12},{9,13},{10,... | collective-permute-start | bytes 1572872 | tf_op jit(solution)/shard_map/ppermute | solution.py:56
  247.7 155.0 %reduce-scatter.5.cloned.1.call-start = ((), (), s32[]{:S(2)}) async-start(), calls=%async_computation.6 | async-start | bytes 1638400 | tf_op jit(solution)/shard_map/reduce_scatter | solution.py:760
  249.3 15.0 %collective-permute-start.18 = (bf16[2,64,1024]{2,1,0:T(8,128)(2,1)S(1)}, bf16[2,64,1024]{2,1,0:T(8,128)(2,1)S(1)}, u32[]{:S(2)}, u32[]{:S(2)}) collective-permute-start(bf16[2,64,1024]{2,1,0:T(8,128)(2,1)S(1)} %slice_bitcast_fusion.9), channel_id=1, source_target_pairs={{0,4},{1,5},{2,6},{3,7},{4,0},{5,1},{6,2},{7,3},{8,12},{9,13},{10,... | collective-permute-start | bytes 786440 | tf_op jit(solution)/shard_map/ppermute | solution.py:56
  250.9 13.3 %collective-permute-start.19 = (bf16[2,64,1024]{2,1,0:T(8,128)(2,1)S(1)}, bf16[2,64,1024]{2,1,0:T(8,128)(2,1)S(1)}, u32[]{:S(2)}, u32[]{:S(2)}) collective-permute-start(bf16[2,64,1024]{2,1,0:T(8,128)(2,1)S(1)} %slice_bitcast_fusion.8), channel_id=1, source_target_pairs={{0,8},{1,9},{2,10},{3,11},{4,12},{5,13},{6,14},{7,15},{8,0},{9,1},... | collective-permute-start | bytes 786440 | tf_op jit(solution)/shard_map/ppermute | solution.py:56
  264.4 5.0 %collective-permute-start.21 = (bf16[64,1024]{1,0:T(8,128)(2,1)S(1)}, bf16[64,1024]{1,0:T(8,128)(2,1)S(1)}, u32[]{:S(2)}, u32[]{:S(2)}) collective-permute-start(bf16[64,1024]{1,0:T(8,128)(2,1)S(1)} %slice_bitcast_fusion.11), channel_id=1, source_target_pairs={{0,1},{1,0},{2,3},{3,2},{4,5},{5,4},{6,7},{7,6},{8,9},{9,8},{10,11... | collective-permute-start | bytes 393224 | tf_op jit(solution)/shard_map/ppermute | solution.py:56
  265.1 6.7 %collective-permute-start.20 = (bf16[64,1024]{1,0:T(8,128)(2,1)S(1)}, bf16[64,1024]{1,0:T(8,128)(2,1)S(1)}, u32[]{:S(2)}, u32[]{:S(2)}) collective-permute-start(bf16[64,1024]{1,0:T(8,128)(2,1)S(1)} %slice_bitcast_fusion.13), channel_id=1, source_target_pairs={{0,8},{1,9},{2,10},{3,11},{4,12},{5,13},{6,14},{7,15},{8,0},{9,1},... | collective-permute-start | bytes 393224 | tf_op jit(solution)/shard_map/ppermute | solution.py:56
  272.3 6.4 %collective-permute-start.22 = (bf16[64,2048]{1,0:T(8,128)(2,1)S(1)}, bf16[64,2048]{1,0:T(8,128)(2,1)S(1)}, u32[]{:S(2)}, u32[]{:S(2)}) collective-permute-start(bf16[64,2048]{1,0:T(8,128)(2,1)S(1)} %add_convert_fusion.10), channel_id=1, source_target_pairs={{0,1},{1,0},{2,3},{3,2},{4,5},{5,4},{6,7},{7,6},{8,9},{9,8},{10,11... | collective-permute-start | bytes 786440 | tf_op jit(solution)/shard_map/ppermute | solution.py:31
  274.8 27.0 %collective-permute-start.30 = (bf16[512,2048]{1,0:T(8,128)(2,1)}, bf16[512,2048]{1,0:T(8,128)(2,1)}, u32[]{:S(2)}, u32[]{:S(2)}) collective-permute-start(bf16[512,2048]{1,0:T(8,128)(2,1)} %convolution_convert_fusion.1), channel_id=1, source_target_pairs={{0,2},{2,0},{4,6},{6,4},{8,10},{10,8},{12,14},{14,12},{16,18},{18,... | collective-permute-start | bytes 6291464 | tf_op jit(solution)/shard_map/ppermute | solution.py:27
  288.5 2.5 collective-permute-start.23
  296.4 10.4 %collective-permute-start.25 = (bf16[8,128,640]{2,1,0:T(8,128)(2,1)}, bf16[8,128,640]{2,1,0:T(8,128)(2,1)}, u32[]{:S(2)}, u32[]{:S(2)}) collective-permute-start(bf16[8,128,640]{2,1,0:T(8,128)(2,1)} %get-tuple-element.113), channel_id=1, source_target_pairs={{0,2},{2,0},{4,6},{6,4},{8,10},{10,8},{12,14},{14,12},{16,18},{18,... | collective-permute-start | bytes 3932168 | tf_op jit(solution)/shard_map/ppermute | solution.py:27
  297.5 11.7 %collective-permute-start.24 = (bf16[4,128,384]{2,1,0:T(8,128)(2,1)}, bf16[4,128,384]{2,1,0:T(8,128)(2,1)S(1)}, u32[]{:S(2)}, u32[]{:S(2)}) collective-permute-start(bf16[4,128,384]{2,1,0:T(8,128)(2,1)} %slice_bitcast_fusion.4), channel_id=1, source_target_pairs={{0,4},{2,6},{4,0},{6,2},{8,12},{10,14},{12,8},{14,10},{16,20},{18,... | collective-permute-start | bytes 1179656 | tf_op jit(solution)/shard_map/ppermute | solution.py:46
  301.7 6.7 %collective-permute-start.26 = (bf16[8,128,640]{2,1,0:T(8,128)(2,1)}, bf16[8,128,640]{2,1,0:T(8,128)(2,1)S(1)}, u32[]{:S(2)}, u32[]{:S(2)}) collective-permute-start(bf16[8,128,640]{2,1,0:T(8,128)(2,1)} %get-tuple-element.117), channel_id=1, source_target_pairs={{0,2},{2,0},{4,6},{6,4},{8,10},{10,8},{12,14},{14,12},{16,18},{18,... | collective-permute-start | bytes 3932168 | tf_op jit(solution)/shard_map/ppermute | solution.py:27
  304.9 25.6 %collective-permute-start.31 = (bf16[2,2,64,2048]{3,2,1,0:T(8,128)(2,1)S(1)}, bf16[2,2,64,2048]{3,2,1,0:T(8,128)(2,1)S(1)}, u32[]{:S(2)}, u32[]{:S(2)}) collective-permute-start(bf16[2,2,64,2048]{3,2,1,0:T(8,128)(2,1)S(1)} %slice_bitcast_fusion), channel_id=1, source_target_pairs={{0,1},{1,0},{2,3},{3,2},{4,5},{5,4},{6,7},{7,6},{8,9},{9,8},{10,11... | collective-permute-start | bytes 3145736 | tf_op jit(solution)/shard_map/ppermute | solution.py:56
  309.9 22.0 %collective-permute-start.29 = (bf16[128,384]{1,0:T(8,128)(2,1)S(1)}, bf16[128,384]{1,0:T(8,128)(2,1)S(1)}, u32[]{:S(2)}, u32[]{:S(2)}) collective-permute-start(bf16[128,384]{1,0:T(8,128)(2,1)S(1)} %get-tuple-element.242), channel_id=1, source_target_pairs={{24,0},{26,2},{28,4},{30,6},{25,1},{27,3},{29,5},{31,7}} | collective-permute-start | bytes 294920 | tf_op jit(solution)/shard_map/ppermute | solution.py:41
  311.2 20.7 %collective-permute-start.28 = (bf16[128,384]{1,0:T(8,128)(2,1)S(1)}, bf16[128,384]{1,0:T(8,128)(2,1)S(1)}, u32[]{:S(2)}, u32[]{:S(2)}) collective-permute-start(bf16[128,384]{1,0:T(8,128)(2,1)S(1)} %get-tuple-element.243), channel_id=1, source_target_pairs={{16,0},{18,2},{20,4},{22,6},{24,8},{26,10},{28,12},{30,14},{17,1},... | collective-permute-start | bytes 294920 | tf_op jit(solution)/shard_map/ppermute | solution.py:41
  312.5 19.5 %collective-permute-start.27 = (bf16[128,384]{1,0:T(8,128)(2,1)S(1)}, bf16[128,384]{1,0:T(8,128)(2,1)S(1)}, u32[]{:S(2)}, u32[]{:S(2)}) collective-permute-start(bf16[128,384]{1,0:T(8,128)(2,1)S(1)} %get-tuple-element.244), channel_id=1, source_target_pairs={{8,0},{10,2},{12,4},{14,6},{16,8},{18,10},{20,12},{22,14},{24,16},... | collective-permute-start | bytes 294920 | tf_op jit(solution)/shard_map/ppermute | solution.py:41
  315.9 23.8 %collective-permute-start.41 = (bf16[4,128,640]{2,1,0:T(8,128)(2,1)}, bf16[4,128,640]{2,1,0:T(8,128)(2,1)}, u32[]{:S(2)}, u32[]{:S(2)}) collective-permute-start(bf16[4,128,640]{2,1,0:T(8,128)(2,1)} %slice.330), channel_id=1, source_target_pairs={{0,4},{2,6},{4,0},{6,2},{8,12},{10,14},{12,8},{14,10},{16,20},{18,... | collective-permute-start | bytes 1966088 | tf_op jit(solution)/shard_map/ppermute | solution.py:46
  330.5 16.8 %collective-permute-start.42 = (bf16[4,128,640]{2,1,0:T(8,128)(2,1)}, bf16[4,128,640]{2,1,0:T(8,128)(2,1)}, u32[]{:S(2)}, u32[]{:S(2)}) collective-permute-start(bf16[4,128,640]{2,1,0:T(8,128)(2,1)} %slice.332), channel_id=1, source_target_pairs={{0,4},{2,6},{4,0},{6,2},{8,12},{10,14},{12,8},{14,10},{16,20},{18,... | collective-permute-start | bytes 1966088 | tf_op jit(solution)/shard_map/ppermute | solution.py:46
  336.1 11.3 %copy-start.4 = (bf16[8,128,640]{2,1,0:T(8,128)(2,1)S(1)}, bf16[8,128,640]{2,1,0:T(8,128)(2,1)}, u32[]{:S(2)}) copy-start(bf16[8,128,640]{2,1,0:T(8,128)(2,1)} %copy-done.3) | copy-start | bytes 3932164
  339.7 10.1 %collective-permute-start.32 = (bf16[8,144,384]{2,1,0:T(8,128)(2,1)}, bf16[8,144,384]{2,1,0:T(8,128)(2,1)}, u32[]{:S(2)}, u32[]{:S(2)}) collective-permute-start(bf16[8,144,384]{2,1,0:T(8,128)(2,1)} %get-tuple-element.130), channel_id=1, source_target_pairs={{0,2},{2,0},{4,6},{6,4},{8,10},{10,8},{12,14},{14,12},{16,18},{18,... | collective-permute-start | bytes 2654216 | tf_op jit(solution)/shard_map/ppermute | solution.py:27
  351.5 11.1 %collective-permute-start.33 = (bf16[4,144,384]{2,1,0:T(8,128)(2,1)S(1)}, bf16[4,144,384]{2,1,0:T(8,128)(2,1)S(1)}, u32[]{:S(2)}, u32[]{:S(2)}) collective-permute-start(bf16[4,144,384]{2,1,0:T(8,128)(2,1)S(1)} %slice.389), channel_id=1, source_target_pairs={{0,4},{2,6},{4,0},{6,2},{8,12},{10,14},{12,8},{14,10},{16,20},{18,... | collective-permute-start | bytes 1327112 | tf_op jit(solution)/shard_map/ppermute | solution.py:46
  356.5 21.0 %collective-permute-start.40 = (bf16[128,2048]{1,0:T(8,128)(2,1)S(1)}, bf16[128,2048]{1,0:T(8,128)(2,1)S(1)}, u32[]{:S(2)}, u32[]{:S(2)}) collective-permute-start(bf16[128,2048]{1,0:T(8,128)(2,1)S(1)} %fusion.2), channel_id=1, source_target_pairs={{0,1},{1,0},{2,3},{3,2},{4,5},{5,4},{6,7},{7,6},{8,9},{9,8},{10,11... | collective-permute-start | bytes 1572872 | tf_op jit(solution)/shard_map/ppermute | solution.py:31
  362.8 15.0 %collective-permute-start.37 = (bf16[2,64,2048]{2,1,0:T(8,128)(2,1)S(1)}, bf16[2,64,2048]{2,1,0:T(8,128)(2,1)S(1)}, u32[]{:S(2)}, u32[]{:S(2)}) collective-permute-start(bf16[2,64,2048]{2,1,0:T(8,128)(2,1)S(1)} %fusion.27), channel_id=1, source_target_pairs={{0,4},{1,5},{2,6},{3,7},{4,0},{5,1},{6,2},{7,3},{8,12},{9,13},{10,... | collective-permute-start | bytes 1572872 | tf_op jit(solution)/shard_map/ppermute | solution.py:56
  364.8 42.6 %collective-permute-start.36 = (bf16[144,384]{1,0:T(8,128)(2,1)}, bf16[144,384]{1,0:T(8,128)(2,1)}, u32[]{:S(2)}, u32[]{:S(2)}) collective-permute-start(bf16[144,384]{1,0:T(8,128)(2,1)} %get-tuple-element.236), channel_id=1, source_target_pairs={{0,24},{2,26},{4,28},{6,30},{8,0},{10,2},{12,4},{14,6},{16,8},{18,... | collective-permute-start | bytes 331784 | tf_op jit(solution)/shard_map/ppermute | solution.py:41
  376.3 31.2 %collective-permute-start.35 = (bf16[144,384]{1,0:T(8,128)(2,1)}, bf16[144,384]{1,0:T(8,128)(2,1)}, u32[]{:S(2)}, u32[]{:S(2)}) collective-permute-start(bf16[144,384]{1,0:T(8,128)(2,1)} %get-tuple-element.237), channel_id=1, source_target_pairs={{0,16},{2,18},{4,20},{6,22},{8,24},{10,26},{12,28},{14,30},{16,0},... | collective-permute-start | bytes 331784 | tf_op jit(solution)/shard_map/ppermute | solution.py:41
  376.3 31.2 %collective-permute-start.34 = (bf16[144,384]{1,0:T(8,128)(2,1)}, bf16[144,384]{1,0:T(8,128)(2,1)}, u32[]{:S(2)}, u32[]{:S(2)}) collective-permute-start(bf16[144,384]{1,0:T(8,128)(2,1)} %get-tuple-element.238), channel_id=1, source_target_pairs={{0,8},{2,10},{4,12},{6,14},{8,16},{10,18},{12,20},{14,22},{16,24},... | collective-permute-start | bytes 331784 | tf_op jit(solution)/shard_map/ppermute | solution.py:41
  379.6 21.9 %collective-permute-start.38 = (bf16[64,2048]{1,0:T(8,128)(2,1)}, bf16[64,2048]{1,0:T(8,128)(2,1)}, u32[]{:S(2)}, u32[]{:S(2)}) collective-permute-start(bf16[64,2048]{1,0:T(8,128)(2,1)} %fusion.36), channel_id=1, source_target_pairs={{0,8},{1,9},{2,10},{3,11},{4,12},{5,13},{6,14},{7,15},{8,0},{9,1},... | collective-permute-start | bytes 786440 | tf_op jit(solution)/shard_map/ppermute | solution.py:56
  383.5 38.2 %all-to-all-start.1 = ((bf16[8,960,128]{2,1,0:T(8,128)(2,1)}), bf16[8,960,128]{2,1,0:T(8,128)(2,1)S(1)}, u32[]{:S(2)}, u32[]{:S(2)}) async-start(bf16[8,960,128]{2,1,0:T(8,128)(2,1)} %reduce-scatter.3.cloned.1.call-done), calls=%async_computation.2 | async-start | bytes 3932160 | tf_op jit(solution)/shard_map/all_to_all | solution.py:159
  404.7 18.6 %copy-start.10 = (bf16[128,1664]{1,0:T(8,128)(2,1)S(1)}, bf16[128,1664]{1,0:T(8,128)(2,1)}, u32[]{:S(2)}) copy-start(bf16[128,1664]{1,0:T(8,128)(2,1)} %pack_weights.1) | copy-start | bytes 1277956
  424.5 8.6 %collective-permute-start.44 = (f32[264]{0:T(512)S(1)}, f32[264]{0:T(512)S(1)}, u32[]{:S(2)}, u32[]{:S(2)}) collective-permute-start(f32[264]{0:T(512)S(1)} %pad_maximum_fusion.16), channel_id=1, source_target_pairs={{0,1},{1,0},{2,3},{3,2},{4,5},{5,4},{6,7},{7,6},{8,9},{9,8},{10,11... | collective-permute-start | bytes 3176 | tf_op jit(solution)/shard_map/ppermute | solution.py:31
  426.8 7.4 %collective-permute-start.43 = (bf16[128,384]{1,0:T(8,128)(2,1)S(1)}, bf16[128,384]{1,0:T(8,128)(2,1)S(1)}, u32[]{:S(2)}, u32[]{:S(2)}) collective-permute-start(bf16[128,384]{1,0:T(8,128)(2,1)S(1)} %slice.560), channel_id=1, source_target_pairs={{0,1},{1,0},{2,3},{3,2},{4,5},{5,4},{6,7},{7,6},{8,9},{9,8},{10,11... | collective-permute-start | bytes 294920 | tf_op jit(solution)/shard_map/ppermute | solution.py:31
  427.4 8.8 %collective-permute-start.39 = (bf16[64,2048]{1,0:T(8,128)(2,1)}, bf16[64,2048]{1,0:T(8,128)(2,1)S(1)}, u32[]{:S(2)}, u32[]{:S(2)}) collective-permute-start(bf16[64,2048]{1,0:T(8,128)(2,1)} %add_convert_fusion.9), channel_id=1, source_target_pairs={{0,1},{1,0},{2,3},{3,2},{4,5},{5,4},{6,7},{7,6},{8,9},{9,8},{10,11... | collective-permute-start | bytes 786440 | tf_op jit(solution)/shard_map/ppermute | solution.py:31
  (21 other events, 96.4 us)
Sparse Core Ops, SparseCore 0:
  10.3 70.5 all-gather.1
  247.8 109.1 reduce-scatter.2
  360.0 42.4 reduce-scatter.4

commit v6 on v5

--- a/solution.py
+++ b/solution.py
@@ -58,7 +58,8 @@
 
 def gather_earlier(block, span, weights):
     far = jnp.stack([block] + [shift_far(block, k, span, False) for k in range(1, span // 4)])
-    same, weights = lax.optimization_barrier((jnp.stack([far, swap_near(far)]), weights))
+    far, weights = lax.optimization_barrier((far, weights))
+    same = jnp.stack([far, swap_near(far)])
     return same, swap_core(same), weights
 
 

time: 451 us -> 445 us (0.987)
  starting transfers between devices: 80.5 us -> 75 us
    all_to_all x1, waiting for transfers between devices: 37 us -> 0.01 us  [body(): lax.all_to_all(w_ff, 'row', split_axis=0, concat_axis=0, tiled=True)]
    ppermute x5, waiting for transfers between devices: 16.9 us -> 48.5 us  [swap_near(): return lax.ppermute(block, 'row', [(i, i ^ 2) for i in range(rows)])]
    ppermute x16, waiting for transfers between devices: 97.4 us -> 108 us  [swap_cube(): return lax.ppermute(block, ('row', 'col'), route)]
    all_gather x1, waiting for transfers between devices: 10.4 us -> 2.99 us  [body(): w_all = lax.all_gather(w_packed, 'row', axis=0, tiled=True)]
    ppermute x16, starting transfers between devices: 29.9 us -> 24.5 us  [swap_cube(): return lax.ppermute(block, ('row', 'col'), route)]
    unnamed x100 -> x106, local copies, waits for them, and re-layouts: 12 us -> 14.7 us
  transfers between devices with their start and end apart: 50 -> 50, of which waited for: 26 -> 26; matrix products, arithmetic and copies ran while one was open for 17% -> 19% of each run, Pallas kernels for 8% -> 9%
where the time goes in v6:
time: 445 us; the launch traced here: 439 us
  waiting for transfers between devices  195 us (44%)
  starting transfers between devices  75 us (17%)
  Pallas kernels  45.4 us (10%)
  other arithmetic  45.4 us (10%)
  matrix products  30.4 us (7%)
  local copies, waits for them, and re-layouts  30 us (7%)
  between operations  17.9 us (4%)
    ppermute x16, waiting for transfers between devices, swap_cube(): return lax.ppermute(block, ('row', 'col'), route)  108 us
    ppermute x5, waiting for transfers between devices, swap_near(): return lax.ppermute(block, 'row', [(i, i ^ 2) for i in range(rows)])  48.5 us
    dot_general x9, matrix products, dot(): return lax.dot_general(a, b, (dims, ((), ())), preferred_element_type=F32)  30.4 us
    ppermute x16, starting transfers between devices, swap_cube(): return lax.ppermute(block, ('row', 'col'), route)  24.5 us
    ppermute x9, starting transfers between devices, shift_far(): return lax.ppermute(block, 'row', route)  24 us
    unnamed x106, local copies, waits for them, and re-layouts  14.7 us
    ppermute x6, waiting for transfers between devices, swap_col(): return lax.ppermute(block, 'col', [(0, 1), (1, 0)])  12.2 us
    all_to_all x1, waiting for transfers between devices, exchange_group(): lax.all_to_all(blocks, 'row', split_axis=0, concat_axis=0, tiled=True, ax...  11.7 us
  transfers between devices with their start and end apart: 50, of which 26 were waited for; matrix products, arithmetic and copies ran while one was open for 19% of the time, Pallas kernels for 9%

profile of v6, /device:TPU:0, one launch (start us, length us, event | category | flops | bytes accessed | tf_op | source)
XLA Modules:
  0.0 439.4 jit_solution(15660983638990457975)
XLA Ops:
  7.2 2.0 pack_weights.1
  9.3 1.7 constant_dynamic-update-slice_fusion.4
  11.0 3.0 collective-permute-start
  14.0 6.3 %collective-permute-done = bf16[64,2048]{1,0:T(8,128)(2,1)S(1)} collective-permute-done((bf16[64,2048]{1,0:T(8,128)(2,1)S(1)}, bf16[64,2048]{1,0:T(8,128)(2,1)S(1)}, u32[]{:S(2)}, u32[]{:S(2)}) %collective-permute-start) | collective-permute-done | bytes 262176 | tf_op jit(solution)/shard_map/ppermute | solution.py:56
  20.4 1.8 collective-permute-start.1
  22.1 16.0 %collective-permute-done.1 = bf16[128,2048]{1,0:T(8,128)(2,1)S(1)} collective-permute-done((bf16[128,2048]{1,0:T(8,128)(2,1)S(1)}, bf16[128,2048]{1,0:T(8,128)(2,1)S(1)}, u32[]{:S(2)}, u32[]{:S(2)}) %collective-permute-start.1) | collective-permute-done | bytes 524320 | tf_op jit(solution)/shard_map/ppermute | solution.py:56
  41.3 21.8 %collective-permute-done.2 = bf16[256,2048]{1,0:T(8,128)(2,1)S(1)} collective-permute-done((bf16[256,2048]{1,0:T(8,128)(2,1)}, bf16[256,2048]{1,0:T(8,128)(2,1)S(1)}, u32[]{:S(2)}, u32[]{:S(2)}) %collective-permute-start.2) | collective-permute-done | bytes 1048608 | tf_op jit(solution)/shard_map/ppermute | solution.py:56
  65.9 2.2 copy.78
  69.4 1.6 maximum_bitcast_fusion
  74.7 3.2 constant_dynamic-update-slice_fusion.og_ref
  77.9 3.0 all-gather.2.cloned.1.call-done.w_ref
  80.9 5.7 %project_heads.1 = (f32[128,1024]{1,0:T(8,128)}, bf16[128,1024]{1,0:T(8,128)(2,1)}, bf16[128,384]{1,0:T(8,128)(2,1)}) custom-call(bf16[128,2048]{1,0:T(8,128)(2,1)} %multiply_convert_fusion.3.act_ref.left_ref, bf16[2048,1664]{1,0:T(8,128)(2,1)} %all-gather.2.cloned.1.call-done.w_ref, f32[1,1024]{1,0:T(1,128)} %pad_maximum_fusion.15.gain_ref, ...), custom_call_target="tpu_custom_call" | custom-call | flops 536870912 | bytes 4194304 | tf_op jit(solution)/shard_map/project_heads/pallas_call | solution.py:226
  86.6 3.9 collective-permute-start.6
  91.7 2.5 collective-permute-start.4
  94.2 2.2 pad_maximum_fusion
  97.5 7.4 %all-to-all-start = ((bf16[16,128,960]{1,2,0:T(8,128)(2,1)}), bf16[16,128,960]{1,2,0:T(8,128)(2,1)}, u32[]{:S(2)}, u32[]{:S(2)}) async-start(bf16[16,128,960]{1,2,0:T(8,128)(2,1)} %pad_maximum_fusion), calls=%async_computation | async-start | bytes 7864320 | tf_op jit(solution)/shard_map/all_to_all | solution.py:665
  104.9 1.9 collective-permute-start.7
  106.9 37.8 %collective-permute-done.7 = bf16[4,128,384]{2,1,0:T(8,128)(2,1)S(1)} collective-permute-done((bf16[4,128,384]{2,1,0:T(8,128)(2,1)S(1)}, bf16[4,128,384]{2,1,0:T(8,128)(2,1)S(1)}, u32[]{:S(2)}, u32[]{:S(2)}) %collective-permute-start.7) | collective-permute-done | bytes 393248 | tf_op jit(solution)/shard_map/ppermute | solution.py:46
  150.7 4.2 attention_forward.1
  154.9 2.8 convolution_convert_fusion.3
  159.4 7.0 %collective-permute-done.9 = bf16[64,2048]{1,0:T(8,128)(2,1)S(1)} collective-permute-done((bf16[64,2048]{1,0:T(8,128)(2,1)S(1)}, bf16[64,2048]{1,0:T(8,128)(2,1)S(1)}, u32[]{:S(2)}, u32[]{:S(2)}) %collective-permute-start.9) | collective-permute-done | bytes 262176 | tf_op jit(solution)/shard_map/ppermute | solution.py:31
  169.8 5.6 %collective-permute-done.10 = bf16[64,2048]{1,0:T(8,128)(2,1)S(1)} collective-permute-done((bf16[64,2048]{1,0:T(8,128)(2,1)S(1)}, bf16[64,2048]{1,0:T(8,128)(2,1)S(1)}, u32[]{:S(2)}, u32[]{:S(2)}) %collective-permute-start.10) | collective-permute-done | bytes 262176 | tf_op jit(solution)/shard_map/ppermute | solution.py:56
  176.2 3.5 collective-permute-start.11
  179.7 2.8 copy_bitcast_fusion
  182.6 12.5 %collective-permute-done.13 = bf16[2,64,2048]{2,1,0:T(8,128)(2,1)S(1)} collective-permute-done((bf16[2,64,2048]{2,1,0:T(8,128)(2,1)}, bf16[2,64,2048]{2,1,0:T(8,128)(2,1)S(1)}, u32[]{:S(2)}, u32[]{:S(2)}) %collective-permute-start.13) | collective-permute-done | bytes 524320 | tf_op jit(solution)/shard_map/ppermute | solution.py:56
  195.1 8.5 %collective-permute-done.12 = bf16[2,64,2048]{2,1,0:T(8,128)(2,1)S(1)} collective-permute-done((bf16[2,64,2048]{2,1,0:T(8,128)(2,1)}, bf16[2,64,2048]{2,1,0:T(8,128)(2,1)S(1)}, u32[]{:S(2)}, u32[]{:S(2)}) %collective-permute-start.12) | collective-permute-done | bytes 524320 | tf_op jit(solution)/shard_map/ppermute | solution.py:56
  203.6 1.7 collective-permute-done.11
  205.7 4.0 collective-permute-done.14
  209.9 3.5 fusion.10
  213.4 5.8 %multiply_convert_fusion.1 = (bf16[1024,320]{1,0:T(8,128)(2,1)S(1)}, bf16[1024,320]{1,0:T(8,128)(2,1)S(1)}, bf16[1024,320]{1,0:T(8,128)(2,1)}) fusion(f32[1024,640]{1,0:T(8,128)S(1)} %fusion.10, bf16[1024,2048]{1,0:T(8,128)(2,1)} %constant_dynamic-update-slice_fusion.og_ref, bf16[2048,960]{0,1:T(8,128)(2,1)S(1)} %copy_bitcast_fusion), kind=kOutput, calls=%fused_computation.26 | convolution fusion | flops 1347092480 | bytes 10616832 | tf_op jit(solution)/shard_map/dot_general | solution.py:22
  219.1 1.8 convolution_convert_fusion.2
  222.7 2.5 collective-permute-done.15
  225.2 1.9 add_convert_fusion.1
  231.7 11.2 %feed_forward_weight_grads.1 = bf16[16,960,128]{2,1,0:T(8,128)(2,1)} custom-call(bf16[1024,2048]{1,0:T(8,128)(2,1)} %copy-done.6, bf16[1024,2048]{1,0:T(8,128)(2,1)} %constant_dynamic-update-slice_fusion.og_ref, bf16[1024,640]{1,0:T(8,128)(2,1)} %pad_maximum_fusion.2.d_ref, bf16[1024,320]{1,0:T(8,128)(2,1)} %get-tuple-element.102.inner_ref), custom_call_target="tpu_custom_call" | custom-call | tf_op jit(solution)/shard_map/feed_forward_weight_grads/pallas_call | solution.py:343
  249.3 4.0 convolution_convert_fusion
  253.2 3.9 convolution_convert_fusion.1
  259.4 2.9 collective-permute-done.21
  262.4 2.7 collective-permute-done.20
  267.7 4.3 collective-permute-done.22
  272.0 3.1 fusion.13.grad_ref
  275.1 6.7 %attention_backward.1 = (bf16[128,640]{1,0:T(8,128)(2,1)}, f32[1,128]{1,0:T(1,128)}, bf16[2,4,128,384]{3,2,1,0:T(8,128)(2,1)}, bf16[2,4,128,384]{3,2,1,0:T(8,128)(2,1)}) custom-call(s32[2]{0:T(128)} %pad_add_fusion.1.bounds_ref, s32[2,128]{1,0:T(2,128)} %pad_add_fusion.limits_ref, bf16[128,1024]{1,0:T(8,128)(2,1)} %get-tuple-element.81.q_ref, ...), custom_call_target="tpu_custom_call" | custom-call | tf_op jit(solution)/shard_map/attention_backward/pallas_call | solution.py:526
  286.5 3.2 weight_rows.3
  291.2 3.1 weight_rows.4
  294.4 3.0 add_convert_fusion
  297.5 1.7 collective-permute-start.31
  299.2 1.6 add_convert_fusion.3
  309.8 13.3 %collective-permute-done.31 = bf16[2,2,64,2048]{3,2,1,0:T(8,128)(2,1)S(1)} collective-permute-done((bf16[2,2,64,2048]{3,2,1,0:T(8,128)(2,1)S(1)}, bf16[2,2,64,2048]{3,2,1,0:T(8,128)(2,1)S(1)}, u32[]{:S(2)}, u32[]{:S(2)}) %collective-permute-start.31) | collective-permute-done | bytes 1048608 | tf_op jit(solution)/shard_map/ppermute | solution.py:56
  323.1 1.6 collective-permute-start.42
  325.8 2.5 key_value_heads_back.1
  330.1 2.8 weight_rows.5
  334.3 5.5 %collective-permute-done.42 = bf16[4,128,640]{2,1,0:T(8,128)(2,1)} collective-permute-done((bf16[4,128,640]{2,1,0:T(8,128)(2,1)}, bf16[4,128,640]{2,1,0:T(8,128)(2,1)}, u32[]{:S(2)}, u32[]{:S(2)}) %collective-permute-start.42) | collective-permute-done | bytes 655392 | tf_op jit(solution)/shard_map/ppermute | solution.py:46
  342.3 1.7 add_convert_fusion.4
  344.0 1.7 collective-permute-start.33
  345.8 3.7 fusion.2
  351.0 4.1 collective-permute-done.33
  355.3 1.7 collective-permute-start.37
  357.7 11.3 %collective-permute-start.36 = (bf16[144,384]{1,0:T(8,128)(2,1)}, bf16[144,384]{1,0:T(8,128)(2,1)}, u32[]{:S(2)}, u32[]{:S(2)}) collective-permute-start(bf16[144,384]{1,0:T(8,128)(2,1)} %get-tuple-element.236), channel_id=1, source_target_pairs={{0,24},{2,26},{4,28},{6,30},{8,0},{10,2},{12,4},{14,6},{16,8},{18,... | collective-permute-start | bytes 331784 | tf_op jit(solution)/shard_map/ppermute | solution.py:41
  372.2 2.5 collective-permute-start.38
  376.3 3.6 all-to-all-start.1
  379.9 15.1 %collective-permute-done.38 = bf16[64,2048]{1,0:T(8,128)(2,1)} collective-permute-done((bf16[64,2048]{1,0:T(8,128)(2,1)}, bf16[64,2048]{1,0:T(8,128)(2,1)}, u32[]{:S(2)}, u32[]{:S(2)}) %collective-permute-start.38) | collective-permute-done | bytes 262176 | tf_op jit(solution)/shard_map/ppermute | solution.py:56
  396.2 3.6 reduce-scatter.5.cloned.1.call-done
  402.6 1.9 copy.89
  404.5 11.7 %all-to-all-done.1.in_ref = bf16[8,960,128]{2,1,0:T(8,128)(2,1)S(1)} async-done(((bf16[8,960,128]{2,1,0:T(8,128)(2,1)}), bf16[8,960,128]{2,1,0:T(8,128)(2,1)S(1)}, u32[]{:S(2)}, u32[]{:S(2)}) %all-to-all-start.1) | async-done | bytes 1966112 | tf_op jit(solution)/shard_map/all_to_all | solution.py:160
  423.3 4.2 feed_forward_grads.1
  (280 shorter events, 85.7 us)
Async XLA Ops:
  7.2 73.7 %all-gather.2.cloned.1.call-start = ((), (), s32[]{:S(2)}) async-start(), calls=%async_computation.4 | async-start | bytes 7241728 | tf_op jit(solution)/shard_map/all_gather | solution.py:633
  9.2 31.3 %copy-start.35 = (f32[64]{0:T(128)S(1)}, f32[64]{0:T(128)}, u32[]{:S(2)}) copy-start(f32[64]{0:T(128)} %param.23) | copy-start | bytes 772
  9.2 31.4 %copy-start.33 = (f32[64]{0:T(128)S(1)}, f32[64]{0:T(128)}, u32[]{:S(2)}) copy-start(f32[64]{0:T(128)} %param.24) | copy-start | bytes 772
  9.2 31.4 %copy-start.32 = (pred[3,128]{1,0:T(4,128)(4,1)S(1)}, pred[3,128]{1,0:T(4,128)(4,1)}, u32[]{:S(2)}) copy-start(pred[3,128]{1,0:T(4,128)(4,1)} %constant.199.clone.1) | copy-start | bytes 1156
  11.0 9.3 %collective-permute-start = (bf16[64,2048]{1,0:T(8,128)(2,1)S(1)}, bf16[64,2048]{1,0:T(8,128)(2,1)S(1)}, u32[]{:S(2)}, u32[]{:S(2)}) collective-permute-start(bf16[64,2048]{1,0:T(8,128)(2,1)S(1)} %get-tuple-element.215), channel_id=1, source_target_pairs={{0,8},{1,9},{2,10},{3,11},{4,12},{5,13},{6,14},{7,15},{8,0},{9,1},... | collective-permute-start | bytes 786440 | tf_op jit(solution)/shard_map/ppermute | solution.py:56
  20.4 17.7 %collective-permute-start.1 = (bf16[128,2048]{1,0:T(8,128)(2,1)S(1)}, bf16[128,2048]{1,0:T(8,128)(2,1)S(1)}, u32[]{:S(2)}, u32[]{:S(2)}) collective-permute-start(bf16[128,2048]{1,0:T(8,128)(2,1)S(1)} %pad_maximum_fusion.6), channel_id=1, source_target_pairs={{0,4},{1,5},{2,6},{3,7},{4,0},{5,1},{6,2},{7,3},{8,12},{9,13},{10,... | collective-permute-start | bytes 1572872 | tf_op jit(solution)/shard_map/ppermute | solution.py:56
  39.1 24.0 %collective-permute-start.2 = (bf16[256,2048]{1,0:T(8,128)(2,1)}, bf16[256,2048]{1,0:T(8,128)(2,1)S(1)}, u32[]{:S(2)}, u32[]{:S(2)}) collective-permute-start(bf16[256,2048]{1,0:T(8,128)(2,1)} %pad_maximum_fusion.4), channel_id=1, source_target_pairs={{0,1},{1,0},{2,3},{3,2},{4,5},{5,4},{6,7},{7,6},{8,9},{9,8},{10,11... | collective-permute-start | bytes 3145736 | tf_op jit(solution)/shard_map/ppermute | solution.py:56
  40.7 24.0 %copy-start.30 = (f32[1,1,3,128]{3,1,2,0:T(1,128)}, f32[1,1,3,128]{3,1,2,0:T(1,128)S(1)}, u32[]{:S(2)}) copy-start(f32[1,1,3,128]{3,1,2,0:T(1,128)S(1)} %copy.106) | copy-start | bytes 4612
  41.3 23.5 %copy-start.34 = (s32[128]{0:T(128)S(1)}, s32[128]{0:T(128)}, u32[]{:S(2)}) copy-start(s32[128]{0:T(128)} %param.26) | copy-start | bytes 1540
  41.3 23.5 %copy-start.20 = (bf16[128,2560]{1,0:T(8,128)(2,1)S(1)}, bf16[128,2560]{1,0:T(8,128)(2,1)}, u32[]{:S(2)}) copy-start(bf16[128,2560]{1,0:T(8,128)(2,1)} %param.18) | copy-start | bytes 1966084
  64.8 10.0 %collective-permute-start.3 = (bf16[512,2048]{1,0:T(8,128)(2,1)}, bf16[512,2048]{1,0:T(8,128)(2,1)}, u32[]{:S(2)}, u32[]{:S(2)}) collective-permute-start(bf16[512,2048]{1,0:T(8,128)(2,1)} %pad_maximum_fusion.1), channel_id=1, source_target_pairs={{0,2},{2,0},{4,6},{6,4},{8,10},{10,8},{12,14},{14,12},{16,18},{18,... | collective-permute-start | bytes 6291464 | tf_op jit(solution)/shard_map/ppermute | solution.py:27
  86.5 10.9 %copy-start.26 = (bf16[128,384]{1,0:T(8,128)(2,1)S(1)}, bf16[128,384]{1,0:T(8,128)(2,1)}, u32[]{:S(2)}) copy-start(bf16[128,384]{1,0:T(8,128)(2,1)} %get-tuple-element.82) | copy-start | bytes 294916
  86.6 9.9 %collective-permute-start.6 = (bf16[128,384]{1,0:T(8,128)(2,1)}, bf16[128,384]{1,0:T(8,128)(2,1)S(1)}, u32[]{:S(2)}, u32[]{:S(2)}) collective-permute-start(bf16[128,384]{1,0:T(8,128)(2,1)} %get-tuple-element.82), channel_id=1, source_target_pairs={{0,24},{2,26},{4,28},{6,30},{1,25},{3,27},{5,29},{7,31}} | collective-permute-start | bytes 294920 | tf_op jit(solution)/shard_map/ppermute | solution.py:41
  90.4 6.0 %collective-permute-start.5 = (bf16[128,384]{1,0:T(8,128)(2,1)}, bf16[128,384]{1,0:T(8,128)(2,1)S(1)}, u32[]{:S(2)}, u32[]{:S(2)}) collective-permute-start(bf16[128,384]{1,0:T(8,128)(2,1)} %get-tuple-element.82), channel_id=1, source_target_pairs={{0,16},{2,18},{4,20},{6,22},{8,24},{10,26},{12,28},{14,30},{1,17},... | collective-permute-start | bytes 294920 | tf_op jit(solution)/shard_map/ppermute | solution.py:41
  91.7 5.7 %collective-permute-start.4 = (bf16[128,384]{1,0:T(8,128)(2,1)}, bf16[128,384]{1,0:T(8,128)(2,1)S(1)}, u32[]{:S(2)}, u32[]{:S(2)}) collective-permute-start(bf16[128,384]{1,0:T(8,128)(2,1)} %get-tuple-element.82), channel_id=1, source_target_pairs={{0,8},{2,10},{4,12},{6,14},{8,16},{10,18},{12,20},{14,22},{16,24},... | collective-permute-start | bytes 294920 | tf_op jit(solution)/shard_map/ppermute | solution.py:41
  97.5 47.4 %copy-start.31 = (s32[2048]{0:T(1024)S(1)}, s32[2048]{0:T(1024)}, u32[]{:S(2)}) copy-start(s32[2048]{0:T(1024)} %param.25) | copy-start | bytes 24580
  97.5 82.2 %all-to-all-start = ((bf16[16,128,960]{1,2,0:T(8,128)(2,1)}), bf16[16,128,960]{1,2,0:T(8,128)(2,1)}, u32[]{:S(2)}, u32[]{:S(2)}) async-start(bf16[16,128,960]{1,2,0:T(8,128)(2,1)} %pad_maximum_fusion), calls=%async_computation | async-start | bytes 7864320 | tf_op jit(solution)/shard_map/all_to_all | solution.py:665
  104.9 271.4 %reduce-scatter.3.cloned.1.call-start = ((), (), s32[]{:S(2)}) async-start(), calls=%async_computation.5 | async-start | bytes 5898240 | tf_op jit(solution)/shard_map/reduce_scatter | solution.py:712
  104.9 39.8 %collective-permute-start.7 = (bf16[4,128,384]{2,1,0:T(8,128)(2,1)S(1)}, bf16[4,128,384]{2,1,0:T(8,128)(2,1)S(1)}, u32[]{:S(2)}, u32[]{:S(2)}) collective-permute-start(bf16[4,128,384]{2,1,0:T(8,128)(2,1)S(1)} %pad_maximum_fusion.11), channel_id=1, source_target_pairs={{0,4},{2,6},{4,0},{6,2},{8,12},{10,14},{12,8},{14,10},{16,20},{18,... | collective-permute-start | bytes 1179656 | tf_op jit(solution)/shard_map/ppermute | solution.py:46
  144.8 5.0 %collective-permute-start.8 = (bf16[2,4,128,384]{3,2,1,0:T(8,128)(2,1)S(1)}, bf16[2,4,128,384]{3,2,1,0:T(8,128)(2,1)S(1)}, u32[]{:S(2)}, u32[]{:S(2)}) collective-permute-start(bf16[2,4,128,384]{3,2,1,0:T(8,128)(2,1)S(1)} %pad_maximum_fusion.5.same_ref), channel_id=1, source_target_pairs={{0,2},{2,0},{4,6},{6,4},{8,10},{10,8},{12,14},{14,12},{16,18},{18,... | collective-permute-start | bytes 2359304 | tf_op jit(solution)/shard_map/ppermute | solution.py:27
  157.7 8.7 %collective-permute-start.9 = (bf16[64,2048]{1,0:T(8,128)(2,1)S(1)}, bf16[64,2048]{1,0:T(8,128)(2,1)S(1)}, u32[]{:S(2)}, u32[]{:S(2)}) collective-permute-start(bf16[64,2048]{1,0:T(8,128)(2,1)S(1)} %constant_dynamic-slice_fusion), channel_id=1, source_target_pairs={{0,1},{1,0},{2,3},{3,2},{4,5},{5,4},{6,7},{7,6},{8,9},{9,8},{10,11... | collective-permute-start | bytes 786440 | tf_op jit(solution)/shard_map/ppermute | solution.py:31
  167.5 7.9 %collective-permute-start.10 = (bf16[64,2048]{1,0:T(8,128)(2,1)S(1)}, bf16[64,2048]{1,0:T(8,128)(2,1)S(1)}, u32[]{:S(2)}, u32[]{:S(2)}) collective-permute-start(bf16[64,2048]{1,0:T(8,128)(2,1)S(1)} %get-tuple-element.211), channel_id=1, source_target_pairs={{0,1},{1,0},{2,3},{3,2},{4,5},{5,4},{6,7},{7,6},{8,9},{9,8},{10,11... | collective-permute-start | bytes 786440 | tf_op jit(solution)/shard_map/ppermute | solution.py:56
  176.2 18.8 %collective-permute-start.13 = (bf16[2,64,2048]{2,1,0:T(8,128)(2,1)}, bf16[2,64,2048]{2,1,0:T(8,128)(2,1)S(1)}, u32[]{:S(2)}, u32[]{:S(2)}) collective-permute-start(bf16[2,64,2048]{2,1,0:T(8,128)(2,1)} %pad_maximum_fusion.7), channel_id=1, source_target_pairs={{0,12},{1,13},{2,14},{3,15},{4,8},{5,9},{6,10},{7,11},{8,4},{9,5},... | collective-permute-start | bytes 1572872 | tf_op jit(solution)/shard_map/ppermute | solution.py:56
  176.2 27.4 %collective-permute-start.12 = (bf16[2,64,2048]{2,1,0:T(8,128)(2,1)}, bf16[2,64,2048]{2,1,0:T(8,128)(2,1)S(1)}, u32[]{:S(2)}, u32[]{:S(2)}) collective-permute-start(bf16[2,64,2048]{2,1,0:T(8,128)(2,1)} %pad_maximum_fusion.7), channel_id=1, source_target_pairs={{0,4},{1,5},{2,6},{3,7},{4,0},{5,1},{6,2},{7,3},{8,12},{9,13},{10,... | collective-permute-start | bytes 1572872 | tf_op jit(solution)/shard_map/ppermute | solution.py:56
  176.2 29.0 %collective-permute-start.11 = (bf16[2,64,2048]{2,1,0:T(8,128)(2,1)}, bf16[2,64,2048]{2,1,0:T(8,128)(2,1)S(1)}, u32[]{:S(2)}, u32[]{:S(2)}) collective-permute-start(bf16[2,64,2048]{2,1,0:T(8,128)(2,1)} %pad_maximum_fusion.7), channel_id=1, source_target_pairs={{0,8},{1,9},{2,10},{3,11},{4,12},{5,13},{6,14},{7,15},{8,0},{9,1},... | collective-permute-start | bytes 1572872 | tf_op jit(solution)/shard_map/ppermute | solution.py:56
  179.7 25.5 %copy-start.29 = (bf16[512,2048]{1,0:T(8,128)(2,1)S(1)}, bf16[512,2048]{1,0:T(8,128)(2,1)}, u32[]{:S(2)}) copy-start(bf16[512,2048]{1,0:T(8,128)(2,1)} %get-tuple-element.210) | copy-start | bytes 6291460
  179.7 25.6 %copy-start.5 = (bf16[1024,2048]{1,0:T(8,128)(2,1)S(1)}, bf16[1024,2048]{1,0:T(8,128)(2,1)}, u32[]{:S(2)}) copy-start(bf16[1024,2048]{1,0:T(8,128)(2,1)} %constant_dynamic-update-slice_fusion.9) | copy-start | bytes 12582916
  182.6 42.6 %copy-start.9 = (bf16[2048,960]{0,1:T(8,128)(2,1)}, bf16[2048,960]{0,1:T(8,128)(2,1)S(1)}, u32[]{:S(2)}) copy-start(bf16[2048,960]{0,1:T(8,128)(2,1)S(1)} %copy_bitcast_fusion) | copy-start | bytes 11796484
  205.5 4.2 collective-permute-start.14
  221.0 4.2 collective-permute-start.15
  228.7 14.3 %collective-permute-start.16 = (bf16[2,2,64,1024]{3,2,1,0:T(8,128)(2,1)S(1)}, bf16[2,2,64,1024]{3,2,1,0:T(8,128)(2,1)S(1)}, u32[]{:S(2)}, u32[]{:S(2)}) collective-permute-start(bf16[2,2,64,1024]{3,2,1,0:T(8,128)(2,1)S(1)} %slice_bitcast_fusion.2), channel_id=1, source_target_pairs={{0,1},{1,0},{2,3},{3,2},{4,5},{5,4},{6,7},{7,6},{8,9},{9,8},{10,11... | collective-permute-start | bytes 1572872 | tf_op jit(solution)/shard_map/ppermute | solution.py:56
  230.2 14.0 %collective-permute-start.17 = (bf16[2,2,64,1024]{3,2,0,1:T(8,128)(2,1)}, bf16[2,2,64,1024]{3,2,0,1:T(8,128)(2,1)}, u32[]{:S(2)}, u32[]{:S(2)}) collective-permute-start(bf16[2,2,64,1024]{3,2,0,1:T(8,128)(2,1)} %bitcast.183), channel_id=1, source_target_pairs={{0,4},{1,5},{2,6},{3,7},{4,0},{5,1},{6,2},{7,3},{8,12},{9,13},{10,... | collective-permute-start | bytes 1572872 | tf_op jit(solution)/shard_map/ppermute | solution.py:56
  245.5 154.3 %reduce-scatter.5.cloned.1.call-start = ((), (), s32[]{:S(2)}) async-start(), calls=%async_computation.6 | async-start | bytes 1638400 | tf_op jit(solution)/shard_map/reduce_scatter | solution.py:761
  247.1 10.1 %collective-permute-start.18 = (bf16[2,64,1024]{2,1,0:T(8,128)(2,1)S(1)}, bf16[2,64,1024]{2,1,0:T(8,128)(2,1)S(1)}, u32[]{:S(2)}, u32[]{:S(2)}) collective-permute-start(bf16[2,64,1024]{2,1,0:T(8,128)(2,1)S(1)} %slice_bitcast_fusion.9), channel_id=1, source_target_pairs={{0,4},{1,5},{2,6},{3,7},{4,0},{5,1},{6,2},{7,3},{8,12},{9,13},{10,... | collective-permute-start | bytes 786440 | tf_op jit(solution)/shard_map/ppermute | solution.py:56
  248.6 8.5 %collective-permute-start.19 = (bf16[2,64,1024]{2,1,0:T(8,128)(2,1)S(1)}, bf16[2,64,1024]{2,1,0:T(8,128)(2,1)S(1)}, u32[]{:S(2)}, u32[]{:S(2)}) collective-permute-start(bf16[2,64,1024]{2,1,0:T(8,128)(2,1)S(1)} %slice_bitcast_fusion.8), channel_id=1, source_target_pairs={{0,8},{1,9},{2,10},{3,11},{4,12},{5,13},{6,14},{7,15},{8,0},{9,1},... | collective-permute-start | bytes 786440 | tf_op jit(solution)/shard_map/ppermute | solution.py:56
  257.3 5.0 %collective-permute-start.21 = (bf16[64,1024]{1,0:T(8,128)(2,1)S(1)}, bf16[64,1024]{1,0:T(8,128)(2,1)S(1)}, u32[]{:S(2)}, u32[]{:S(2)}) collective-permute-start(bf16[64,1024]{1,0:T(8,128)(2,1)S(1)} %slice_bitcast_fusion.11), channel_id=1, source_target_pairs={{0,1},{1,0},{2,3},{3,2},{4,5},{5,4},{6,7},{7,6},{8,9},{9,8},{10,11... | collective-permute-start | bytes 393224 | tf_op jit(solution)/shard_map/ppermute | solution.py:56
  257.9 7.1 %collective-permute-start.20 = (bf16[64,1024]{1,0:T(8,128)(2,1)S(1)}, bf16[64,1024]{1,0:T(8,128)(2,1)S(1)}, u32[]{:S(2)}, u32[]{:S(2)}) collective-permute-start(bf16[64,1024]{1,0:T(8,128)(2,1)S(1)} %slice_bitcast_fusion.13), channel_id=1, source_target_pairs={{0,8},{1,9},{2,10},{3,11},{4,12},{5,13},{6,14},{7,15},{8,0},{9,1},... | collective-permute-start | bytes 393224 | tf_op jit(solution)/shard_map/ppermute | solution.py:56
  265.5 6.4 %collective-permute-start.22 = (bf16[64,2048]{1,0:T(8,128)(2,1)S(1)}, bf16[64,2048]{1,0:T(8,128)(2,1)S(1)}, u32[]{:S(2)}, u32[]{:S(2)}) collective-permute-start(bf16[64,2048]{1,0:T(8,128)(2,1)S(1)} %add_convert_fusion.10), channel_id=1, source_target_pairs={{0,1},{1,0},{2,3},{3,2},{4,5},{5,4},{6,7},{7,6},{8,9},{9,8},{10,11... | collective-permute-start | bytes 786440 | tf_op jit(solution)/shard_map/ppermute | solution.py:31
  267.7 26.7 %collective-permute-start.30 = (bf16[512,2048]{1,0:T(8,128)(2,1)}, bf16[512,2048]{1,0:T(8,128)(2,1)}, u32[]{:S(2)}, u32[]{:S(2)}) collective-permute-start(bf16[512,2048]{1,0:T(8,128)(2,1)} %convolution_convert_fusion.1), channel_id=1, source_target_pairs={{0,2},{2,0},{4,6},{6,4},{8,10},{10,8},{12,14},{14,12},{16,18},{18,... | collective-permute-start | bytes 6291464 | tf_op jit(solution)/shard_map/ppermute | solution.py:27
  272.0 10.5 %copy-start.13 = (bf16[64,2048]{1,0:T(8,128)(2,1)}, bf16[64,2048]{1,0:T(8,128)(2,1)S(1)}, u32[]{:S(2)}) copy-start(bf16[64,2048]{1,0:T(8,128)(2,1)S(1)} %get-tuple-element.229) | copy-start | bytes 786436
  281.8 2.5 collective-permute-start.23
  289.6 9.6 %collective-permute-start.25 = (bf16[8,128,640]{2,1,0:T(8,128)(2,1)}, bf16[8,128,640]{2,1,0:T(8,128)(2,1)}, u32[]{:S(2)}, u32[]{:S(2)}) collective-permute-start(bf16[8,128,640]{2,1,0:T(8,128)(2,1)} %get-tuple-element.113), channel_id=1, source_target_pairs={{0,2},{2,0},{4,6},{6,4},{8,10},{10,8},{12,14},{14,12},{16,18},{18,... | collective-permute-start | bytes 3932168 | tf_op jit(solution)/shard_map/ppermute | solution.py:27
  290.7 11.7 %collective-permute-start.24 = (bf16[4,128,384]{2,1,0:T(8,128)(2,1)}, bf16[4,128,384]{2,1,0:T(8,128)(2,1)S(1)}, u32[]{:S(2)}, u32[]{:S(2)}) collective-permute-start(bf16[4,128,384]{2,1,0:T(8,128)(2,1)} %slice_bitcast_fusion.4), channel_id=1, source_target_pairs={{0,4},{2,6},{4,0},{6,2},{8,12},{10,14},{12,8},{14,10},{16,20},{18,... | collective-permute-start | bytes 1179656 | tf_op jit(solution)/shard_map/ppermute | solution.py:46
  294.3 6.6 %collective-permute-start.26 = (bf16[8,128,640]{2,1,0:T(8,128)(2,1)}, bf16[8,128,640]{2,1,0:T(8,128)(2,1)S(1)}, u32[]{:S(2)}, u32[]{:S(2)}) collective-permute-start(bf16[8,128,640]{2,1,0:T(8,128)(2,1)} %get-tuple-element.117), channel_id=1, source_target_pairs={{0,2},{2,0},{4,6},{6,4},{8,10},{10,8},{12,14},{14,12},{16,18},{18,... | collective-permute-start | bytes 3932168 | tf_op jit(solution)/shard_map/ppermute | solution.py:27
  297.5 25.6 %collective-permute-start.31 = (bf16[2,2,64,2048]{3,2,1,0:T(8,128)(2,1)S(1)}, bf16[2,2,64,2048]{3,2,1,0:T(8,128)(2,1)S(1)}, u32[]{:S(2)}, u32[]{:S(2)}) collective-permute-start(bf16[2,2,64,2048]{3,2,1,0:T(8,128)(2,1)S(1)} %slice_bitcast_fusion), channel_id=1, source_target_pairs={{0,1},{1,0},{2,3},{3,2},{4,5},{5,4},{6,7},{7,6},{8,9},{9,8},{10,11... | collective-permute-start | bytes 3145736 | tf_op jit(solution)/shard_map/ppermute | solution.py:56
  303.2 21.9 %collective-permute-start.29 = (bf16[128,384]{1,0:T(8,128)(2,1)S(1)}, bf16[128,384]{1,0:T(8,128)(2,1)S(1)}, u32[]{:S(2)}, u32[]{:S(2)}) collective-permute-start(bf16[128,384]{1,0:T(8,128)(2,1)S(1)} %get-tuple-element.242), channel_id=1, source_target_pairs={{24,0},{26,2},{28,4},{30,6},{25,1},{27,3},{29,5},{31,7}} | collective-permute-start | bytes 294920 | tf_op jit(solution)/shard_map/ppermute | solution.py:41
  304.4 20.6 %collective-permute-start.28 = (bf16[128,384]{1,0:T(8,128)(2,1)S(1)}, bf16[128,384]{1,0:T(8,128)(2,1)S(1)}, u32[]{:S(2)}, u32[]{:S(2)}) collective-permute-start(bf16[128,384]{1,0:T(8,128)(2,1)S(1)} %get-tuple-element.243), channel_id=1, source_target_pairs={{16,0},{18,2},{20,4},{22,6},{24,8},{26,10},{28,12},{30,14},{17,1},... | collective-permute-start | bytes 294920 | tf_op jit(solution)/shard_map/ppermute | solution.py:41
  305.7 19.4 %collective-permute-start.27 = (bf16[128,384]{1,0:T(8,128)(2,1)S(1)}, bf16[128,384]{1,0:T(8,128)(2,1)S(1)}, u32[]{:S(2)}, u32[]{:S(2)}) collective-permute-start(bf16[128,384]{1,0:T(8,128)(2,1)S(1)} %get-tuple-element.244), channel_id=1, source_target_pairs={{8,0},{10,2},{12,4},{14,6},{16,8},{18,10},{20,12},{22,14},{24,16},... | collective-permute-start | bytes 294920 | tf_op jit(solution)/shard_map/ppermute | solution.py:41
  309.1 23.7 %collective-permute-start.41 = (bf16[4,128,640]{2,1,0:T(8,128)(2,1)}, bf16[4,128,640]{2,1,0:T(8,128)(2,1)}, u32[]{:S(2)}, u32[]{:S(2)}) collective-permute-start(bf16[4,128,640]{2,1,0:T(8,128)(2,1)} %slice.330), channel_id=1, source_target_pairs={{0,4},{2,6},{4,0},{6,2},{8,12},{10,14},{12,8},{14,10},{16,20},{18,... | collective-permute-start | bytes 1966088 | tf_op jit(solution)/shard_map/ppermute | solution.py:46
  323.1 16.7 %collective-permute-start.42 = (bf16[4,128,640]{2,1,0:T(8,128)(2,1)}, bf16[4,128,640]{2,1,0:T(8,128)(2,1)}, u32[]{:S(2)}, u32[]{:S(2)}) collective-permute-start(bf16[4,128,640]{2,1,0:T(8,128)(2,1)} %slice.332), channel_id=1, source_target_pairs={{0,4},{2,6},{4,0},{6,2},{8,12},{10,14},{12,8},{14,10},{16,20},{18,... | collective-permute-start | bytes 1966088 | tf_op jit(solution)/shard_map/ppermute | solution.py:46
  329.2 10.6 %copy-start.4 = (bf16[8,128,640]{2,1,0:T(8,128)(2,1)S(1)}, bf16[8,128,640]{2,1,0:T(8,128)(2,1)}, u32[]{:S(2)}) copy-start(bf16[8,128,640]{2,1,0:T(8,128)(2,1)} %copy-done.3) | copy-start | bytes 3932164
  332.8 9.4 %collective-permute-start.32 = (bf16[8,144,384]{2,1,0:T(8,128)(2,1)}, bf16[8,144,384]{2,1,0:T(8,128)(2,1)}, u32[]{:S(2)}, u32[]{:S(2)}) collective-permute-start(bf16[8,144,384]{2,1,0:T(8,128)(2,1)} %get-tuple-element.130), channel_id=1, source_target_pairs={{0,2},{2,0},{4,6},{6,4},{8,10},{10,8},{12,14},{14,12},{16,18},{18,... | collective-permute-start | bytes 2654216 | tf_op jit(solution)/shard_map/ppermute | solution.py:27
  344.0 11.1 %collective-permute-start.33 = (bf16[4,144,384]{2,1,0:T(8,128)(2,1)S(1)}, bf16[4,144,384]{2,1,0:T(8,128)(2,1)S(1)}, u32[]{:S(2)}, u32[]{:S(2)}) collective-permute-start(bf16[4,144,384]{2,1,0:T(8,128)(2,1)S(1)} %slice.389), channel_id=1, source_target_pairs={{0,4},{2,6},{4,0},{6,2},{8,12},{10,14},{12,8},{14,10},{16,20},{18,... | collective-permute-start | bytes 1327112 | tf_op jit(solution)/shard_map/ppermute | solution.py:46
  349.5 20.5 %collective-permute-start.40 = (bf16[128,2048]{1,0:T(8,128)(2,1)S(1)}, bf16[128,2048]{1,0:T(8,128)(2,1)S(1)}, u32[]{:S(2)}, u32[]{:S(2)}) collective-permute-start(bf16[128,2048]{1,0:T(8,128)(2,1)S(1)} %fusion.2), channel_id=1, source_target_pairs={{0,1},{1,0},{2,3},{3,2},{4,5},{5,4},{6,7},{7,6},{8,9},{9,8},{10,11... | collective-permute-start | bytes 1572872 | tf_op jit(solution)/shard_map/ppermute | solution.py:31
  355.3 15.1 %collective-permute-start.37 = (bf16[2,64,2048]{2,1,0:T(8,128)(2,1)S(1)}, bf16[2,64,2048]{2,1,0:T(8,128)(2,1)S(1)}, u32[]{:S(2)}, u32[]{:S(2)}) collective-permute-start(bf16[2,64,2048]{2,1,0:T(8,128)(2,1)S(1)} %fusion.27), channel_id=1, source_target_pairs={{0,4},{1,5},{2,6},{3,7},{4,0},{5,1},{6,2},{7,3},{8,12},{9,13},{10,... | collective-permute-start | bytes 1572872 | tf_op jit(solution)/shard_map/ppermute | solution.py:56
  357.7 46.7 %collective-permute-start.36 = (bf16[144,384]{1,0:T(8,128)(2,1)}, bf16[144,384]{1,0:T(8,128)(2,1)}, u32[]{:S(2)}, u32[]{:S(2)}) collective-permute-start(bf16[144,384]{1,0:T(8,128)(2,1)} %get-tuple-element.236), channel_id=1, source_target_pairs={{0,24},{2,26},{4,28},{6,30},{8,0},{10,2},{12,4},{14,6},{16,8},{18,... | collective-permute-start | bytes 331784 | tf_op jit(solution)/shard_map/ppermute | solution.py:41
  369.1 35.4 %collective-permute-start.35 = (bf16[144,384]{1,0:T(8,128)(2,1)}, bf16[144,384]{1,0:T(8,128)(2,1)}, u32[]{:S(2)}, u32[]{:S(2)}) collective-permute-start(bf16[144,384]{1,0:T(8,128)(2,1)} %get-tuple-element.237), channel_id=1, source_target_pairs={{0,16},{2,18},{4,20},{6,22},{8,24},{10,26},{12,28},{14,30},{16,0},... | collective-permute-start | bytes 331784 | tf_op jit(solution)/shard_map/ppermute | solution.py:41
  369.1 35.4 %collective-permute-start.34 = (bf16[144,384]{1,0:T(8,128)(2,1)}, bf16[144,384]{1,0:T(8,128)(2,1)}, u32[]{:S(2)}, u32[]{:S(2)}) collective-permute-start(bf16[144,384]{1,0:T(8,128)(2,1)} %get-tuple-element.238), channel_id=1, source_target_pairs={{0,8},{2,10},{4,12},{6,14},{8,16},{10,18},{12,20},{14,22},{16,24},... | collective-permute-start | bytes 331784 | tf_op jit(solution)/shard_map/ppermute | solution.py:41
  372.2 22.8 %collective-permute-start.38 = (bf16[64,2048]{1,0:T(8,128)(2,1)}, bf16[64,2048]{1,0:T(8,128)(2,1)}, u32[]{:S(2)}, u32[]{:S(2)}) collective-permute-start(bf16[64,2048]{1,0:T(8,128)(2,1)} %fusion.36), channel_id=1, source_target_pairs={{0,8},{1,9},{2,10},{3,11},{4,12},{5,13},{6,14},{7,15},{8,0},{9,1},... | collective-permute-start | bytes 786440 | tf_op jit(solution)/shard_map/ppermute | solution.py:56
  376.3 39.9 %all-to-all-start.1 = ((bf16[8,960,128]{2,1,0:T(8,128)(2,1)}), bf16[8,960,128]{2,1,0:T(8,128)(2,1)S(1)}, u32[]{:S(2)}, u32[]{:S(2)}) async-start(bf16[8,960,128]{2,1,0:T(8,128)(2,1)} %reduce-scatter.3.cloned.1.call-done), calls=%async_computation.2 | async-start | bytes 3932160 | tf_op jit(solution)/shard_map/all_to_all | solution.py:160
  401.8 16.0 %copy-start.12 = (bf16[128,1664]{1,0:T(8,128)(2,1)S(1)}, bf16[128,1664]{1,0:T(8,128)(2,1)}, u32[]{:S(2)}) copy-start(bf16[128,1664]{1,0:T(8,128)(2,1)} %pack_weights.1) | copy-start | bytes 1277956
  419.0 8.5 %collective-permute-start.44 = (f32[264]{0:T(512)S(1)}, f32[264]{0:T(512)S(1)}, u32[]{:S(2)}, u32[]{:S(2)}) collective-permute-start(f32[264]{0:T(512)S(1)} %pad_maximum_fusion.16), channel_id=1, source_target_pairs={{0,1},{1,0},{2,3},{3,2},{4,5},{5,4},{6,7},{7,6},{8,9},{9,8},{10,11... | collective-permute-start | bytes 3176 | tf_op jit(solution)/shard_map/ppermute | solution.py:31
  421.2 7.4 %collective-permute-start.43 = (bf16[128,384]{1,0:T(8,128)(2,1)S(1)}, bf16[128,384]{1,0:T(8,128)(2,1)S(1)}, u32[]{:S(2)}, u32[]{:S(2)}) collective-permute-start(bf16[128,384]{1,0:T(8,128)(2,1)S(1)} %slice.560), channel_id=1, source_target_pairs={{0,1},{1,0},{2,3},{3,2},{4,5},{5,4},{6,7},{7,6},{8,9},{9,8},{10,11... | collective-permute-start | bytes 294920 | tf_op jit(solution)/shard_map/ppermute | solution.py:31
  421.9 8.7 %collective-permute-start.39 = (bf16[64,2048]{1,0:T(8,128)(2,1)}, bf16[64,2048]{1,0:T(8,128)(2,1)S(1)}, u32[]{:S(2)}, u32[]{:S(2)}) collective-permute-start(bf16[64,2048]{1,0:T(8,128)(2,1)} %add_convert_fusion.9), channel_id=1, source_target_pairs={{0,1},{1,0},{2,3},{3,2},{4,5},{5,4},{6,7},{7,6},{8,9},{9,8},{10,11... | collective-permute-start | bytes 786440 | tf_op jit(solution)/shard_map/ppermute | solution.py:31
  (24 other events, 93.4 us)
Sparse Core Ops, SparseCore 0:
  10.3 70.5 all-gather.1
  245.6 106.8 reduce-scatter.2
  355.5 44.2 reduce-scatter.4

commit v7 on v6

--- a/solution.py
+++ b/solution.py
@@ -760,8 +760,7 @@
     grad_oq = jnp.concatenate([grad_o, grad_q], axis=2)
     grad_oq = lax.psum_scatter(
         grad_oq, "row", scatter_dimension=0, tiled=True, axis_index_groups=far_groups()
-    )[0].astype(F32)
-    grad_o, grad_q = grad_oq[:, :q_width].T, grad_oq[:, q_width:]
+    )
     d_kv, k_gain_part = kv_back_call(kv_parts, raw, kv_gain, kv_flag, cosine, sine)
     d_one = jnp.concatenate([d_q, d_kv], axis=1)
 
@@ -782,6 +781,8 @@
     grad_kv, grads_ff, ffn_out = lax.optimization_barrier(
         (over_far(kv_partial, rows, True, True), grads_ff, halve(ffn_out, 0, 2 * cols))
     )
+    grad_oq = after(grad_oq, grads_ff)[0].astype(F32)
+    grad_o, grad_q = grad_oq[:, :q_width].T, grad_oq[:, q_width:]
     out_half = (hidden + ffn_out).astype(BF16)
     output = halves(out_half, swap_col(out_half), col)
     grad_kv = add_up(grad_kv)

time: 445 us -> 460 us (1.034)
  waiting for transfers between devices: 195 us -> 211 us
  starting transfers between devices: 75 us -> 80.2 us
    ppermute x16, waiting for transfers between devices: 108 us -> 123 us  [swap_cube(): return lax.ppermute(block, ('row', 'col'), route)]
    all_to_all x1, waiting for transfers between devices: 11.7 us -> 0.01 us  [exchange_group(): lax.all_to_all(blocks, 'row', split_axis=0, concat_axis=0, tiled=True, ax...]
    ppermute x5, waiting for transfers between devices: 48.5 us -> 58.8 us  [swap_near(): return lax.ppermute(block, 'row', [(i, i ^ 2) for i in range(rows)])]
    ppermute x16, starting transfers between devices: 24.5 us -> 29.6 us  [swap_cube(): return lax.ppermute(block, ('row', 'col'), route)]
    unnamed x106 -> x116, local copies, waits for them, and re-layouts: 14.7 us -> 13.4 us
  transfers between devices with their start and end apart: 50 -> 50, of which waited for: 26 -> 26; matrix products, arithmetic and copies ran while one was open for 19% -> 18% of each run, Pallas kernels for 9% -> 8%
where the time goes in v7:
time: 460 us; the launch traced here: 455 us
  waiting for transfers between devices  211 us (46%)
  starting transfers between devices  80.2 us (17%)
  Pallas kernels  45.4 us (10%)
  other arithmetic  41.9 us (9%)
  matrix products  30.5 us (7%)
  local copies, waits for them, and re-layouts  28 us (6%)
  between operations  18 us (4%)
    ppermute x16, waiting for transfers between devices, swap_cube(): return lax.ppermute(block, ('row', 'col'), route)  123 us
    ppermute x5, waiting for transfers between devices, swap_near(): return lax.ppermute(block, 'row', [(i, i ^ 2) for i in range(rows)])  58.8 us
    dot_general x9, matrix products, dot(): return lax.dot_general(a, b, (dims, ((), ())), preferred_element_type=F32)  30.5 us
    ppermute x16, starting transfers between devices, swap_cube(): return lax.ppermute(block, ('row', 'col'), route)  29.6 us
    ppermute x9, starting transfers between devices, shift_far(): return lax.ppermute(block, 'row', route)  22 us
    ppermute x6, waiting for transfers between devices, swap_col(): return lax.ppermute(block, 'col', [(0, 1), (1, 0)])  15 us
    unnamed x116, local copies, waits for them, and re-layouts  13.4 us
    pallas_call x1, Pallas kernels, ff_grads_call(): pl.pallas_call(ff_grads_kernel, grid=(rows // parts,), in_specs=[column,...  11.2 us
  transfers between devices with their start and end apart: 50, of which 26 were waited for; matrix products, arithmetic and copies ran while one was open for 18% of the time, Pallas kernels for 8%

profile of v7, /device:TPU:0, one launch (start us, length us, event | category | flops | bytes accessed | tf_op | source)
XLA Modules:
  0.0 454.5 jit_solution(14198794413777565585)
XLA Ops:
  7.2 2.0 pack_weights.1
  9.3 1.7 constant_dynamic-update-slice_fusion.4
  11.0 3.0 collective-permute-start
  14.0 6.3 %collective-permute-done = bf16[64,2048]{1,0:T(8,128)(2,1)S(1)} collective-permute-done((bf16[64,2048]{1,0:T(8,128)(2,1)S(1)}, bf16[64,2048]{1,0:T(8,128)(2,1)S(1)}, u32[]{:S(2)}, u32[]{:S(2)}) %collective-permute-start) | collective-permute-done | bytes 262176 | tf_op jit(solution)/shard_map/ppermute | solution.py:56
  20.4 1.8 collective-permute-start.1
  22.1 16.0 %collective-permute-done.1 = bf16[128,2048]{1,0:T(8,128)(2,1)S(1)} collective-permute-done((bf16[128,2048]{1,0:T(8,128)(2,1)S(1)}, bf16[128,2048]{1,0:T(8,128)(2,1)S(1)}, u32[]{:S(2)}, u32[]{:S(2)}) %collective-permute-start.1) | collective-permute-done | bytes 524320 | tf_op jit(solution)/shard_map/ppermute | solution.py:56
  41.3 21.8 %collective-permute-done.2 = bf16[256,2048]{1,0:T(8,128)(2,1)S(1)} collective-permute-done((bf16[256,2048]{1,0:T(8,128)(2,1)}, bf16[256,2048]{1,0:T(8,128)(2,1)S(1)}, u32[]{:S(2)}, u32[]{:S(2)}) %collective-permute-start.2) | collective-permute-done | bytes 1048608 | tf_op jit(solution)/shard_map/ppermute | solution.py:56
  65.9 2.2 copy.78
  69.4 1.6 maximum_bitcast_fusion
  74.7 3.2 constant_dynamic-update-slice_fusion.og_ref
  77.9 3.0 all-gather.2.cloned.1.call-done.w_ref
  80.9 5.7 %project_heads.1 = (f32[128,1024]{1,0:T(8,128)}, bf16[128,1024]{1,0:T(8,128)(2,1)}, bf16[128,384]{1,0:T(8,128)(2,1)}) custom-call(bf16[128,2048]{1,0:T(8,128)(2,1)} %multiply_convert_fusion.3.act_ref.left_ref, bf16[2048,1664]{1,0:T(8,128)(2,1)} %all-gather.2.cloned.1.call-done.w_ref, f32[1,1024]{1,0:T(1,128)} %pad_maximum_fusion.15.gain_ref, ...), custom_call_target="tpu_custom_call" | custom-call | flops 536870912 | bytes 4194304 | tf_op jit(solution)/shard_map/project_heads/pallas_call | solution.py:226
  86.6 3.9 collective-permute-start.6
  91.7 2.5 collective-permute-start.4
  94.2 2.2 pad_maximum_fusion
  97.5 7.3 %all-to-all-start = ((bf16[16,128,960]{1,2,0:T(8,128)(2,1)}), bf16[16,128,960]{1,2,0:T(8,128)(2,1)}, u32[]{:S(2)}, u32[]{:S(2)}) async-start(bf16[16,128,960]{1,2,0:T(8,128)(2,1)} %pad_maximum_fusion), calls=%async_computation | async-start | bytes 7864320 | tf_op jit(solution)/shard_map/all_to_all | solution.py:665
  104.9 1.9 collective-permute-start.7
  106.8 37.8 %collective-permute-done.7 = bf16[4,128,384]{2,1,0:T(8,128)(2,1)S(1)} collective-permute-done((bf16[4,128,384]{2,1,0:T(8,128)(2,1)S(1)}, bf16[4,128,384]{2,1,0:T(8,128)(2,1)S(1)}, u32[]{:S(2)}, u32[]{:S(2)}) %collective-permute-start.7) | collective-permute-done | bytes 393248 | tf_op jit(solution)/shard_map/ppermute | solution.py:46
  150.7 4.2 attention_forward.1
  154.8 2.8 convolution_convert_fusion.3
  157.7 1.6 collective-permute-start.9
  159.4 7.0 %collective-permute-done.9 = bf16[64,2048]{1,0:T(8,128)(2,1)S(1)} collective-permute-done((bf16[64,2048]{1,0:T(8,128)(2,1)S(1)}, bf16[64,2048]{1,0:T(8,128)(2,1)S(1)}, u32[]{:S(2)}, u32[]{:S(2)}) %collective-permute-start.9) | collective-permute-done | bytes 262176 | tf_op jit(solution)/shard_map/ppermute | solution.py:31
  169.7 5.6 %collective-permute-done.10 = bf16[64,2048]{1,0:T(8,128)(2,1)S(1)} collective-permute-done((bf16[64,2048]{1,0:T(8,128)(2,1)S(1)}, bf16[64,2048]{1,0:T(8,128)(2,1)S(1)}, u32[]{:S(2)}, u32[]{:S(2)}) %collective-permute-start.10) | collective-permute-done | bytes 262176 | tf_op jit(solution)/shard_map/ppermute | solution.py:56
  176.2 3.5 collective-permute-start.11
  179.7 2.8 copy_bitcast_fusion
  182.5 12.5 %collective-permute-done.13 = bf16[2,64,2048]{2,1,0:T(8,128)(2,1)S(1)} collective-permute-done((bf16[2,64,2048]{2,1,0:T(8,128)(2,1)}, bf16[2,64,2048]{2,1,0:T(8,128)(2,1)S(1)}, u32[]{:S(2)}, u32[]{:S(2)}) %collective-permute-start.13) | collective-permute-done | bytes 524320 | tf_op jit(solution)/shard_map/ppermute | solution.py:56
  195.0 8.5 %collective-permute-done.12 = bf16[2,64,2048]{2,1,0:T(8,128)(2,1)S(1)} collective-permute-done((bf16[2,64,2048]{2,1,0:T(8,128)(2,1)}, bf16[2,64,2048]{2,1,0:T(8,128)(2,1)S(1)}, u32[]{:S(2)}, u32[]{:S(2)}) %collective-permute-start.12) | collective-permute-done | bytes 524320 | tf_op jit(solution)/shard_map/ppermute | solution.py:56
  203.6 1.7 collective-permute-done.11
  205.7 4.0 collective-permute-done.14
  209.9 3.4 fusion.10
  213.3 5.8 %multiply_convert_fusion.1 = (bf16[1024,320]{1,0:T(8,128)(2,1)S(1)}, bf16[1024,320]{1,0:T(8,128)(2,1)S(1)}, bf16[1024,320]{1,0:T(8,128)(2,1)}) fusion(f32[1024,640]{1,0:T(8,128)S(1)} %fusion.10, bf16[1024,2048]{1,0:T(8,128)(2,1)} %constant_dynamic-update-slice_fusion.og_ref, bf16[2048,960]{0,1:T(8,128)(2,1)S(1)} %copy_bitcast_fusion), kind=kOutput, calls=%fused_computation.26 | convolution fusion | flops 1347092480 | bytes 10616832 | tf_op jit(solution)/shard_map/dot_general | solution.py:22
  219.1 1.8 convolution_convert_fusion.2
  222.6 2.5 collective-permute-done.15
  225.2 1.8 add_convert_fusion.1
  231.9 11.2 %feed_forward_weight_grads.1 = bf16[16,960,128]{2,1,0:T(8,128)(2,1)} custom-call(bf16[1024,2048]{1,0:T(8,128)(2,1)} %copy-done.6, bf16[1024,2048]{1,0:T(8,128)(2,1)} %constant_dynamic-update-slice_fusion.og_ref, bf16[1024,640]{1,0:T(8,128)(2,1)} %pad_maximum_fusion.2.d_ref, bf16[1024,320]{1,0:T(8,128)(2,1)} %get-tuple-element.103.inner_ref), custom_call_target="tpu_custom_call" | custom-call | tf_op jit(solution)/shard_map/feed_forward_weight_grads/pallas_call | solution.py:343
  249.5 3.9 convolution_convert_fusion
  253.5 3.9 convolution_convert_fusion.1
  259.6 2.9 collective-permute-done.21
  262.6 2.8 collective-permute-done.20
  267.9 4.3 collective-permute-done.22
  272.3 3.1 fusion.13.grad_ref
  275.4 6.7 %attention_backward.1 = (bf16[128,640]{1,0:T(8,128)(2,1)}, f32[1,128]{1,0:T(1,128)}, bf16[2,4,128,384]{3,2,1,0:T(8,128)(2,1)}, bf16[2,4,128,384]{3,2,1,0:T(8,128)(2,1)}) custom-call(s32[2]{0:T(128)} %pad_add_fusion.1.bounds_ref, s32[2,128]{1,0:T(2,128)} %pad_add_fusion.limits_ref, bf16[128,1024]{1,0:T(8,128)(2,1)} %get-tuple-element.82.q_ref, ...), custom_call_target="tpu_custom_call" | custom-call | tf_op jit(solution)/shard_map/attention_backward/pallas_call | solution.py:526
  286.7 3.1 weight_rows.3
  291.4 3.1 weight_rows.4
  294.6 3.0 add_convert_fusion
  297.8 1.6 collective-permute-start.31
  299.4 1.6 add_convert_fusion.3
  308.1 15.2 %collective-permute-done.31 = bf16[2,2,64,2048]{3,2,1,0:T(8,128)(2,1)S(1)} collective-permute-done((bf16[2,2,64,2048]{3,2,1,0:T(8,128)(2,1)S(1)}, bf16[2,2,64,2048]{3,2,1,0:T(8,128)(2,1)S(1)}, u32[]{:S(2)}, u32[]{:S(2)}) %collective-permute-start.31) | collective-permute-done | bytes 1048608 | tf_op jit(solution)/shard_map/ppermute | solution.py:56
  323.3 1.7 convert_add_fusion
  325.0 2.2 collective-permute-done.28.refs_2_
  328.0 2.5 key_value_heads_back.1
  332.2 2.8 weight_rows.5
  339.9 12.7 %collective-permute-done.42 = bf16[4,128,640]{2,1,0:T(8,128)(2,1)S(1)} collective-permute-done((bf16[4,128,640]{2,1,0:T(8,128)(2,1)S(1)}, bf16[4,128,640]{2,1,0:T(8,128)(2,1)S(1)}, u32[]{:S(2)}, u32[]{:S(2)}) %collective-permute-start.42) | collective-permute-done | bytes 655392 | tf_op jit(solution)/shard_map/ppermute | solution.py:46
  354.8 7.1 %collective-permute-done.33 = bf16[4,144,384]{2,1,0:T(8,128)(2,1)} collective-permute-done((bf16[4,144,384]{2,1,0:T(8,128)(2,1)}, bf16[4,144,384]{2,1,0:T(8,128)(2,1)}, u32[]{:S(2)}, u32[]{:S(2)}) %collective-permute-start.33) | collective-permute-done | bytes 442400 | tf_op jit(solution)/shard_map/ppermute | solution.py:46
  361.9 1.9 add_convert_fusion.8
  363.8 6.5 %all-to-all-start.1 = ((bf16[8,960,128]{2,1,0:T(8,128)(2,1)}), bf16[8,960,128]{2,1,0:T(8,128)(2,1)S(1)}, u32[]{:S(2)}, u32[]{:S(2)}) async-start(bf16[8,960,128]{2,1,0:T(8,128)(2,1)} %reduce-scatter.3.cloned.1.call-done), calls=%async_computation.2 | async-start | bytes 3932160 | tf_op jit(solution)/shard_map/all_to_all | solution.py:160
  370.3 3.9 fusion.2
  375.8 2.1 collective-permute-start.37
  378.6 9.2 %collective-permute-start.36 = (bf16[144,384]{1,0:T(8,128)(2,1)S(1)}, bf16[144,384]{1,0:T(8,128)(2,1)S(1)}, u32[]{:S(2)}, u32[]{:S(2)}) collective-permute-start(bf16[144,384]{1,0:T(8,128)(2,1)S(1)} %get-tuple-element.238), channel_id=1, source_target_pairs={{0,24},{2,26},{4,28},{6,30},{8,0},{10,2},{12,4},{14,6},{16,8},{18,... | collective-permute-start | bytes 331784 | tf_op jit(solution)/shard_map/ppermute | solution.py:41
  389.2 10.7 %collective-permute-done.37 = bf16[2,64,2048]{2,1,0:T(8,128)(2,1)S(1)} collective-permute-done((bf16[2,64,2048]{2,1,0:T(8,128)(2,1)S(1)}, bf16[2,64,2048]{2,1,0:T(8,128)(2,1)S(1)}, u32[]{:S(2)}, u32[]{:S(2)}) %collective-permute-start.37) | collective-permute-done | bytes 524320 | tf_op jit(solution)/shard_map/ppermute | solution.py:56
  400.1 7.5 %collective-permute-start.38 = (bf16[64,2048]{1,0:T(8,128)(2,1)S(1)}, bf16[64,2048]{1,0:T(8,128)(2,1)S(1)}, u32[]{:S(2)}, u32[]{:S(2)}) collective-permute-start(bf16[64,2048]{1,0:T(8,128)(2,1)S(1)} %fusion.36), channel_id=1, source_target_pairs={{0,8},{1,9},{2,10},{3,11},{4,12},{5,13},{6,14},{7,15},{8,0},{9,1},... | collective-permute-start | bytes 786440 | tf_op jit(solution)/shard_map/ppermute | solution.py:56
  409.1 17.6 %collective-permute-done.38 = bf16[64,2048]{1,0:T(8,128)(2,1)S(1)} collective-permute-done((bf16[64,2048]{1,0:T(8,128)(2,1)S(1)}, bf16[64,2048]{1,0:T(8,128)(2,1)S(1)}, u32[]{:S(2)}, u32[]{:S(2)}) %collective-permute-start.38) | collective-permute-done | bytes 262176 | tf_op jit(solution)/shard_map/ppermute | solution.py:56
  429.6 4.2 feed_forward_grads.1
  440.7 3.7 collective-permute-done.44
  (291 shorter events, 80.3 us)
Async XLA Ops:
  7.2 73.7 %all-gather.2.cloned.1.call-start = ((), (), s32[]{:S(2)}) async-start(), calls=%async_computation.4 | async-start | bytes 7241728 | tf_op jit(solution)/shard_map/all_gather | solution.py:633
  9.2 31.3 %copy-start.40 = (f32[64]{0:T(128)S(1)}, f32[64]{0:T(128)}, u32[]{:S(2)}) copy-start(f32[64]{0:T(128)} %param.23) | copy-start | bytes 772
  9.2 31.4 %copy-start.38 = (f32[64]{0:T(128)S(1)}, f32[64]{0:T(128)}, u32[]{:S(2)}) copy-start(f32[64]{0:T(128)} %param.24) | copy-start | bytes 772
  9.2 31.4 %copy-start.37 = (pred[3,128]{1,0:T(4,128)(4,1)S(1)}, pred[3,128]{1,0:T(4,128)(4,1)}, u32[]{:S(2)}) copy-start(pred[3,128]{1,0:T(4,128)(4,1)} %constant.199.clone.1) | copy-start | bytes 1156
  11.0 9.3 %collective-permute-start = (bf16[64,2048]{1,0:T(8,128)(2,1)S(1)}, bf16[64,2048]{1,0:T(8,128)(2,1)S(1)}, u32[]{:S(2)}, u32[]{:S(2)}) collective-permute-start(bf16[64,2048]{1,0:T(8,128)(2,1)S(1)} %get-tuple-element.217), channel_id=1, source_target_pairs={{0,8},{1,9},{2,10},{3,11},{4,12},{5,13},{6,14},{7,15},{8,0},{9,1},... | collective-permute-start | bytes 786440 | tf_op jit(solution)/shard_map/ppermute | solution.py:56
  20.4 17.7 %collective-permute-start.1 = (bf16[128,2048]{1,0:T(8,128)(2,1)S(1)}, bf16[128,2048]{1,0:T(8,128)(2,1)S(1)}, u32[]{:S(2)}, u32[]{:S(2)}) collective-permute-start(bf16[128,2048]{1,0:T(8,128)(2,1)S(1)} %pad_maximum_fusion.6), channel_id=1, source_target_pairs={{0,4},{1,5},{2,6},{3,7},{4,0},{5,1},{6,2},{7,3},{8,12},{9,13},{10,... | collective-permute-start | bytes 1572872 | tf_op jit(solution)/shard_map/ppermute | solution.py:56
  39.1 24.0 %collective-permute-start.2 = (bf16[256,2048]{1,0:T(8,128)(2,1)}, bf16[256,2048]{1,0:T(8,128)(2,1)S(1)}, u32[]{:S(2)}, u32[]{:S(2)}) collective-permute-start(bf16[256,2048]{1,0:T(8,128)(2,1)} %pad_maximum_fusion.4), channel_id=1, source_target_pairs={{0,1},{1,0},{2,3},{3,2},{4,5},{5,4},{6,7},{7,6},{8,9},{9,8},{10,11... | collective-permute-start | bytes 3145736 | tf_op jit(solution)/shard_map/ppermute | solution.py:56
  40.7 24.0 %copy-start.35 = (f32[1,1,3,128]{3,1,2,0:T(1,128)}, f32[1,1,3,128]{3,1,2,0:T(1,128)S(1)}, u32[]{:S(2)}) copy-start(f32[1,1,3,128]{3,1,2,0:T(1,128)S(1)} %copy.106) | copy-start | bytes 4612
  41.3 23.5 %copy-start.39 = (s32[128]{0:T(128)S(1)}, s32[128]{0:T(128)}, u32[]{:S(2)}) copy-start(s32[128]{0:T(128)} %param.26) | copy-start | bytes 1540
  41.3 23.5 %copy-start.23 = (bf16[128,2560]{1,0:T(8,128)(2,1)S(1)}, bf16[128,2560]{1,0:T(8,128)(2,1)}, u32[]{:S(2)}) copy-start(bf16[128,2560]{1,0:T(8,128)(2,1)} %param.18) | copy-start | bytes 1966084
  64.8 9.9 %collective-permute-start.3 = (bf16[512,2048]{1,0:T(8,128)(2,1)}, bf16[512,2048]{1,0:T(8,128)(2,1)}, u32[]{:S(2)}, u32[]{:S(2)}) collective-permute-start(bf16[512,2048]{1,0:T(8,128)(2,1)} %pad_maximum_fusion.1), channel_id=1, source_target_pairs={{0,2},{2,0},{4,6},{6,4},{8,10},{10,8},{12,14},{14,12},{16,18},{18,... | collective-permute-start | bytes 6291464 | tf_op jit(solution)/shard_map/ppermute | solution.py:27
  86.5 10.9 %copy-start.31 = (bf16[128,384]{1,0:T(8,128)(2,1)S(1)}, bf16[128,384]{1,0:T(8,128)(2,1)}, u32[]{:S(2)}) copy-start(bf16[128,384]{1,0:T(8,128)(2,1)} %get-tuple-element.83) | copy-start | bytes 294916
  86.6 9.9 %collective-permute-start.6 = (bf16[128,384]{1,0:T(8,128)(2,1)}, bf16[128,384]{1,0:T(8,128)(2,1)S(1)}, u32[]{:S(2)}, u32[]{:S(2)}) collective-permute-start(bf16[128,384]{1,0:T(8,128)(2,1)} %get-tuple-element.83), channel_id=1, source_target_pairs={{0,24},{2,26},{4,28},{6,30},{1,25},{3,27},{5,29},{7,31}} | collective-permute-start | bytes 294920 | tf_op jit(solution)/shard_map/ppermute | solution.py:41
  90.4 6.0 %collective-permute-start.5 = (bf16[128,384]{1,0:T(8,128)(2,1)}, bf16[128,384]{1,0:T(8,128)(2,1)S(1)}, u32[]{:S(2)}, u32[]{:S(2)}) collective-permute-start(bf16[128,384]{1,0:T(8,128)(2,1)} %get-tuple-element.83), channel_id=1, source_target_pairs={{0,16},{2,18},{4,20},{6,22},{8,24},{10,26},{12,28},{14,30},{1,17},... | collective-permute-start | bytes 294920 | tf_op jit(solution)/shard_map/ppermute | solution.py:41
  91.7 5.7 %collective-permute-start.4 = (bf16[128,384]{1,0:T(8,128)(2,1)}, bf16[128,384]{1,0:T(8,128)(2,1)S(1)}, u32[]{:S(2)}, u32[]{:S(2)}) collective-permute-start(bf16[128,384]{1,0:T(8,128)(2,1)} %get-tuple-element.83), channel_id=1, source_target_pairs={{0,8},{2,10},{4,12},{6,14},{8,16},{10,18},{12,20},{14,22},{16,24},... | collective-permute-start | bytes 294920 | tf_op jit(solution)/shard_map/ppermute | solution.py:41
  97.5 47.4 %copy-start.36 = (s32[2048]{0:T(1024)S(1)}, s32[2048]{0:T(1024)}, u32[]{:S(2)}) copy-start(s32[2048]{0:T(1024)} %param.25) | copy-start | bytes 24580
  97.5 82.1 %all-to-all-start = ((bf16[16,128,960]{1,2,0:T(8,128)(2,1)}), bf16[16,128,960]{1,2,0:T(8,128)(2,1)}, u32[]{:S(2)}, u32[]{:S(2)}) async-start(bf16[16,128,960]{1,2,0:T(8,128)(2,1)} %pad_maximum_fusion), calls=%async_computation | async-start | bytes 7864320 | tf_op jit(solution)/shard_map/all_to_all | solution.py:665
  104.9 258.9 %reduce-scatter.3.cloned.1.call-start = ((), (), s32[]{:S(2)}) async-start(), calls=%async_computation.5 | async-start | bytes 5898240 | tf_op jit(solution)/shard_map/reduce_scatter | solution.py:712
  104.9 39.8 %collective-permute-start.7 = (bf16[4,128,384]{2,1,0:T(8,128)(2,1)S(1)}, bf16[4,128,384]{2,1,0:T(8,128)(2,1)S(1)}, u32[]{:S(2)}, u32[]{:S(2)}) collective-permute-start(bf16[4,128,384]{2,1,0:T(8,128)(2,1)S(1)} %pad_maximum_fusion.11), channel_id=1, source_target_pairs={{0,4},{2,6},{4,0},{6,2},{8,12},{10,14},{12,8},{14,10},{16,20},{18,... | collective-permute-start | bytes 1179656 | tf_op jit(solution)/shard_map/ppermute | solution.py:46
  144.8 5.0 %collective-permute-start.8 = (bf16[2,4,128,384]{3,2,1,0:T(8,128)(2,1)S(1)}, bf16[2,4,128,384]{3,2,1,0:T(8,128)(2,1)S(1)}, u32[]{:S(2)}, u32[]{:S(2)}) collective-permute-start(bf16[2,4,128,384]{3,2,1,0:T(8,128)(2,1)S(1)} %pad_maximum_fusion.5.same_ref), channel_id=1, source_target_pairs={{0,2},{2,0},{4,6},{6,4},{8,10},{10,8},{12,14},{14,12},{16,18},{18,... | collective-permute-start | bytes 2359304 | tf_op jit(solution)/shard_map/ppermute | solution.py:27
  157.7 8.7 %collective-permute-start.9 = (bf16[64,2048]{1,0:T(8,128)(2,1)S(1)}, bf16[64,2048]{1,0:T(8,128)(2,1)S(1)}, u32[]{:S(2)}, u32[]{:S(2)}) collective-permute-start(bf16[64,2048]{1,0:T(8,128)(2,1)S(1)} %constant_dynamic-slice_fusion), channel_id=1, source_target_pairs={{0,1},{1,0},{2,3},{3,2},{4,5},{5,4},{6,7},{7,6},{8,9},{9,8},{10,11... | collective-permute-start | bytes 786440 | tf_op jit(solution)/shard_map/ppermute | solution.py:31
  167.5 7.9 %collective-permute-start.10 = (bf16[64,2048]{1,0:T(8,128)(2,1)S(1)}, bf16[64,2048]{1,0:T(8,128)(2,1)S(1)}, u32[]{:S(2)}, u32[]{:S(2)}) collective-permute-start(bf16[64,2048]{1,0:T(8,128)(2,1)S(1)} %get-tuple-element.213), channel_id=1, source_target_pairs={{0,1},{1,0},{2,3},{3,2},{4,5},{5,4},{6,7},{7,6},{8,9},{9,8},{10,11... | collective-permute-start | bytes 786440 | tf_op jit(solution)/shard_map/ppermute | solution.py:56
  176.2 18.8 %collective-permute-start.13 = (bf16[2,64,2048]{2,1,0:T(8,128)(2,1)}, bf16[2,64,2048]{2,1,0:T(8,128)(2,1)S(1)}, u32[]{:S(2)}, u32[]{:S(2)}) collective-permute-start(bf16[2,64,2048]{2,1,0:T(8,128)(2,1)} %pad_maximum_fusion.7), channel_id=1, source_target_pairs={{0,12},{1,13},{2,14},{3,15},{4,8},{5,9},{6,10},{7,11},{8,4},{9,5},... | collective-permute-start | bytes 1572872 | tf_op jit(solution)/shard_map/ppermute | solution.py:56
  176.2 27.4 %collective-permute-start.12 = (bf16[2,64,2048]{2,1,0:T(8,128)(2,1)}, bf16[2,64,2048]{2,1,0:T(8,128)(2,1)S(1)}, u32[]{:S(2)}, u32[]{:S(2)}) collective-permute-start(bf16[2,64,2048]{2,1,0:T(8,128)(2,1)} %pad_maximum_fusion.7), channel_id=1, source_target_pairs={{0,4},{1,5},{2,6},{3,7},{4,0},{5,1},{6,2},{7,3},{8,12},{9,13},{10,... | collective-permute-start | bytes 1572872 | tf_op jit(solution)/shard_map/ppermute | solution.py:56
  176.2 29.0 %collective-permute-start.11 = (bf16[2,64,2048]{2,1,0:T(8,128)(2,1)}, bf16[2,64,2048]{2,1,0:T(8,128)(2,1)S(1)}, u32[]{:S(2)}, u32[]{:S(2)}) collective-permute-start(bf16[2,64,2048]{2,1,0:T(8,128)(2,1)} %pad_maximum_fusion.7), channel_id=1, source_target_pairs={{0,8},{1,9},{2,10},{3,11},{4,12},{5,13},{6,14},{7,15},{8,0},{9,1},... | collective-permute-start | bytes 1572872 | tf_op jit(solution)/shard_map/ppermute | solution.py:56
  179.7 25.5 %copy-start.34 = (bf16[512,2048]{1,0:T(8,128)(2,1)S(1)}, bf16[512,2048]{1,0:T(8,128)(2,1)}, u32[]{:S(2)}) copy-start(bf16[512,2048]{1,0:T(8,128)(2,1)} %get-tuple-element.212) | copy-start | bytes 6291460
  179.7 25.7 %copy-start.5 = (bf16[1024,2048]{1,0:T(8,128)(2,1)S(1)}, bf16[1024,2048]{1,0:T(8,128)(2,1)}, u32[]{:S(2)}) copy-start(bf16[1024,2048]{1,0:T(8,128)(2,1)} %constant_dynamic-update-slice_fusion.9) | copy-start | bytes 12582916
  182.5 42.6 %copy-start.9 = (bf16[2048,960]{0,1:T(8,128)(2,1)}, bf16[2048,960]{0,1:T(8,128)(2,1)S(1)}, u32[]{:S(2)}) copy-start(bf16[2048,960]{0,1:T(8,128)(2,1)S(1)} %copy_bitcast_fusion) | copy-start | bytes 11796484
  205.5 4.2 collective-permute-start.14
  220.9 4.2 collective-permute-start.15
  228.9 14.2 %collective-permute-start.16 = (bf16[2,2,64,1024]{3,2,1,0:T(8,128)(2,1)}, bf16[2,2,64,1024]{3,2,1,0:T(8,128)(2,1)S(1)}, u32[]{:S(2)}, u32[]{:S(2)}) collective-permute-start(bf16[2,2,64,1024]{3,2,1,0:T(8,128)(2,1)} %slice_bitcast_fusion.2), channel_id=1, source_target_pairs={{0,1},{1,0},{2,3},{3,2},{4,5},{5,4},{6,7},{7,6},{8,9},{9,8},{10,11... | collective-permute-start | bytes 1572872 | tf_op jit(solution)/shard_map/ppermute | solution.py:56
  230.4 14.0 %collective-permute-start.17 = (bf16[2,2,64,1024]{3,2,0,1:T(8,128)(2,1)}, bf16[2,2,64,1024]{3,2,0,1:T(8,128)(2,1)}, u32[]{:S(2)}, u32[]{:S(2)}) collective-permute-start(bf16[2,2,64,1024]{3,2,0,1:T(8,128)(2,1)} %bitcast.183), channel_id=1, source_target_pairs={{0,4},{1,5},{2,6},{3,7},{4,0},{5,1},{6,2},{7,3},{8,12},{9,13},{10,... | collective-permute-start | bytes 1572872 | tf_op jit(solution)/shard_map/ppermute | solution.py:56
  245.7 188.3 %reduce-scatter.5.cloned.1.call-start = ((), (), s32[]{:S(2)}) async-start(), calls=%async_computation.6 | async-start | bytes 1638400 | tf_op jit(solution)/shard_map/reduce_scatter | solution.py:761
  247.3 10.0 %collective-permute-start.18 = (bf16[2,64,1024]{2,1,0:T(8,128)(2,1)S(1)}, bf16[2,64,1024]{2,1,0:T(8,128)(2,1)S(1)}, u32[]{:S(2)}, u32[]{:S(2)}) collective-permute-start(bf16[2,64,1024]{2,1,0:T(8,128)(2,1)S(1)} %slice_bitcast_fusion.9), channel_id=1, source_target_pairs={{0,4},{1,5},{2,6},{3,7},{4,0},{5,1},{6,2},{7,3},{8,12},{9,13},{10,... | collective-permute-start | bytes 786440 | tf_op jit(solution)/shard_map/ppermute | solution.py:56
  248.9 8.5 %collective-permute-start.19 = (bf16[2,64,1024]{2,1,0:T(8,128)(2,1)S(1)}, bf16[2,64,1024]{2,1,0:T(8,128)(2,1)S(1)}, u32[]{:S(2)}, u32[]{:S(2)}) collective-permute-start(bf16[2,64,1024]{2,1,0:T(8,128)(2,1)S(1)} %slice_bitcast_fusion.8), channel_id=1, source_target_pairs={{0,8},{1,9},{2,10},{3,11},{4,12},{5,13},{6,14},{7,15},{8,0},{9,1},... | collective-permute-start | bytes 786440 | tf_op jit(solution)/shard_map/ppermute | solution.py:56
  257.5 9.8 %copy-start.41 = (f32[64]{0:T(128)S(1)}, f32[64]{0:T(128)}, u32[]{:S(2)}) copy-start(f32[64]{0:T(128)} %param.23) | copy-start | bytes 772
  257.5 5.0 %collective-permute-start.21 = (bf16[64,1024]{1,0:T(8,128)(2,1)S(1)}, bf16[64,1024]{1,0:T(8,128)(2,1)S(1)}, u32[]{:S(2)}, u32[]{:S(2)}) collective-permute-start(bf16[64,1024]{1,0:T(8,128)(2,1)S(1)} %slice_bitcast_fusion.11), channel_id=1, source_target_pairs={{0,1},{1,0},{2,3},{3,2},{4,5},{5,4},{6,7},{7,6},{8,9},{9,8},{10,11... | collective-permute-start | bytes 393224 | tf_op jit(solution)/shard_map/ppermute | solution.py:56
  258.1 7.2 %collective-permute-start.20 = (bf16[64,1024]{1,0:T(8,128)(2,1)S(1)}, bf16[64,1024]{1,0:T(8,128)(2,1)S(1)}, u32[]{:S(2)}, u32[]{:S(2)}) collective-permute-start(bf16[64,1024]{1,0:T(8,128)(2,1)S(1)} %slice_bitcast_fusion.13), channel_id=1, source_target_pairs={{0,8},{1,9},{2,10},{3,11},{4,12},{5,13},{6,14},{7,15},{8,0},{9,1},... | collective-permute-start | bytes 393224 | tf_op jit(solution)/shard_map/ppermute | solution.py:56
  265.8 6.4 %collective-permute-start.22 = (bf16[64,2048]{1,0:T(8,128)(2,1)S(1)}, bf16[64,2048]{1,0:T(8,128)(2,1)S(1)}, u32[]{:S(2)}, u32[]{:S(2)}) collective-permute-start(bf16[64,2048]{1,0:T(8,128)(2,1)S(1)} %add_convert_fusion.10), channel_id=1, source_target_pairs={{0,1},{1,0},{2,3},{3,2},{4,5},{5,4},{6,7},{7,6},{8,9},{9,8},{10,11... | collective-permute-start | bytes 786440 | tf_op jit(solution)/shard_map/ppermute | solution.py:31
  267.9 26.7 %collective-permute-start.30 = (bf16[512,2048]{1,0:T(8,128)(2,1)}, bf16[512,2048]{1,0:T(8,128)(2,1)}, u32[]{:S(2)}, u32[]{:S(2)}) collective-permute-start(bf16[512,2048]{1,0:T(8,128)(2,1)} %convolution_convert_fusion.1), channel_id=1, source_target_pairs={{0,2},{2,0},{4,6},{6,4},{8,10},{10,8},{12,14},{14,12},{16,18},{18,... | collective-permute-start | bytes 6291464 | tf_op jit(solution)/shard_map/ppermute | solution.py:27
  272.3 10.5 %copy-start.12 = (bf16[64,2048]{1,0:T(8,128)(2,1)}, bf16[64,2048]{1,0:T(8,128)(2,1)S(1)}, u32[]{:S(2)}) copy-start(bf16[64,2048]{1,0:T(8,128)(2,1)S(1)} %get-tuple-element.231) | copy-start | bytes 786436
  282.0 2.5 collective-permute-start.23
  289.8 9.6 %collective-permute-start.25 = (bf16[8,128,640]{2,1,0:T(8,128)(2,1)}, bf16[8,128,640]{2,1,0:T(8,128)(2,1)}, u32[]{:S(2)}, u32[]{:S(2)}) collective-permute-start(bf16[8,128,640]{2,1,0:T(8,128)(2,1)} %get-tuple-element.114), channel_id=1, source_target_pairs={{0,2},{2,0},{4,6},{6,4},{8,10},{10,8},{12,14},{14,12},{16,18},{18,... | collective-permute-start | bytes 3932168 | tf_op jit(solution)/shard_map/ppermute | solution.py:27
  290.9 11.7 %collective-permute-start.24 = (bf16[4,128,384]{2,1,0:T(8,128)(2,1)}, bf16[4,128,384]{2,1,0:T(8,128)(2,1)S(1)}, u32[]{:S(2)}, u32[]{:S(2)}) collective-permute-start(bf16[4,128,384]{2,1,0:T(8,128)(2,1)} %slice_bitcast_fusion.4), channel_id=1, source_target_pairs={{0,4},{2,6},{4,0},{6,2},{8,12},{10,14},{12,8},{14,10},{16,20},{18,... | collective-permute-start | bytes 1179656 | tf_op jit(solution)/shard_map/ppermute | solution.py:46
  294.6 6.5 %collective-permute-start.26 = (bf16[8,128,640]{2,1,0:T(8,128)(2,1)}, bf16[8,128,640]{2,1,0:T(8,128)(2,1)S(1)}, u32[]{:S(2)}, u32[]{:S(2)}) collective-permute-start(bf16[8,128,640]{2,1,0:T(8,128)(2,1)} %get-tuple-element.118), channel_id=1, source_target_pairs={{0,2},{2,0},{4,6},{6,4},{8,10},{10,8},{12,14},{14,12},{16,18},{18,... | collective-permute-start | bytes 3932168 | tf_op jit(solution)/shard_map/ppermute | solution.py:27
  297.8 25.6 %collective-permute-start.31 = (bf16[2,2,64,2048]{3,2,1,0:T(8,128)(2,1)S(1)}, bf16[2,2,64,2048]{3,2,1,0:T(8,128)(2,1)S(1)}, u32[]{:S(2)}, u32[]{:S(2)}) collective-permute-start(bf16[2,2,64,2048]{3,2,1,0:T(8,128)(2,1)S(1)} %slice_bitcast_fusion), channel_id=1, source_target_pairs={{0,1},{1,0},{2,3},{3,2},{4,5},{5,4},{6,7},{7,6},{8,9},{9,8},{10,11... | collective-permute-start | bytes 3145736 | tf_op jit(solution)/shard_map/ppermute | solution.py:56
  303.4 21.7 %collective-permute-start.29 = (bf16[128,384]{1,0:T(8,128)(2,1)S(1)}, bf16[128,384]{1,0:T(8,128)(2,1)S(1)}, u32[]{:S(2)}, u32[]{:S(2)}) collective-permute-start(bf16[128,384]{1,0:T(8,128)(2,1)S(1)} %get-tuple-element.244), channel_id=1, source_target_pairs={{24,0},{26,2},{28,4},{30,6},{25,1},{27,3},{29,5},{31,7}} | collective-permute-start | bytes 294920 | tf_op jit(solution)/shard_map/ppermute | solution.py:41
  304.6 22.6 %collective-permute-start.28 = (bf16[128,384]{1,0:T(8,128)(2,1)S(1)}, bf16[128,384]{1,0:T(8,128)(2,1)S(1)}, u32[]{:S(2)}, u32[]{:S(2)}) collective-permute-start(bf16[128,384]{1,0:T(8,128)(2,1)S(1)} %get-tuple-element.245), channel_id=1, source_target_pairs={{16,0},{18,2},{20,4},{22,6},{24,8},{26,10},{28,12},{30,14},{17,1},... | collective-permute-start | bytes 294920 | tf_op jit(solution)/shard_map/ppermute | solution.py:41
  305.9 21.3 %collective-permute-start.27 = (bf16[128,384]{1,0:T(8,128)(2,1)S(1)}, bf16[128,384]{1,0:T(8,128)(2,1)S(1)}, u32[]{:S(2)}, u32[]{:S(2)}) collective-permute-start(bf16[128,384]{1,0:T(8,128)(2,1)S(1)} %get-tuple-element.246), channel_id=1, source_target_pairs={{8,0},{10,2},{12,4},{14,6},{16,8},{18,10},{20,12},{22,14},{24,16},... | collective-permute-start | bytes 294920 | tf_op jit(solution)/shard_map/ppermute | solution.py:41
  307.6 28.8 %collective-permute-start.41 = (bf16[4,128,640]{2,1,0:T(8,128)(2,1)S(1)}, bf16[4,128,640]{2,1,0:T(8,128)(2,1)}, u32[]{:S(2)}, u32[]{:S(2)}) collective-permute-start(bf16[4,128,640]{2,1,0:T(8,128)(2,1)S(1)} %slice.330), channel_id=1, source_target_pairs={{0,4},{2,6},{4,0},{6,2},{8,12},{10,14},{12,8},{14,10},{16,20},{18,... | collective-permute-start | bytes 1966088 | tf_op jit(solution)/shard_map/ppermute | solution.py:46
  335.0 2.6 collective-permute-start.32
  335.1 17.6 %collective-permute-start.42 = (bf16[4,128,640]{2,1,0:T(8,128)(2,1)S(1)}, bf16[4,128,640]{2,1,0:T(8,128)(2,1)S(1)}, u32[]{:S(2)}, u32[]{:S(2)}) collective-permute-start(bf16[4,128,640]{2,1,0:T(8,128)(2,1)S(1)} %slice.332), channel_id=1, source_target_pairs={{0,4},{2,6},{4,0},{6,2},{8,12},{10,14},{12,8},{14,10},{16,20},{18,... | collective-permute-start | bytes 1966088 | tf_op jit(solution)/shard_map/ppermute | solution.py:46
  338.7 23.2 %collective-permute-start.33 = (bf16[4,144,384]{2,1,0:T(8,128)(2,1)}, bf16[4,144,384]{2,1,0:T(8,128)(2,1)}, u32[]{:S(2)}, u32[]{:S(2)}) collective-permute-start(bf16[4,144,384]{2,1,0:T(8,128)(2,1)} %slice.389), channel_id=1, source_target_pairs={{0,4},{2,6},{4,0},{6,2},{8,12},{10,14},{12,8},{14,10},{16,20},{18,... | collective-permute-start | bytes 1327112 | tf_op jit(solution)/shard_map/ppermute | solution.py:46
  363.8 64.2 %all-to-all-start.1 = ((bf16[8,960,128]{2,1,0:T(8,128)(2,1)}), bf16[8,960,128]{2,1,0:T(8,128)(2,1)S(1)}, u32[]{:S(2)}, u32[]{:S(2)}) async-start(bf16[8,960,128]{2,1,0:T(8,128)(2,1)} %reduce-scatter.3.cloned.1.call-done), calls=%async_computation.2 | async-start | bytes 3932160 | tf_op jit(solution)/shard_map/all_to_all | solution.py:160
  374.3 14.6 %collective-permute-start.40 = (bf16[128,2048]{1,0:T(8,128)(2,1)S(1)}, bf16[128,2048]{1,0:T(8,128)(2,1)S(1)}, u32[]{:S(2)}, u32[]{:S(2)}) collective-permute-start(bf16[128,2048]{1,0:T(8,128)(2,1)S(1)} %fusion.2), channel_id=1, source_target_pairs={{0,1},{1,0},{2,3},{3,2},{4,5},{5,4},{6,7},{7,6},{8,9},{9,8},{10,11... | collective-permute-start | bytes 1572872 | tf_op jit(solution)/shard_map/ppermute | solution.py:31
  375.8 24.1 %collective-permute-start.37 = (bf16[2,64,2048]{2,1,0:T(8,128)(2,1)S(1)}, bf16[2,64,2048]{2,1,0:T(8,128)(2,1)S(1)}, u32[]{:S(2)}, u32[]{:S(2)}) collective-permute-start(bf16[2,64,2048]{2,1,0:T(8,128)(2,1)S(1)} %fusion.27), channel_id=1, source_target_pairs={{0,4},{1,5},{2,6},{3,7},{4,0},{5,1},{6,2},{7,3},{8,12},{9,13},{10,... | collective-permute-start | bytes 1572872 | tf_op jit(solution)/shard_map/ppermute | solution.py:56
  378.6 48.1 %collective-permute-start.36 = (bf16[144,384]{1,0:T(8,128)(2,1)S(1)}, bf16[144,384]{1,0:T(8,128)(2,1)S(1)}, u32[]{:S(2)}, u32[]{:S(2)}) collective-permute-start(bf16[144,384]{1,0:T(8,128)(2,1)S(1)} %get-tuple-element.238), channel_id=1, source_target_pairs={{0,24},{2,26},{4,28},{6,30},{8,0},{10,2},{12,4},{14,6},{16,8},{18,... | collective-permute-start | bytes 331784 | tf_op jit(solution)/shard_map/ppermute | solution.py:41
  387.7 39.0 %collective-permute-start.35 = (bf16[144,384]{1,0:T(8,128)(2,1)S(1)}, bf16[144,384]{1,0:T(8,128)(2,1)S(1)}, u32[]{:S(2)}, u32[]{:S(2)}) collective-permute-start(bf16[144,384]{1,0:T(8,128)(2,1)S(1)} %get-tuple-element.239), channel_id=1, source_target_pairs={{0,16},{2,18},{4,20},{6,22},{8,24},{10,26},{12,28},{14,30},{16,0},... | collective-permute-start | bytes 331784 | tf_op jit(solution)/shard_map/ppermute | solution.py:41
  387.7 19.8 %copy-start.13 = (bf16[64,2048]{1,0:T(8,128)(2,1)S(1)}, bf16[64,2048]{1,0:T(8,128)(2,1)}, u32[]{:S(2)}) copy-start(bf16[64,2048]{1,0:T(8,128)(2,1)} %copy-done.12) | copy-start | bytes 786436
  387.7 40.2 %collective-permute-start.34 = (bf16[144,384]{1,0:T(8,128)(2,1)S(1)}, bf16[144,384]{1,0:T(8,128)(2,1)}, u32[]{:S(2)}, u32[]{:S(2)}) collective-permute-start(bf16[144,384]{1,0:T(8,128)(2,1)S(1)} %get-tuple-element.240), channel_id=1, source_target_pairs={{0,8},{2,10},{4,12},{6,14},{8,16},{10,18},{12,20},{14,22},{16,24},... | collective-permute-start | bytes 331784 | tf_op jit(solution)/shard_map/ppermute | solution.py:41
  400.1 26.5 %collective-permute-start.38 = (bf16[64,2048]{1,0:T(8,128)(2,1)S(1)}, bf16[64,2048]{1,0:T(8,128)(2,1)S(1)}, u32[]{:S(2)}, u32[]{:S(2)}) collective-permute-start(bf16[64,2048]{1,0:T(8,128)(2,1)S(1)} %fusion.36), channel_id=1, source_target_pairs={{0,8},{1,9},{2,10},{3,11},{4,12},{5,13},{6,14},{7,15},{8,0},{9,1},... | collective-permute-start | bytes 786440 | tf_op jit(solution)/shard_map/ppermute | solution.py:56
  434.0 11.6 %collective-permute-start.43 = (bf16[128,384]{1,0:T(8,128)(2,1)S(1)}, bf16[128,384]{1,0:T(8,128)(2,1)S(1)}, u32[]{:S(2)}, u32[]{:S(2)}) collective-permute-start(bf16[128,384]{1,0:T(8,128)(2,1)S(1)} %slice.560), channel_id=1, source_target_pairs={{0,1},{1,0},{2,3},{3,2},{4,5},{5,4},{6,7},{7,6},{8,9},{9,8},{10,11... | collective-permute-start | bytes 294920 | tf_op jit(solution)/shard_map/ppermute | solution.py:31
  435.5 11.2 %collective-permute-start.39 = (bf16[64,2048]{1,0:T(8,128)(2,1)S(1)}, bf16[64,2048]{1,0:T(8,128)(2,1)S(1)}, u32[]{:S(2)}, u32[]{:S(2)}) collective-permute-start(bf16[64,2048]{1,0:T(8,128)(2,1)S(1)} %add_convert_fusion.9), channel_id=1, source_target_pairs={{0,1},{1,0},{2,3},{3,2},{4,5},{5,4},{6,7},{7,6},{8,9},{9,8},{10,11... | collective-permute-start | bytes 786440 | tf_op jit(solution)/shard_map/ppermute | solution.py:31
  438.2 6.2 %collective-permute-start.44 = (f32[264]{0:T(512)S(1)}, f32[264]{0:T(512)S(1)}, u32[]{:S(2)}, u32[]{:S(2)}) collective-permute-start(f32[264]{0:T(512)S(1)} %pad_maximum_fusion.16), channel_id=1, source_target_pairs={{0,1},{1,0},{2,3},{3,2},{4,5},{5,4},{6,7},{7,6},{8,9},{9,8},{10,11... | collective-permute-start | bytes 3176 | tf_op jit(solution)/shard_map/ppermute | solution.py:31
  (30 other events, 102.5 us)
Sparse Core Ops, SparseCore 0:
  10.3 70.5 all-gather.1
  245.8 106.8 reduce-scatter.2
  355.1 55.8 reduce-scatter.4
